TPU v7x, 32 devices: a whole 2x2x4 slice. The times are simulated.
32 devices in a mesh: blk: 16 (over z, y, core), fsdp: 2 (over x).
Axes of the slice: x: 2, y: 2, z: 4, core: 2. Of those that a mesh axis runs over, the one named last changes fastest.
Arguments:
- latents: bfloat16 [3, 16, 512, 1024], P(None, 'blk', 'fsdp'), may hold values from -6 to 6
- pixels: bfloat16 [3, 32768, 261], P(None, 'blk'), may hold values from -6 to 6
- segment_ids: int32 [3, 32768], P(None, 'blk'), may hold values from 0 to 16, as said below
- pad_ids: int32 [3], replicated, may hold values from 0 to 16
- block_map: int32 [3, 17], replicated, may hold values from 0 to 15, as said below
- norm_gains: bfloat16 [4, 1024], P(None, 'fsdp'), may hold values from 0.099609375 to 1.8984375
- norm_biases: bfloat16 [4, 1024], P(None, 'fsdp'), may hold values from -2 to 2
- pixel_gain: bfloat16 [261], replicated, may hold values from 0.099609375 to 1.8984375
- pixel_bias: bfloat16 [261], replicated, may hold values from -2 to 2
- cross_query: bfloat16 [1024, 1024], P('fsdp'), may hold values from -0.1875 to 0.1875
- cross_kv: bfloat16 [261, 2048], P(None, 'fsdp'), may hold values from -0.375 to 0.375
- cross_out: bfloat16 [1024, 1024], P('fsdp'), may hold values from -4 to 4
- cross_up: bfloat16 [1024, 1024], P('fsdp'), may hold values from -0.1875 to 0.1875
- cross_down: bfloat16 [1024, 1024], P('fsdp'), may hold values from -0.1875 to 0.1875
- self_qkv: bfloat16 [1024, 3072], P('fsdp'), may hold values from -0.1875 to 0.1875
- self_out: bfloat16 [1024, 1024], P('fsdp'), may hold values from -2 to 2
- self_up: bfloat16 [1024, 1024], P('fsdp'), may hold values from -0.1875 to 0.1875
- self_down: bfloat16 [1024, 1024], P('fsdp'), may hold values from -0.1875 to 0.1875
- cotangent: bfloat16 [3, 16, 512, 1024], P(None, 'blk', 'fsdp'), may hold values from -6 to 6
Outputs:
- mixed: bfloat16 [3, 16, 512, 1024], P(None, 'blk', 'fsdp')
- latents_grad: float32 [3, 16, 512, 1024], P(None, 'blk', 'fsdp')
- norm_gains_grad: float32 [4, 1024], P(None, 'fsdp')
- norm_biases_grad: float32 [4, 1024], P(None, 'fsdp')
- pixel_gain_grad: float32 [261], replicated
- pixel_bias_grad: float32 [261], replicated
- cross_query_grad: float32 [1024, 1024], P('fsdp')
- cross_kv_grad: float32 [261, 2048], P(None, 'fsdp')
- cross_out_grad: float32 [1024, 1024], P('fsdp')
- cross_up_grad: float32 [1024, 1024], P('fsdp')
- cross_down_grad: float32 [1024, 1024], P('fsdp')
- self_qkv_grad: float32 [1024, 3072], P('fsdp')
- self_out_grad: float32 [1024, 1024], P('fsdp')
- self_up_grad: float32 [1024, 1024], P('fsdp')
- self_down_grad: float32 [1024, 1024], P('fsdp')
Inputs may be any that keep to these rules, and one draw needn't show every extreme that they name: `segment_ids`: each value of 0 to 16 other than the micro-batch's pad id names one image. Images are packed one after another in increasing order of their values, each in consecutive slots, and the pad id fills the slots after the last image. An image has 1024 to 1792 slots, except one image of each micro-batch that has exactly 3072. `block_map`: over the values other than the micro-batch's pad id it is a permutation of the 16 latent blocks; at the pad id it holds some block.
All inputs are finite; a program needn't handle non-finite values.
Results may differ from a plain program's by a relative error of at most 0.02.
Values may be sent and summed in bfloat16 or wider, within the bound.
No kernel may reach another device: no remote copies, remote signals or barrier semaphores. Data moves between devices by JAX's collectives and lax.ppermute only.
A program may use at most 320 MiB of HBM per device.

v0:
```python
import jax
import jax.numpy as jnp
from jax import lax
from jax.sharding import PartitionSpec as P

HEADS = 8


epsilon = 1e-05
masked_score = -1e30


def merged(part, axis, combine):
    gathered = jax.tree.map(lambda a: lax.all_gather(a, axis), part)

    def take(source):
        return jax.tree.map(lambda a: lax.dynamic_index_in_dim(a, source, 0, False), gathered)

    return lax.fori_loop(
        1, lax.axis_size(axis), lambda source, state: combine(state, take(source)), take(0)
    )


def layer_norm(inputs, scaler, offset):
    centre = inputs - jnp.mean(inputs, axis=-1, keepdims=True)
    spread = jnp.mean(centre * centre, axis=-1, keepdims=True)
    return centre * lax.rsqrt(spread + epsilon) * scaler + offset


def product(matrix_a, matrix_b):
    return jnp.dot(matrix_a, matrix_b, preferred_element_type=jnp.float32)


def product_tn(matrix_a, matrix_b):
    return lax.dot_general(
        matrix_a, matrix_b, (((0,), (0,)), ((), ())), preferred_element_type=jnp.float32
    )


def product_nt(matrix_a, matrix_b):
    return lax.dot_general(
        matrix_a, matrix_b, (((1,), (1,)), ((), ())), preferred_element_type=jnp.float32
    )


def exact_gelu(inputs):
    return jax.nn.gelu(inputs, approximate=False)


def fetch_weights(
    gain_rows,
    bias_rows,
    cross_query,
    cross_kv,
    cross_out,
    cross_up,
    cross_down,
    self_qkv,
    self_out,
    self_up,
    self_down,
):
    return (
        lax.all_gather(gain_rows, "fsdp", axis=1, tiled=True),
        lax.all_gather(bias_rows, "fsdp", axis=1, tiled=True),
        lax.all_gather(cross_query, "fsdp", axis=0, tiled=True),
        lax.all_gather(cross_kv, "fsdp", axis=1, tiled=True),
        lax.all_gather(cross_out, "fsdp", axis=0, tiled=True),
        lax.all_gather(cross_up, "fsdp", axis=0, tiled=True),
        lax.all_gather(cross_down, "fsdp", axis=0, tiled=True),
        lax.all_gather(self_qkv, "fsdp", axis=0, tiled=True),
        lax.all_gather(self_out, "fsdp", axis=0, tiled=True),
        lax.all_gather(self_up, "fsdp", axis=0, tiled=True),
        lax.all_gather(self_down, "fsdp", axis=0, tiled=True),
    )


def feed_forward(inputs, scaler, offset, w_up, w_down):
    hidden, norm_back = jax.vjp(layer_norm, inputs, scaler, offset)
    hidden = hidden.astype(jnp.bfloat16)
    upward = product(hidden, w_up)
    active, gelu_back = jax.vjp(exact_gelu, upward)
    active = active.astype(jnp.bfloat16)
    return (product(active, w_down), (norm_back, hidden, gelu_back, active))


def feed_backward(upstream, stored, w_up, w_down):
    norm_back, hidden, gelu_back, active = stored
    grad_low = upstream.astype(jnp.bfloat16)
    grad_down = product_tn(active, grad_low)
    grad_active = product_nt(grad_low, w_down)
    grad_upward = gelu_back(grad_active)[0].astype(jnp.bfloat16)
    grad_up = product_tn(hidden, grad_upward)
    grad_hidden = product_nt(grad_upward, w_up)
    grad_inputs, grad_scaler, grad_offset = norm_back(grad_hidden)
    return (upstream + grad_inputs, grad_up, grad_down, grad_scaler, grad_offset)


def self_forward(inputs, scaler, offset, w_triple, w_self_out):
    row_count, model_width = inputs.shape
    head_size = model_width // HEADS
    hidden, norm_back = jax.vjp(layer_norm, inputs, scaler, offset)
    hidden = hidden.astype(jnp.bfloat16)
    triple = product(hidden, w_triple).astype(jnp.bfloat16)
    gathered = lax.all_gather(triple[:, model_width:], "fsdp", axis=0, tiled=True)
    q_heads = triple[:, :model_width].reshape(row_count, HEADS, head_size)
    k_heads = gathered[:, :model_width].reshape(-1, HEADS, head_size)
    v_heads = gathered[:, model_width:].reshape(-1, HEADS, head_size)
    scores = jnp.einsum(
        "qhd,khd->hqk", q_heads, k_heads, preferred_element_type=jnp.float32
    ) * head_size ** (-0.5)
    shares = jax.nn.softmax(scores, axis=-1)
    shares_low = shares.astype(jnp.bfloat16)
    blended = jnp.einsum("hqk,khd->qhd", shares_low, v_heads, preferred_element_type=jnp.float32)
    blended = blended.reshape(row_count, model_width).astype(jnp.bfloat16)
    return (
        product(blended, w_self_out),
        (norm_back, hidden, q_heads, k_heads, v_heads, shares, shares_low, blended),
    )


def self_backward(upstream, stored, w_triple, w_self_out):
    norm_back, hidden, q_heads, k_heads, v_heads, shares, shares_low, blended = stored
    row_count, head_count, head_size = q_heads.shape
    model_width = head_count * head_size
    scaling = head_size ** (-0.5)
    grad_low = upstream.astype(jnp.bfloat16)
    grad_self_out = product_tn(blended, grad_low)
    grad_blended = (
        product_nt(grad_low, w_self_out)
        .astype(jnp.bfloat16)
        .reshape(row_count, head_count, head_size)
    )
    grad_shares = jnp.einsum(
        "qhd,khd->hqk", grad_blended, v_heads, preferred_element_type=jnp.float32
    )
    inner_sum = jnp.sum(shares * grad_shares, axis=-1, keepdims=True)
    grad_scores = (shares * (grad_shares - inner_sum)).astype(jnp.bfloat16)
    grad_q = (
        jnp.einsum("hqk,khd->qhd", grad_scores, k_heads, preferred_element_type=jnp.float32)
        * scaling
    )
    grad_k = (
        jnp.einsum("hqk,qhd->khd", grad_scores, q_heads, preferred_element_type=jnp.float32)
        * scaling
    )
    grad_v = jnp.einsum(
        "hqk,qhd->khd", shares_low, grad_blended, preferred_element_type=jnp.float32
    )
    pair_grads = jnp.concatenate(
        [grad_k.reshape(-1, model_width), grad_v.reshape(-1, model_width)], axis=1
    )
    own_pair = lax.psum_scatter(
        pair_grads.astype(jnp.bfloat16), "fsdp", scatter_dimension=0, tiled=True
    )
    grad_triple_rows = jnp.concatenate(
        [grad_q.reshape(row_count, model_width).astype(jnp.bfloat16), own_pair], axis=1
    )
    grad_triple = product_tn(hidden, grad_triple_rows)
    grad_hidden = product_nt(grad_triple_rows, w_triple)
    grad_inputs, grad_scaler, grad_offset = norm_back(grad_hidden)
    return (upstream + grad_inputs, grad_triple, grad_self_out, grad_scaler, grad_offset)


def pixel_pairs(pixel_rows, pixel_scaler, pixel_offset, w_pair, model_width):
    normed = layer_norm(pixel_rows, pixel_scaler, pixel_offset).astype(jnp.bfloat16)
    pair_rows = product(normed, w_pair).astype(jnp.bfloat16)
    return (pair_rows[:, :model_width], pair_rows[:, model_width:])


def settle_pixels(own_pair, pixel_rows, pixel_scaler, pixel_offset, w_pair):
    row_count = own_pair.shape[0]
    offset_row = lax.axis_index("fsdp") * row_count
    own_rows = lax.dynamic_slice_in_dim(pixel_rows, offset_row, row_count, 0)
    normed, norm_back = jax.vjp(layer_norm, own_rows, pixel_scaler, pixel_offset)
    grad_pair = product_tn(normed.astype(jnp.bfloat16), own_pair)
    grad_normed = product_nt(own_pair, w_pair)
    unused, grad_scaler, grad_offset = norm_back(grad_normed)
    return (grad_pair, grad_scaler, grad_offset)


def window_layout(segments, padding, block_table, window_count):
    label_count = block_table.shape[0]
    changed = (segments[1:] != segments[:-1]).astype(jnp.int32)
    run_index = jnp.concatenate([jnp.zeros((1,), jnp.int32), jnp.cumsum(changed)])
    picks = jnp.arange(window_count, dtype=jnp.int32)
    member = run_index[None, :] == picks[:, None]
    window_label = jnp.max(jnp.where(member, segments[None, :], -1), axis=1)
    labels = jnp.arange(label_count, dtype=jnp.int32)
    owners = jnp.where(labels == padding, -1, block_table)
    owner = jnp.sum(jnp.where(window_label[:, None] == labels[None, :], owners[None, :], 0), axis=1)
    owner = jnp.where(window_label < 0, -1, owner)
    inside = member & (owner[:, None] >= 0)
    return (owner, inside)


def window_scores(selected, key_rows, inside, scaling):
    scores = (
        jnp.einsum("wrd,pd->wrp", selected, key_rows, preferred_element_type=jnp.float32) * scaling
    )
    return jnp.where(inside[:, None, :], scores, masked_score)


def window_shares(scores, inside, row_top, row_total):
    return (
        jnp.where(inside[:, None, :], jnp.exp(scores - row_top[..., None]), 0.0)
        / row_total[..., None]
    )


def place_rows(values, safe, valid, images):
    kept = jnp.where(valid.reshape((-1,) + (1,) * (values.ndim - 1)), values, 0.0)
    return jnp.zeros((images,) + values.shape[1:], jnp.float32).at[safe].add(kept)


def combine_stats(earlier, latter):
    row_top = jnp.maximum(earlier[0], latter[0])
    return (
        row_top,
        earlier[1] * jnp.exp(earlier[0] - row_top) + latter[1] * jnp.exp(latter[0] - row_top),
    )


def on_device(
    latents,
    pixels,
    segment_ids,
    pad_ids,
    block_map,
    norm_gains,
    norm_biases,
    pixel_gain,
    pixel_bias,
    cross_query,
    cross_kv,
    cross_out,
    cross_up,
    cross_down,
    self_qkv,
    self_out,
    self_up,
    self_down,
    cotangent,
):
    micro_count = latents.shape[0]
    model_width = latents.shape[3]
    images = lax.axis_size("blk")
    scaling = model_width ** (-0.5)
    window_count = 3
    pixel_scaler = pixel_gain.astype(jnp.float32)
    pixel_offset = pixel_bias.astype(jnp.float32)
    totals = None
    outputs = []
    input_grads = []
    for microbatch in range(micro_count):
        fetched = fetch_weights(
            norm_gains,
            norm_biases,
            cross_query,
            cross_kv,
            cross_out,
            cross_up,
            cross_down,
            self_qkv,
            self_out,
            self_up,
            self_down,
        )
        gain_rows = fetched[0].astype(jnp.float32)
        bias_rows = fetched[1].astype(jnp.float32)
        w_query = fetched[2]
        w_pair = fetched[3]
        w_out = fetched[4]
        w_up = fetched[5]
        w_down = fetched[6]
        w_triple = fetched[7]
        w_self_out = fetched[8]
        w_self_up = fetched[9]
        w_self_down = fetched[10]
        latent = latents[microbatch, 0].astype(jnp.float32)
        hidden, first_norm = jax.vjp(layer_norm, latent, gain_rows[0], bias_rows[0])
        hidden = hidden.astype(jnp.bfloat16)
        queries = product(hidden, w_query).astype(jnp.bfloat16)
        owner, inside = window_layout(
            segment_ids[microbatch], pad_ids[microbatch], block_map[microbatch], window_count
        )
        safe = jnp.clip(owner, 0, images - 1)
        valid = owner >= 0
        pixel_rows = pixels[microbatch].astype(jnp.float32)
        key_rows, value_rows = pixel_pairs(
            pixel_rows, pixel_scaler, pixel_offset, w_pair, model_width
        )
        all_queries = lax.all_gather(queries[None], "blk", axis=0, tiled=True)
        selected = jnp.take(all_queries, safe, axis=0)
        scores = window_scores(selected, key_rows, inside, scaling)
        local_top = jnp.max(scores, axis=-1)
        local_total = jnp.sum(
            jnp.where(inside[:, None, :], jnp.exp(scores - local_top[..., None]), 0.0), axis=-1
        )
        row_count = local_top.shape[1]
        top_table = (
            jnp.full((images, row_count), masked_score, jnp.float32)
            .at[safe]
            .max(jnp.where(valid[:, None], local_top, masked_score))
        )
        total_table = place_rows(local_total, safe, valid, images)
        row_top, row_total = merged((top_table, total_table), "blk", combine_stats)
        top_window = jnp.take(row_top, safe, axis=0)
        total_window = jnp.take(row_total, safe, axis=0)
        shares = window_shares(scores, inside, top_window, total_window)
        shares_low = shares.astype(jnp.bfloat16)
        partial_value = jnp.einsum(
            "wrp,pd->wrd", shares_low, value_rows, preferred_element_type=jnp.float32
        )
        attended = (
            lax.psum_scatter(
                place_rows(partial_value, safe, valid, images).astype(jnp.bfloat16),
                "blk",
                scatter_dimension=0,
                tiled=True,
            )
            .astype(jnp.float32)[0]
            .astype(jnp.bfloat16)
        )
        first_sum = latent + product(attended, w_out)
        branch, stored_one = feed_forward(first_sum, gain_rows[1], bias_rows[1], w_up, w_down)
        second_sum = first_sum + branch
        branch, stored_two = self_forward(
            second_sum, gain_rows[2], bias_rows[2], w_triple, w_self_out
        )
        third_sum = second_sum + branch
        branch, stored_three = feed_forward(
            third_sum, gain_rows[3], bias_rows[3], w_self_up, w_self_down
        )
        outputs.append((third_sum + branch).astype(jnp.bfloat16)[None])
        upstream = cotangent[microbatch, 0].astype(jnp.float32)
        upstream, grad_self_up, grad_self_down, gain_three, bias_three = feed_backward(
            upstream, stored_three, w_self_up, w_self_down
        )
        upstream, grad_triple, grad_self_out, gain_two, bias_two = self_backward(
            upstream, stored_two, w_triple, w_self_out
        )
        upstream, grad_up, grad_down, gain_one, bias_one = feed_backward(
            upstream, stored_one, w_up, w_down
        )
        branch_low = upstream.astype(jnp.bfloat16)
        grad_out = product_tn(attended, branch_low)
        grad_attended = product_nt(branch_low, w_out).astype(jnp.bfloat16)
        grad_all = lax.all_gather(grad_attended[None], "blk", axis=0, tiled=True)
        grad_window = jnp.take(grad_all, safe, axis=0)
        scores = window_scores(selected, key_rows, inside, scaling)
        shares = window_shares(scores, inside, top_window, total_window)
        shares_low = shares.astype(jnp.bfloat16)
        grad_shares = jnp.einsum(
            "wrd,pd->wrp", grad_window, value_rows, preferred_element_type=jnp.float32
        )
        inner_table = place_rows(jnp.sum(shares * grad_shares, axis=-1), safe, valid, images)
        inner_all = lax.psum(inner_table, "blk")
        inner_window = jnp.take(inner_all, safe, axis=0)
        grad_scores = (shares * (grad_shares - inner_window[..., None])).astype(jnp.bfloat16)
        partial_value = (
            jnp.einsum("wrp,pd->wrd", grad_scores, key_rows, preferred_element_type=jnp.float32)
            * scaling
        )
        grad_queries = (
            lax.psum_scatter(
                place_rows(partial_value, safe, valid, images).astype(jnp.bfloat16),
                "blk",
                scatter_dimension=0,
                tiled=True,
            )
            .astype(jnp.float32)[0]
            .astype(jnp.bfloat16)
        )
        grad_keys = (
            jnp.einsum("wrp,wrd->pd", grad_scores, selected, preferred_element_type=jnp.float32)
            * scaling
        )
        grad_values = jnp.einsum(
            "wrp,wrd->pd", shares_low, grad_window, preferred_element_type=jnp.float32
        )
        own_pair = lax.psum_scatter(
            jnp.concatenate([grad_keys, grad_values], axis=1).astype(jnp.bfloat16),
            "fsdp",
            scatter_dimension=0,
            tiled=True,
        )
        grad_pair, gain_pixel, bias_pixel = settle_pixels(
            own_pair, pixel_rows, pixel_scaler, pixel_offset, w_pair
        )
        grad_query = product_tn(hidden, grad_queries)
        grad_hidden = product_nt(grad_queries, w_query)
        grad_latent, gain_zero, bias_zero = first_norm(grad_hidden)
        input_grads.append((upstream + grad_latent)[None])
        step_grads = (
            jnp.stack([gain_zero, gain_one, gain_two, gain_three]),
            jnp.stack([bias_zero, bias_one, bias_two, bias_three]),
            gain_pixel,
            bias_pixel,
            grad_query,
            grad_pair,
            grad_out,
            grad_up,
            grad_down,
            grad_triple,
            grad_self_out,
            grad_self_up,
            grad_self_down,
        )
        totals = step_grads if totals is None else jax.tree.map(jnp.add, totals, step_grads)
    pixel_stack = jnp.stack([totals[2], totals[3]])
    pixel_spread = jnp.broadcast_to(pixel_stack[None], (lax.axis_size("fsdp"),) + pixel_stack.shape)
    shards = (
        lax.psum_scatter(
            totals[0].astype(jnp.bfloat16), "fsdp", scatter_dimension=1, tiled=True
        ).astype(jnp.float32),
        lax.psum_scatter(
            totals[1].astype(jnp.bfloat16), "fsdp", scatter_dimension=1, tiled=True
        ).astype(jnp.float32),
        lax.psum_scatter(
            totals[4].astype(jnp.bfloat16), "fsdp", scatter_dimension=0, tiled=True
        ).astype(jnp.float32),
        lax.psum_scatter(
            totals[5].astype(jnp.bfloat16), "fsdp", scatter_dimension=1, tiled=True
        ).astype(jnp.float32),
        lax.psum_scatter(
            totals[6].astype(jnp.bfloat16), "fsdp", scatter_dimension=0, tiled=True
        ).astype(jnp.float32),
        lax.psum_scatter(
            totals[7].astype(jnp.bfloat16), "fsdp", scatter_dimension=0, tiled=True
        ).astype(jnp.float32),
        lax.psum_scatter(
            totals[8].astype(jnp.bfloat16), "fsdp", scatter_dimension=0, tiled=True
        ).astype(jnp.float32),
        lax.psum_scatter(
            totals[9].astype(jnp.bfloat16), "fsdp", scatter_dimension=0, tiled=True
        ).astype(jnp.float32),
        lax.psum_scatter(
            totals[10].astype(jnp.bfloat16), "fsdp", scatter_dimension=0, tiled=True
        ).astype(jnp.float32),
        lax.psum_scatter(
            totals[11].astype(jnp.bfloat16), "fsdp", scatter_dimension=0, tiled=True
        ).astype(jnp.float32),
        lax.psum_scatter(
            totals[12].astype(jnp.bfloat16), "fsdp", scatter_dimension=0, tiled=True
        ).astype(jnp.float32),
        lax.psum_scatter(
            pixel_spread.astype(jnp.bfloat16), "fsdp", scatter_dimension=0, tiled=True
        ).astype(jnp.float32),
    )
    summed = (
        lax.psum(shards[0].astype(jnp.bfloat16), "blk").astype(jnp.float32),
        lax.psum(shards[1].astype(jnp.bfloat16), "blk").astype(jnp.float32),
        lax.psum(shards[2].astype(jnp.bfloat16), "blk").astype(jnp.float32),
        lax.psum(shards[3].astype(jnp.bfloat16), "blk").astype(jnp.float32),
        lax.psum(shards[4].astype(jnp.bfloat16), "blk").astype(jnp.float32),
        lax.psum(shards[5].astype(jnp.bfloat16), "blk").astype(jnp.float32),
        lax.psum(shards[6].astype(jnp.bfloat16), "blk").astype(jnp.float32),
        lax.psum(shards[7].astype(jnp.bfloat16), "blk").astype(jnp.float32),
        lax.psum(shards[8].astype(jnp.bfloat16), "blk").astype(jnp.float32),
        lax.psum(shards[9].astype(jnp.bfloat16), "blk").astype(jnp.float32),
        lax.psum(shards[10].astype(jnp.bfloat16), "blk").astype(jnp.float32),
        lax.psum(shards[11].astype(jnp.bfloat16), "blk").astype(jnp.float32),
    )
    return (
        jnp.stack(outputs),
        jnp.stack(input_grads),
        summed[0],
        summed[1],
        summed[11][0, 0],
        summed[11][0, 1],
        summed[2],
        summed[3],
        summed[4],
        summed[5],
        summed[6],
        summed[7],
        summed[8],
        summed[9],
        summed[10],
    )


def solution(mesh):
    placed = (
        P(None, "blk", "fsdp", None),
        P(None, "blk", None),
        P(None, "blk"),
        P(),
        P(),
        P(None, "fsdp"),
        P(None, "fsdp"),
        P(),
        P(),
        P("fsdp", None),
        P(None, "fsdp"),
        P("fsdp", None),
        P("fsdp", None),
        P("fsdp", None),
        P("fsdp", None),
        P("fsdp", None),
        P("fsdp", None),
        P("fsdp", None),
        P(None, "blk", "fsdp", None),
    )
    return jax.shard_map(
        on_device,
        mesh=mesh,
        in_specs=placed,
        out_specs=(
            P(None, "blk", "fsdp", None),
            P(None, "blk", "fsdp", None),
            P(None, "fsdp"),
            P(None, "fsdp"),
            P(),
            P(),
            P("fsdp", None),
            P(None, "fsdp"),
            P("fsdp", None),
            P("fsdp", None),
            P("fsdp", None),
            P("fsdp", None),
            P("fsdp", None),
            P("fsdp", None),
            P("fsdp", None),
        ),
        check_vma=False,
    )
```

profile of v0, /device:TPU:0, one launch (start us, length us, event | category | flops | bytes accessed | tf_op | source)
XLA Modules:
  0.0 3019.5 jit_solution(17941017896798244617)
XLA Ops:
  78.3 68.2 %all-gather.55.cloned.1.call-done = bf16[4096,1024]{1,0:T(8,128)(2,1)} async-done(((bf16[256,1024]{1,0:T(8,128)(2,1)}), bf16[4096,1024]{1,0:T(8,128)(2,1)}) %all-gather.55.cloned.1.call-update) | async-done | bytes 8388624 | tf_op jit(solution)/shard_map/all_gather | solution.py:293
  344.2 23.5 reduce-scatter.28.cloned.1.call-done
  370.6 31.6 %all-gather.37.cloned.1.call-done = bf16[1024,1024]{1,0:T(8,128)(2,1)} async-done(((bf16[512,1024]{1,0:T(8,128)(2,1)}), bf16[1024,1024]{1,0:T(8,128)(2,1)}) %all-gather.37.cloned.1.call-update) | async-done | bytes 2097168 | tf_op jit(solution)/shard_map/all_gather | solution.py:69
  407.6 29.2 all-gather.39.cloned.1.call-done
  439.8 79.0 %all-gather.41.cloned.1.call-done = bf16[1024,3072]{1,0:T(8,128)(2,1)} async-done(((bf16[512,3072]{1,0:T(8,128)(2,1)}), bf16[1024,3072]{1,0:T(8,128)(2,1)}) %all-gather.41.cloned.1.call-update) | async-done | bytes 6291472 | tf_op jit(solution)/shard_map/all_gather | solution.py:71
  526.3 101.1 %reduce-scatter.32.cloned.1.call-done = bf16[1,256,1024]{2,1,0:T(8,128)(2,1)} async-done(((bf16[16,256,1024]{2,1,0:T(8,128)(2,1)}), bf16[1,256,1024]{2,1,0:T(8,128)(2,1)}) %reduce-scatter.32.cloned.1.call-update) | async-done | bytes 524304 | tf_op jit(solution)/shard_map/reduce_scatter | solution.py:316
  700.6 31.7 %all-gather.53.cloned.1.call-done = bf16[512,2048]{1,0:T(8,128)(2,1)} async-done(((bf16[256,2048]{1,0:T(8,128)(2,1)}), bf16[512,2048]{1,0:T(8,128)(2,1)}) %all-gather.53.cloned.1.call-update) | async-done | bytes 2097168 | tf_op jit(solution)/shard_map/all_gather | solution.py:105
  773.1 28.3 all-gather.49.cloned.1.call-done
  866.4 28.5 reduce-scatter.42.cloned.1.call-done
  923.9 70.5 %all-gather.61.cloned.1.call-done = bf16[4096,1024]{1,0:T(8,128)(2,1)} async-done(((bf16[256,1024]{1,0:T(8,128)(2,1)}), bf16[4096,1024]{1,0:T(8,128)(2,1)}) %all-gather.61.cloned.1.call-update) | async-done | bytes 8388624 | tf_op jit(solution)/shard_map/all_gather | solution.py:349
  1011.3 59.1 %all-gather.65.cloned.1.call-done = bf16[4096,1024]{1,0:T(8,128)(2,1)} async-done(((bf16[256,1024]{1,0:T(8,128)(2,1)}), bf16[4096,1024]{1,0:T(8,128)(2,1)}) %all-gather.65.cloned.1.call-update) | async-done | bytes 8388624 | tf_op jit(solution)/shard_map/all_gather | solution.py:349
  1088.1 59.3 %all-reduce.4 = (f32[16,256]{1,0:T(8,128)S(1)}, f32[16,256]{1,0:T(8,128)S(1)}) all-reduce(f32[16,256]{1,0:T(8,128)S(1)} %scatter_custom_fusion.9, f32[16,256]{1,0:T(8,128)S(1)} %scatter_custom_fusion.13), channel_id=1, replica_groups=mesh['blk'=16,'fsdp'=2] {'blk'}, use_global_device_ids=true, to_apply=%region_82.85 | all-reduce | flops 8192 | bytes 65536 | tf_op jit(solution)/shard_map/psum | solution.py:358
  1231.5 58.7 %reduce-scatter.44.cloned.1.call-done = bf16[1,256,1024]{2,1,0:T(8,128)(2,1)} async-done(((bf16[16,256,1024]{2,1,0:T(8,128)(2,1)}), bf16[1,256,1024]{2,1,0:T(8,128)(2,1)}) %reduce-scatter.44.cloned.1.call-update) | async-done | bytes 524304 | tf_op jit(solution)/shard_map/reduce_scatter | solution.py:366
  1292.7 105.9 %reduce-scatter.36.cloned.1.call-done = bf16[1,256,1024]{2,1,0:T(8,128)(2,1)} async-done(((bf16[16,256,1024]{2,1,0:T(8,128)(2,1)}), bf16[1,256,1024]{2,1,0:T(8,128)(2,1)}) %reduce-scatter.36.cloned.1.call-update) | async-done | bytes 524304 | tf_op jit(solution)/shard_map/reduce_scatter | solution.py:366
  1416.8 64.8 %all-gather.57.cloned.1.call-done = bf16[4096,1024]{1,0:T(8,128)(2,1)} async-done(((bf16[256,1024]{1,0:T(8,128)(2,1)}), bf16[4096,1024]{1,0:T(8,128)(2,1)}) %all-gather.57.cloned.1.call-update) | async-done | bytes 8388624 | tf_op jit(solution)/shard_map/all_gather | solution.py:293
  1571.3 102.9 %reduce-scatter.30.cloned.1.call-done = bf16[1,256,1024]{2,1,0:T(8,128)(2,1)} async-done(((bf16[16,256,1024]{2,1,0:T(8,128)(2,1)}), bf16[1,256,1024]{2,1,0:T(8,128)(2,1)}) %reduce-scatter.30.cloned.1.call-update) | async-done | bytes 524304 | tf_op jit(solution)/shard_map/reduce_scatter | solution.py:316
  1693.6 28.9 all-gather.51.cloned.1.call-done
  1762.8 28.2 reduce-scatter.38.cloned.1.call-done
  1808.4 75.0 %all-gather.63.cloned.1.call-done = bf16[4096,1024]{1,0:T(8,128)(2,1)} async-done(((bf16[256,1024]{1,0:T(8,128)(2,1)}), bf16[4096,1024]{1,0:T(8,128)(2,1)}) %all-gather.63.cloned.1.call-update) | async-done | bytes 8388624 | tf_op jit(solution)/shard_map/all_gather | solution.py:349
  1897.8 59.5 %psum.106 = f32[16,256]{1,0:T(8,128)S(1)} all-reduce(f32[16,256]{1,0:T(8,128)S(1)} %scatter_custom_fusion.11), channel_id=1, replica_groups=mesh['blk'=16,'fsdp'=2] {'blk'}, use_global_device_ids=true, to_apply=%region_97.100 | all-reduce | flops 4096 | bytes 32768 | tf_op jit(solution)/shard_map/psum | solution.py:358
  2153.6 44.7 %reduce-scatter.46.cloned.1.call-done = bf16[1024,2048]{0,1:T(8,128)(2,1)} async-done(((bf16[2048,2048]{0,1:T(8,128)(2,1)}), bf16[1024,2048]{0,1:T(8,128)(2,1)}) %reduce-scatter.46.cloned.1.call-update) | async-done | bytes 4194320 | tf_op jit(solution)/shard_map/reduce_scatter | solution.py:382
  2203.6 96.3 %reduce-scatter.48.cloned.1.call-done = bf16[1024,2048]{0,1:T(8,128)(2,1)} async-done(((bf16[2048,2048]{0,1:T(8,128)(2,1)}), bf16[1024,2048]{0,1:T(8,128)(2,1)}) %reduce-scatter.48.cloned.1.call-update) | async-done | bytes 4194320 | tf_op jit(solution)/shard_map/reduce_scatter | solution.py:382
  2305.9 95.5 %reduce-scatter.50.cloned.1.call-done = bf16[1024,2048]{0,1:T(8,128)(2,1)} async-done(((bf16[2048,2048]{0,1:T(8,128)(2,1)}), bf16[1024,2048]{0,1:T(8,128)(2,1)}) %reduce-scatter.50.cloned.1.call-update) | async-done | bytes 4194320 | tf_op jit(solution)/shard_map/reduce_scatter | solution.py:382
  2436.1 34.8 %reduce-scatter.66.cloned.1.call-done = bf16[512,1024]{1,0:T(8,128)(2,1)} async-done(((bf16[1024,1024]{1,0:T(8,128)(2,1)}), bf16[512,1024]{1,0:T(8,128)(2,1)}) %reduce-scatter.66.cloned.1.call-update) | async-done | bytes 1048592 | tf_op jit(solution)/shard_map/reduce_scatter | solution.py:441
  2470.9 34.5 %reduce-scatter.64.cloned.1.call-done = bf16[512,1024]{1,0:T(8,128)(2,1)} async-done(((bf16[1024,1024]{1,0:T(8,128)(2,1)}), bf16[512,1024]{1,0:T(8,128)(2,1)}) %reduce-scatter.64.cloned.1.call-update) | async-done | bytes 1048592 | tf_op jit(solution)/shard_map/reduce_scatter | solution.py:438
  2505.4 34.8 %reduce-scatter.60.cloned.1.call-done = bf16[512,1024]{1,0:T(8,128)(2,1)} async-done(((bf16[1024,1024]{1,0:T(8,128)(2,1)}), bf16[512,1024]{1,0:T(8,128)(2,1)}) %reduce-scatter.60.cloned.1.call-update) | async-done | bytes 1048592 | tf_op jit(solution)/shard_map/reduce_scatter | solution.py:432
  2540.2 34.7 %reduce-scatter.58.cloned.1.call-done = bf16[512,1024]{1,0:T(8,128)(2,1)} async-done(((bf16[1024,1024]{1,0:T(8,128)(2,1)}), bf16[512,1024]{1,0:T(8,128)(2,1)}) %reduce-scatter.58.cloned.1.call-update) | async-done | bytes 1048592 | tf_op jit(solution)/shard_map/reduce_scatter | solution.py:429
  2574.8 34.6 %reduce-scatter.56.cloned.1.call-done = bf16[512,1024]{1,0:T(8,128)(2,1)} async-done(((bf16[1024,1024]{1,0:T(8,128)(2,1)}), bf16[512,1024]{1,0:T(8,128)(2,1)}) %reduce-scatter.56.cloned.1.call-update) | async-done | bytes 1048592 | tf_op jit(solution)/shard_map/reduce_scatter | solution.py:426
  2609.5 79.8 %reduce-scatter.62.cloned.1.call-done = bf16[512,3072]{1,0:T(8,128)(2,1)} async-done(((bf16[1024,3072]{1,0:T(8,128)(2,1)}), bf16[512,3072]{1,0:T(8,128)(2,1)}) %reduce-scatter.62.cloned.1.call-update) | async-done | bytes 3145744 | tf_op jit(solution)/shard_map/reduce_scatter | solution.py:435
  2689.3 34.8 %reduce-scatter.52.cloned.1.call-done = bf16[512,1024]{1,0:T(8,128)(2,1)} async-done(((bf16[1024,1024]{1,0:T(8,128)(2,1)}), bf16[512,1024]{1,0:T(8,128)(2,1)}) %reduce-scatter.52.cloned.1.call-update) | async-done | bytes 1048592 | tf_op jit(solution)/shard_map/reduce_scatter | solution.py:420
  2786.0 36.1 %all-reduce.5 = (bf16[4,512]{1,0:T(4,128)(2,1)S(1)}, bf16[4,512]{1,0:T(4,128)(2,1)S(1)}, bf16[1,2,261]{2,1,0:T(2,128)(2,1)S(1)}) all-reduce(bf16[4,512]{1,0:T(4,128)(2,1)S(1)} %copy.161, bf16[4,512]{1,0:T(4,128)(2,1)S(1)} %copy.163, bf16[1,2,261]{2,1,0:T(2,128)(2,1)S(1)} %constant_dynamic-slice_fusion), channel_id=1, replica_groups=mesh['blk'=16,'fsdp'=2] {'blk'}, use_global_device_ids=true, to_apply=%region_130.133 | all-reduce | flops 4618 | bytes 18472 | tf_op jit(solution)/shard_map/psum | solution.py:452
  2823.9 171.3 %all-reduce.9.cloned.1.call-done = (bf16[512,1024]{1,0:T(8,128)(2,1)}, bf16[261,1024]{1,0:T(8,128)(2,1)}, bf16[512,1024]{1,0:T(8,128)(2,1)}, bf16[512,1024]{1,0:...) async-done(((bf16[512,1024]{1,0:T(8,128)(2,1)}, ...) | async-done | bytes 11020304 | tf_op jit(solution)/shard_map/psum | solution.py:454
  (1185 shorter events, 1136.3 us)
Async XLA Ops:
  48.6 201.8 %all-gather.59.cloned.1.call-start = ((), (), s32[]{:S(2)}) async-start(), calls=%async_computation.58 | async-start | bytes 8912896 | tf_op jit(solution)/shard_map/all_gather | solution.py:293
  51.9 292.3 %all-gather.35.cloned.1.call-start = ((), (), s32[]{:S(2)}) async-start(), calls=%async_computation.26 | async-start | bytes 3145728 | tf_op jit(solution)/shard_map/all_gather | solution.py:68
  52.5 315.2 %reduce-scatter.28.cloned.1.call-start = ((), (), s32[]{:S(2)}) async-start(), calls=%async_computation.25 | async-start | bytes 8912896 | tf_op jit(solution)/shard_map/reduce_scatter | solution.py:316
  238.4 163.7 %all-gather.37.cloned.1.call-start = ((), (), s32[]{:S(2)}) async-start(), calls=%async_computation.27 | async-start | bytes 3145728 | tf_op jit(solution)/shard_map/all_gather | solution.py:69
  239.2 197.7 %all-gather.39.cloned.1.call-start = ((), (), s32[]{:S(2)}) async-start(), calls=%async_computation.28 | async-start | bytes 3145728 | tf_op jit(solution)/shard_map/all_gather | solution.py:70
  239.9 278.9 %all-gather.41.cloned.1.call-start = ((), (), s32[]{:S(2)}) async-start(), calls=%async_computation.29 | async-start | bytes 9437184 | tf_op jit(solution)/shard_map/all_gather | solution.py:71
  240.7 386.8 %reduce-scatter.32.cloned.1.call-start = ((), (), s32[]{:S(2)}) async-start(), calls=%async_computation.36 | async-start | bytes 8912896 | tf_op jit(solution)/shard_map/reduce_scatter | solution.py:316
  344.1 318.3 %all-gather.43.cloned.1.call-start = ((), (), s32[]{:S(2)}) async-start(), calls=%async_computation.30 | async-start | bytes 3145728 | tf_op jit(solution)/shard_map/all_gather | solution.py:105
  525.7 171.3 %all-gather.45.cloned.1.call-start = ((), (), s32[]{:S(2)}) async-start(), calls=%async_computation.31 | async-start | bytes 3145728 | tf_op jit(solution)/shard_map/all_gather | solution.py:72
  526.3 206.0 %all-gather.53.cloned.1.call-start = ((), (), s32[]{:S(2)}) async-start(), calls=%async_computation.37 | async-start | bytes 3145728 | tf_op jit(solution)/shard_map/all_gather | solution.py:105
  641.2 160.2 %all-gather.49.cloned.1.call-start = ((), (), s32[]{:S(2)}) async-start(), calls=%async_computation.33 | async-start | bytes 3145728 | tf_op jit(solution)/shard_map/all_gather | solution.py:74
  641.8 218.4 %reduce-scatter.34.cloned.1.call-start = ((), (), s32[]{:S(2)}) async-start(), calls=%async_computation.38 | async-start | bytes 3145728 | tf_op jit(solution)/shard_map/reduce_scatter | solution.py:153
  923.9 366.3 %reduce-scatter.44.cloned.1.call-start = ((), (), s32[]{:S(2)}) async-start(), calls=%async_computation.43 | async-start | bytes 8912896 | tf_op jit(solution)/shard_map/reduce_scatter | solution.py:366
  1188.3 210.3 %reduce-scatter.36.cloned.1.call-start = ((), (), s32[]{:S(2)}) async-start(), calls=%async_computation.39 | async-start | bytes 8912896 | tf_op jit(solution)/shard_map/reduce_scatter | solution.py:366
  1230.8 250.7 %all-gather.57.cloned.1.call-start = ((), (), s32[]{:S(2)}) async-start(), calls=%async_computation.57 | async-start | bytes 8912896 | tf_op jit(solution)/shard_map/all_gather | solution.py:293
  1406.7 267.4 %reduce-scatter.30.cloned.1.call-start = ((), (), s32[]{:S(2)}) async-start(), calls=%async_computation.34 | async-start | bytes 8912896 | tf_op jit(solution)/shard_map/reduce_scatter | solution.py:316
  1808.4 334.7 %reduce-scatter.40.cloned.1.call-start = ((), (), s32[]{:S(2)}) async-start(), calls=%async_computation.41 | async-start | bytes 8912896 | tf_op jit(solution)/shard_map/reduce_scatter | solution.py:366
  1994.9 203.4 %reduce-scatter.46.cloned.1.call-start = ((), (), s32[]{:S(2)}) async-start(), calls=%async_computation.44 | async-start | bytes 12582912 | tf_op jit(solution)/shard_map/reduce_scatter | solution.py:382
  2021.9 278.0 %reduce-scatter.48.cloned.1.call-start = ((), (), s32[]{:S(2)}) async-start(), calls=%async_computation.45 | async-start | bytes 12582912 | tf_op jit(solution)/shard_map/reduce_scatter | solution.py:382
  2048.1 353.2 %reduce-scatter.50.cloned.1.call-start = ((), (), s32[]{:S(2)}) async-start(), calls=%async_computation.46 | async-start | bytes 12582912 | tf_op jit(solution)/shard_map/reduce_scatter | solution.py:382
  2074.2 361.9 %reduce-scatter.68.cloned.1.call-start = ((), (), s32[]{:S(2)}) async-start(), calls=%async_computation.55 | async-start | bytes 3145728 | tf_op jit(solution)/shard_map/reduce_scatter | solution.py:444
  2081.1 389.8 %reduce-scatter.66.cloned.1.call-start = ((), (), s32[]{:S(2)}) async-start(), calls=%async_computation.54 | async-start | bytes 3145728 | tf_op jit(solution)/shard_map/reduce_scatter | solution.py:441
  2086.9 418.5 %reduce-scatter.64.cloned.1.call-start = ((), (), s32[]{:S(2)}) async-start(), calls=%async_computation.53 | async-start | bytes 3145728 | tf_op jit(solution)/shard_map/reduce_scatter | solution.py:438
  2091.6 448.6 %reduce-scatter.60.cloned.1.call-start = ((), (), s32[]{:S(2)}) async-start(), calls=%async_computation.51 | async-start | bytes 3145728 | tf_op jit(solution)/shard_map/reduce_scatter | solution.py:432
  2097.1 477.8 %reduce-scatter.58.cloned.1.call-start = ((), (), s32[]{:S(2)}) async-start(), calls=%async_computation.50 | async-start | bytes 3145728 | tf_op jit(solution)/shard_map/reduce_scatter | solution.py:429
  2104.1 505.4 %reduce-scatter.56.cloned.1.call-start = ((), (), s32[]{:S(2)}) async-start(), calls=%async_computation.49 | async-start | bytes 3145728 | tf_op jit(solution)/shard_map/reduce_scatter | solution.py:426
  2109.4 579.8 %reduce-scatter.62.cloned.1.call-start = ((), (), s32[]{:S(2)}) async-start(), calls=%async_computation.52 | async-start | bytes 9437184 | tf_op jit(solution)/shard_map/reduce_scatter | solution.py:435
  2137.9 586.2 %reduce-scatter.52.cloned.1.call-start = ((), (), s32[]{:S(2)}) async-start(), calls=%async_computation.47 | async-start | bytes 3145728 | tf_op jit(solution)/shard_map/reduce_scatter | solution.py:420
  2147.8 599.6 %reduce-scatter.54.cloned.1.call-start = ((), (), s32[]{:S(2)}) async-start(), calls=%async_computation.48 | async-start | bytes 1622016 | tf_op jit(solution)/shard_map/reduce_scatter | solution.py:423
  2407.0 358.0 %reduce-scatter.72.cloned.1.call-start = ((), (), s32[]{:S(2)}) async-start(), calls=%async_computation.63 | async-start | bytes 393216
  2413.3 362.1 %reduce-scatter.70.cloned.1.call-start = ((), (), s32[]{:S(2)}) async-start(), calls=%async_computation.62 | async-start | bytes 393216
  2418.1 577.1 %all-reduce.9.cloned.1.call-start = ((), (), s32[]{:S(2)}) async-start(), calls=%async_computation.64 | async-start | bytes 22052864 | tf_op jit(solution)/shard_map/psum | solution.py:454
  (338 other events, 12657.7 us)
Sparse Core Ops, SparseCore 0:
  9.6 35.7 all-gather.30
  71.5 74.9 all-gather.54
  149.1 75.8 all-gather.58
  226.4 32.1 all-gather.34
  262.4 105.2 reduce-scatter.27
  369.3 32.8 all-gather.36
  403.7 33.1 all-gather.38
  438.4 80.3 all-gather.40
  522.7 104.6 reduce-scatter.31
  629.6 32.8 all-gather.42
  663.9 33.1 all-gather.44
  699.2 33.1 all-gather.52
  733.7 33.1 all-gather.46
  768.3 33.1 all-gather.48
  863.0 31.8 reduce-scatter.41
  919.5 74.8 all-gather.60
  997.2 73.1 all-gather.64
  1188.4 101.7 reduce-scatter.43
  1294.2 104.3 reduce-scatter.35
  1406.8 74.6 all-gather.56
  1571.3 102.7 reduce-scatter.29
  1689.6 32.8 all-gather.50
  1808.5 74.8 all-gather.62
  1995.0 101.7 reduce-scatter.39
  2099.3 99.0 reduce-scatter.45
  2200.6 99.2 reduce-scatter.47
  2302.1 99.2 reduce-scatter.49
  2439.0 31.8 reduce-scatter.65
  2508.3 31.8 reduce-scatter.59
  2577.6 31.8 reduce-scatter.55
  2612.2 77.0 reduce-scatter.61
  2780.3 214.8 all-reduce.8
  (10 shorter events, 256.1 us)
where the time goes:
time: 3030 us; the launch traced here: 3020 us
  waiting for transfers between devices  1860 us (61%)
  matrix products  446 us (15%)
  blocking collectives  287 us (9%)
  other arithmetic  225 us (7%)
  local copies, waits for them, and re-layouts  172 us (6%)
    reduce_scatter x6, waiting for transfers between devices, on_device(): lax.psum_scatter(place_rows(partial_value, safe, valid, images).astype(jn...  392 us
    reduce_scatter x3, waiting for transfers between devices, on_device(): lax.psum_scatter(jnp.concatenate([grad_keys, grad_values], axis=1).astype...  236 us
    all_gather x3, waiting for transfers between devices, on_device(): grad_all = lax.all_gather(grad_attended[None], 'blk', axis=0, tiled=True)  205 us
    psum x1, waiting for transfers between devices, on_device(): lax.psum(shards[2].astype(jnp.bfloat16), 'blk').astype(jnp.float32)  171 us
    all_gather x3, waiting for transfers between devices, on_device(): all_queries = lax.all_gather(queries[None], 'blk', axis=0, tiled=True)  133 us
    psum x2, blocking collectives, on_device(): inner_all = lax.psum(inner_table, 'blk')  119 us
    all_gather x6, blocking collectives, merged(): gathered = jax.tree.map(lambda a: lax.all_gather(a, axis), part)  117 us
    dot_general x27, matrix products, product(): return jnp.dot(matrix_a, matrix_b, preferred_element_type=jnp.float32)  97.8 us
  transfers between devices with their start and end apart: 42, of which 38 were waited for; matrix products, arithmetic and copies ran while one was open for 17% of the time, Pallas kernels for 0%

commit v1 on v0

v1 whole, which is shorter than its diff:
```python
import functools

import jax
import jax.numpy as jnp
from jax import lax
from jax.experimental import pallas as pl
from jax.experimental.pallas import tpu as pltpu
from jax.sharding import PartitionSpec as P

HEADS = 8
FEATURE_ROWS = 272
VMEM_LIMIT = 56 * 1024 * 1024

epsilon = 1e-05
masked_score = -1e30
low_type = jnp.bfloat16


def product(a, b):
    return jnp.dot(a, b, preferred_element_type=jnp.float32)


def product_tn(a, b):
    return lax.dot_general(a, b, (((0,), (0,)), ((), ())), preferred_element_type=jnp.float32)


def product_nt(a, b):
    return lax.dot_general(a, b, (((1,), (1,)), ((), ())), preferred_element_type=jnp.float32)


def normalise(rows):
    centre = rows - jnp.mean(rows, axis=-1, keepdims=True)
    scale = lax.rsqrt(jnp.mean(centre * centre, axis=-1, keepdims=True) + epsilon)
    return centre * scale, scale


def norm_backward(upstream, normed, scale, gain):
    gain_term = jnp.sum(upstream * normed, axis=0)
    bias_term = jnp.sum(upstream, axis=0)
    inner = upstream * gain
    down = scale * (
        inner
        - jnp.mean(inner, axis=-1, keepdims=True)
        - normed * jnp.mean(inner * normed, axis=-1, keepdims=True)
    )
    return down, gain_term, bias_term


def feed_forward(rows, gain, bias, w_up, w_down):
    normed, scale = normalise(rows)
    hidden = (normed * gain + bias).astype(low_type)
    upward = product(hidden, w_up)
    share = 0.5 * (1.0 + lax.erf(upward * (0.5**0.5)))
    slope = share + upward * jnp.exp(-0.5 * upward * upward) * 0.3989422804014327
    active = (upward * share).astype(low_type)
    return rows + product(active, w_down), (hidden, slope, active)


def feed_backward(upstream, low, rows, stored, gain, w_up, w_down):
    hidden, slope, active = stored
    grad_down = product_tn(active, low)
    grad_upward = (product_nt(low, w_down) * slope).astype(low_type)
    grad_up = product_tn(hidden, grad_upward)
    normed, scale = normalise(rows)
    down, gain_term, bias_term = norm_backward(product_nt(grad_upward, w_up), normed, scale, gain)
    return upstream + down, grad_up, grad_down, gain_term, bias_term


def nt(a, b):
    return lax.dot_general(a, b, (((1,), (1,)), ((), ())), preferred_element_type=jnp.float32)


def tn(a, b):
    return lax.dot_general(a, b, (((0,), (0,)), ((), ())), preferred_element_type=jnp.float32)


def params(*semantics):
    return pltpu.CompilerParams(dimension_semantics=semantics, vmem_limit_bytes=VMEM_LIMIT)


def pixel_kernel(micro_ref, pixel_ref, count_ref, out_ref):
    features = pixel_ref.shape[1]
    width = out_ref.shape[3]
    pixels = pixel_ref[0].astype(jnp.float32)
    centre = pixels - jnp.mean(pixels, axis=0, keepdims=True)
    spread = jnp.mean(centre * centre, axis=0, keepdims=True)
    normed = centre * lax.rsqrt(spread + epsilon)
    pad = jnp.zeros((FEATURE_ROWS - features, normed.shape[1]), jnp.float32)
    tall = jnp.concatenate([normed, pad], axis=0)
    row = lax.broadcasted_iota(jnp.int32, (FEATURE_ROWS, width), 0)
    high, rest = count_ref[0][:1, :width], count_ref[0][1:2, :width]
    for part in range(out_ref.shape[0]):
        piece = tall[:, part * width : (part + 1) * width]
        piece = jnp.where(row == features, 1.0, piece)
        piece = jnp.where(row == features + 1, high, jnp.where(row == features + 2, rest, piece))
        out_ref[part, 0] = piece.astype(low_type)


def prepare_pixels(pixels, micro, counts, width):
    routed = micro.shape[0]
    features, slots = pixels.shape[1:]
    step = min(slots, 1024)
    return pl.pallas_call(
        pixel_kernel,
        out_shape=jax.ShapeDtypeStruct((slots // width, routed, FEATURE_ROWS, width), low_type),
        grid_spec=pltpu.PrefetchScalarGridSpec(
            num_scalar_prefetch=1,
            grid=(routed, slots // step),
            in_specs=[
                pl.BlockSpec((1, features, step), lambda i, s, m: (m[i], 0, s)),
                pl.BlockSpec((1, 8, 128), lambda i, s, m: (i, 0, 0)),
            ],
            out_specs=pl.BlockSpec((step // width, 1, FEATURE_ROWS, width), lambda i, s, m: (s, i, 0, 0)),
        ),
        compiler_params=params("arbitrary", "arbitrary"),
        name="prepare_pixels",
    )(micro, pixels, counts)


def side_by_side(ref):
    return jnp.concatenate([ref[tile, 0] for tile in range(ref.shape[0])], axis=1)


def cross_forward_kernel(items, big_ref, query_ref, first_ref, second_ref, mask_ref, out_ref):
    item = pl.program_id(0) // items
    lanes = mask_ref.shape[2] // 2

    def attend(features, mask):
        scores = product(query_ref[...], features) + mask
        top = jnp.max(scores, axis=-1, keepdims=True)
        weights = jnp.exp(scores - top)
        total = jnp.sum(weights, axis=-1, keepdims=True)
        out_ref[...] = nt(weights.astype(low_type), features) / total

    @pl.when(big_ref[item] == 0)
    def small():
        attend(side_by_side(first_ref), mask_ref[0][:1, :lanes])

    @pl.when(big_ref[item] != 0)
    def large():
        both = jnp.concatenate([side_by_side(first_ref), side_by_side(second_ref)], axis=1)
        attend(both, mask_ref[0][:1])


def cross_backward_kernel(items, big_ref, query_ref, grad_ref, first_ref, second_ref, mask_ref, out_ref):
    item = pl.program_id(0) // items
    lanes = mask_ref.shape[2] // 2

    def attend(features, mask):
        scores = product(query_ref[...], features) + mask
        top = jnp.max(scores, axis=-1, keepdims=True)
        weights = jnp.exp(scores - top)
        shares = weights / jnp.sum(weights, axis=-1, keepdims=True)
        grad_shares = product(grad_ref[...], features)
        inner = jnp.sum(shares * grad_shares, axis=-1, keepdims=True)
        grad_scores = (shares * (grad_shares - inner)).astype(low_type)
        out_ref[...] = nt(grad_scores, features)

    @pl.when(big_ref[item] == 0)
    def small():
        attend(side_by_side(first_ref), mask_ref[0][:1, :lanes])

    @pl.when(big_ref[item] != 0)
    def large():
        both = jnp.concatenate([side_by_side(first_ref), side_by_side(second_ref)], axis=1)
        attend(both, mask_ref[0][:1])


def cross_call(kernel, big, rows, first, second, mask, block, per_item):
    count = rows[0].shape[0]
    tiles, width = first.shape[0], first.shape[3]
    row_spec = pl.BlockSpec((block, FEATURE_ROWS), lambda i, big: (i, 0))
    tile_spec = pl.BlockSpec((tiles, 1, FEATURE_ROWS, width), lambda i, big: (0, i // per_item, 0, 0))
    return pl.pallas_call(
        functools.partial(kernel, per_item),
        out_shape=jax.ShapeDtypeStruct((count, FEATURE_ROWS), jnp.float32),
        grid_spec=pltpu.PrefetchScalarGridSpec(
            num_scalar_prefetch=1,
            grid=(count // block,),
            in_specs=[row_spec] * len(rows)
            + [tile_spec, tile_spec]
            + [pl.BlockSpec((1, 8, mask.shape[2]), lambda i, big: (i // per_item, 0, 0))],
            out_specs=row_spec,
        ),
        compiler_params=params("arbitrary"),
        name="cross_attention",
    )(big, *rows, first, second, mask)


def self_forward_kernel(groups, scaling, q_ref, k_ref, v_ref, more_k_ref, more_v_ref, out_ref):
    for q_rows, own, more in groups:
        keys, values = keys_of(own, more, k_ref, v_ref, more_k_ref, more_v_ref)
        scores = nt(q_ref[q_rows], keys) * scaling
        weights = jnp.exp(scores - jnp.max(scores, axis=-1, keepdims=True))
        total = jnp.sum(weights, axis=-1, keepdims=True)
        out_ref[q_rows, :] = (product(weights.astype(low_type), values) / total).astype(low_type)


def keys_of(own, more, k_ref, v_ref, more_k_ref, more_v_ref):
    keys, values = [], []
    if own is not None:
        keys.append(k_ref[own])
        values.append(v_ref[own])
    if more is not None:
        keys.append(more_k_ref[more])
        values.append(more_v_ref[more])
    if len(keys) == 1:
        return keys[0], values[0]
    return jnp.concatenate(keys, axis=0), jnp.concatenate(values, axis=0)


def self_backward_kernel(
    groups,
    scaling,
    q_ref,
    k_ref,
    v_ref,
    more_k_ref,
    more_v_ref,
    grad_ref,
    dq_ref,
    dk_ref,
    dv_ref,
    more_dk_ref,
    more_dv_ref,
):
    for q_rows, own, more in groups:
        keys, values = keys_of(own, more, k_ref, v_ref, more_k_ref, more_v_ref)
        queries = q_ref[q_rows]
        grads = grad_ref[q_rows]
        scores = nt(keys, queries) * scaling
        weights = jnp.exp(scores - jnp.max(scores, axis=0, keepdims=True))
        shares = weights / jnp.sum(weights, axis=0, keepdims=True)
        grad_shares = nt(values, grads)
        inner = jnp.sum(shares * grad_shares, axis=0, keepdims=True)
        grad_scores = (shares * (grad_shares - inner)).astype(low_type)
        dq_ref[q_rows, :] = (tn(grad_scores, keys) * scaling).astype(low_type)
        dk = (product(grad_scores, queries) * scaling).astype(low_type)
        dv = product(shares.astype(low_type), grads).astype(low_type)
        split = 0
        if own is not None:
            split = own.stop - own.start
            dk_ref[own, :] = dk[:split]
            dv_ref[own, :] = dv[:split]
        if more is not None:
            more_dk_ref[more, :] = dk[split:]
            more_dv_ref[more, :] = dv[split:]


def self_specs(triple, more, heads):
    rows, width = triple.shape[0], triple.shape[1] // 3 // heads
    extra = more.shape[0]
    return [
        pl.BlockSpec((rows, width), lambda h: (0, h)),
        pl.BlockSpec((rows, width), lambda h: (0, heads + h)),
        pl.BlockSpec((rows, width), lambda h: (0, 2 * heads + h)),
        pl.BlockSpec((extra, width), lambda h: (0, h)),
        pl.BlockSpec((extra, width), lambda h: (0, heads + h)),
    ]


def self_forward(triple, more, groups):
    rows, model = triple.shape[0], triple.shape[1] // 3
    head = model // HEADS
    return pl.pallas_call(
        functools.partial(self_forward_kernel, groups, head**-0.5),
        out_shape=jax.ShapeDtypeStruct((rows, model), low_type),
        grid=(HEADS,),
        in_specs=self_specs(triple, more, HEADS),
        out_specs=pl.BlockSpec((rows, head), lambda h: (0, h)),
        compiler_params=params("arbitrary"),
        name="self_forward",
    )(triple, triple, triple, more, more)


def self_backward(triple, more, grads, groups):
    rows, model = triple.shape[0], triple.shape[1] // 3
    head = model // HEADS
    extra = more.shape[0]
    row_spec = pl.BlockSpec((rows, head), lambda h: (0, h))
    extra_spec = pl.BlockSpec((extra, head), lambda h: (0, h))
    return pl.pallas_call(
        functools.partial(self_backward_kernel, groups, head**-0.5),
        out_shape=[jax.ShapeDtypeStruct((rows, model), low_type)] * 3
        + [jax.ShapeDtypeStruct((extra, model), low_type)] * 2,
        grid=(HEADS,),
        in_specs=self_specs(triple, more, HEADS) + [row_spec],
        out_specs=[row_spec] * 3 + [extra_spec] * 2,
        compiler_params=params("arbitrary"),
        name="self_backward",
    )(triple, triple, triple, more, more, grads)


def ordered(bit, own, other, axis=0):
    first = jnp.where(bit == 0, own, other)
    last = jnp.where(bit == 0, other, own)
    return jnp.concatenate([first, last], axis=axis)


def half_of(array, bit, axis):
    size = array.shape[axis] // 2
    return lax.dynamic_slice_in_dim(array, bit * size, size, axis)


def swap(array, axis_name, mask):
    size = lax.axis_size(axis_name)
    return lax.ppermute(array, axis_name, [(i, i ^ mask) for i in range(size)])


class Plan:
    def __init__(self, micro_count, rows):
        self.blocks = lax.axis_size("blk")
        self.shards = lax.axis_size("fsdp")
        self.b = lax.axis_index("blk")
        self.x = lax.axis_index("fsdp")
        self.core = self.b & 1
        self.rows = rows
        self.micro_count = micro_count
        self.paired = self.shards == 2 and self.blocks % 2 == 0 and micro_count == 3
        if self.paired:
            self.micro = jnp.stack([self.x, jnp.int32(2)]).astype(jnp.int32)
            self.block_rows = rows
            self.per_item = 2
            self.groups = (
                (slice(0, 2 * rows), slice(0, 2 * rows), None),
                (slice(2 * rows, 3 * rows), slice(2 * rows, 3 * rows), slice(0, rows)),
            )
        else:
            self.micro = jnp.arange(micro_count, dtype=jnp.int32)
            self.block_rows = rows
            self.per_item = 1
            whole = rows * self.shards
            self.groups = tuple(
                (slice(i * rows, (i + 1) * rows), None, slice(i * whole, (i + 1) * whole))
                for i in range(micro_count)
            )

    def block_of(self, item, device):
        if self.paired and item == 1:
            return (device | 1) - 1 + self.x
        return device

    def turn(self, array):
        places = []
        for x in range(2):
            for b in range(self.blocks):
                core = b % 2
                places.append((b * 2 + x, (b - core + x) * 2 + core))
        return lax.ppermute(array, ("blk", "fsdp"), places)

    def spread(self, arrays, gate):
        if not self.paired:
            return [array.reshape(-1, array.shape[-1]) for array in arrays]
        rows = self.rows
        own = [lax.dynamic_index_in_dim(array, self.x, 0, False) for array in arrays]
        away = [lax.dynamic_index_in_dim(array, 1 - self.x, 0, False) for array in arrays]
        away = swap(jnp.concatenate(away, axis=0), "fsdp", 1)
        last = self.turn(jnp.concatenate([array[2] for array in arrays], axis=0))
        away, last = after(away, gate), after(last, gate)
        return [
            jnp.concatenate(
                [own[i], away[i * rows : (i + 1) * rows], last[i * rows : (i + 1) * rows]], axis=0
            )
            for i in range(len(arrays))
        ]

    def send_back(self, array):
        if not self.paired:
            return (array,)
        own, away, shared = (array[i * self.rows : (i + 1) * self.rows] for i in range(3))
        return own, swap(away, "fsdp", 1), self.turn(shared)

    def placed(self, parts):
        if not self.paired:
            return parts[0].reshape(self.micro_count, self.rows, -1)
        own, other, shared = parts
        return jnp.stack([jnp.where(self.x == 0, own, other), jnp.where(self.x == 0, other, own), shared])

    def columns(self, pair, norms, gate):
        if not self.paired:
            return (
                lax.all_gather(pair, "fsdp", axis=1, tiled=True),
                lax.all_gather(norms, "fsdp", axis=1, tiled=True),
            )
        rows, width = pair.shape
        flat = norms.reshape(-1, width)
        other = after(swap(jnp.concatenate([pair, flat], axis=0), "fsdp", 1), gate)
        return (
            ordered(self.x, pair, other[:rows], 1),
            ordered(self.x, norms, other[rows:].reshape(norms.shape), 1),
        )

    def fetch(self, weights):
        if not self.paired:
            return None
        model = weights[0].shape[1] if weights[0].shape[0] * 2 >= weights[0].shape[1] else weights[0].shape[0] * 2
        halves = []
        for weight in weights:
            half = half_of(weight, self.core, 0)
            halves += [half[:, at : at + model] for at in range(0, half.shape[1], model)]
        return swap(jnp.concatenate(halves, axis=0), "fsdp", 1)

    def whole(self, weights, near):
        if not self.paired:
            return [lax.all_gather(weight, "fsdp", axis=0, tiled=True) for weight in weights]
        far = swap(near, "blk", 1)
        model = near.shape[1]
        half = weights[0].shape[0] // 2
        results, at = [], 0
        for weight in weights:
            parts = []
            for column in range(0, weight.shape[1], model):
                away = ordered(self.core, near[at : at + half], far[at : at + half])
                parts.append(ordered(self.x, weight[:, column : column + model], away))
                at += half
            results.append(parts[0] if len(parts) == 1 else jnp.concatenate(parts, axis=1))
        return results

    def partner_rows(self, pairs):
        if self.paired:
            return swap(pairs[2 * self.rows :], "blk", 1)
        wide = pairs.reshape(self.micro_count, self.rows, -1)
        return lax.all_gather(wide, "fsdp", axis=1, tiled=True).reshape(-1, wide.shape[-1])

    def own_pairs(self, own, more):
        if self.paired:
            back = swap(more, "blk", 1).astype(jnp.float32)
            last = own[2 * self.rows :].astype(jnp.float32) + back
            return jnp.concatenate([own[: 2 * self.rows], last.astype(low_type)], axis=0)
        wide = more.reshape(self.micro_count, self.rows * self.shards, -1)
        back = lax.psum_scatter(wide, "fsdp", scatter_dimension=1, tiled=True)
        return back.reshape(-1, back.shape[-1])


def added(kept, received):
    return (kept.astype(jnp.float32) + received.astype(jnp.float32)).astype(low_type)


def after(value, *others):
    return lax.optimization_barrier((value,) + others)[0]


class Group:
    def __init__(self, plan, units, order):
        self.plan = plan
        self.units = units
        self.order = order
        core = plan.core
        self.send = jnp.concatenate([half_of(unit, 1 - core, 1) for unit in units], axis=1)
        self.kept = jnp.concatenate([half_of(unit, core, 1) for unit in units], axis=1)
        self.way = ("blk", 1)

    def halve(self, received, bit, axis, way):
        self.send = added(half_of(self.kept, 1 - bit, axis), half_of(received, 1 - bit, axis))
        self.kept = added(half_of(self.kept, bit, axis), half_of(received, bit, axis))
        self.way = way

    def push(self):
        received = swap(self.send, *self.way)
        step, self.order = self.order[:1], self.order[1:]
        plan = self.plan
        if step == "x":
            mask = plan.shards // 2
            while mask > 1:
                self.halve(received, jnp.where((plan.x & mask) > 0, 1, 0), 0, ("fsdp", mask))
                received = swap(self.send, *self.way)
                mask //= 2
            self.halve(received, plan.x & 1, 0, ("fsdp", 1))
            return self.send
        if step == "y":
            self.halve(received, (plan.b >> 1) & 1, 1, ("blk", 2))
            return self.send
        self.send = added(self.kept, received)[0]
        return self.send

    def chips_sum(self):
        blocks = self.plan.blocks
        groups = [list(range(low, blocks, 4)) for low in range(4)]
        rows, width = self.send.shape
        parts = lax.all_to_all(
            self.send, "blk", split_axis=0, concat_axis=0, axis_index_groups=groups, tiled=True
        )
        parts = parts.reshape(blocks // 4, rows * 4 // blocks, width).astype(jnp.float32)
        self.held = jnp.sum(parts, axis=0).astype(low_type)
        return self.held

    def finish(self):
        other = swap(self.held, "blk", 1)
        results, at = [], 0
        for unit in self.units:
            size = unit.shape[1] // 2
            own_part, other_part = self.held[at : at + size], other[at : at + size]
            results.append(ordered(self.plan.core, own_part, other_part).astype(jnp.float32))
            at += size
        return results


def chips_spread(groups):
    plan = groups[0].plan
    blocks = plan.blocks
    same_core = [
        [z * 4 + y * 2 + core for y in range(2) for z in range(blocks // 4)] for core in range(2)
    ]
    sizes = [group.held.shape[0] for group in groups]
    held = jnp.concatenate([group.held for group in groups], axis=0)
    held = lax.all_gather(held, "blk", axis_index_groups=same_core)
    at = 0
    for group, size in zip(groups, sizes):
        group.held = held[:, at : at + size].reshape(-1, held.shape[2])
        at += size


def route_pixels(plan, pixels, segment_ids, pad_ids, block_map):
    blocks, labels = plan.blocks, block_map.shape[1]
    slots, features = pixels.shape[1:]
    width = slots // blocks
    routed = plan.micro.shape[0]
    label_ids = jnp.arange(labels, dtype=jnp.int32)

    def of_items(array):
        return jnp.stack([lax.dynamic_index_in_dim(array, plan.micro[i], 0, False) for i in range(routed)])

    picked = of_items(segment_ids)
    counts = jnp.sum((picked[:, None, :] == label_ids[None, :, None]).astype(jnp.int32), axis=2)
    counts = jnp.stack([counts >> 4, counts & 15], axis=1).astype(jnp.float32)
    counts = jnp.pad(counts, ((0, 0), (0, 6), (0, 128 - labels)))
    chunks = prepare_pixels(jnp.swapaxes(pixels, 1, 2), plan.micro, counts, width)
    spread = lax.all_to_all(chunks, "blk", split_axis=0, concat_axis=0, tiled=True)
    arrived = spread[:, :, features + 1 : features + 3, :labels].astype(jnp.int32)
    totals = jnp.sum(16 * arrived[:, :, 0] + arrived[:, :, 1], axis=0)
    owners = of_items(block_map)
    images = label_ids[None, :] != of_items(pad_ids)[:, None]
    totals = jnp.where(images, totals, 0)
    earlier = label_ids[None, :] < label_ids[:, None]
    starts = jnp.sum(jnp.where(earlier[None], totals[:, None, :], 0), axis=2)
    devices = jnp.arange(blocks, dtype=jnp.int32)

    def extents(wanted):
        hit = (owners[:, None, :] == wanted[:, :, None]) & images[:, None, :]
        start = jnp.sum(jnp.where(hit, starts[:, None, :], 0), axis=2)
        return start, start + jnp.sum(jnp.where(hit, totals[:, None, :], 0), axis=2)

    def chunk_at(start, place):
        first = start // width
        return first + ((place - first) & (blocks - 1))

    def source_of(chunk):
        return jnp.clip(chunk // blocks, 0, blocks - 1)

    item = jnp.arange(routed, dtype=jnp.int32)
    wanted = jnp.stack([plan.block_of(i, devices) for i in range(routed)])
    start, finish = extents(wanted)
    flat = spread.reshape(blocks * routed, FEATURE_ROWS, width)
    piece_at = source_of(chunk_at(start, plan.b)) * routed + item[:, None]
    pieces = jnp.take(flat, piece_at.T.reshape(-1), axis=0, mode="clip")
    pieces = pieces.reshape(blocks, routed, FEATURE_ROWS, width)
    first = lax.all_to_all(pieces, "blk", split_axis=0, concat_axis=0, tiled=True)
    largest = jnp.argmax(totals, axis=1)
    largest_start = jnp.sum(jnp.where(label_ids[None, :] == largest[:, None], starts, 0), axis=1)
    second_at = source_of(chunk_at(largest_start, plan.b) + blocks) * routed + item
    second = lax.all_gather(jnp.take(flat, second_at, axis=0, mode="clip"), "blk", axis=0, tiled=False)
    mine = jnp.stack([plan.block_of(i, plan.b) for i in range(routed)])[:, None]
    start, finish = extents(mine)
    slot = (width * chunk_at(start, devices[None, :]))[:, :, None] + jnp.arange(width, dtype=jnp.int32)
    slot = slot.reshape(routed, -1)
    slot = jnp.concatenate([slot, slot + width * blocks], axis=1)
    mask = jnp.where((slot >= start) & (slot < finish), 0.0, masked_score)
    mask = jnp.broadcast_to(mask[:, None, :], (routed, 8, mask.shape[1]))
    big = ((finish - 1) // width - start // width >= blocks).astype(jnp.int32)[:, 0]
    if width < 128:
        join = 128 // width

        def merged(array):
            parts = array.reshape(blocks // join, join, routed, FEATURE_ROWS, width)
            return parts.transpose(0, 2, 3, 1, 4).reshape(blocks // join, routed, FEATURE_ROWS, 128)

        first, second = merged(first), merged(second)
    return chunks, pieces, first, second, mask, big


def on_device(
    latents,
    pixels,
    segment_ids,
    pad_ids,
    block_map,
    norm_gains,
    norm_biases,
    pixel_gain,
    pixel_bias,
    cross_query,
    cross_kv,
    cross_out,
    cross_up,
    cross_down,
    self_qkv,
    self_out,
    self_up,
    self_down,
    cotangent,
):
    micro_count, unused, rows, model = latents.shape
    features = pixels.shape[2]
    plan = Plan(micro_count, rows)
    scaling = model**-0.5

    chunks, pieces, first, second, mask, big = route_pixels(plan, pixels, segment_ids, pad_ids, block_map)
    if plan.paired:
        latents, cotangent = after(latents, chunks), after(cotangent, chunks)
        cross_kv, cross_query = after(cross_kv, chunks), after(cross_query, chunks)
    latent, upstream = plan.spread([latents[:, 0], cotangent[:, 0]], pieces)
    latent, upstream = latent.astype(jnp.float32), upstream.astype(jnp.float32)
    w_pair, norms = plan.columns(cross_kv, jnp.concatenate([norm_gains, norm_biases], axis=0), pieces)
    norms = norms.astype(jnp.float32)
    gains, biases = norms[:4], norms[4:]
    w_key, w_value = w_pair[:, :model], w_pair[:, model:]
    early = [cross_query]
    middle = [cross_out, cross_up, cross_down]
    late = [self_qkv, self_out, self_up, self_down]
    near_early, near_middle, near_late = plan.fetch(early), plan.fetch(middle), plan.fetch(late)
    if plan.paired:
        near_early, near_middle = after(near_early, pieces), after(near_middle, pieces)
        near_late = after(near_late, first)
    (w_query,) = plan.whole(early, near_early)
    w_out, w_up, w_down = plan.whole(middle, near_middle)
    w_triple, w_self_out, w_self_up, w_self_down = plan.whole(late, near_late)
    pixel_scaler = pixel_gain.astype(jnp.float32)
    pixel_offset = pixel_bias.astype(jnp.float32)

    def widened(rows_f32, scale):
        against = jnp.sum(rows_f32 * pixel_offset, axis=-1, keepdims=True)
        wide = jnp.concatenate([rows_f32 * pixel_scaler, against], axis=1) * scale
        return jnp.pad(wide, ((0, 0), (0, FEATURE_ROWS - features - 1))).astype(low_type)

    def narrowed(wide):
        return wide[:, :features] * pixel_scaler + wide[:, features : features + 1] * pixel_offset

    normed, scale = normalise(latent)
    hidden = (normed * gains[0] + biases[0]).astype(low_type)
    queries = product(hidden, w_query).astype(low_type)
    query_features = product_nt(queries, w_key)
    wide_queries = widened(query_features, scaling)
    summed = cross_call(
        cross_forward_kernel, big, [wide_queries], first, second, mask, plan.block_rows, plan.per_item
    )
    attended_features = narrowed(summed).astype(low_type)
    attended = product(attended_features, w_value).astype(low_type)
    first_sum = latent + product(attended, w_out)
    second_sum, stored_one = feed_forward(first_sum, gains[1], biases[1], w_up, w_down)
    normed_two, scale_two = normalise(second_sum)
    hidden_two = (normed_two * gains[2] + biases[2]).astype(low_type)
    triple = product(hidden_two, w_triple).astype(low_type)
    more = plan.partner_rows(triple[:, model:])
    blended = self_forward(triple, more, plan.groups)
    third_sum = second_sum + product(blended, w_self_out)
    mixed, stored_three = feed_forward(third_sum, gains[3], biases[3], w_self_up, w_self_down)
    mixed = plan.send_back(mixed.astype(low_type))

    def unit(grad):
        return grad.astype(low_type).reshape(plan.shards, -1, model)

    low = upstream.astype(low_type)
    upstream, grad_self_up, grad_self_down, gain_three, bias_three = feed_backward(
        upstream, low, third_sum, stored_three, gains[3], w_self_up, w_self_down
    )
    low = upstream.astype(low_type)
    grad_self_out = product_tn(blended, low)
    one = Group(plan, [unit(grad_self_up), unit(grad_self_down), unit(grad_self_out)], "xy")
    grad_blended = product_nt(low, w_self_out).astype(low_type)
    grad_blended = after(grad_blended, one.send)
    dq, dk, dv, more_dk, more_dv = self_backward(triple, more, grad_blended, plan.groups)
    pairs = plan.own_pairs(
        jnp.concatenate([dk, dv], axis=1), jnp.concatenate([more_dk, more_dv], axis=1)
    )
    pairs = after(pairs, one.push())
    grad_q = product_tn(hidden_two, dq)
    grad_k = product_tn(hidden_two, pairs[:, :model])
    grad_v = product_tn(hidden_two, pairs[:, model:])
    grad_hidden = product_nt(jnp.concatenate([dq, pairs], axis=1), w_triple)
    down, gain_two, bias_two = norm_backward(grad_hidden, normed_two, scale_two, gains[2])
    upstream = upstream + down
    low = upstream.astype(low_type)
    grad_down = product_tn(stored_one[2], low)
    two = Group(plan, [unit(grad_q), unit(grad_k), unit(grad_v), unit(grad_down)], "xy")
    low = after(low, one.push(), two.send, *mixed[1:2])
    upstream, grad_up, unused, gain_one, bias_one = feed_backward(
        upstream, low, first_sum, stored_one, gains[1], w_up, w_down
    )
    upstream = after(upstream, two.push(), *mixed[2:])
    low = upstream.astype(low_type)
    grad_out = product_tn(attended, low)
    grad_attended = product_nt(low, w_out).astype(low_type)
    grad_value = product_tn(attended_features, grad_attended)
    grad_features = product_nt(grad_attended, w_value)
    three = Group(plan, [unit(grad_up), unit(grad_out)], "yx")
    wide_grads = after(widened(grad_features, 1.0), one.push(), three.send)
    score_sums = cross_call(
        cross_backward_kernel,
        big,
        [wide_queries, wide_grads],
        first,
        second,
        mask,
        plan.block_rows,
        plan.per_item,
    )
    score_sums = after(score_sums, one.chips_sum(), three.push())
    key_sums = (narrowed(score_sums) * scaling).astype(low_type)
    grad_queries = product(key_sums, w_key).astype(low_type)
    grad_key = product_tn(key_sums, queries)
    pixel_gain_term = jnp.sum(
        query_features * score_sums[:, :features] * scaling + grad_features * summed[:, :features], axis=0
    )
    pixel_bias_term = jnp.sum(
        query_features * score_sums[:, features : features + 1] * scaling
        + grad_features * summed[:, features : features + 1],
        axis=0,
    )
    grad_query = product_tn(hidden, grad_queries)
    down, gain_zero, bias_zero = norm_backward(product_nt(grad_queries, w_query), normed, scale, gains[0])
    latents_grad = (upstream + down).astype(low_type)

    shards = plan.shards
    width = 2 * model // shards
    rows_of_pair = jnp.pad(jnp.concatenate([grad_key, grad_value], axis=1), ((0, 264 - features), (0, 0)))
    norm_terms = jnp.stack(
        [gain_zero, gain_one, gain_two, gain_three, bias_zero, bias_one, bias_two, bias_three]
    )
    pixel_terms = jnp.pad(jnp.stack([pixel_gain_term, pixel_bias_term]), ((0, 0), (0, 512 - features)))
    pixel_rows = pixel_terms.reshape(1, -1, width)
    tall = jnp.concatenate(
        [
            rows_of_pair.reshape(264, shards, width).transpose(1, 0, 2),
            norm_terms.reshape(8, shards, model // shards).transpose(1, 0, 2).reshape(shards, 4, width),
            jnp.broadcast_to(pixel_rows, (shards,) + pixel_rows.shape[1:]),
            jnp.zeros((shards, 384 - 268 - pixel_rows.shape[1], width), jnp.float32),
        ],
        axis=1,
    )
    four = Group(plan, [unit(grad_query), tall.astype(low_type).reshape(shards, -1, model)], "yx")
    four.send = after(four.send, two.push())
    chips_spread([one])
    four.send = after(four.push(), three.push())
    two.send = after(two.push(), four.send)
    latents_grad = after(latents_grad, two.send)
    three.send = after(three.push(), two.send)
    two.chips_sum()
    three.send = after(three.send, two.held)
    four.send = after(four.push(), three.send)
    chips_spread([two])
    three.chips_sum()
    four.send = after(four.push(), three.held)
    four.chips_sum()
    chips_spread([three, four])
    latents_grad = plan.placed(plan.send_back(latents_grad)).astype(jnp.float32)
    grad_self_up, grad_self_down, grad_self_out = one.finish()
    grad_q, grad_k, grad_v, grad_down = two.finish()
    grad_up, grad_out = three.finish()
    grad_query, tall = four.finish()
    tall = tall.reshape(384, width)
    norm_part = tall[264:268].reshape(8, model // shards)
    pixel_part = tall[268 : 268 + pixel_rows.shape[1]].reshape(2, 512)
    return (
        plan.placed(mixed)[:, None],
        latents_grad[:, None],
        norm_part[:4],
        norm_part[4:],
        pixel_part[0, :features],
        pixel_part[1, :features],
        grad_query,
        tall[:features],
        grad_out,
        grad_up,
        grad_down,
        jnp.concatenate([grad_q, grad_k, grad_v], axis=1),
        grad_self_out,
        grad_self_up,
        grad_self_down,
    )


def solution(mesh):
    placed = (
        P(None, "blk", "fsdp", None),
        P(None, "blk", None),
        P(None, "blk"),
        P(),
        P(),
        P(None, "fsdp"),
        P(None, "fsdp"),
        P(),
        P(),
        P("fsdp", None),
        P(None, "fsdp"),
        P("fsdp", None),
        P("fsdp", None),
        P("fsdp", None),
        P("fsdp", None),
        P("fsdp", None),
        P("fsdp", None),
        P("fsdp", None),
        P(None, "blk", "fsdp", None),
    )
    return jax.shard_map(
        on_device,
        mesh=mesh,
        in_specs=placed,
        out_specs=(
            P(None, "blk", "fsdp", None),
            P(None, "blk", "fsdp", None),
            P(None, "fsdp"),
            P(None, "fsdp"),
            P(),
            P(),
            P("fsdp", None),
            P(None, "fsdp"),
            P("fsdp", None),
            P("fsdp", None),
            P("fsdp", None),
            P("fsdp", None),
            P("fsdp", None),
            P("fsdp", None),
            P("fsdp", None),
        ),
        check_vma=False,
    )
```

time: 3030 us -> 709 us (0.23)
  waiting for transfers between devices: 1860 us -> 177 us
  matrix products: 446 us -> 96.8 us
  blocking collectives: 287 us -> 49 us
  local copies, waits for them, and re-layouts: 172 us -> 62.3 us
  starting transfers between devices: 4.89 us -> 90 us
  other arithmetic: 225 us -> 153 us
  Pallas kernels: 0 us -> 51.7 us
    reduce_scatter x21 -> x0, waiting for transfers between devices: 1030 us -> none  [the longest x6 392 us: on_device(): lax.psum_scatter(place_rows(partial_value, safe, valid, images).astype(jn...]
    all_gather x18 -> x4, waiting for transfers between devices: 648 us -> 18.2 us  [the longest x3 18.2 us: chips_spread(): held = lax.all_gather(held, 'blk', axis_index_groups=same_core)]
    dot_general x114 -> x32, matrix products: 432 us -> 96.8 us  [the longest x10 39.7 us: product_nt(): lax.dot_general(a, b, (((1,), (1,)), ((), ())), preferred_element_type=jn...]
    psum x1 -> x0, waiting for transfers between devices: 171 us -> none  [on_device(): lax.psum(shards[2].astype(jnp.bfloat16), 'blk').astype(jnp.float32)]
    psum x3 -> x0, blocking collectives: 155 us -> none  [the longest x2 119 us: on_device(): inner_all = lax.psum(inner_table, 'blk')]
    ppermute x0 -> x31, waiting for transfers between devices: none -> 138 us  [the longest x28 138 us: swap(): return lax.ppermute(array, axis_name, [(i, i ^ mask) for i in range(size)])]
    all_gather x8 -> x0, blocking collectives: 127 us -> none  [the longest x6 117 us: merged(): gathered = jax.tree.map(lambda a: lax.all_gather(a, axis), part)]
    ppermute x0 -> x31, starting transfers between devices: none -> 61.2 us  [the longest x28 45.7 us: swap(): return lax.ppermute(array, axis_name, [(i, i ^ mask) for i in range(size)])]
  transfers between devices with their start and end apart: 42 -> 39, of which waited for: 38 -> 14; matrix products, arithmetic and copies ran while one was open for 17% -> 34% of each run, Pallas kernels for 0% -> 5%
where the time goes in v1:
time: 709 us; the launch traced here: 697 us
  waiting for transfers between devices  177 us (25%)
  other arithmetic  153 us (22%)
  matrix products  96.8 us (14%)
  starting transfers between devices  90 us (13%)
  local copies, waits for them, and re-layouts  62.3 us (9%)
  Pallas kernels  51.7 us (7%)
  blocking collectives  49 us (7%)
  between operations  16.5 us (2%)
    ppermute x28, waiting for transfers between devices, swap(): return lax.ppermute(array, axis_name, [(i, i ^ mask) for i in range(size)])  138 us
    all_to_all x2, blocking collectives, chips_sum(): lax.all_to_all(self.send, 'blk', split_axis=0, concat_axis=0, axis_index_...  49 us
    ppermute x28, starting transfers between devices, swap(): return lax.ppermute(array, axis_name, [(i, i ^ mask) for i in range(size)])  45.7 us
    dot_general x10, matrix products, product_nt(): lax.dot_general(a, b, (((1,), (1,)), ((), ())), preferred_element_type=jn...  39.7 us
    convert_element_type x9, other arithmetic, added(): (kept.astype(jnp.float32) + received.astype(jnp.float32)).astype(low_type)  33.2 us
    dot_general x10, matrix products, product(): return jnp.dot(a, b, preferred_element_type=jnp.float32)  32.5 us
    select_n x17, other arithmetic, ordered(): first = jnp.where(bit == 0, own, other)  25.5 us
    dot_general x12, matrix products, product_tn(): lax.dot_general(a, b, (((0,), (0,)), ((), ())), preferred_element_type=jn...  24.6 us
  transfers between devices with their start and end apart: 39, of which 14 were waited for; matrix products, arithmetic and copies ran while one was open for 34% of the time, Pallas kernels for 5%

profile of v1, /device:TPU:0, one launch (start us, length us, event | category | flops | bytes accessed | tf_op | source)
XLA Modules:
  0.0 696.7 jit_solution(16317266340413454416)
XLA Ops:
  12.4 5.1 prepare_pixels.1
  17.5 7.5 %all-to-all-start = ((bf16[16,2,272,128]{3,2,1,0:T(8,128)(2,1)}), bf16[16,2,272,128]{3,2,1,0:T(8,128)(2,1)S(1)}, u32[]{:S(2)}, u32[]{:S(2)}) async-start(bf16[16,2,272,128]{3,2,1,0:T(8,128)(2,1)} %prepare_pixels.1), calls=%async_computation | async-start | bytes 4456448 | tf_op jit(solution)/shard_map/all_to_all | solution.py:528
  39.7 9.4 %collective-permute-start.1 = (bf16[512,1024]{1,0:T(8,128)(2,1)}, bf16[512,1024]{1,0:T(8,128)(2,1)}, u32[]{:S(2)}, u32[]{:S(2)}) collective-permute-start(bf16[512,1024]{1,0:T(8,128)(2,1)} %pad_maximum_fusion.32), channel_id=1, source_target_pairs={{0,0},{2,1},{4,4},{6,5},{8,8},{10,9},{12,12},{14,13},{16,16},{18,1... | collective-permute-start | bytes 3145736 | tf_op jit(solution)/shard_map/ppermute | solution.py:349
  54.7 13.8 %all-to-all-done = bf16[16,2,272,128]{3,2,1,0:T(8,128)(2,1)S(1)} async-done(((bf16[16,2,272,128]{3,2,1,0:T(8,128)(2,1)}), bf16[16,2,272,128]{3,2,1,0:T(8,128)(2,1)S(1)}, u32[]{:S(2)}, u32[]{:S(2)}) %all-to-all-start) | async-done | bytes 2228256 | tf_op jit(solution)/shard_map/all_to_all | solution.py:528
  73.8 11.7 %all-to-all-start.1 = ((bf16[16,2,272,128]{3,2,1,0:T(8,128)(2,1)}), bf16[16,2,272,128]{3,2,1,0:T(8,128)(2,1)S(1)}, u32[]{:S(2)}, u32[]{:S(2)}) async-start(bf16[16,2,272,128]{3,2,1,0:T(8,128)(2,1)} %bitcast.151), calls=%async_computation.1 | async-start | bytes 4456448 | tf_op jit(solution)/shard_map/all_to_all | solution.py:557
  90.1 21.7 %collective-permute-done = bf16[512,1024]{1,0:T(8,128)(2,1)} collective-permute-done((bf16[512,1024]{1,0:T(8,128)(2,1)}, bf16[512,1024]{1,0:T(8,128)(2,1)}, u32[]{:S(2)}, u32[]{:S(2)}) %collective-permute-start) | collective-permute-done | bytes 1048608 | tf_op jit(solution)/shard_map/ppermute | solution.py:307
  117.2 19.0 %collective-permute-start.6 = (bf16[768,1024]{1,0:T(8,128)(2,1)}, bf16[768,1024]{1,0:T(8,128)(2,1)S(1)}, u32[]{:S(2)}, u32[]{:S(2)}) collective-permute-start(bf16[768,1024]{1,0:T(8,128)(2,1)} %collective-permute-done.5), channel_id=1, source_target_pairs={{0,2},{2,0},{4,6},{6,4},{8,10},{10,8},{12,14},{14,12},{16,18},{18,... | collective-permute-start | bytes 4718600 | tf_op jit(solution)/shard_map/ppermute | solution.py:307
  154.8 8.8 %cross_attention.2 = f32[768,272]{1,0:T(8,128)} custom-call(s32[2]{0:T(128)} %get-tuple-element.221.big_ref, bf16[768,272]{1,0:T(8,128)(2,1)} %pad.23.query_ref, bf16[16,2,272,128]{3,2,1,0:T(8,128)(2,1)} %copy-done.1, bf16[16,2,272,128]{3,2,1,0:T(8,128)(2,1)} %bitcast.149, f32[2,8,4096]{2,1,0:T(8,128)} %broadcast_in_dim.82.mask_ref), custom_call_target="tpu_custom_call" | custom-call | tf_op jit(solution)/shard_map/cross_attention/pallas_call | solution.py:174
  167.6 22.4 %collective-permute-done.7 = bf16[1536,1024]{1,0:T(8,128)(2,1)} collective-permute-done((bf16[1536,1024]{1,0:T(8,128)(2,1)}, bf16[1536,1024]{1,0:T(8,128)(2,1)}, u32[]{:S(2)}, u32[]{:S(2)}) %collective-permute-start.7) | collective-permute-done | bytes 3145760 | tf_op jit(solution)/shard_map/ppermute | solution.py:307
  208.6 11.2 %convolution_convert_fusion.q_ref.k_ref.v_ref = bf16[768,3072]{1,0:T(8,128)(2,1)S(1)} fusion(bf16[768,1024]{1,0:T(8,128)(2,1)S(1)} %add_convert_fusion.6, bf16[512,1024]{1,0:T(8,128)(2,1)} %get-tuple-element.266, bf16[512,1024]{1,0:T(8,128)(2,1)} %get-tuple-element.267, bf16[512,1024]{1,0:T(8,128)(2,1)} %get-tuple-element.264, ...), kind=kOutput, calls=%fused_computation.3 | convolution fusion | flops 4871946240 | bytes 12582912 | tf_op jit(solution)/shard_map/dot_general | solution.py:20
  228.3 10.0 %self_forward.1 = bf16[768,1024]{1,0:T(8,128)(2,1)} custom-call(bf16[768,3072]{1,0:T(8,128)(2,1)} %copy-done, bf16[768,3072]{1,0:T(8,128)(2,1)} %copy-done, bf16[768,3072]{1,0:T(8,128)(2,1)} %copy-done, bf16[256,2048]{1,0:T(8,128)(2,1)} %collective-permute-done.9.more_k_ref.more_v_ref, bf16[256,2048]{1,0:T(8,128)(2,1)} %collective-permute-done.9.more_k_ref.more_v_ref), custom_call_target="tpu_custom_call" | custom-call | tf_op jit(solution)/shard_map/self_forward/pallas_call | solution.py:265
  271.6 17.7 %self_backward.1 = (bf16[768,1024]{1,0:T(8,128)(2,1)}, bf16[768,1024]{1,0:T(8,128)(2,1)}, bf16[768,1024]{1,0:T(8,128)(2,1)}, bf16[256,1024]{1,0:T(8,128)(2,1)}, bf16[256,1024]{1,0:T(8,128)(2,1)}) custom-call(bf16[768,3072]{1,0:T(8,128)(2,1)} %copy-done, bf16[768,3072]{1,0:T(8,128)(2,1)} %copy-done, bf16[768,3072]{1,0:T(8,128)(2,1)} %copy-done, ...), custom_call_target="tpu_custom_call" | custom-call | tf_op jit(solution)/shard_map/self_backward/pallas_call | solution.py:282
  300.5 5.2 add_convert_fusion.2
  306.9 11.3 %multiply_reduce_fusion.1 = (bf16[1024]{0:T(1024)(128)(2,1)S(1)}, f32[768]{0:T(1024)S(1)}, f32[768]{0:T(1024)S(1)}, bf16[1024]{0:T(1024)(128)(2,1)S(1)}, f32[768,1024]{1,0:T(8,128)}) fusion(f32[768,1024]{1,0:T(8,128)S(1)} %get-tuple-element.372, f32[768]{0:T(1024)S(1)} %add_rsqrt_fusion.1, f32[768]{0:T(1024)S(1)} %broadcast_multiply_fusion.10, ...), kind=kOutput, calls=%fused_computation.49 | convolution fusion | flops 4886097920 | bytes 17321984 | tf_op jit(solution)/shard_map/dot_general | solution.py:28
  335.5 5.3 collective-permute-start.11
  358.3 4.9 collective-permute-done.16
  365.7 4.7 all-to-all-start.2
  370.8 7.8 %add_convert_fusion = (bf16[1,1024,1024]{2,1,0:T(8,128)(2,1)}, bf16[1,1024,1024]{2,1,0:T(8,128)(2,1)}) fusion(bf16[2,1024,1024]{2,1,0:T(8,128)(2,1)} %collective-permute-done.15, s32[]{:T(128)S(6)} %select_n.588, bf16[2,1024,1024]{2,1,0:T(8,128)(2,1)} %pad_maximum_fusion.1, s32[]{:T(128)S(6)} %select_n.587), kind=kLoop, calls=%fused_computation.15 | loop fusion | flops 8388608 | bytes 12582920 | tf_op jit(solution)/shard_map/convert_element_type | solution.py:436
  383.6 4.5 all-to-all-done.2
  390.1 5.6 collective-permute-start.18
  403.6 10.0 %cross_attention.3 = f32[768,272]{1,0:T(8,128)} custom-call(s32[2]{0:T(128)} %get-tuple-element.221.big_ref, bf16[768,272]{1,0:T(8,128)(2,1)} %pad.23.query_ref, bf16[768,272]{1,0:T(8,128)(2,1)} %fusion.53.grad_ref, bf16[16,2,272,128]{3,2,1,0:T(8,128)(2,1)} %copy-done.1, bf16[16,2,272,128]{3,2,1,0:T(8,128)(2,1)} %bitcast.150, ...), custom_call_target="tpu_custom_call" | custom-call | tf_op jit(solution)/shard_map/cross_attention/pallas_call | solution.py:174
  416.1 5.1 add_convert_fusion.8
  447.1 26.1 %collective-permute-done.21 = bf16[2,256,1024]{2,1,0:T(8,128)(2,1)} collective-permute-done((bf16[2,256,1024]{2,1,0:T(8,128)(2,1)}, bf16[2,256,1024]{2,1,0:T(8,128)(2,1)}, u32[]{:S(2)}, u32[]{:S(2)}) %collective-permute-start.21) | collective-permute-done | bytes 1048608 | tf_op jit(solution)/shard_map/ppermute | solution.py:307
  475.4 28.3 %collective-permute-done.19 = bf16[1,512,1024]{2,1,0:T(8,128)(2,1)} collective-permute-done((bf16[1,512,1024]{2,1,0:T(8,128)(2,1)}, bf16[1,512,1024]{2,1,0:T(8,128)(2,1)}, u32[]{:S(2)}, u32[]{:S(2)}) %collective-permute-start.19) | collective-permute-done | bytes 1048608 | tf_op jit(solution)/shard_map/ppermute | solution.py:307
  506.2 4.4 add_convert_fusion.14
  510.6 29.2 %all_to_all.46 = bf16[4,128,1024]{2,1,0:T(8,128)(2,1)} all-to-all(bf16[4,128,1024]{2,1,0:T(8,128)(2,1)S(1)} %bitcast.157), channel_id=1, replica_groups={{0,8,16,24},{2,10,18,26},{4,12,20,28},{6,14,22,30},{1,9,17,25},{3,11,19..., dimensions={0} | all-to-all | bytes 2097152 | tf_op jit(solution)/shard_map/all_to_all | solution.py:480
  545.9 10.6 %collective-permute-done.24 = bf16[1,256,1024]{2,1,0:T(8,128)(2,1)S(1)} collective-permute-done((bf16[1,256,1024]{2,1,0:T(8,128)(2,1)}, bf16[1,256,1024]{2,1,0:T(8,128)(2,1)S(1)}, u32[]{:S(2)}, u32[]{:S(2)}) %collective-permute-start.24) | collective-permute-done | bytes 524320 | tf_op jit(solution)/shard_map/ppermute | solution.py:307
  569.8 8.4 %collective-permute-done.26 = bf16[1,224,1024]{2,1,0:T(8,128)(2,1)S(1)} collective-permute-done((bf16[1,224,1024]{2,1,0:T(8,128)(2,1)S(1)}, bf16[1,224,1024]{2,1,0:T(8,128)(2,1)S(1)}, u32[]{:S(2)}, u32[]{:S(2)}) %collective-permute-start.26) | collective-permute-done | bytes 458784 | tf_op jit(solution)/shard_map/ppermute | solution.py:307
  584.3 19.8 %all_to_all.47 = bf16[4,56,1024]{2,1,0:T(8,128)(2,1)} all-to-all(bf16[4,56,1024]{2,1,0:T(8,128)(2,1)} %bitcast.174), channel_id=1, replica_groups={{0,8,16,24},{2,10,18,26},{4,12,20,28},{6,14,22,30},{1,9,17,25},{3,11,19..., dimensions={0} | all-to-all | bytes 917504 | tf_op jit(solution)/shard_map/all_to_all | solution.py:480
  614.0 10.2 %collective-permute-done.22 = bf16[256,1024]{1,0:T(8,128)(2,1)S(1)} collective-permute-done((bf16[256,1024]{1,0:T(8,128)(2,1)S(1)}, bf16[256,1024]{1,0:T(8,128)(2,1)S(1)}, u32[]{:S(2)}, u32[]{:S(2)}) %collective-permute-start.22) | collective-permute-done | bytes 524320 | tf_op jit(solution)/shard_map/ppermute | solution.py:307
  633.3 18.1 %all-gather.11.cloned.1.call-done = bf16[960,1024]{1,0:T(8,128)(2,1)} async-done(((bf16[120,1024]{1,0:T(8,128)(2,1)}), bf16[960,1024]{1,0:T(8,128)(2,1)}) %all-gather.11.cloned.1.call-update) | async-done | bytes 1966096 | tf_op jit(solution)/shard_map/all_gather | solution.py:506
  659.3 20.3 %maximum_convert_fusion = f32[512,3072]{1,0:T(8,128)} fusion(bf16[256,1024]{1,0:T(8,128)(2,1)S(1)} %get-tuple-element.247, bf16[256,1024]{1,0:T(8,128)(2,1)S(1)} %get-tuple-element.246, bf16[256,1024]{1,0:T(8,128)(2,1)S(1)} %get-tuple-element.245, bf16[256,1024]{1,0:T(8,128)(2,1)S(1)} %get-tuple-element.244, bf16[256,1024]{1,0:T(8,128)(2,1)S(1)} %get-tuple-element.243, ...), kind=kLoop, calls=%fused_computation.47 | loop fusion | flops 18874368 | bytes 9437184 | tf_op jit(solution)/shard_map/concatenate | solution.py:775
  (565 shorter events, 281.9 us)
Async XLA Ops:
  17.5 50.9 %all-to-all-start = ((bf16[16,2,272,128]{3,2,1,0:T(8,128)(2,1)}), bf16[16,2,272,128]{3,2,1,0:T(8,128)(2,1)S(1)}, u32[]{:S(2)}, u32[]{:S(2)}) async-start(bf16[16,2,272,128]{3,2,1,0:T(8,128)(2,1)} %prepare_pixels.1), calls=%async_computation | async-start | bytes 4456448 | tf_op jit(solution)/shard_map/all_to_all | solution.py:528
  28.7 57.0 %collective-permute-start.5 = (bf16[768,1024]{1,0:T(8,128)(2,1)}, bf16[768,1024]{1,0:T(8,128)(2,1)}, u32[]{:S(2)}, u32[]{:S(2)}) collective-permute-start(bf16[768,1024]{1,0:T(8,128)(2,1)} %pad_maximum_fusion.15), channel_id=1, source_target_pairs={{0,1},{1,0},{2,3},{3,2},{4,5},{5,4},{6,7},{7,6},{8,9},{9,8},{10,11... | collective-permute-start | bytes 4718600 | tf_op jit(solution)/shard_map/ppermute | solution.py:307
  31.0 56.2 %collective-permute-start.3 = (bf16[256,1024]{1,0:T(8,128)(2,1)}, bf16[256,1024]{1,0:T(8,128)(2,1)}, u32[]{:S(2)}, u32[]{:S(2)}) collective-permute-start(bf16[256,1024]{1,0:T(8,128)(2,1)} %constant_dynamic-slice_fusion.25), channel_id=1, source_target_pairs={{0,1},{1,0},{2,3},{3,2},{4,5},{5,4},{6,7},{7,6},{8,9},{9,8},{10,11... | collective-permute-start | bytes 1572872 | tf_op jit(solution)/shard_map/ppermute | solution.py:307
  32.6 56.7 %collective-permute-start.2 = (bf16[265,1024]{1,0:T(8,128)(2,1)S(1)}, bf16[265,1024]{1,0:T(8,128)(2,1)}, u32[]{:S(2)}, u32[]{:S(2)}) collective-permute-start(bf16[265,1024]{1,0:T(8,128)(2,1)S(1)} %pad_maximum_fusion.44), channel_id=1, source_target_pairs={{0,1},{1,0},{2,3},{3,2},{4,5},{5,4},{6,7},{7,6},{8,9},{9,8},{10,11... | collective-permute-start | bytes 1628168 | tf_op jit(solution)/shard_map/ppermute | solution.py:307
  38.1 73.7 %collective-permute-start = (bf16[512,1024]{1,0:T(8,128)(2,1)}, bf16[512,1024]{1,0:T(8,128)(2,1)}, u32[]{:S(2)}, u32[]{:S(2)}) collective-permute-start(bf16[512,1024]{1,0:T(8,128)(2,1)} %pad_maximum_fusion.31), channel_id=1, source_target_pairs={{0,1},{1,0},{2,3},{3,2},{4,5},{5,4},{6,7},{7,6},{8,9},{9,8},{10,11... | collective-permute-start | bytes 3145736 | tf_op jit(solution)/shard_map/ppermute | solution.py:307
  39.7 75.2 %collective-permute-start.1 = (bf16[512,1024]{1,0:T(8,128)(2,1)}, bf16[512,1024]{1,0:T(8,128)(2,1)}, u32[]{:S(2)}, u32[]{:S(2)}) collective-permute-start(bf16[512,1024]{1,0:T(8,128)(2,1)} %pad_maximum_fusion.32), channel_id=1, source_target_pairs={{0,0},{2,1},{4,4},{6,5},{8,8},{10,9},{12,12},{14,13},{16,16},{18,1... | collective-permute-start | bytes 3145736 | tf_op jit(solution)/shard_map/ppermute | solution.py:349
  73.8 79.6 %all-to-all-start.1 = ((bf16[16,2,272,128]{3,2,1,0:T(8,128)(2,1)}), bf16[16,2,272,128]{3,2,1,0:T(8,128)(2,1)S(1)}, u32[]{:S(2)}, u32[]{:S(2)}) async-start(bf16[16,2,272,128]{3,2,1,0:T(8,128)(2,1)} %bitcast.151), calls=%async_computation.1 | async-start | bytes 4456448 | tf_op jit(solution)/shard_map/all_to_all | solution.py:557
  85.6 67.8 %all-gather.9.cloned.1.call-start = ((), (), s32[]{:S(2)}) async-start(), calls=%async_computation.6 | async-start | bytes 2367488 | tf_op jit(solution)/shard_map/all_gather | solution.py:561
  85.6 104.4 %collective-permute-start.7 = (bf16[1536,1024]{1,0:T(8,128)(2,1)}, bf16[1536,1024]{1,0:T(8,128)(2,1)}, u32[]{:S(2)}, u32[]{:S(2)}) collective-permute-start(bf16[1536,1024]{1,0:T(8,128)(2,1)} %copy-done.94), channel_id=1, source_target_pairs={{0,1},{1,0},{2,3},{3,2},{4,5},{5,4},{6,7},{7,6},{8,9},{9,8},{10,11... | collective-permute-start | bytes 9437192 | tf_op jit(solution)/shard_map/ppermute | solution.py:307
  87.2 50.0 %collective-permute-start.4 = (bf16[256,1024]{1,0:T(8,128)(2,1)}, bf16[256,1024]{1,0:T(8,128)(2,1)}, u32[]{:S(2)}, u32[]{:S(2)}) collective-permute-start(bf16[256,1024]{1,0:T(8,128)(2,1)} %collective-permute-done.3), channel_id=1, source_target_pairs={{0,2},{2,0},{4,6},{6,4},{8,10},{10,8},{12,14},{14,12},{16,18},{18,... | collective-permute-start | bytes 1572872 | tf_op jit(solution)/shard_map/ppermute | solution.py:307
  117.2 28.7 %collective-permute-start.6 = (bf16[768,1024]{1,0:T(8,128)(2,1)}, bf16[768,1024]{1,0:T(8,128)(2,1)S(1)}, u32[]{:S(2)}, u32[]{:S(2)}) collective-permute-start(bf16[768,1024]{1,0:T(8,128)(2,1)} %collective-permute-done.5), channel_id=1, source_target_pairs={{0,2},{2,0},{4,6},{6,4},{8,10},{10,8},{12,14},{14,12},{16,18},{18,... | collective-permute-start | bytes 4718600 | tf_op jit(solution)/shard_map/ppermute | solution.py:307
  263.1 37.3 %collective-permute-start.13 = (bf16[2,768,1024]{2,1,0:T(8,128)(2,1)}, bf16[2,768,1024]{2,1,0:T(8,128)(2,1)}, u32[]{:S(2)}, u32[]{:S(2)}) collective-permute-start(bf16[2,768,1024]{2,1,0:T(8,128)(2,1)} %pad_maximum_fusion.2), channel_id=1, source_target_pairs={{0,2},{2,0},{4,6},{6,4},{8,10},{10,8},{12,14},{14,12},{16,18},{18,... | collective-permute-start | bytes 9437192 | tf_op jit(solution)/shard_map/ppermute | solution.py:307
  267.8 64.9 %collective-permute-start.10 = (bf16[256,1024]{1,0:T(8,128)(2,1)}, bf16[256,1024]{1,0:T(8,128)(2,1)}, u32[]{:S(2)}, u32[]{:S(2)}) collective-permute-start(bf16[256,1024]{1,0:T(8,128)(2,1)} %slice.447), channel_id=1, source_target_pairs={{0,1},{1,0},{2,3},{3,2},{4,5},{5,4},{6,7},{7,6},{8,9},{9,8},{10,11... | collective-permute-start | bytes 1572872 | tf_op jit(solution)/shard_map/ppermute | solution.py:307
  305.6 37.7 %collective-permute-start.14 = (bf16[1,768,1024]{2,1,0:T(8,128)(2,1)}, bf16[1,768,1024]{2,1,0:T(8,128)(2,1)}, u32[]{:S(2)}, u32[]{:S(2)}) collective-permute-start(bf16[1,768,1024]{2,1,0:T(8,128)(2,1)} %get-tuple-element.227), channel_id=1, source_target_pairs={{0,1},{1,0},{2,3},{3,2},{4,5},{5,4},{6,7},{7,6},{8,9},{9,8},{10,11... | collective-permute-start | bytes 4718600 | tf_op jit(solution)/shard_map/ppermute | solution.py:307
  332.8 38.0 %collective-permute-start.15 = (bf16[2,1024,1024]{2,1,0:T(8,128)(2,1)}, bf16[2,1024,1024]{2,1,0:T(8,128)(2,1)}, u32[]{:S(2)}, u32[]{:S(2)}) collective-permute-start(bf16[2,1024,1024]{2,1,0:T(8,128)(2,1)} %pad_maximum_fusion), channel_id=1, source_target_pairs={{0,2},{2,0},{4,6},{6,4},{8,10},{10,8},{12,14},{14,12},{16,18},{18,... | collective-permute-start | bytes 12582920 | tf_op jit(solution)/shard_map/ppermute | solution.py:307
  335.5 43.1 %collective-permute-start.11 = (bf16[256,1024]{1,0:T(8,128)(2,1)}, bf16[256,1024]{1,0:T(8,128)(2,1)}, u32[]{:S(2)}, u32[]{:S(2)}) collective-permute-start(bf16[256,1024]{1,0:T(8,128)(2,1)} %get-tuple-element.328), channel_id=1, source_target_pairs={{0,0},{2,1},{4,4},{6,5},{8,8},{10,9},{12,12},{14,13},{16,16},{18,1... | collective-permute-start | bytes 1572872 | tf_op jit(solution)/shard_map/ppermute | solution.py:349
  345.5 17.7 %collective-permute-start.16 = (bf16[1,384,1024]{2,1,0:T(8,128)(2,1)S(1)}, bf16[1,384,1024]{2,1,0:T(8,128)(2,1)S(1)}, u32[]{:S(2)}, u32[]{:S(2)}) collective-permute-start(bf16[1,384,1024]{2,1,0:T(8,128)(2,1)S(1)} %add_convert_fusion.18), channel_id=1, source_target_pairs={{0,4},{2,6},{4,0},{6,2},{8,12},{10,14},{12,8},{14,10},{16,20},{18,... | collective-permute-start | bytes 2359304 | tf_op jit(solution)/shard_map/ppermute | solution.py:307
  365.7 22.4 %all-to-all-start.2 = ((bf16[4,96,1024]{2,1,0:T(8,128)(2,1)}), bf16[4,96,1024]{2,1,0:T(8,128)(2,1)}, u32[]{:S(2)}, u32[]{:S(2)}) async-start(bf16[4,96,1024]{2,1,0:T(8,128)(2,1)} %bitcast.162), calls=%async_computation.2 | async-start | bytes 1572864 | tf_op jit(solution)/shard_map/all_to_all | solution.py:480
  370.4 235.6 %all-gather.15.cloned.1.call-start = ((), (), s32[]{:S(2)}) async-start(), calls=%async_computation.9 | async-start | bytes 1769472 | tf_op jit(solution)/shard_map/all_gather | solution.py:506
  383.4 32.6 %collective-permute-start.17 = (bf16[2,512,1024]{2,1,0:T(8,128)(2,1)}, bf16[2,512,1024]{2,1,0:T(8,128)(2,1)}, u32[]{:S(2)}, u32[]{:S(2)}) collective-permute-start(bf16[2,512,1024]{2,1,0:T(8,128)(2,1)} %pad_maximum_fusion.12), channel_id=1, source_target_pairs={{0,2},{2,0},{4,6},{6,4},{8,10},{10,8},{12,14},{14,12},{16,18},{18,... | collective-permute-start | bytes 6291464 | tf_op jit(solution)/shard_map/ppermute | solution.py:307
  390.1 51.3 %collective-permute-start.18 = (bf16[1,1024,1024]{2,1,0:T(8,128)(2,1)}, bf16[1,1024,1024]{2,1,0:T(8,128)(2,1)}, u32[]{:S(2)}, u32[]{:S(2)}) collective-permute-start(bf16[1,1024,1024]{2,1,0:T(8,128)(2,1)} %get-tuple-element.225), channel_id=1, source_target_pairs={{0,1},{1,0},{2,3},{3,2},{4,5},{5,4},{6,7},{7,6},{8,9},{9,8},{10,11... | collective-permute-start | bytes 6291464 | tf_op jit(solution)/shard_map/ppermute | solution.py:307
  444.8 61.4 %collective-permute-start.20 = (bf16[2,448,1024]{2,1,0:T(8,128)(2,1)}, bf16[2,448,1024]{2,1,0:T(8,128)(2,1)}, u32[]{:S(2)}, u32[]{:S(2)}) collective-permute-start(bf16[2,448,1024]{2,1,0:T(8,128)(2,1)} %pad_maximum_fusion.13), channel_id=1, source_target_pairs={{0,2},{2,0},{4,6},{6,4},{8,10},{10,8},{12,14},{14,12},{16,18},{18,... | collective-permute-start | bytes 5505032 | tf_op jit(solution)/shard_map/ppermute | solution.py:307
  444.8 28.4 %collective-permute-start.21 = (bf16[2,256,1024]{2,1,0:T(8,128)(2,1)}, bf16[2,256,1024]{2,1,0:T(8,128)(2,1)}, u32[]{:S(2)}, u32[]{:S(2)}) collective-permute-start(bf16[2,256,1024]{2,1,0:T(8,128)(2,1)} %get-tuple-element.249), channel_id=1, source_target_pairs={{0,4},{2,6},{4,0},{6,2},{8,12},{10,14},{12,8},{14,10},{16,20},{18,... | collective-permute-start | bytes 3145736 | tf_op jit(solution)/shard_map/ppermute | solution.py:307
  446.4 57.3 %collective-permute-start.19 = (bf16[1,512,1024]{2,1,0:T(8,128)(2,1)}, bf16[1,512,1024]{2,1,0:T(8,128)(2,1)}, u32[]{:S(2)}, u32[]{:S(2)}) collective-permute-start(bf16[1,512,1024]{2,1,0:T(8,128)(2,1)} %add_convert_fusion.10), channel_id=1, source_target_pairs={{0,4},{2,6},{4,0},{6,2},{8,12},{10,14},{12,8},{14,10},{16,20},{18,... | collective-permute-start | bytes 3145736 | tf_op jit(solution)/shard_map/ppermute | solution.py:307
  446.9 159.3 %all-gather.13.cloned.1.call-start = ((), (), s32[]{:S(2)}) async-start(), calls=%async_computation.8 | async-start | bytes 2359296 | tf_op jit(solution)/shard_map/all_gather | solution.py:506
  542.0 24.2 %collective-permute-start.25 = (bf16[2,224,1024]{2,1,0:T(8,128)(2,1)}, bf16[2,224,1024]{2,1,0:T(8,128)(2,1)}, u32[]{:S(2)}, u32[]{:S(2)}) collective-permute-start(bf16[2,224,1024]{2,1,0:T(8,128)(2,1)} %get-tuple-element.68), channel_id=1, source_target_pairs={{0,4},{2,6},{4,0},{6,2},{8,12},{10,14},{12,8},{14,10},{16,20},{18,... | collective-permute-start | bytes 2752520 | tf_op jit(solution)/shard_map/ppermute | solution.py:307
  558.8 24.4 %all-to-all-start.4 = ((bf16[4,64,1024]{2,1,0:T(8,128)(2,1)}), bf16[4,64,1024]{2,1,0:T(8,128)(2,1)}, u32[]{:S(2)}, u32[]{:S(2)}) async-start(bf16[4,64,1024]{2,1,0:T(8,128)(2,1)} %bitcast.173), calls=%async_computation.4 | async-start | bytes 1048576 | tf_op jit(solution)/shard_map/all_to_all | solution.py:480
  562.9 88.5 %all-gather.11.cloned.1.call-start = ((), (), s32[]{:S(2)}) async-start(), calls=%async_computation.7 | async-start | bytes 2211840 | tf_op jit(solution)/shard_map/all_gather | solution.py:506
  606.0 19.0 %collective-permute-start.30 = (bf16[768,1024]{1,0:T(8,128)(2,1)}, bf16[768,1024]{1,0:T(8,128)(2,1)}, u32[]{:S(2)}, u32[]{:S(2)}) collective-permute-start(bf16[768,1024]{1,0:T(8,128)(2,1)} %all-gather.15.cloned.1.call-done), channel_id=1, source_target_pairs={{0,2},{2,0},{4,6},{6,4},{8,10},{10,8},{12,14},{14,12},{16,18},{18,... | collective-permute-start | bytes 4718600 | tf_op jit(solution)/shard_map/ppermute | solution.py:307
  606.1 49.7 %collective-permute-start.29 = (bf16[1024,1024]{1,0:T(8,128)(2,1)}, bf16[1024,1024]{1,0:T(8,128)(2,1)}, u32[]{:S(2)}, u32[]{:S(2)}) collective-permute-start(bf16[1024,1024]{1,0:T(8,128)(2,1)} %all-gather.13.cloned.1.call-done), channel_id=1, source_target_pairs={{0,2},{2,0},{4,6},{6,4},{8,10},{10,8},{12,14},{14,12},{16,18},{18,... | collective-permute-start | bytes 6291464 | tf_op jit(solution)/shard_map/ppermute | solution.py:307
  655.3 24.4 %collective-permute-start.27 = (bf16[448,1024]{1,0:T(8,128)(2,1)S(1)}, bf16[448,1024]{1,0:T(8,128)(2,1)S(1)}, u32[]{:S(2)}, u32[]{:S(2)}) collective-permute-start(bf16[448,1024]{1,0:T(8,128)(2,1)S(1)} %bitcast.158), channel_id=1, source_target_pairs={{0,2},{2,0},{4,6},{6,4},{8,10},{10,8},{12,14},{14,12},{16,18},{18,... | collective-permute-start | bytes 2752520 | tf_op jit(solution)/shard_map/ppermute | solution.py:307
  655.3 30.0 %collective-permute-start.28 = (bf16[512,1024]{1,0:T(8,128)(2,1)}, bf16[512,1024]{1,0:T(8,128)(2,1)}, u32[]{:S(2)}, u32[]{:S(2)}) collective-permute-start(bf16[512,1024]{1,0:T(8,128)(2,1)} %bitcast.63), channel_id=1, source_target_pairs={{0,2},{2,0},{4,6},{6,4},{8,10},{10,8},{12,14},{14,12},{16,18},{18,... | collective-permute-start | bytes 3145736 | tf_op jit(solution)/shard_map/ppermute | solution.py:307
  (140 other events, 1426.8 us)
Sparse Core Ops, SparseCore 0:
  89.3 61.2 all-gather.8
  447.0 56.3 all-gather.14
  542.2 60.1 all-gather.12
  606.1 45.3 all-gather.10

commit v2 on v1

--- a/solution.py
+++ b/solution.py
@@ -218,12 +218,13 @@
     more_k_ref,
     more_v_ref,
     grad_ref,
-    dq_ref,
-    dk_ref,
-    dv_ref,
-    more_dk_ref,
-    more_dv_ref,
+    wide_ref,
+    more_ref,
 ):
+    head = q_ref.shape[1]
+    model = wide_ref.shape[1] // 3
+    column = pl.multiple_of(pl.program_id(0) * head, head)
+    at_q, at_k, at_v = (pl.ds(pl.multiple_of(part * model + column, head), head) for part in range(3))
     for q_rows, own, more in groups:
         keys, values = keys_of(own, more, k_ref, v_ref, more_k_ref, more_v_ref)
         queries = q_ref[q_rows]
@@ -234,17 +235,17 @@
         grad_shares = nt(values, grads)
         inner = jnp.sum(shares * grad_shares, axis=0, keepdims=True)
         grad_scores = (shares * (grad_shares - inner)).astype(low_type)
-        dq_ref[q_rows, :] = (tn(grad_scores, keys) * scaling).astype(low_type)
+        wide_ref[q_rows, at_q] = (tn(grad_scores, keys) * scaling).astype(low_type)
         dk = (product(grad_scores, queries) * scaling).astype(low_type)
         dv = product(shares.astype(low_type), grads).astype(low_type)
         split = 0
         if own is not None:
             split = own.stop - own.start
-            dk_ref[own, :] = dk[:split]
-            dv_ref[own, :] = dv[:split]
+            wide_ref[own, at_k] = dk[:split]
+            wide_ref[own, at_v] = dv[:split]
         if more is not None:
-            more_dk_ref[more, :] = dk[split:]
-            more_dv_ref[more, :] = dv[split:]
+            more_ref[more, at_q] = dk[split:]
+            more_ref[more, at_k] = dv[split:]
 
 
 def self_specs(triple, more, heads):
@@ -277,18 +278,46 @@
     rows, model = triple.shape[0], triple.shape[1] // 3
     head = model // HEADS
     extra = more.shape[0]
-    row_spec = pl.BlockSpec((rows, head), lambda h: (0, h))
-    extra_spec = pl.BlockSpec((extra, head), lambda h: (0, h))
     return pl.pallas_call(
         functools.partial(self_backward_kernel, groups, head**-0.5),
-        out_shape=[jax.ShapeDtypeStruct((rows, model), low_type)] * 3
-        + [jax.ShapeDtypeStruct((extra, model), low_type)] * 2,
+        out_shape=[
+            jax.ShapeDtypeStruct((rows, 3 * model), low_type),
+            jax.ShapeDtypeStruct((extra, 2 * model), low_type),
+        ],
         grid=(HEADS,),
-        in_specs=self_specs(triple, more, HEADS) + [row_spec],
-        out_specs=[row_spec] * 3 + [extra_spec] * 2,
+        in_specs=self_specs(triple, more, HEADS) + [pl.BlockSpec((rows, head), lambda h: (0, h))],
+        out_specs=[
+            pl.BlockSpec((rows, 3 * model), lambda h: (0, 0)),
+            pl.BlockSpec((extra, 2 * model), lambda h: (0, 0)),
+        ],
         compiler_params=params("arbitrary"),
         name="self_backward",
     )(triple, triple, triple, more, more, grads)
+
+
+def widen_kernel(places, core_ref, *refs):
+    out_ref = refs[-1]
+    count = (len(refs) - 1) // 2
+    first = core_ref[0] == 0
+    for i, (source, at, size) in enumerate(places):
+        own = refs[source][at : at + size]
+        other = refs[count + source][at : at + size]
+        columns = slice(i * own.shape[1], (i + 1) * own.shape[1])
+        out_ref[:size, columns] = jnp.where(first, own, other).astype(jnp.float32)
+        out_ref[size:, columns] = jnp.where(first, other, own).astype(jnp.float32)
+
+
+def widen(core, own, other, places):
+    rows, width = 2 * places[0][2], len(places) * own[0].shape[1]
+    return pl.pallas_call(
+        functools.partial(widen_kernel, tuple(places)),
+        out_shape=jax.ShapeDtypeStruct((rows, width), jnp.float32),
+        in_specs=[pl.BlockSpec(memory_space=pltpu.SMEM)]
+        + [pl.BlockSpec(memory_space=pltpu.VMEM)] * (2 * len(own)),
+        out_specs=pl.BlockSpec(memory_space=pltpu.VMEM),
+        compiler_params=pltpu.CompilerParams(vmem_limit_bytes=VMEM_LIMIT),
+        name="widen",
+    )(core.reshape(1).astype(jnp.int32), *own, *other)
 
 
 def ordered(bit, own, other, axis=0):
@@ -314,9 +343,10 @@
         self.b = lax.axis_index("blk")
         self.x = lax.axis_index("fsdp")
         self.core = self.b & 1
+        self.side = (self.b >> 1) & 1
         self.rows = rows
         self.micro_count = micro_count
-        self.paired = self.shards == 2 and self.blocks % 2 == 0 and micro_count == 3
+        self.paired = self.shards == 2 and self.blocks % 4 == 0 and micro_count == 3
         if self.paired:
             self.micro = jnp.stack([self.x, jnp.int32(2)]).astype(jnp.int32)
             self.block_rows = rows
@@ -335,6 +365,9 @@
                 for i in range(micro_count)
             )
 
+    def same_core(self):
+        return [list(range(core, self.blocks, 2)) for core in range(2)]
+
     def block_of(self, item, device):
         if self.paired and item == 1:
             return (device | 1) - 1 + self.x
@@ -348,21 +381,12 @@
                 places.append((b * 2 + x, (b - core + x) * 2 + core))
         return lax.ppermute(array, ("blk", "fsdp"), places)
 
-    def spread(self, arrays, gate):
+    def spread(self, array):
         if not self.paired:
-            return [array.reshape(-1, array.shape[-1]) for array in arrays]
-        rows = self.rows
-        own = [lax.dynamic_index_in_dim(array, self.x, 0, False) for array in arrays]
-        away = [lax.dynamic_index_in_dim(array, 1 - self.x, 0, False) for array in arrays]
-        away = swap(jnp.concatenate(away, axis=0), "fsdp", 1)
-        last = self.turn(jnp.concatenate([array[2] for array in arrays], axis=0))
-        away, last = after(away, gate), after(last, gate)
-        return [
-            jnp.concatenate(
-                [own[i], away[i * rows : (i + 1) * rows], last[i * rows : (i + 1) * rows]], axis=0
-            )
-            for i in range(len(arrays))
-        ]
+            return (array.reshape(-1, array.shape[-1]),)
+        own = lax.dynamic_index_in_dim(array, self.x, 0, False)
+        away = swap(lax.dynamic_index_in_dim(array, 1 - self.x, 0, False), "fsdp", 1)
+        return own, away, self.turn(array[2])
 
     def send_back(self, array):
         if not self.paired:
@@ -376,44 +400,42 @@
         own, other, shared = parts
         return jnp.stack([jnp.where(self.x == 0, own, other), jnp.where(self.x == 0, other, own), shared])
 
-    def columns(self, pair, norms, gate):
+    def columns(self, pair, norms):
         if not self.paired:
             return (
                 lax.all_gather(pair, "fsdp", axis=1, tiled=True),
                 lax.all_gather(norms, "fsdp", axis=1, tiled=True),
             )
-        rows, width = pair.shape
-        flat = norms.reshape(-1, width)
-        other = after(swap(jnp.concatenate([pair, flat], axis=0), "fsdp", 1), gate)
+        flat = norms.reshape(-1, pair.shape[1])
+        return (swap(jnp.concatenate([pair, flat], axis=0), "fsdp", 1),)
+
+    def joined(self, pair, norms, other):
+        if not self.paired:
+            return other
+        rows = pair.shape[0]
         return (
-            ordered(self.x, pair, other[:rows], 1),
-            ordered(self.x, norms, other[rows:].reshape(norms.shape), 1),
+            ordered(self.x, pair, other[0][:rows], 1),
+            ordered(self.x, norms, other[0][rows:].reshape(norms.shape), 1),
         )
 
-    def fetch(self, weights):
+    def fetch(self, weights, chips):
         if not self.paired:
             return None
-        model = weights[0].shape[1] if weights[0].shape[0] * 2 >= weights[0].shape[1] else weights[0].shape[0] * 2
-        halves = []
-        for weight in weights:
-            half = half_of(weight, self.core, 0)
-            halves += [half[:, at : at + model] for at in range(0, half.shape[1], model)]
-        return swap(jnp.concatenate(halves, axis=0), "fsdp", 1)
-
-    def whole(self, weights, near):
+        part = self.core if chips == 1 else 2 * self.core + self.side
+        size = weights[0].shape[0] // (2 * chips)
+        parts = [lax.dynamic_slice_in_dim(weight, part * size, size, 0) for weight in weights]
+        return jnp.concatenate(parts, axis=1)
+
+    def whole(self, weights, near, chips):
         if not self.paired:
             return [lax.all_gather(weight, "fsdp", axis=0, tiled=True) for weight in weights]
-        far = swap(near, "blk", 1)
-        model = near.shape[1]
-        half = weights[0].shape[0] // 2
+        if chips == 2:
+            near = ordered(self.side, near, swap(near, "blk", 2))
+        away = ordered(self.core, near, swap(near, "blk", 1))
         results, at = [], 0
         for weight in weights:
-            parts = []
-            for column in range(0, weight.shape[1], model):
-                away = ordered(self.core, near[at : at + half], far[at : at + half])
-                parts.append(ordered(self.x, weight[:, column : column + model], away))
-                at += half
-            results.append(parts[0] if len(parts) == 1 else jnp.concatenate(parts, axis=1))
+            results.append(ordered(self.x, weight, away[:, at : at + weight.shape[1]]))
+            at += weight.shape[1]
         return results
 
     def partner_rows(self, pairs):
@@ -422,14 +444,16 @@
         wide = pairs.reshape(self.micro_count, self.rows, -1)
         return lax.all_gather(wide, "fsdp", axis=1, tiled=True).reshape(-1, wide.shape[-1])
 
-    def own_pairs(self, own, more):
+    def own_pairs(self, wide, more):
+        model = wide.shape[1] // 3
         if self.paired:
             back = swap(more, "blk", 1).astype(jnp.float32)
-            last = own[2 * self.rows :].astype(jnp.float32) + back
-            return jnp.concatenate([own[: 2 * self.rows], last.astype(low_type)], axis=0)
-        wide = more.reshape(self.micro_count, self.rows * self.shards, -1)
-        back = lax.psum_scatter(wide, "fsdp", scatter_dimension=1, tiled=True)
-        return back.reshape(-1, back.shape[-1])
+            first = 2 * self.rows
+            last = (wide[first:, model:].astype(jnp.float32) + back).astype(low_type)
+            return lax.dynamic_update_slice(wide, last, (first, model))
+        split = more.reshape(self.micro_count, self.rows * self.shards, -1)
+        back = lax.psum_scatter(split, "fsdp", scatter_dimension=1, tiled=True)
+        return lax.dynamic_update_slice(wide, back.reshape(-1, back.shape[-1]), (0, model))
 
 
 def added(kept, received):
@@ -441,76 +465,68 @@
 
 
 class Group:
-    def __init__(self, plan, units, order):
+    def __init__(self, plan, units):
         self.plan = plan
-        self.units = units
-        self.order = order
+        self.sizes = [unit.shape[1] // 2 for unit in units]
         core = plan.core
         self.send = jnp.concatenate([half_of(unit, 1 - core, 1) for unit in units], axis=1)
         self.kept = jnp.concatenate([half_of(unit, core, 1) for unit in units], axis=1)
-        self.way = ("blk", 1)
-
-    def halve(self, received, bit, axis, way):
-        self.send = added(half_of(self.kept, 1 - bit, axis), half_of(received, 1 - bit, axis))
-        self.kept = added(half_of(self.kept, bit, axis), half_of(received, bit, axis))
-        self.way = way
-
-    def push(self):
-        received = swap(self.send, *self.way)
-        step, self.order = self.order[:1], self.order[1:]
-        plan = self.plan
-        if step == "x":
-            mask = plan.shards // 2
-            while mask > 1:
-                self.halve(received, jnp.where((plan.x & mask) > 0, 1, 0), 0, ("fsdp", mask))
-                received = swap(self.send, *self.way)
-                mask //= 2
-            self.halve(received, plan.x & 1, 0, ("fsdp", 1))
-            return self.send
-        if step == "y":
-            self.halve(received, (plan.b >> 1) & 1, 1, ("blk", 2))
-            return self.send
-        self.send = added(self.kept, received)[0]
+
+    def over_core(self):
+        received = swap(self.send, "blk", 1)
+        mask = self.plan.shards // 2
+        while mask:
+            bit = jnp.where((self.plan.x & mask) > 0, 1, 0)
+            self.send = added(half_of(self.kept, 1 - bit, 0), half_of(received, 1 - bit, 0))
+            self.kept = added(half_of(self.kept, bit, 0), half_of(received, bit, 0))
+            if mask > 1:
+                received = swap(self.send, "fsdp", mask)
+            mask //= 2
         return self.send
 
-    def chips_sum(self):
-        blocks = self.plan.blocks
-        groups = [list(range(low, blocks, 4)) for low in range(4)]
-        rows, width = self.send.shape
+    def over_fsdp(self, *earlier):
+        received = swap(self.send, "fsdp", 1)
+        if earlier:
+            received = after(received, *earlier)
+        self.total = added(self.kept, received)[0]
+        return self.total
+
+    def over_chips(self, *earlier):
+        same_core = self.plan.same_core()
+        rows, width = self.total.shape
         parts = lax.all_to_all(
-            self.send, "blk", split_axis=0, concat_axis=0, axis_index_groups=groups, tiled=True
+            self.total, "blk", split_axis=0, concat_axis=0, axis_index_groups=same_core, tiled=True
         )
-        parts = parts.reshape(blocks // 4, rows * 4 // blocks, width).astype(jnp.float32)
+        if earlier:
+            parts = after(parts, *earlier)
+        count = len(same_core[0])
+        parts = parts.reshape(count, rows // count, width).astype(jnp.float32)
         self.held = jnp.sum(parts, axis=0).astype(low_type)
         return self.held
 
     def finish(self):
-        other = swap(self.held, "blk", 1)
+        self.other = swap(self.held, "blk", 1)
         results, at = [], 0
-        for unit in self.units:
-            size = unit.shape[1] // 2
-            own_part, other_part = self.held[at : at + size], other[at : at + size]
+        for size in self.sizes:
+            own_part, other_part = self.held[at : at + size], self.other[at : at + size]
             results.append(ordered(self.plan.core, own_part, other_part).astype(jnp.float32))
             at += size
         return results
 
 
-def chips_spread(groups):
+def back_from_chips(groups):
     plan = groups[0].plan
-    blocks = plan.blocks
-    same_core = [
-        [z * 4 + y * 2 + core for y in range(2) for z in range(blocks // 4)] for core in range(2)
-    ]
     sizes = [group.held.shape[0] for group in groups]
     held = jnp.concatenate([group.held for group in groups], axis=0)
-    held = lax.all_gather(held, "blk", axis_index_groups=same_core)
+    held = lax.all_gather(held, "blk", axis_index_groups=plan.same_core())
     at = 0
     for group, size in zip(groups, sizes):
         group.held = held[:, at : at + size].reshape(-1, held.shape[2])
         at += size
-
-
-def route_pixels(plan, pixels, segment_ids, pad_ids, block_map):
+    return held
+
+
+def route_pixels(plan, pixels, segment_ids, pad_ids, block_map, fetch):
     blocks, labels = plan.blocks, block_map.shape[1]
     slots, features = pixels.shape[1:]
     width = slots // blocks
@@ -554,6 +570,9 @@
     piece_at = source_of(chunk_at(start, plan.b)) * routed + item[:, None]
     pieces = jnp.take(flat, piece_at.T.reshape(-1), axis=0, mode="clip")
     pieces = pieces.reshape(blocks, routed, FEATURE_ROWS, width)
+    fetched, sent = fetch(chunks, pieces)
+    if sent is not None:
+        pieces = after(pieces, sent)
     first = lax.all_to_all(pieces, "blk", split_axis=0, concat_axis=0, tiled=True)
     largest = jnp.argmax(totals, axis=1)
     largest_start = jnp.sum(jnp.where(label_ids[None, :] == largest[:, None], starts, 0), axis=1)
@@ -575,7 +594,7 @@
             return parts.transpose(0, 2, 3, 1, 4).reshape(blocks // join, routed, FEATURE_ROWS, 128)
 
         first, second = merged(first), merged(second)
-    return chunks, pieces, first, second, mask, big
+    return fetched, first, second, mask, big
 
 
 def on_device(
@@ -604,26 +623,32 @@
     plan = Plan(micro_count, rows)
     scaling = model**-0.5
 
-    chunks, pieces, first, second, mask, big = route_pixels(plan, pixels, segment_ids, pad_ids, block_map)
-    if plan.paired:
-        latents, cotangent = after(latents, chunks), after(cotangent, chunks)
-        cross_kv, cross_query = after(cross_kv, chunks), after(cross_query, chunks)
-    latent, upstream = plan.spread([latents[:, 0], cotangent[:, 0]], pieces)
-    latent, upstream = latent.astype(jnp.float32), upstream.astype(jnp.float32)
-    w_pair, norms = plan.columns(cross_kv, jnp.concatenate([norm_gains, norm_biases], axis=0), pieces)
+    norm_rows = jnp.concatenate([norm_gains, norm_biases], axis=0)
+    early, middle = [cross_query], [cross_out, cross_up, cross_down]
+    late, last = [self_qkv], [self_out, self_up, self_down]
+
+    def fetch(chunks, pieces):
+        if not plan.paired:
+            return (plan.spread(latents[:, 0]), plan.columns(cross_kv, norm_rows)) + (None,) * 4, None
+        latent = plan.spread(after(latents, chunks)[:, 0])
+        near_early = swap(plan.fetch([after(cross_query, chunks)], 1), "fsdp", 1)
+        other = plan.columns(after(cross_kv, chunks), norm_rows)
+        send = plan.fetch([after(middle[0], near_early, *latent[1:], *other)] + middle[1:], 1)
+        near_middle = swap(send, "fsdp", 1)
+        near_late = swap(plan.fetch([after(late[0], send, pieces)], 2), "fsdp", 1)
+        near_last = swap(plan.fetch([after(last[0], send, pieces)] + last[1:], 2), "fsdp", 1)
+        latent = (latent[0],) + tuple(after(part, pieces) for part in latent[1:])
+        near_early, other = after(near_early, pieces), (after(other[0], pieces),)
+        return (latent, other, near_early, near_middle, near_late, near_last), send
+
+    fetched, first, second, mask, big = route_pixels(plan, pixels, segment_ids, pad_ids, block_map, fetch)
+    latent, other, near_early, near_middle, near_late, near_last = fetched
+    latent = jnp.concatenate(latent, axis=0).astype(jnp.float32)
+    w_pair, norms = plan.joined(cross_kv, norm_rows, other)
     norms = norms.astype(jnp.float32)
     gains, biases = norms[:4], norms[4:]
     w_key, w_value = w_pair[:, :model], w_pair[:, model:]
-    early = [cross_query]
-    middle = [cross_out, cross_up, cross_down]
-    late = [self_qkv, self_out, self_up, self_down]
-    near_early, near_middle, near_late = plan.fetch(early), plan.fetch(middle), plan.fetch(late)
-    if plan.paired:
-        near_early, near_middle = after(near_early, pieces), after(near_middle, pieces)
-        near_late = after(near_late, first)
-    (w_query,) = plan.whole(early, near_early)
-    w_out, w_up, w_down = plan.whole(middle, near_middle)
-    w_triple, w_self_out, w_self_up, w_self_down = plan.whole(late, near_late)
+    (w_query,) = plan.whole(early, near_early, 1)
     pixel_scaler = pixel_gain.astype(jnp.float32)
     pixel_offset = pixel_bias.astype(jnp.float32)
 
@@ -640,9 +665,17 @@
     queries = product(hidden, w_query).astype(low_type)
     query_features = product_nt(queries, w_key)
     wide_queries = widened(query_features, scaling)
+    if plan.paired:
+        near_middle, near_late = after(near_middle, wide_queries), after(near_late, first)
+    w_out, w_up, w_down = plan.whole(middle, near_middle, 1)
+    (w_triple,) = plan.whole(late, near_late, 2)
     summed = cross_call(
         cross_forward_kernel, big, [wide_queries], first, second, mask, plan.block_rows, plan.per_item
     )
+    if plan.paired:
+        near_last, cotangent = after(near_last, summed), after(cotangent, summed)
+    w_self_out, w_self_up, w_self_down = plan.whole(last, near_last, 2)
+    upstream = plan.spread(cotangent[:, 0])
     attended_features = narrowed(summed).astype(low_type)
     attended = product(attended_features, w_value).astype(low_type)
     first_sum = latent + product(attended, w_out)
@@ -654,46 +687,46 @@
     blended = self_forward(triple, more, plan.groups)
     third_sum = second_sum + product(blended, w_self_out)
     mixed, stored_three = feed_forward(third_sum, gains[3], biases[3], w_self_up, w_self_down)
-    mixed = plan.send_back(mixed.astype(low_type))
+    mixed = mixed.astype(low_type)
 
     def unit(grad):
         return grad.astype(low_type).reshape(plan.shards, -1, model)
 
+    if plan.paired:
+        upstream = (upstream[0],) + tuple(after(part, third_sum) for part in upstream[1:])
+    upstream = jnp.concatenate(upstream, axis=0).astype(jnp.float32)
     low = upstream.astype(low_type)
     upstream, grad_self_up, grad_self_down, gain_three, bias_three = feed_backward(
         upstream, low, third_sum, stored_three, gains[3], w_self_up, w_self_down
     )
     low = upstream.astype(low_type)
     grad_self_out = product_tn(blended, low)
-    one = Group(plan, [unit(grad_self_up), unit(grad_self_down), unit(grad_self_out)], "xy")
+    grad_self_out = product_tn(blended, low)
+    one = Group(plan, [unit(grad_self_up), unit(grad_self_down), unit(grad_self_out)])
     grad_blended = product_nt(low, w_self_out).astype(low_type)
-    grad_blended = after(grad_blended, one.send)
-    dq, dk, dv, more_dk, more_dv = self_backward(triple, more, grad_blended, plan.groups)
-    pairs = plan.own_pairs(
-        jnp.concatenate([dk, dv], axis=1), jnp.concatenate([more_dk, more_dv], axis=1)
-    )
-    pairs = after(pairs, one.push())
-    grad_q = product_tn(hidden_two, dq)
-    grad_k = product_tn(hidden_two, pairs[:, :model])
-    grad_v = product_tn(hidden_two, pairs[:, model:])
-    grad_hidden = product_nt(jnp.concatenate([dq, pairs], axis=1), w_triple)
+    grad_blended = after(grad_blended, one.over_core(), mixed)
+    triple_grads, more_grads = self_backward(triple, more, grad_blended, plan.groups)
+    triple_grads = plan.own_pairs(triple_grads, more_grads)
+    two = Group(
+        plan, [unit(product_tn(hidden_two, triple_grads[:, i * model : (i + 1) * model])) for i in range(3)]
+    )
+    triple_grads = after(triple_grads, two.send, one.over_fsdp())
+    grad_hidden = product_nt(triple_grads, w_triple)
     down, gain_two, bias_two = norm_backward(grad_hidden, normed_two, scale_two, gains[2])
     upstream = upstream + down
     low = upstream.astype(low_type)
     grad_down = product_tn(stored_one[2], low)
-    two = Group(plan, [unit(grad_q), unit(grad_k), unit(grad_v), unit(grad_down)], "xy")
-    low = after(low, one.push(), two.send, *mixed[1:2])
+    low = after(low, two.over_core())
     upstream, grad_up, unused, gain_one, bias_one = feed_backward(
         upstream, low, first_sum, stored_one, gains[1], w_up, w_down
     )
-    upstream = after(upstream, two.push(), *mixed[2:])
     low = upstream.astype(low_type)
     grad_out = product_tn(attended, low)
+    three = Group(plan, [unit(grad_up), unit(grad_down), unit(grad_out)])
     grad_attended = product_nt(low, w_out).astype(low_type)
     grad_value = product_tn(attended_features, grad_attended)
     grad_features = product_nt(grad_attended, w_value)
-    three = Group(plan, [unit(grad_up), unit(grad_out)], "yx")
-    wide_grads = after(widened(grad_features, 1.0), one.push(), three.send)
+    wide_grads = after(widened(grad_features, 1.0), three.send, one.over_chips())
     score_sums = cross_call(
         cross_backward_kernel,
         big,
@@ -704,7 +737,7 @@
         plan.block_rows,
         plan.per_item,
     )
-    score_sums = after(score_sums, one.chips_sum(), three.push())
+    score_sums = after(score_sums, two.over_fsdp(), three.over_core())
     key_sums = (narrowed(score_sums) * scaling).astype(low_type)
     grad_queries = product(key_sums, w_key).astype(low_type)
     grad_key = product_tn(key_sums, queries)
@@ -737,25 +770,23 @@
         ],
         axis=1,
     )
-    four = Group(plan, [unit(grad_query), tall.astype(low_type).reshape(shards, -1, model)], "yx")
-    four.send = after(four.send, two.push())
-    chips_spread([one])
-    four.send = after(four.push(), three.push())
-    two.send = after(two.push(), four.send)
-    latents_grad = after(latents_grad, two.send)
-    three.send = after(three.push(), two.send)
-    two.chips_sum()
-    three.send = after(three.send, two.held)
-    four.send = after(four.push(), three.send)
-    chips_spread([two])
-    three.chips_sum()
-    four.send = after(four.push(), three.held)
-    four.chips_sum()
-    chips_spread([three, four])
-    latents_grad = plan.placed(plan.send_back(latents_grad)).astype(jnp.float32)
+    four = Group(plan, [unit(grad_query), tall.astype(low_type).reshape(shards, -1, model)])
+    two.over_chips(four.send)
+    early_sums = back_from_chips([one, two])
+    four.over_core()
+    three.over_fsdp(four.send)
+    four.over_fsdp(three.total)
+    mixed = plan.send_back(after(mixed, four.total))
+    latents_grad = plan.send_back(after(latents_grad, four.total))
+    three.over_chips(four.total, early_sums)
+    four.over_chips(three.held)
+    back_from_chips([three, four])
     grad_self_up, grad_self_down, grad_self_out = one.finish()
-    grad_q, grad_k, grad_v, grad_down = two.finish()
-    grad_up, grad_out = three.finish()
+    two.finish()
+    half = two.sizes[0]
+    grad_triple = widen(plan.core, [two.held], [two.other], [(0, i * half, half) for i in range(3)])
+    latents_grad = plan.placed(latents_grad).astype(jnp.float32)
+    grad_up, grad_down, grad_out = three.finish()
     grad_query, tall = four.finish()
     tall = tall.reshape(384, width)
     norm_part = tall[264:268].reshape(8, model // shards)
@@ -772,7 +803,7 @@
         grad_out,
         grad_up,
         grad_down,
-        jnp.concatenate([grad_q, grad_k, grad_v], axis=1),
+        grad_triple,
         grad_self_out,
         grad_self_up,
         grad_self_down,

time: 709 us -> 670 us (0.945)
  waiting for transfers between devices: 177 us -> 230 us
  blocking collectives: 49 us -> 0 us
  other arithmetic: 153 us -> 122 us
  starting transfers between devices: 90 us -> 78.5 us
  Pallas kernels: 51.7 us -> 59.4 us
    all_to_all x2 -> x4, waiting for transfers between devices: 7.32 us -> 83 us  [over_chips(): lax.all_to_all(self.total, 'blk', split_axis=0, concat_axis=0, axis_index...]
    all_to_all x2 -> x0, blocking collectives: 49 us -> none  [chips_sum(): lax.all_to_all(self.send, 'blk', split_axis=0, concat_axis=0, axis_index_...]
    ppermute x28 -> x29, waiting for transfers between devices: 138 us -> 98.4 us  [swap(): return lax.ppermute(array, axis_name, [(i, i ^ mask) for i in range(size)])]
    all_to_all x1, waiting for transfers between devices: 0.01 us -> 28.8 us  [route_pixels(): lax.all_to_all(pieces, 'blk', split_axis=0, concat_axis=0, tiled=True)]
    concatenate x9 -> x8, other arithmetic: 28.8 us -> 5.81 us  [the longest x2 2.18 us: fetch(): return jnp.concatenate(parts, axis=1)]
    ppermute x28 -> x29, starting transfers between devices: 45.7 us -> 26.2 us  [swap(): return lax.ppermute(array, axis_name, [(i, i ^ mask) for i in range(size)])]
    all_to_all x2 -> x4, starting transfers between devices: 8.85 us -> 24.9 us  [over_chips(): lax.all_to_all(self.total, 'blk', split_axis=0, concat_axis=0, axis_index...]
    all_to_all x1, waiting for transfers between devices: 13.8 us -> 0.01 us  [route_pixels(): lax.all_to_all(chunks, 'blk', split_axis=0, concat_axis=0, tiled=True)]
  transfers between devices with their start and end apart: 39 -> 42, of which waited for: 14 -> 14; matrix products, arithmetic and copies ran while one was open for 34% -> 32% of each run, Pallas kernels for 5% -> 5%
where the time goes in v2:
time: 670 us; the launch traced here: 664 us
  waiting for transfers between devices  230 us (34%)
  other arithmetic  122 us (18%)
  matrix products  99.6 us (15%)
  starting transfers between devices  78.5 us (12%)
  Pallas kernels  59.4 us (9%)
  local copies, waits for them, and re-layouts  58.2 us (9%)
  between operations  16 us (2%)
    ppermute x29, waiting for transfers between devices, swap(): return lax.ppermute(array, axis_name, [(i, i ^ mask) for i in range(size)])  98.4 us
    all_to_all x4, waiting for transfers between devices, over_chips(): lax.all_to_all(self.total, 'blk', split_axis=0, concat_axis=0, axis_index...  83 us
    dot_general x10, matrix products, product_nt(): lax.dot_general(a, b, (((1,), (1,)), ((), ())), preferred_element_type=jn...  43 us
    dot_general x10, matrix products, product(): return jnp.dot(a, b, preferred_element_type=jnp.float32)  30.2 us
    all_to_all x1, waiting for transfers between devices, route_pixels(): lax.all_to_all(pieces, 'blk', split_axis=0, concat_axis=0, tiled=True)  28.8 us
    dot_general x12, matrix products, product_tn(): lax.dot_general(a, b, (((0,), (0,)), ((), ())), preferred_element_type=jn...  26.4 us
    ppermute x29, starting transfers between devices, swap(): return lax.ppermute(array, axis_name, [(i, i ^ mask) for i in range(size)])  26.2 us
    convert_element_type x8, other arithmetic, added(): (kept.astype(jnp.float32) + received.astype(jnp.float32)).astype(low_type)  26.1 us
  transfers between devices with their start and end apart: 42, of which 14 were waited for; matrix products, arithmetic and copies ran while one was open for 32% of the time, Pallas kernels for 5%

profile of v2, /device:TPU:0, one launch (start us, length us, event | category | flops | bytes accessed | tf_op | source)
XLA Modules:
  0.0 664.1 jit_solution(3666019952930851746)
XLA Ops:
  12.4 5.1 prepare_pixels.1
  17.5 7.5 %all-to-all-start = ((bf16[16,2,272,128]{3,2,1,0:T(8,128)(2,1)}), bf16[16,2,272,128]{3,2,1,0:T(8,128)(2,1)S(1)}, u32[]{:S(2)}, u32[]{:S(2)}) async-start(bf16[16,2,272,128]{3,2,1,0:T(8,128)(2,1)} %prepare_pixels.1), calls=%async_computation | async-start | bytes 4456448 | tf_op jit(solution)/shard_map/all_to_all | solution.py:544
  43.7 25.7 %collective-permute-done = bf16[256,1024]{1,0:T(8,128)(2,1)} collective-permute-done((bf16[256,1024]{1,0:T(8,128)(2,1)}, bf16[256,1024]{1,0:T(8,128)(2,1)}, u32[]{:S(2)}, u32[]{:S(2)}) %collective-permute-start) | collective-permute-done | bytes 524320 | tf_op jit(solution)/shard_map/ppermute | solution.py:336
  89.4 9.1 %all-to-all-start.1 = ((bf16[16,2,272,128]{3,2,1,0:T(8,128)(2,1)}), bf16[16,2,272,128]{3,2,1,0:T(8,128)(2,1)S(1)}, u32[]{:S(2)}, u32[]{:S(2)}) async-start(bf16[16,2,272,128]{3,2,1,0:T(8,128)(2,1)} %bitcast.150), calls=%async_computation.1 | async-start | bytes 4456448 | tf_op jit(solution)/shard_map/all_to_all | solution.py:576
  125.1 28.8 %all-to-all-done.1.first_ref = bf16[16,2,272,128]{3,2,1,0:T(8,128)(2,1)S(1)} async-done(((bf16[16,2,272,128]{3,2,1,0:T(8,128)(2,1)}), bf16[16,2,272,128]{3,2,1,0:T(8,128)(2,1)S(1)}, u32[]{:S(2)}, u32[]{:S(2)}) %all-to-all-start.1) | async-done | bytes 2228256 | tf_op jit(solution)/shard_map/all_to_all | solution.py:576
  158.2 8.3 %cross_attention.2 = f32[768,272]{1,0:T(8,128)} custom-call(s32[2]{0:T(128)} %get-tuple-element.223.big_ref, bf16[768,272]{1,0:T(8,128)(2,1)} %pad.23.query_ref, bf16[16,2,272,128]{3,2,1,0:T(8,128)(2,1)} %copy-done.1, bf16[16,2,272,128]{3,2,1,0:T(8,128)(2,1)} %bitcast.148, f32[2,8,4096]{2,1,0:T(8,128)} %broadcast_in_dim.82.mask_ref), custom_call_target="tpu_custom_call" | custom-call | tf_op jit(solution)/shard_map/cross_attention/pallas_call | solution.py:174
  170.1 6.0 collective-permute-start.15
  199.7 5.3 convolution_convert_fusion.q_ref.k_ref.v_ref
  211.4 10.8 %self_forward.1 = bf16[768,1024]{1,0:T(8,128)(2,1)} custom-call(bf16[768,3072]{1,0:T(8,128)(2,1)} %copy-done, bf16[768,3072]{1,0:T(8,128)(2,1)} %copy-done, bf16[768,3072]{1,0:T(8,128)(2,1)} %copy-done, bf16[256,2048]{1,0:T(8,128)(2,1)} %collective-permute-done.10.more_k_ref.more_v_ref, bf16[256,2048]{1,0:T(8,128)(2,1)} %collective-permute-done.10.more_k_ref.more_v_ref), custom_call_target="tpu_custom_call" | custom-call | tf_op jit(solution)/shard_map/self_forward/pallas_call | solution.py:266
  230.3 4.3 fusion.21
  266.4 20.1 %self_backward.1 = (bf16[768,3072]{1,0:T(8,128)(2,1)}, bf16[256,2048]{1,0:T(8,128)(2,1)}) custom-call(bf16[768,3072]{1,0:T(8,128)(2,1)} %copy-done, bf16[768,3072]{1,0:T(8,128)(2,1)} %copy-done, bf16[768,3072]{1,0:T(8,128)(2,1)} %copy-done, bf16[256,2048]{1,0:T(8,128)(2,1)} %collective-permute-done.10.more_k_ref.more_v_ref, ...), custom_call_target="tpu_custom_call" | custom-call | tf_op jit(solution)/shard_map/self_backward/pallas_call | solution.py:281
  301.3 11.3 %multiply_reduce_fusion.1 = (bf16[1024]{0:T(1024)(128)(2,1)S(1)}, f32[768]{0:T(1024)S(1)}, f32[768]{0:T(1024)S(1)}, bf16[1024]{0:T(1024)(128)(2,1)S(1)}, f32[768,1024]{1,0:T(8,128)}) fusion(f32[768,1024]{1,0:T(8,128)S(1)} %get-tuple-element.346, f32[768]{0:T(1024)S(1)} %add_rsqrt_fusion.1, f32[768]{0:T(1024)S(1)} %broadcast_multiply_fusion.10, ...), kind=kOutput, calls=%fused_computation.57 | convolution fusion | flops 4851494912 | bytes 17321984 | tf_op jit(solution)/shard_map/dot_general | solution.py:28
  339.9 4.1 add_convert_fusion.5
  343.9 10.6 %all-to-all-start.2 = ((bf16[8,96,1024]{2,1,0:T(8,128)(2,1)}), bf16[8,96,1024]{2,1,0:T(8,128)(2,1)}, u32[]{:S(2)}, u32[]{:S(2)}) async-start(bf16[8,96,1024]{2,1,0:T(8,128)(2,1)} %bitcast.156), calls=%async_computation.2 | async-start | bytes 3145728 | tf_op jit(solution)/shard_map/all_to_all | solution.py:497
  366.9 25.4 %all-to-all-done.2 = bf16[8,96,1024]{2,1,0:T(8,128)(2,1)} async-done(((bf16[8,96,1024]{2,1,0:T(8,128)(2,1)}), bf16[8,96,1024]{2,1,0:T(8,128)(2,1)}, u32[]{:S(2)}, u32[]{:S(2)}) %all-to-all-start.2) | async-done | bytes 1572896 | tf_op jit(solution)/shard_map/all_to_all | solution.py:497
  394.0 10.0 %cross_attention.3 = f32[768,272]{1,0:T(8,128)} custom-call(s32[2]{0:T(128)} %get-tuple-element.223.big_ref, bf16[768,272]{1,0:T(8,128)(2,1)} %pad.23.query_ref, bf16[768,272]{1,0:T(8,128)(2,1)} %fusion.53.grad_ref, bf16[16,2,272,128]{3,2,1,0:T(8,128)(2,1)} %copy-done.1, bf16[16,2,272,128]{3,2,1,0:T(8,128)(2,1)} %bitcast.149, ...), custom_call_target="tpu_custom_call" | custom-call | tf_op jit(solution)/shard_map/cross_attention/pallas_call | solution.py:174
  404.0 4.1 add_convert_fusion
  408.0 4.3 all-to-all-start.4
  422.8 5.5 fusion.10
  440.3 4.2 collective-permute-start.27
  444.4 5.2 all-to-all-done.4
  454.9 24.4 %collective-permute-done.27 = bf16[1,768,1024]{2,1,0:T(8,128)(2,1)} collective-permute-done((bf16[1,768,1024]{2,1,0:T(8,128)(2,1)}, bf16[1,768,1024]{2,1,0:T(8,128)(2,1)}, u32[]{:S(2)}, u32[]{:S(2)}) %collective-permute-start.27) | collective-permute-done | bytes 1572896 | tf_op jit(solution)/shard_map/ppermute | solution.py:336
  479.3 4.1 add_convert_fusion.2
  483.4 5.8 all-to-all-start.3
  490.9 20.0 %collective-permute-done.22 = bf16[1,448,1024]{2,1,0:T(8,128)(2,1)S(1)} collective-permute-done((bf16[1,448,1024]{2,1,0:T(8,128)(2,1)}, bf16[1,448,1024]{2,1,0:T(8,128)(2,1)S(1)}, u32[]{:S(2)}, u32[]{:S(2)}) %collective-permute-start.22) | collective-permute-done | bytes 917536 | tf_op jit(solution)/shard_map/ppermute | solution.py:336
  513.6 31.4 %all-to-all-done.3 = bf16[8,96,1024]{2,1,0:T(8,128)(2,1)S(1)} async-done(((bf16[8,96,1024]{2,1,0:T(8,128)(2,1)}), bf16[8,96,1024]{2,1,0:T(8,128)(2,1)S(1)}, u32[]{:S(2)}, u32[]{:S(2)}) %all-to-all-start.3) | async-done | bytes 1572896 | tf_op jit(solution)/shard_map/all_to_all | solution.py:497
  546.2 4.2 all-to-all-start.5
  552.5 21.0 %all-to-all-done.5 = bf16[8,56,1024]{2,1,0:T(8,128)(2,1)} async-done(((bf16[8,56,1024]{2,1,0:T(8,128)(2,1)}), bf16[8,56,1024]{2,1,0:T(8,128)(2,1)}, u32[]{:S(2)}, u32[]{:S(2)}) %all-to-all-start.5) | async-done | bytes 917536 | tf_op jit(solution)/shard_map/all_to_all | solution.py:497
  583.3 11.0 %collective-permute-done.25 = bf16[256,1024]{1,0:T(8,128)(2,1)S(1)} collective-permute-done((bf16[256,1024]{1,0:T(8,128)(2,1)S(1)}, bf16[256,1024]{1,0:T(8,128)(2,1)S(1)}, u32[]{:S(2)}, u32[]{:S(2)}) %collective-permute-start.25) | collective-permute-done | bytes 524320 | tf_op jit(solution)/shard_map/ppermute | solution.py:336
  595.1 9.4 %collective-permute-done.23 = bf16[256,1024]{1,0:T(8,128)(2,1)S(1)} collective-permute-done((bf16[256,1024]{1,0:T(8,128)(2,1)S(1)}, bf16[256,1024]{1,0:T(8,128)(2,1)S(1)}, u32[]{:S(2)}, u32[]{:S(2)}) %collective-permute-start.23) | collective-permute-done | bytes 524320 | tf_op jit(solution)/shard_map/ppermute | solution.py:336
  608.0 20.0 %all-gather.11.cloned.1.call-done = bf16[1216,1024]{1,0:T(8,128)(2,1)} async-done(((bf16[152,1024]{1,0:T(8,128)(2,1)}), bf16[1216,1024]{1,0:T(8,128)(2,1)}) %all-gather.11.cloned.1.call-update) | async-done | bytes 2490384 | tf_op jit(solution)/shard_map/all_gather | solution.py:521
  634.7 5.0 widen.1
  (546 shorter events, 276.0 us)
Async XLA Ops:
  17.5 53.1 %all-to-all-start = ((bf16[16,2,272,128]{3,2,1,0:T(8,128)(2,1)}), bf16[16,2,272,128]{3,2,1,0:T(8,128)(2,1)S(1)}, u32[]{:S(2)}, u32[]{:S(2)}) async-start(bf16[16,2,272,128]{3,2,1,0:T(8,128)(2,1)} %prepare_pixels.1), calls=%async_computation | async-start | bytes 4456448 | tf_op jit(solution)/shard_map/all_to_all | solution.py:544
  25.1 132.4 %all-gather.7.cloned.1.call-start = ((), (), s32[]{:S(2)}) async-start(), calls=%async_computation.6 | async-start | bytes 2367488 | tf_op jit(solution)/shard_map/all_gather | solution.py:580
  26.0 17.7 %collective-permute-start.3 = (bf16[256,1024]{1,0:T(8,128)(2,1)}, bf16[256,1024]{1,0:T(8,128)(2,1)}, u32[]{:S(2)}, u32[]{:S(2)}) collective-permute-start(bf16[256,1024]{1,0:T(8,128)(2,1)} %constant_dynamic-slice_fusion.29), channel_id=1, source_target_pairs={{0,1},{1,0},{2,3},{3,2},{4,5},{5,4},{6,7},{7,6},{8,9},{9,8},{10,11... | collective-permute-start | bytes 1572872 | tf_op jit(solution)/shard_map/ppermute | solution.py:336
  29.4 39.9 %collective-permute-start.2 = (bf16[265,1024]{1,0:T(8,128)(2,1)}, bf16[265,1024]{1,0:T(8,128)(2,1)}, u32[]{:S(2)}, u32[]{:S(2)}) collective-permute-start(bf16[265,1024]{1,0:T(8,128)(2,1)} %pad_maximum_fusion.41), channel_id=1, source_target_pairs={{0,1},{1,0},{2,3},{3,2},{4,5},{5,4},{6,7},{7,6},{8,9},{9,8},{10,11... | collective-permute-start | bytes 1628168 | tf_op jit(solution)/shard_map/ppermute | solution.py:336
  34.2 35.1 %collective-permute-start = (bf16[256,1024]{1,0:T(8,128)(2,1)}, bf16[256,1024]{1,0:T(8,128)(2,1)}, u32[]{:S(2)}, u32[]{:S(2)}) collective-permute-start(bf16[256,1024]{1,0:T(8,128)(2,1)} %get-tuple-element.311), channel_id=1, source_target_pairs={{0,1},{1,0},{2,3},{3,2},{4,5},{5,4},{6,7},{7,6},{8,9},{9,8},{10,11... | collective-permute-start | bytes 1572872 | tf_op jit(solution)/shard_map/ppermute | solution.py:336
  70.6 42.0 %collective-permute-start.5 = (bf16[256,3072]{1,0:T(8,128)(2,1)}, bf16[256,3072]{1,0:T(8,128)(2,1)}, u32[]{:S(2)}, u32[]{:S(2)}) collective-permute-start(bf16[256,3072]{1,0:T(8,128)(2,1)} %pad_maximum_fusion.19), channel_id=1, source_target_pairs={{0,1},{1,0},{2,3},{3,2},{4,5},{5,4},{6,7},{7,6},{8,9},{9,8},{10,11... | collective-permute-start | bytes 4718600 | tf_op jit(solution)/shard_map/ppermute | solution.py:336
  83.3 19.1 %collective-permute-start.4 = (bf16[256,1024]{1,0:T(8,128)(2,1)}, bf16[256,1024]{1,0:T(8,128)(2,1)}, u32[]{:S(2)}, u32[]{:S(2)}) collective-permute-start(bf16[256,1024]{1,0:T(8,128)(2,1)} %collective-permute-done.3), channel_id=1, source_target_pairs={{0,2},{2,0},{4,6},{6,4},{8,10},{10,8},{12,14},{14,12},{16,18},{18,... | collective-permute-start | bytes 1572872 | tf_op jit(solution)/shard_map/ppermute | solution.py:336
  89.4 64.6 %all-to-all-start.1 = ((bf16[16,2,272,128]{3,2,1,0:T(8,128)(2,1)}), bf16[16,2,272,128]{3,2,1,0:T(8,128)(2,1)S(1)}, u32[]{:S(2)}, u32[]{:S(2)}) async-start(bf16[16,2,272,128]{3,2,1,0:T(8,128)(2,1)} %bitcast.150), calls=%async_computation.1 | async-start | bytes 4456448 | tf_op jit(solution)/shard_map/all_to_all | solution.py:576
  100.8 24.4 %collective-permute-start.7 = (bf16[128,3072]{1,0:T(8,128)(2,1)S(1)}, bf16[128,3072]{1,0:T(8,128)(2,1)}, u32[]{:S(2)}, u32[]{:S(2)}) collective-permute-start(bf16[128,3072]{1,0:T(8,128)(2,1)S(1)} %constant_dynamic-slice_fusion.25), channel_id=1, source_target_pairs={{0,1},{1,0},{2,3},{3,2},{4,5},{5,4},{6,7},{7,6},{8,9},{9,8},{10,11... | collective-permute-start | bytes 2359304 | tf_op jit(solution)/shard_map/ppermute | solution.py:336
  113.8 54.2 %collective-permute-start.11 = (bf16[128,3072]{1,0:T(8,128)(2,1)}, bf16[128,3072]{1,0:T(8,128)(2,1)}, u32[]{:S(2)}, u32[]{:S(2)}) collective-permute-start(bf16[128,3072]{1,0:T(8,128)(2,1)} %pad_maximum_fusion.40), channel_id=1, source_target_pairs={{0,1},{1,0},{2,3},{3,2},{4,5},{5,4},{6,7},{7,6},{8,9},{9,8},{10,11... | collective-permute-start | bytes 2359304 | tf_op jit(solution)/shard_map/ppermute | solution.py:336
  153.9 36.5 %collective-permute-start.8 = (bf16[128,3072]{1,0:T(8,128)(2,1)}, bf16[128,3072]{1,0:T(8,128)(2,1)}, u32[]{:S(2)}, u32[]{:S(2)}) collective-permute-start(bf16[128,3072]{1,0:T(8,128)(2,1)} %collective-permute-done.7), channel_id=1, source_target_pairs={{0,4},{2,6},{4,0},{6,2},{8,12},{10,14},{12,8},{14,10},{16,20},{18,... | collective-permute-start | bytes 2359304 | tf_op jit(solution)/shard_map/ppermute | solution.py:336
  168.0 26.1 %collective-permute-start.12 = (bf16[128,3072]{1,0:T(8,128)(2,1)}, bf16[128,3072]{1,0:T(8,128)(2,1)S(1)}, u32[]{:S(2)}, u32[]{:S(2)}) collective-permute-start(bf16[128,3072]{1,0:T(8,128)(2,1)} %collective-permute-done.11), channel_id=1, source_target_pairs={{0,4},{2,6},{4,0},{6,2},{8,12},{10,14},{12,8},{14,10},{16,20},{18,... | collective-permute-start | bytes 2359304 | tf_op jit(solution)/shard_map/ppermute | solution.py:336
  170.1 55.5 %collective-permute-start.15 = (bf16[256,1024]{1,0:T(8,128)(2,1)}, bf16[256,1024]{1,0:T(8,128)(2,1)}, u32[]{:S(2)}, u32[]{:S(2)}) collective-permute-start(bf16[256,1024]{1,0:T(8,128)(2,1)} %get-tuple-element.303), channel_id=1, source_target_pairs={{0,0},{2,1},{4,4},{6,5},{8,8},{10,9},{12,12},{14,13},{16,16},{18,1... | collective-permute-start | bytes 1572872 | tf_op jit(solution)/shard_map/ppermute | solution.py:382
  176.1 49.5 %collective-permute-start.14 = (bf16[256,1024]{1,0:T(8,128)(2,1)}, bf16[256,1024]{1,0:T(8,128)(2,1)}, u32[]{:S(2)}, u32[]{:S(2)}) collective-permute-start(bf16[256,1024]{1,0:T(8,128)(2,1)} %get-tuple-element.304), channel_id=1, source_target_pairs={{0,1},{1,0},{2,3},{3,2},{4,5},{5,4},{6,7},{7,6},{8,9},{9,8},{10,11... | collective-permute-start | bytes 1572872 | tf_op jit(solution)/shard_map/ppermute | solution.py:336
  300.1 18.8 %collective-permute-start.18 = (bf16[2,768,1024]{2,1,0:T(8,128)(2,1)S(1)}, bf16[2,768,1024]{2,1,0:T(8,128)(2,1)S(1)}, u32[]{:S(2)}, u32[]{:S(2)}) collective-permute-start(bf16[2,768,1024]{2,1,0:T(8,128)(2,1)S(1)} %pad_maximum_fusion.6), channel_id=1, source_target_pairs={{0,2},{2,0},{4,6},{6,4},{8,10},{10,8},{12,14},{14,12},{16,18},{18,... | collective-permute-start | bytes 9437192 | tf_op jit(solution)/shard_map/ppermute | solution.py:336
  300.3 39.5 %collective-permute-start.19 = (bf16[1,768,1024]{2,1,0:T(8,128)(2,1)}, bf16[1,768,1024]{2,1,0:T(8,128)(2,1)}, u32[]{:S(2)}, u32[]{:S(2)}) collective-permute-start(bf16[1,768,1024]{2,1,0:T(8,128)(2,1)} %add_convert_fusion.8), channel_id=1, source_target_pairs={{0,1},{1,0},{2,3},{3,2},{4,5},{5,4},{6,7},{7,6},{8,9},{9,8},{10,11... | collective-permute-start | bytes 4718600 | tf_op jit(solution)/shard_map/ppermute | solution.py:336
  339.8 73.0 %collective-permute-start.20 = (bf16[2,768,1024]{2,1,0:T(8,128)(2,1)}, bf16[2,768,1024]{2,1,0:T(8,128)(2,1)}, u32[]{:S(2)}, u32[]{:S(2)}) collective-permute-start(bf16[2,768,1024]{2,1,0:T(8,128)(2,1)} %pad_maximum_fusion.8), channel_id=1, source_target_pairs={{0,2},{2,0},{4,6},{6,4},{8,10},{10,8},{12,14},{14,12},{16,18},{18,... | collective-permute-start | bytes 9437192 | tf_op jit(solution)/shard_map/ppermute | solution.py:336
  343.9 48.3 %all-to-all-start.2 = ((bf16[8,96,1024]{2,1,0:T(8,128)(2,1)}), bf16[8,96,1024]{2,1,0:T(8,128)(2,1)}, u32[]{:S(2)}, u32[]{:S(2)}) async-start(bf16[8,96,1024]{2,1,0:T(8,128)(2,1)} %bitcast.156), calls=%async_computation.2 | async-start | bytes 3145728 | tf_op jit(solution)/shard_map/all_to_all | solution.py:497
  354.5 49.4 %collective-permute-start.28 = (bf16[1,768,1024]{2,1,0:T(8,128)(2,1)}, bf16[1,768,1024]{2,1,0:T(8,128)(2,1)}, u32[]{:S(2)}, u32[]{:S(2)}) collective-permute-start(bf16[1,768,1024]{2,1,0:T(8,128)(2,1)} %add_convert_fusion.7), channel_id=1, source_target_pairs={{0,1},{1,0},{2,3},{3,2},{4,5},{5,4},{6,7},{7,6},{8,9},{9,8},{10,11... | collective-permute-start | bytes 4718600 | tf_op jit(solution)/shard_map/ppermute | solution.py:336
  408.0 41.6 %all-to-all-start.4 = ((bf16[8,96,1024]{2,1,0:T(8,128)(2,1)}), bf16[8,96,1024]{2,1,0:T(8,128)(2,1)}, u32[]{:S(2)}, u32[]{:S(2)}) async-start(bf16[8,96,1024]{2,1,0:T(8,128)(2,1)} %bitcast.153), calls=%async_computation.4 | async-start | bytes 3145728 | tf_op jit(solution)/shard_map/all_to_all | solution.py:497
  412.3 138.3 %all-gather.9.cloned.1.call-start = ((), (), s32[]{:S(2)}) async-start(), calls=%async_computation.7 | async-start | bytes 3538944 | tf_op jit(solution)/shard_map/all_gather | solution.py:521
  440.3 39.0 %collective-permute-start.27 = (bf16[1,768,1024]{2,1,0:T(8,128)(2,1)}, bf16[1,768,1024]{2,1,0:T(8,128)(2,1)}, u32[]{:S(2)}, u32[]{:S(2)}) collective-permute-start(bf16[1,768,1024]{2,1,0:T(8,128)(2,1)} %add_convert_fusion.4), channel_id=1, source_target_pairs={{0,1},{1,0},{2,3},{3,2},{4,5},{5,4},{6,7},{7,6},{8,9},{9,8},{10,11... | collective-permute-start | bytes 4718600 | tf_op jit(solution)/shard_map/ppermute | solution.py:336
  483.4 61.7 %all-to-all-start.3 = ((bf16[8,96,1024]{2,1,0:T(8,128)(2,1)}), bf16[8,96,1024]{2,1,0:T(8,128)(2,1)S(1)}, u32[]{:S(2)}, u32[]{:S(2)}) async-start(bf16[8,96,1024]{2,1,0:T(8,128)(2,1)} %bitcast.157), calls=%async_computation.3 | async-start | bytes 3145728 | tf_op jit(solution)/shard_map/all_to_all | solution.py:497
  489.2 21.8 %collective-permute-start.22 = (bf16[1,448,1024]{2,1,0:T(8,128)(2,1)}, bf16[1,448,1024]{2,1,0:T(8,128)(2,1)S(1)}, u32[]{:S(2)}, u32[]{:S(2)}) collective-permute-start(bf16[1,448,1024]{2,1,0:T(8,128)(2,1)} %add_convert_fusion.15), channel_id=1, source_target_pairs={{0,1},{1,0},{2,3},{3,2},{4,5},{5,4},{6,7},{7,6},{8,9},{9,8},{10,11... | collective-permute-start | bytes 2752520 | tf_op jit(solution)/shard_map/ppermute | solution.py:336
  546.2 27.3 %all-to-all-start.5 = ((bf16[8,56,1024]{2,1,0:T(8,128)(2,1)}), bf16[8,56,1024]{2,1,0:T(8,128)(2,1)}, u32[]{:S(2)}, u32[]{:S(2)}) async-start(bf16[8,56,1024]{2,1,0:T(8,128)(2,1)} %bitcast.160), calls=%async_computation.5 | async-start | bytes 1835008 | tf_op jit(solution)/shard_map/all_to_all | solution.py:497
  550.4 77.6 %all-gather.11.cloned.1.call-start = ((), (), s32[]{:S(2)}) async-start(), calls=%async_computation.8 | async-start | bytes 2801664 | tf_op jit(solution)/shard_map/all_gather | solution.py:521
  579.4 14.9 %collective-permute-start.25 = (bf16[256,1024]{1,0:T(8,128)(2,1)S(1)}, bf16[256,1024]{1,0:T(8,128)(2,1)S(1)}, u32[]{:S(2)}, u32[]{:S(2)}) collective-permute-start(bf16[256,1024]{1,0:T(8,128)(2,1)S(1)} %slice.254), channel_id=1, source_target_pairs={{0,1},{1,0},{2,3},{3,2},{4,5},{5,4},{6,7},{7,6},{8,9},{9,8},{10,11... | collective-permute-start | bytes 1572872 | tf_op jit(solution)/shard_map/ppermute | solution.py:336
  582.4 50.2 %collective-permute-start.32 = (bf16[768,1024]{1,0:T(8,128)(2,1)}, bf16[768,1024]{1,0:T(8,128)(2,1)}, u32[]{:S(2)}, u32[]{:S(2)}) collective-permute-start(bf16[768,1024]{1,0:T(8,128)(2,1)} %bitcast.70), channel_id=1, source_target_pairs={{0,2},{2,0},{4,6},{6,4},{8,10},{10,8},{12,14},{14,12},{16,18},{18,... | collective-permute-start | bytes 4718600 | tf_op jit(solution)/shard_map/ppermute | solution.py:336
  582.4 22.1 %collective-permute-start.23 = (bf16[256,1024]{1,0:T(8,128)(2,1)S(1)}, bf16[256,1024]{1,0:T(8,128)(2,1)S(1)}, u32[]{:S(2)}, u32[]{:S(2)}) collective-permute-start(bf16[256,1024]{1,0:T(8,128)(2,1)S(1)} %slice.251), channel_id=1, source_target_pairs={{0,1},{1,0},{2,3},{3,2},{4,5},{5,4},{6,7},{7,6},{8,9},{9,8},{10,11... | collective-permute-start | bytes 1572872 | tf_op jit(solution)/shard_map/ppermute | solution.py:336
  583.1 51.6 %collective-permute-start.31 = (bf16[768,1024]{1,0:T(8,128)(2,1)S(1)}, bf16[768,1024]{1,0:T(8,128)(2,1)}, u32[]{:S(2)}, u32[]{:S(2)}) collective-permute-start(bf16[768,1024]{1,0:T(8,128)(2,1)S(1)} %bitcast.151), channel_id=1, source_target_pairs={{0,2},{2,0},{4,6},{6,4},{8,10},{10,8},{12,14},{14,12},{16,18},{18,... | collective-permute-start | bytes 4718600 | tf_op jit(solution)/shard_map/ppermute | solution.py:336
  604.6 24.9 %collective-permute-start.24 = (bf16[256,1024]{1,0:T(8,128)(2,1)S(1)}, bf16[256,1024]{1,0:T(8,128)(2,1)}, u32[]{:S(2)}, u32[]{:S(2)}) collective-permute-start(bf16[256,1024]{1,0:T(8,128)(2,1)S(1)} %get-tuple-element.299), channel_id=1, source_target_pairs={{0,0},{2,1},{4,4},{6,5},{8,8},{10,9},{12,12},{14,13},{16,16},{18,1... | collective-permute-start | bytes 1572872 | tf_op jit(solution)/shard_map/ppermute | solution.py:382
  632.3 18.8 %collective-permute-start.30 = (bf16[768,1024]{1,0:T(8,128)(2,1)S(1)}, bf16[768,1024]{1,0:T(8,128)(2,1)}, u32[]{:S(2)}, u32[]{:S(2)}) collective-permute-start(bf16[768,1024]{1,0:T(8,128)(2,1)S(1)} %bitcast.154), channel_id=1, source_target_pairs={{0,2},{2,0},{4,6},{6,4},{8,10},{10,8},{12,14},{14,12},{16,18},{18,... | collective-permute-start | bytes 4718600 | tf_op jit(solution)/shard_map/ppermute | solution.py:336
  (139 other events, 1191.2 us)
Sparse Core Ops, SparseCore 0:
  83.4 70.3 all-gather.6
  452.3 87.4 all-gather.8
  575.7 52.2 all-gather.10

commit v3 on v2

--- a/solution.py
+++ b/solution.py
@@ -489,7 +489,7 @@
         if earlier:
             received = after(received, *earlier)
         self.total = added(self.kept, received)[0]
-        return self.total
+        return received
 
     def over_chips(self, *earlier):
         same_core = self.plan.same_core()
@@ -499,10 +499,10 @@
         )
         if earlier:
             parts = after(parts, *earlier)
-        count = len(same_core[0])
+        arrived, count = parts, len(same_core[0])
         parts = parts.reshape(count, rows // count, width).astype(jnp.float32)
         self.held = jnp.sum(parts, axis=0).astype(low_type)
-        return self.held
+        return arrived
 
     def finish(self):
         self.other = swap(self.held, "blk", 1)
@@ -702,15 +702,18 @@
     low = upstream.astype(low_type)
     grad_self_out = product_tn(blended, low)
     grad_self_out = product_tn(blended, low)
-    one = Group(plan, [unit(grad_self_up), unit(grad_self_down), unit(grad_self_out)])
+    one = Group(plan, [unit(grad_self_up), unit(grad_self_down)])
     grad_blended = product_nt(low, w_self_out).astype(low_type)
     grad_blended = after(grad_blended, one.over_core(), mixed)
     triple_grads, more_grads = self_backward(triple, more, grad_blended, plan.groups)
+    triple_grads, more_grads = after((triple_grads, more_grads), one.over_fsdp())
     triple_grads = plan.own_pairs(triple_grads, more_grads)
     two = Group(
-        plan, [unit(product_tn(hidden_two, triple_grads[:, i * model : (i + 1) * model])) for i in range(3)]
-    )
-    triple_grads = after(triple_grads, two.send, one.over_fsdp())
+        plan,
+        [unit(product_tn(hidden_two, triple_grads[:, i * model : (i + 1) * model])) for i in range(3)]
+        + [unit(grad_self_out)],
+    )
+    triple_grads = after(triple_grads, two.send)
     grad_hidden = product_nt(triple_grads, w_triple)
     down, gain_two, bias_two = norm_backward(grad_hidden, normed_two, scale_two, gains[2])
     upstream = upstream + down
@@ -720,13 +723,13 @@
     upstream, grad_up, unused, gain_one, bias_one = feed_backward(
         upstream, low, first_sum, stored_one, gains[1], w_up, w_down
     )
-    low = upstream.astype(low_type)
+    low = after(upstream.astype(low_type), one.over_chips())
     grad_out = product_tn(attended, low)
     three = Group(plan, [unit(grad_up), unit(grad_down), unit(grad_out)])
     grad_attended = product_nt(low, w_out).astype(low_type)
     grad_value = product_tn(attended_features, grad_attended)
     grad_features = product_nt(grad_attended, w_value)
-    wide_grads = after(widened(grad_features, 1.0), three.send, one.over_chips())
+    wide_grads = after(widened(grad_features, 1.0), two.over_fsdp(), three.over_core())
     score_sums = cross_call(
         cross_backward_kernel,
         big,
@@ -737,7 +740,6 @@
         plan.block_rows,
         plan.per_item,
     )
-    score_sums = after(score_sums, two.over_fsdp(), three.over_core())
     key_sums = (narrowed(score_sums) * scaling).astype(low_type)
     grad_queries = product(key_sums, w_key).astype(low_type)
     grad_key = product_tn(key_sums, queries)
@@ -771,18 +773,17 @@
         axis=1,
     )
     four = Group(plan, [unit(grad_query), tall.astype(low_type).reshape(shards, -1, model)])
-    two.over_chips(four.send)
+    four.send = after(four.send, three.over_fsdp(), two.over_chips())
     early_sums = back_from_chips([one, two])
     four.over_core()
-    three.over_fsdp(four.send)
-    four.over_fsdp(three.total)
-    mixed = plan.send_back(after(mixed, four.total))
-    latents_grad = plan.send_back(after(latents_grad, four.total))
-    three.over_chips(four.total, early_sums)
-    four.over_chips(three.held)
+    arrived = four.over_fsdp(three.total)
+    mixed = plan.send_back(after(mixed, arrived))
+    latents_grad = plan.send_back(after(latents_grad, arrived))
+    arrived = three.over_chips(early_sums)
+    four.over_chips(arrived)
     back_from_chips([three, four])
-    grad_self_up, grad_self_down, grad_self_out = one.finish()
-    two.finish()
+    grad_self_up, grad_self_down = one.finish()
+    grad_self_out = two.finish()[3]
     half = two.sizes[0]
     grad_triple = widen(plan.core, [two.held], [two.other], [(0, i * half, half) for i in range(3)])
     latents_grad = plan.placed(latents_grad).astype(jnp.float32)

time: 670 us -> 666 us (level)
  waiting for transfers between devices: 230 us -> 223 us
    all_to_all x4, waiting for transfers between devices: 83 us -> 68.4 us  [over_chips(): lax.all_to_all(self.total, 'blk', split_axis=0, concat_axis=0, axis_index...]
    unnamed x267 -> x287, local copies, waits for them, and re-layouts: 17.7 us -> 15.4 us
    select_n x15 -> x16, other arithmetic: 22.4 us -> 21.5 us  [ordered(): first = jnp.where(bit == 0, own, other)]
  transfers between devices with their start and end apart: 42 -> 42, of which waited for: 14 -> 13; matrix products, arithmetic and copies ran while one was open for 32% -> 34% of each run, Pallas kernels for 5% -> 8%
where the time goes in v3:
time: 666 us; the launch traced here: 658 us
  waiting for transfers between devices  223 us (33%)
  other arithmetic  119 us (18%)
  matrix products  104 us (16%)
  starting transfers between devices  72.8 us (11%)
  local copies, waits for them, and re-layouts  62.8 us (9%)
  Pallas kernels  59.7 us (9%)
  between operations  16.3 us (2%)
    ppermute x29, waiting for transfers between devices, swap(): return lax.ppermute(array, axis_name, [(i, i ^ mask) for i in range(size)])  103 us
    all_to_all x4, waiting for transfers between devices, over_chips(): lax.all_to_all(self.total, 'blk', split_axis=0, concat_axis=0, axis_index...  68.4 us
    dot_general x10, matrix products, product_nt(): lax.dot_general(a, b, (((1,), (1,)), ((), ())), preferred_element_type=jn...  45.1 us
    dot_general x10, matrix products, product(): return jnp.dot(a, b, preferred_element_type=jnp.float32)  30.3 us
    all_to_all x1, waiting for transfers between devices, route_pixels(): lax.all_to_all(pieces, 'blk', split_axis=0, concat_axis=0, tiled=True)  28.5 us
    dot_general x12, matrix products, product_tn(): lax.dot_general(a, b, (((0,), (0,)), ((), ())), preferred_element_type=jn...  28.3 us
    convert_element_type x8, other arithmetic, added(): (kept.astype(jnp.float32) + received.astype(jnp.float32)).astype(low_type)  28 us
    all_to_all x4, starting transfers between devices, over_chips(): lax.all_to_all(self.total, 'blk', split_axis=0, concat_axis=0, axis_index...  23.7 us
  transfers between devices with their start and end apart: 42, of which 13 were waited for; matrix products, arithmetic and copies ran while one was open for 34% of the time, Pallas kernels for 8%

profile of v3, /device:TPU:0, one launch (start us, length us, event | category | flops | bytes accessed | tf_op | source)
XLA Modules:
  0.0 657.5 jit_solution(4154221663956194331)
XLA Ops:
  12.4 5.1 prepare_pixels.1
  17.5 7.5 %all-to-all-start = ((bf16[16,2,272,128]{3,2,1,0:T(8,128)(2,1)}), bf16[16,2,272,128]{3,2,1,0:T(8,128)(2,1)S(1)}, u32[]{:S(2)}, u32[]{:S(2)}) async-start(bf16[16,2,272,128]{3,2,1,0:T(8,128)(2,1)} %prepare_pixels.1), calls=%async_computation | async-start | bytes 4456448 | tf_op jit(solution)/shard_map/all_to_all | solution.py:544
  43.8 25.5 %collective-permute-done = bf16[256,1024]{1,0:T(8,128)(2,1)} collective-permute-done((bf16[256,1024]{1,0:T(8,128)(2,1)}, bf16[256,1024]{1,0:T(8,128)(2,1)}, u32[]{:S(2)}, u32[]{:S(2)}) %collective-permute-start) | collective-permute-done | bytes 524320 | tf_op jit(solution)/shard_map/ppermute | solution.py:336
  89.3 9.0 %all-to-all-start.1 = ((bf16[16,2,272,128]{3,2,1,0:T(8,128)(2,1)}), bf16[16,2,272,128]{3,2,1,0:T(8,128)(2,1)S(1)}, u32[]{:S(2)}, u32[]{:S(2)}) async-start(bf16[16,2,272,128]{3,2,1,0:T(8,128)(2,1)} %bitcast.158), calls=%async_computation.1 | async-start | bytes 4456448 | tf_op jit(solution)/shard_map/all_to_all | solution.py:576
  125.1 28.5 %all-to-all-done.1.first_ref = bf16[16,2,272,128]{3,2,1,0:T(8,128)(2,1)S(1)} async-done(((bf16[16,2,272,128]{3,2,1,0:T(8,128)(2,1)}), bf16[16,2,272,128]{3,2,1,0:T(8,128)(2,1)S(1)}, u32[]{:S(2)}, u32[]{:S(2)}) %all-to-all-start.1) | async-done | bytes 2228256 | tf_op jit(solution)/shard_map/all_to_all | solution.py:576
  157.9 8.3 %cross_attention.2 = f32[768,272]{1,0:T(8,128)} custom-call(s32[2]{0:T(128)} %get-tuple-element.225.big_ref, bf16[768,272]{1,0:T(8,128)(2,1)} %pad.23.query_ref, bf16[16,2,272,128]{3,2,1,0:T(8,128)(2,1)} %copy-done.1, bf16[16,2,272,128]{3,2,1,0:T(8,128)(2,1)} %bitcast.156, f32[2,8,4096]{2,1,0:T(8,128)} %broadcast_in_dim.82.mask_ref), custom_call_target="tpu_custom_call" | custom-call | tf_op jit(solution)/shard_map/cross_attention/pallas_call | solution.py:174
  169.7 5.6 collective-permute-start.15
  199.6 5.3 convolution_convert_fusion.q_ref.k_ref.v_ref
  211.5 11.0 %self_forward.1 = bf16[768,1024]{1,0:T(8,128)(2,1)} custom-call(bf16[768,3072]{1,0:T(8,128)(2,1)} %copy-done, bf16[768,3072]{1,0:T(8,128)(2,1)} %copy-done, bf16[768,3072]{1,0:T(8,128)(2,1)} %copy-done, bf16[256,2048]{1,0:T(8,128)(2,1)} %collective-permute-done.10.more_k_ref.more_v_ref, bf16[256,2048]{1,0:T(8,128)(2,1)} %collective-permute-done.10.more_k_ref.more_v_ref), custom_call_target="tpu_custom_call" | custom-call | tf_op jit(solution)/shard_map/self_forward/pallas_call | solution.py:266
  244.6 5.7 multiply_reduce_fusion
  263.4 20.0 %self_backward.1 = (bf16[768,3072]{1,0:T(8,128)(2,1)}, bf16[256,2048]{1,0:T(8,128)(2,1)}) custom-call(bf16[768,3072]{1,0:T(8,128)(2,1)} %copy-done, bf16[768,3072]{1,0:T(8,128)(2,1)} %copy-done, bf16[768,3072]{1,0:T(8,128)(2,1)} %copy-done, bf16[256,2048]{1,0:T(8,128)(2,1)} %collective-permute-done.10.more_k_ref.more_v_ref, ...), custom_call_target="tpu_custom_call" | custom-call | tf_op jit(solution)/shard_map/self_backward/pallas_call | solution.py:281
  304.4 9.3 %all-to-all-start.3 = ((bf16[8,64,1024]{2,1,0:T(8,128)(2,1)}), bf16[8,64,1024]{2,1,0:T(8,128)(2,1)}, u32[]{:S(2)}, u32[]{:S(2)}) async-start(bf16[8,64,1024]{2,1,0:T(8,128)(2,1)} %bitcast.169), calls=%async_computation.3 | async-start | bytes 2097152 | tf_op jit(solution)/shard_map/all_to_all | solution.py:497
  313.7 10.1 %multiply_reduce_fusion.1 = (bf16[1024]{0:T(1024)(128)(2,1)S(1)}, f32[768]{0:T(1024)S(1)}, f32[768]{0:T(1024)S(1)}, bf16[1024]{0:T(1024)(128)(2,1)S(1)}, f32[768,1024]{1,0:T(8,128)S(1)}) fusion(f32[768,1024]{1,0:T(8,128)S(1)} %get-tuple-element.350, f32[768]{0:T(1024)S(1)} %add_rsqrt_fusion.1, f32[768]{0:T(1024)S(1)} %broadcast_multiply_fusion.10, ...), kind=kOutput, calls=%fused_computation.56 | convolution fusion | flops 4851494912 | bytes 17321984 | tf_op jit(solution)/shard_map/dot_general | solution.py:28
  330.1 5.4 add_convert_fusion.2
  335.6 4.2 fusion.27
  364.3 36.6 %collective-permute-done.20 = bf16[1,1024,1024]{2,1,0:T(8,128)(2,1)} collective-permute-done((bf16[1,1024,1024]{2,1,0:T(8,128)(2,1)}, bf16[1,1024,1024]{2,1,0:T(8,128)(2,1)}, u32[]{:S(2)}, u32[]{:S(2)}) %collective-permute-start.20) | collective-permute-done | bytes 2097184 | tf_op jit(solution)/shard_map/ppermute | solution.py:336
  400.9 5.0 add_convert_fusion
  405.9 6.0 all-to-all-start.4
  417.7 9.9 %cross_attention.3 = f32[768,272]{1,0:T(8,128)} custom-call(s32[2]{0:T(128)} %get-tuple-element.225.big_ref, bf16[768,272]{1,0:T(8,128)(2,1)} %pad.23.query_ref, bf16[768,272]{1,0:T(8,128)(2,1)} %fusion.53.grad_ref, bf16[16,2,272,128]{3,2,1,0:T(8,128)(2,1)} %copy-done.1, bf16[16,2,272,128]{3,2,1,0:T(8,128)(2,1)} %bitcast.157, ...), custom_call_target="tpu_custom_call" | custom-call | tf_op jit(solution)/shard_map/cross_attention/pallas_call | solution.py:174
  437.0 6.0 fusion.10
  446.0 14.1 %all-to-all-done.4 = bf16[8,128,1024]{2,1,0:T(8,128)(2,1)} async-done(((bf16[8,128,1024]{2,1,0:T(8,128)(2,1)}), bf16[8,128,1024]{2,1,0:T(8,128)(2,1)}, u32[]{:S(2)}, u32[]{:S(2)}) %all-to-all-start.4) | async-done | bytes 2097184 | tf_op jit(solution)/shard_map/all_to_all | solution.py:497
  462.9 4.0 convolution_convert_fusion.1
  469.5 4.2 add_convert_fusion.3
  479.6 22.1 %collective-permute-done.24 = bf16[1,448,1024]{2,1,0:T(8,128)(2,1)S(1)} collective-permute-done((bf16[1,448,1024]{2,1,0:T(8,128)(2,1)S(1)}, bf16[1,448,1024]{2,1,0:T(8,128)(2,1)S(1)}, u32[]{:S(2)}, u32[]{:S(2)}) %collective-permute-start.24) | collective-permute-done | bytes 917536 | tf_op jit(solution)/shard_map/ppermute | solution.py:336
  504.5 34.6 %all-to-all-done.2 = bf16[8,96,1024]{2,1,0:T(8,128)(2,1)S(1)} async-done(((bf16[8,96,1024]{2,1,0:T(8,128)(2,1)}), bf16[8,96,1024]{2,1,0:T(8,128)(2,1)S(1)}, u32[]{:S(2)}, u32[]{:S(2)}) %all-to-all-start.2) | async-done | bytes 1572896 | tf_op jit(solution)/shard_map/all_to_all | solution.py:497
  539.1 4.6 all-to-all-start.5
  547.5 19.6 %all-to-all-done.5 = bf16[8,56,1024]{2,1,0:T(8,128)(2,1)} async-done(((bf16[8,56,1024]{2,1,0:T(8,128)(2,1)}), bf16[8,56,1024]{2,1,0:T(8,128)(2,1)}, u32[]{:S(2)}, u32[]{:S(2)}) %all-to-all-start.5) | async-done | bytes 917536 | tf_op jit(solution)/shard_map/all_to_all | solution.py:497
  571.8 3.9 fusion.14
  576.7 8.5 %collective-permute-done.25 = bf16[256,1024]{1,0:T(8,128)(2,1)S(1)} collective-permute-done((bf16[256,1024]{1,0:T(8,128)(2,1)S(1)}, bf16[256,1024]{1,0:T(8,128)(2,1)S(1)}, u32[]{:S(2)}, u32[]{:S(2)}) %collective-permute-start.25) | collective-permute-done | bytes 524320 | tf_op jit(solution)/shard_map/ppermute | solution.py:336
  589.8 5.5 collective-permute-done.27
  600.5 21.1 %all-gather.11.cloned.1.call-done = bf16[1216,1024]{1,0:T(8,128)(2,1)} async-done(((bf16[152,1024]{1,0:T(8,128)(2,1)}), bf16[1216,1024]{1,0:T(8,128)(2,1)}) %all-gather.11.cloned.1.call-update) | async-done | bytes 2490384 | tf_op jit(solution)/shard_map/all_gather | solution.py:521
  630.2 5.3 widen.1
  (569 shorter events, 269.7 us)
Async XLA Ops:
  17.5 53.1 %all-to-all-start = ((bf16[16,2,272,128]{3,2,1,0:T(8,128)(2,1)}), bf16[16,2,272,128]{3,2,1,0:T(8,128)(2,1)S(1)}, u32[]{:S(2)}, u32[]{:S(2)}) async-start(bf16[16,2,272,128]{3,2,1,0:T(8,128)(2,1)} %prepare_pixels.1), calls=%async_computation | async-start | bytes 4456448 | tf_op jit(solution)/shard_map/all_to_all | solution.py:544
  25.1 132.1 %all-gather.7.cloned.1.call-start = ((), (), s32[]{:S(2)}) async-start(), calls=%async_computation.6 | async-start | bytes 2367488 | tf_op jit(solution)/shard_map/all_gather | solution.py:580
  26.0 17.8 %collective-permute-start.3 = (bf16[256,1024]{1,0:T(8,128)(2,1)}, bf16[256,1024]{1,0:T(8,128)(2,1)}, u32[]{:S(2)}, u32[]{:S(2)}) collective-permute-start(bf16[256,1024]{1,0:T(8,128)(2,1)} %constant_dynamic-slice_fusion.29), channel_id=1, source_target_pairs={{0,1},{1,0},{2,3},{3,2},{4,5},{5,4},{6,7},{7,6},{8,9},{9,8},{10,11... | collective-permute-start | bytes 1572872 | tf_op jit(solution)/shard_map/ppermute | solution.py:336
  29.4 39.9 %collective-permute-start.2 = (bf16[265,1024]{1,0:T(8,128)(2,1)}, bf16[265,1024]{1,0:T(8,128)(2,1)}, u32[]{:S(2)}, u32[]{:S(2)}) collective-permute-start(bf16[265,1024]{1,0:T(8,128)(2,1)} %pad_maximum_fusion.40), channel_id=1, source_target_pairs={{0,1},{1,0},{2,3},{3,2},{4,5},{5,4},{6,7},{7,6},{8,9},{9,8},{10,11... | collective-permute-start | bytes 1628168 | tf_op jit(solution)/shard_map/ppermute | solution.py:336
  34.2 35.1 %collective-permute-start = (bf16[256,1024]{1,0:T(8,128)(2,1)}, bf16[256,1024]{1,0:T(8,128)(2,1)}, u32[]{:S(2)}, u32[]{:S(2)}) collective-permute-start(bf16[256,1024]{1,0:T(8,128)(2,1)} %get-tuple-element.313), channel_id=1, source_target_pairs={{0,1},{1,0},{2,3},{3,2},{4,5},{5,4},{6,7},{7,6},{8,9},{9,8},{10,11... | collective-permute-start | bytes 1572872 | tf_op jit(solution)/shard_map/ppermute | solution.py:336
  70.6 41.8 %collective-permute-start.5 = (bf16[256,3072]{1,0:T(8,128)(2,1)}, bf16[256,3072]{1,0:T(8,128)(2,1)}, u32[]{:S(2)}, u32[]{:S(2)}) collective-permute-start(bf16[256,3072]{1,0:T(8,128)(2,1)} %pad_maximum_fusion.18), channel_id=1, source_target_pairs={{0,1},{1,0},{2,3},{3,2},{4,5},{5,4},{6,7},{7,6},{8,9},{9,8},{10,11... | collective-permute-start | bytes 4718600 | tf_op jit(solution)/shard_map/ppermute | solution.py:336
  83.2 18.9 %collective-permute-start.4 = (bf16[256,1024]{1,0:T(8,128)(2,1)}, bf16[256,1024]{1,0:T(8,128)(2,1)}, u32[]{:S(2)}, u32[]{:S(2)}) collective-permute-start(bf16[256,1024]{1,0:T(8,128)(2,1)} %collective-permute-done.3), channel_id=1, source_target_pairs={{0,2},{2,0},{4,6},{6,4},{8,10},{10,8},{12,14},{14,12},{16,18},{18,... | collective-permute-start | bytes 1572872 | tf_op jit(solution)/shard_map/ppermute | solution.py:336
  89.3 64.3 %all-to-all-start.1 = ((bf16[16,2,272,128]{3,2,1,0:T(8,128)(2,1)}), bf16[16,2,272,128]{3,2,1,0:T(8,128)(2,1)S(1)}, u32[]{:S(2)}, u32[]{:S(2)}) async-start(bf16[16,2,272,128]{3,2,1,0:T(8,128)(2,1)} %bitcast.158), calls=%async_computation.1 | async-start | bytes 4456448 | tf_op jit(solution)/shard_map/all_to_all | solution.py:576
  100.6 24.5 %collective-permute-start.7 = (bf16[128,3072]{1,0:T(8,128)(2,1)S(1)}, bf16[128,3072]{1,0:T(8,128)(2,1)}, u32[]{:S(2)}, u32[]{:S(2)}) collective-permute-start(bf16[128,3072]{1,0:T(8,128)(2,1)S(1)} %constant_dynamic-slice_fusion.25), channel_id=1, source_target_pairs={{0,1},{1,0},{2,3},{3,2},{4,5},{5,4},{6,7},{7,6},{8,9},{9,8},{10,11... | collective-permute-start | bytes 2359304 | tf_op jit(solution)/shard_map/ppermute | solution.py:336
  113.6 54.1 %collective-permute-start.11 = (bf16[128,3072]{1,0:T(8,128)(2,1)}, bf16[128,3072]{1,0:T(8,128)(2,1)}, u32[]{:S(2)}, u32[]{:S(2)}) collective-permute-start(bf16[128,3072]{1,0:T(8,128)(2,1)} %pad_maximum_fusion.39), channel_id=1, source_target_pairs={{0,1},{1,0},{2,3},{3,2},{4,5},{5,4},{6,7},{7,6},{8,9},{9,8},{10,11... | collective-permute-start | bytes 2359304 | tf_op jit(solution)/shard_map/ppermute | solution.py:336
  153.6 36.2 %collective-permute-start.8 = (bf16[128,3072]{1,0:T(8,128)(2,1)}, bf16[128,3072]{1,0:T(8,128)(2,1)}, u32[]{:S(2)}, u32[]{:S(2)}) collective-permute-start(bf16[128,3072]{1,0:T(8,128)(2,1)} %collective-permute-done.7), channel_id=1, source_target_pairs={{0,4},{2,6},{4,0},{6,2},{8,12},{10,14},{12,8},{14,10},{16,20},{18,... | collective-permute-start | bytes 2359304 | tf_op jit(solution)/shard_map/ppermute | solution.py:336
  167.7 26.4 %collective-permute-start.12 = (bf16[128,3072]{1,0:T(8,128)(2,1)}, bf16[128,3072]{1,0:T(8,128)(2,1)S(1)}, u32[]{:S(2)}, u32[]{:S(2)}) collective-permute-start(bf16[128,3072]{1,0:T(8,128)(2,1)} %collective-permute-done.11), channel_id=1, source_target_pairs={{0,4},{2,6},{4,0},{6,2},{8,12},{10,14},{12,8},{14,10},{16,20},{18,... | collective-permute-start | bytes 2359304 | tf_op jit(solution)/shard_map/ppermute | solution.py:336
  169.7 56.2 %collective-permute-start.15 = (bf16[256,1024]{1,0:T(8,128)(2,1)}, bf16[256,1024]{1,0:T(8,128)(2,1)}, u32[]{:S(2)}, u32[]{:S(2)}) collective-permute-start(bf16[256,1024]{1,0:T(8,128)(2,1)} %get-tuple-element.305), channel_id=1, source_target_pairs={{0,0},{2,1},{4,4},{6,5},{8,8},{10,9},{12,12},{14,13},{16,16},{18,1... | collective-permute-start | bytes 1572872 | tf_op jit(solution)/shard_map/ppermute | solution.py:382
  175.3 50.6 %collective-permute-start.14 = (bf16[256,1024]{1,0:T(8,128)(2,1)}, bf16[256,1024]{1,0:T(8,128)(2,1)}, u32[]{:S(2)}, u32[]{:S(2)}) collective-permute-start(bf16[256,1024]{1,0:T(8,128)(2,1)} %get-tuple-element.306), channel_id=1, source_target_pairs={{0,1},{1,0},{2,3},{3,2},{4,5},{5,4},{6,7},{7,6},{8,9},{9,8},{10,11... | collective-permute-start | bytes 1572872 | tf_op jit(solution)/shard_map/ppermute | solution.py:336
  253.2 30.2 %collective-permute-start.17 = (bf16[1,512,1024]{2,1,0:T(8,128)(2,1)}, bf16[1,512,1024]{2,1,0:T(8,128)(2,1)}, u32[]{:S(2)}, u32[]{:S(2)}) collective-permute-start(bf16[1,512,1024]{2,1,0:T(8,128)(2,1)} %add_convert_fusion.13), channel_id=1, source_target_pairs={{0,1},{1,0},{2,3},{3,2},{4,5},{5,4},{6,7},{7,6},{8,9},{9,8},{10,11... | collective-permute-start | bytes 3145736 | tf_op jit(solution)/shard_map/ppermute | solution.py:336
  300.7 29.4 %collective-permute-start.19 = (bf16[2,1024,1024]{2,1,0:T(8,128)(2,1)}, bf16[2,1024,1024]{2,1,0:T(8,128)(2,1)}, u32[]{:S(2)}, u32[]{:S(2)}) collective-permute-start(bf16[2,1024,1024]{2,1,0:T(8,128)(2,1)} %pad_maximum_fusion.1), channel_id=1, source_target_pairs={{0,2},{2,0},{4,6},{6,4},{8,10},{10,8},{12,14},{14,12},{16,18},{18,... | collective-permute-start | bytes 12582920 | tf_op jit(solution)/shard_map/ppermute | solution.py:336
  304.4 48.8 %all-to-all-start.3 = ((bf16[8,64,1024]{2,1,0:T(8,128)(2,1)}), bf16[8,64,1024]{2,1,0:T(8,128)(2,1)}, u32[]{:S(2)}, u32[]{:S(2)}) async-start(bf16[8,64,1024]{2,1,0:T(8,128)(2,1)} %bitcast.169), calls=%async_computation.3 | async-start | bytes 2097152 | tf_op jit(solution)/shard_map/all_to_all | solution.py:497
  352.5 61.4 %collective-permute-start.21 = (bf16[2,768,1024]{2,1,0:T(8,128)(2,1)}, bf16[2,768,1024]{2,1,0:T(8,128)(2,1)}, u32[]{:S(2)}, u32[]{:S(2)}) collective-permute-start(bf16[2,768,1024]{2,1,0:T(8,128)(2,1)} %pad_maximum_fusion.7), channel_id=1, source_target_pairs={{0,2},{2,0},{4,6},{6,4},{8,10},{10,8},{12,14},{14,12},{16,18},{18,... | collective-permute-start | bytes 9437192 | tf_op jit(solution)/shard_map/ppermute | solution.py:336
  352.5 48.4 %collective-permute-start.20 = (bf16[1,1024,1024]{2,1,0:T(8,128)(2,1)}, bf16[1,1024,1024]{2,1,0:T(8,128)(2,1)}, u32[]{:S(2)}, u32[]{:S(2)}) collective-permute-start(bf16[1,1024,1024]{2,1,0:T(8,128)(2,1)} %add_convert_fusion.2), channel_id=1, source_target_pairs={{0,1},{1,0},{2,3},{3,2},{4,5},{5,4},{6,7},{7,6},{8,9},{9,8},{10,11... | collective-permute-start | bytes 6291464 | tf_op jit(solution)/shard_map/ppermute | solution.py:336
  405.9 54.2 %all-to-all-start.4 = ((bf16[8,128,1024]{2,1,0:T(8,128)(2,1)}), bf16[8,128,1024]{2,1,0:T(8,128)(2,1)}, u32[]{:S(2)}, u32[]{:S(2)}) async-start(bf16[8,128,1024]{2,1,0:T(8,128)(2,1)} %bitcast.159), calls=%async_computation.4 | async-start | bytes 4194304 | tf_op jit(solution)/shard_map/all_to_all | solution.py:497
  411.9 133.7 %all-gather.9.cloned.1.call-start = ((), (), s32[]{:S(2)}) async-start(), calls=%async_computation.7 | async-start | bytes 3538944 | tf_op jit(solution)/shard_map/all_gather | solution.py:521
  417.2 52.3 %collective-permute-start.22 = (bf16[1,768,1024]{2,1,0:T(8,128)(2,1)}, bf16[1,768,1024]{2,1,0:T(8,128)(2,1)}, u32[]{:S(2)}, u32[]{:S(2)}) collective-permute-start(bf16[1,768,1024]{2,1,0:T(8,128)(2,1)} %add_convert_fusion.5), channel_id=1, source_target_pairs={{0,1},{1,0},{2,3},{3,2},{4,5},{5,4},{6,7},{7,6},{8,9},{9,8},{10,11... | collective-permute-start | bytes 4718600 | tf_op jit(solution)/shard_map/ppermute | solution.py:336
  473.7 65.4 %all-to-all-start.2 = ((bf16[8,96,1024]{2,1,0:T(8,128)(2,1)}), bf16[8,96,1024]{2,1,0:T(8,128)(2,1)S(1)}, u32[]{:S(2)}, u32[]{:S(2)}) async-start(bf16[8,96,1024]{2,1,0:T(8,128)(2,1)} %bitcast.166), calls=%async_computation.2 | async-start | bytes 3145728 | tf_op jit(solution)/shard_map/all_to_all | solution.py:497
  479.0 22.7 %collective-permute-start.24 = (bf16[1,448,1024]{2,1,0:T(8,128)(2,1)S(1)}, bf16[1,448,1024]{2,1,0:T(8,128)(2,1)S(1)}, u32[]{:S(2)}, u32[]{:S(2)}) collective-permute-start(bf16[1,448,1024]{2,1,0:T(8,128)(2,1)S(1)} %add_convert_fusion.16), channel_id=1, source_target_pairs={{0,1},{1,0},{2,3},{3,2},{4,5},{5,4},{6,7},{7,6},{8,9},{9,8},{10,11... | collective-permute-start | bytes 2752520 | tf_op jit(solution)/shard_map/ppermute | solution.py:336
  539.1 28.0 %all-to-all-start.5 = ((bf16[8,56,1024]{2,1,0:T(8,128)(2,1)}), bf16[8,56,1024]{2,1,0:T(8,128)(2,1)}, u32[]{:S(2)}, u32[]{:S(2)}) async-start(bf16[8,56,1024]{2,1,0:T(8,128)(2,1)} %bitcast.170), calls=%async_computation.5 | async-start | bytes 1835008 | tf_op jit(solution)/shard_map/all_to_all | solution.py:497
  543.7 77.9 %all-gather.11.cloned.1.call-start = ((), (), s32[]{:S(2)}) async-start(), calls=%async_computation.8 | async-start | bytes 2801664 | tf_op jit(solution)/shard_map/all_gather | solution.py:521
  570.3 14.9 %collective-permute-start.25 = (bf16[256,1024]{1,0:T(8,128)(2,1)S(1)}, bf16[256,1024]{1,0:T(8,128)(2,1)S(1)}, u32[]{:S(2)}, u32[]{:S(2)}) collective-permute-start(bf16[256,1024]{1,0:T(8,128)(2,1)S(1)} %slice.263), channel_id=1, source_target_pairs={{0,1},{1,0},{2,3},{3,2},{4,5},{5,4},{6,7},{7,6},{8,9},{9,8},{10,11... | collective-permute-start | bytes 1572872 | tf_op jit(solution)/shard_map/ppermute | solution.py:336
  575.7 19.7 %collective-permute-start.27 = (bf16[256,1024]{1,0:T(8,128)(2,1)S(1)}, bf16[256,1024]{1,0:T(8,128)(2,1)S(1)}, u32[]{:S(2)}, u32[]{:S(2)}) collective-permute-start(bf16[256,1024]{1,0:T(8,128)(2,1)S(1)} %slice.266), channel_id=1, source_target_pairs={{0,1},{1,0},{2,3},{3,2},{4,5},{5,4},{6,7},{7,6},{8,9},{9,8},{10,11... | collective-permute-start | bytes 1572872 | tf_op jit(solution)/shard_map/ppermute | solution.py:336
  576.6 53.6 %collective-permute-start.31 = (bf16[1024,1024]{1,0:T(8,128)(2,1)S(1)}, bf16[1024,1024]{1,0:T(8,128)(2,1)}, u32[]{:S(2)}, u32[]{:S(2)}) collective-permute-start(bf16[1024,1024]{1,0:T(8,128)(2,1)S(1)} %bitcast.160), channel_id=1, source_target_pairs={{0,2},{2,0},{4,6},{6,4},{8,10},{10,8},{12,14},{14,12},{16,18},{18,... | collective-permute-start | bytes 6291464 | tf_op jit(solution)/shard_map/ppermute | solution.py:336
  587.1 35.9 %collective-permute-start.32 = (bf16[512,1024]{1,0:T(8,128)(2,1)}, bf16[512,1024]{1,0:T(8,128)(2,1)}, u32[]{:S(2)}, u32[]{:S(2)}) collective-permute-start(bf16[512,1024]{1,0:T(8,128)(2,1)} %bitcast.69), channel_id=1, source_target_pairs={{0,2},{2,0},{4,6},{6,4},{8,10},{10,8},{12,14},{14,12},{16,18},{18,... | collective-permute-start | bytes 3145736 | tf_op jit(solution)/shard_map/ppermute | solution.py:336
  622.9 15.3 %collective-permute-start.29 = (bf16[448,1024]{1,0:T(8,128)(2,1)S(1)}, bf16[448,1024]{1,0:T(8,128)(2,1)S(1)}, u32[]{:S(2)}, u32[]{:S(2)}) collective-permute-start(bf16[448,1024]{1,0:T(8,128)(2,1)S(1)} %bitcast.171), channel_id=1, source_target_pairs={{0,2},{2,0},{4,6},{6,4},{8,10},{10,8},{12,14},{14,12},{16,18},{18,... | collective-permute-start | bytes 2752520 | tf_op jit(solution)/shard_map/ppermute | solution.py:336
  628.2 15.7 %collective-permute-start.30 = (bf16[768,1024]{1,0:T(8,128)(2,1)}, bf16[768,1024]{1,0:T(8,128)(2,1)}, u32[]{:S(2)}, u32[]{:S(2)}) collective-permute-start(bf16[768,1024]{1,0:T(8,128)(2,1)} %bitcast.64), channel_id=1, source_target_pairs={{0,2},{2,0},{4,6},{6,4},{8,10},{10,8},{12,14},{14,12},{16,18},{18,... | collective-permute-start | bytes 4718600 | tf_op jit(solution)/shard_map/ppermute | solution.py:336
  (149 other events, 1260.4 us)
Sparse Core Ops, SparseCore 0:
  83.3 70.3 all-gather.6
  463.0 82.5 all-gather.8
  569.3 52.2 all-gather.10

commit v4 on v3

--- a/solution.py
+++ b/solution.py
@@ -295,29 +295,25 @@
     )(triple, triple, triple, more, more, grads)
 
 
-def widen_kernel(places, core_ref, *refs):
-    out_ref = refs[-1]
-    count = (len(refs) - 1) // 2
-    first = core_ref[0] == 0
-    for i, (source, at, size) in enumerate(places):
-        own = refs[source][at : at + size]
-        other = refs[count + source][at : at + size]
-        columns = slice(i * own.shape[1], (i + 1) * own.shape[1])
-        out_ref[:size, columns] = jnp.where(first, own, other).astype(jnp.float32)
-        out_ref[size:, columns] = jnp.where(first, other, own).astype(jnp.float32)
-
-
-def widen(core, own, other, places):
-    rows, width = 2 * places[0][2], len(places) * own[0].shape[1]
+def widen_kernel(in_ref, out_ref):
+    out_ref[...] = in_ref[...].astype(jnp.float32).reshape(out_ref.shape)
+
+
+def side_by_side_rows(array, first, size, count):
+    blocks, unused, width = array.shape
+    rows = blocks * size
+    if size % 16:
+        parts = [array[:, (first + i) * size : (first + i + 1) * size] for i in range(count)]
+        return jnp.concatenate([part.reshape(rows, width) for part in parts], axis=1).astype(jnp.float32)
     return pl.pallas_call(
-        functools.partial(widen_kernel, tuple(places)),
-        out_shape=jax.ShapeDtypeStruct((rows, width), jnp.float32),
-        in_specs=[pl.BlockSpec(memory_space=pltpu.SMEM)]
-        + [pl.BlockSpec(memory_space=pltpu.VMEM)] * (2 * len(own)),
-        out_specs=pl.BlockSpec(memory_space=pltpu.VMEM),
-        compiler_params=pltpu.CompilerParams(vmem_limit_bytes=VMEM_LIMIT),
+        widen_kernel,
+        out_shape=jax.ShapeDtypeStruct((rows, count * width), jnp.float32),
+        grid=(count,),
+        in_specs=[pl.BlockSpec((blocks, size, width), lambda i: (0, first + i, 0))],
+        out_specs=pl.BlockSpec((rows, width), lambda i: (0, i)),
+        compiler_params=params("arbitrary"),
         name="widen",
-    )(core.reshape(1).astype(jnp.int32), *own, *other)
+    )(array)
 
 
 def ordered(bit, own, other, axis=0):
@@ -365,9 +361,6 @@
                 for i in range(micro_count)
             )
 
-    def same_core(self):
-        return [list(range(core, self.blocks, 2)) for core in range(2)]
-
     def block_of(self, item, device):
         if self.paired and item == 1:
             return (device | 1) - 1 + self.x
@@ -467,10 +460,13 @@
 class Group:
     def __init__(self, plan, units):
         self.plan = plan
-        self.sizes = [unit.shape[1] // 2 for unit in units]
-        core = plan.core
-        self.send = jnp.concatenate([half_of(unit, 1 - core, 1) for unit in units], axis=1)
-        self.kept = jnp.concatenate([half_of(unit, core, 1) for unit in units], axis=1)
+        count, core = plan.blocks // 2, plan.core
+        pieces = [unit.reshape(plan.shards, count, 2, -1, unit.shape[2]) for unit in units]
+        self.sizes = [piece.shape[3] for piece in pieces]
+        self.send = jnp.concatenate(
+            [lax.dynamic_index_in_dim(piece, 1 - core, 2, False) for piece in pieces], axis=2
+        )
+        self.kept = jnp.concatenate([lax.dynamic_index_in_dim(piece, core, 2, False) for piece in pieces], axis=2)
 
     def over_core(self):
         received = swap(self.send, "blk", 1)
@@ -484,46 +480,33 @@
             mask //= 2
         return self.send
 
-    def over_fsdp(self, *earlier):
+    def over_fsdp(self):
         received = swap(self.send, "fsdp", 1)
-        if earlier:
-            received = after(received, *earlier)
         self.total = added(self.kept, received)[0]
         return received
 
-    def over_chips(self, *earlier):
-        same_core = self.plan.same_core()
-        rows, width = self.total.shape
-        parts = lax.all_to_all(
-            self.total, "blk", split_axis=0, concat_axis=0, axis_index_groups=same_core, tiled=True
-        )
-        if earlier:
-            parts = after(parts, *earlier)
-        arrived, count = parts, len(same_core[0])
-        parts = parts.reshape(count, rows // count, width).astype(jnp.float32)
-        self.held = jnp.sum(parts, axis=0).astype(low_type)
-        return arrived
-
-    def finish(self):
-        self.other = swap(self.held, "blk", 1)
-        results, at = [], 0
-        for size in self.sizes:
-            own_part, other_part = self.held[at : at + size], self.other[at : at + size]
-            results.append(ordered(self.plan.core, own_part, other_part).astype(jnp.float32))
-            at += size
-        return results
-
-
-def back_from_chips(groups):
+
+def over_chips(groups):
     plan = groups[0].plan
-    sizes = [group.held.shape[0] for group in groups]
-    held = jnp.concatenate([group.held for group in groups], axis=0)
-    held = lax.all_gather(held, "blk", axis_index_groups=plan.same_core())
-    at = 0
-    for group, size in zip(groups, sizes):
-        group.held = held[:, at : at + size].reshape(-1, held.shape[2])
+    total = jnp.concatenate([group.total for group in groups], axis=1)
+    same_core = [list(range(core, plan.blocks, 2)) for core in range(2)]
+    arrived = lax.all_to_all(
+        total, "blk", split_axis=0, concat_axis=0, axis_index_groups=same_core, tiled=True
+    )
+    return jnp.sum(arrived.astype(jnp.float32), axis=0).astype(low_type), arrived
+
+
+def from_all(sums):
+    return lax.all_gather(jnp.concatenate(sums, axis=0), "blk", axis=0)
+
+
+def gathered(array, sizes):
+    results, at = [], 0
+    for size in sizes:
+        part = array[:, at : at + size].astype(jnp.float32)
+        results.append(part.reshape(-1, part.shape[2]))
         at += size
-    return held
+    return results
 
 
 def route_pixels(plan, pixels, segment_ids, pad_ids, block_map, fetch):
@@ -708,12 +691,12 @@
     triple_grads, more_grads = self_backward(triple, more, grad_blended, plan.groups)
     triple_grads, more_grads = after((triple_grads, more_grads), one.over_fsdp())
     triple_grads = plan.own_pairs(triple_grads, more_grads)
-    two = Group(
-        plan,
-        [unit(product_tn(hidden_two, triple_grads[:, i * model : (i + 1) * model])) for i in range(3)]
-        + [unit(grad_self_out)],
-    )
-    triple_grads = after(triple_grads, two.send)
+    grad_q, grad_k, grad_v = (
+        unit(product_tn(hidden_two, triple_grads[:, i * model : (i + 1) * model])) for i in range(3)
+    )
+    two, three = Group(plan, [grad_q, grad_k]), Group(plan, [grad_v, unit(grad_self_out)])
+    triple_grads = after(triple_grads, two.send, three.send)
+    sums_one, arrived_one = over_chips([one])
     grad_hidden = product_nt(triple_grads, w_triple)
     down, gain_two, bias_two = norm_backward(grad_hidden, normed_two, scale_two, gains[2])
     upstream = upstream + down
@@ -723,13 +706,13 @@
     upstream, grad_up, unused, gain_one, bias_one = feed_backward(
         upstream, low, first_sum, stored_one, gains[1], w_up, w_down
     )
-    low = after(upstream.astype(low_type), one.over_chips())
+    low = after(upstream.astype(low_type), two.over_fsdp(), three.over_core(), arrived_one)
     grad_out = product_tn(attended, low)
-    three = Group(plan, [unit(grad_up), unit(grad_down), unit(grad_out)])
+    four = Group(plan, [unit(grad_up), unit(grad_down), unit(grad_out)])
     grad_attended = product_nt(low, w_out).astype(low_type)
     grad_value = product_tn(attended_features, grad_attended)
     grad_features = product_nt(grad_attended, w_value)
-    wide_grads = after(widened(grad_features, 1.0), two.over_fsdp(), three.over_core())
+    wide_grads = after(widened(grad_features, 1.0), four.send)
     score_sums = cross_call(
         cross_backward_kernel,
         big,
@@ -740,6 +723,8 @@
         plan.block_rows,
         plan.per_item,
     )
+    score_sums = after(score_sums, three.over_fsdp(), four.over_core())
+    sums_two, arrived_two = over_chips([two, three])
     key_sums = (narrowed(score_sums) * scaling).astype(low_type)
     grad_queries = product(key_sums, w_key).astype(low_type)
     grad_key = product_tn(key_sums, queries)
@@ -772,23 +757,22 @@
         ],
         axis=1,
     )
-    four = Group(plan, [unit(grad_query), tall.astype(low_type).reshape(shards, -1, model)])
-    four.send = after(four.send, three.over_fsdp(), two.over_chips())
-    early_sums = back_from_chips([one, two])
-    four.over_core()
-    arrived = four.over_fsdp(three.total)
+    five = Group(plan, [unit(grad_query), tall.astype(low_type).reshape(shards, -1, model)])
+    five.send = after(five.send, four.over_fsdp(), arrived_two)
+    early_sums = from_all([sums_one, sums_two])
+    sums_four, unused = over_chips([four])
+    five.over_core()
+    arrived = five.over_fsdp()
     mixed = plan.send_back(after(mixed, arrived))
     latents_grad = plan.send_back(after(latents_grad, arrived))
-    arrived = three.over_chips(early_sums)
-    four.over_chips(arrived)
-    back_from_chips([three, four])
-    grad_self_up, grad_self_down = one.finish()
-    grad_self_out = two.finish()[3]
-    half = two.sizes[0]
-    grad_triple = widen(plan.core, [two.held], [two.other], [(0, i * half, half) for i in range(3)])
+    sums_five, unused = over_chips([five])
+    late_sums = from_all([sums_four, sums_five])
+    size = one.sizes[0]
+    grad_self_up, grad_self_down = gathered(early_sums, one.sizes)
+    grad_triple = side_by_side_rows(early_sums, 2, size, 3)
+    (grad_self_out,) = gathered(early_sums[:, 5 * size :], [size])
     latents_grad = plan.placed(latents_grad).astype(jnp.float32)
-    grad_up, grad_down, grad_out = three.finish()
-    grad_query, tall = four.finish()
+    grad_up, grad_down, grad_out, grad_query, tall = gathered(late_sums, four.sizes + five.sizes)
     tall = tall.reshape(384, width)
     norm_part = tall[264:268].reshape(8, model // shards)
     pixel_part = tall[268 : 268 + pixel_rows.shape[1]].reshape(2, 512)

time: 666 us -> 659 us (0.989)
  waiting for transfers between devices: 223 us -> 209 us
  other arithmetic: 119 us -> 126 us
    convert_element_type x8 -> x5, other arithmetic: 28 us -> 11.3 us  [added(): (kept.astype(jnp.float32) + received.astype(jnp.float32)).astype(low_type)]
    squeeze x0 -> x5, other arithmetic: none -> 13.9 us  [over_fsdp(): self.total = added(self.kept, received)[0]]
    reshape x0 -> x8, other arithmetic: none -> 12.8 us  [gathered(): results.append(part.reshape(-1, part.shape[2]))]
    convert_element_type x9 -> x1, other arithmetic: 14.4 us -> 2.75 us  [on_device(): upstream.astype(low_type)]
    all_gather x2, waiting for transfers between devices: 22.9 us -> 12.1 us  [from_all(): return lax.all_gather(jnp.concatenate(sums, axis=0), 'blk', axis=0)]
    dynamic_slice x11 -> x3, local copies, waits for them, and re-layouts: 12.9 us -> 2.36 us  [the longest x2 2.16 us: __init__(): lax.dynamic_index_in_dim(piece, 1 - core, 2, False)]
    squeeze x0 -> x10, local copies, waits for them, and re-layouts: none -> 9.8 us  [the longest x7 6.19 us: __init__(): lax.dynamic_index_in_dim(piece, core, 2, False)]
    all_to_all x4, waiting for transfers between devices: 68.4 us -> 61.7 us  [over_chips(): lax.all_to_all(total, 'blk', split_axis=0, concat_axis=0, axis_index_grou...]
  transfers between devices with their start and end apart: 42 -> 40, of which waited for: 13 -> 14; matrix products, arithmetic and copies ran while one was open for 34% -> 36% of each run, Pallas kernels for 8% -> 8%
where the time goes in v4:
time: 659 us; the launch traced here: 651 us
  waiting for transfers between devices  209 us (32%)
  other arithmetic  126 us (19%)
  matrix products  101 us (15%)
  starting transfers between devices  74.4 us (11%)
  local copies, waits for them, and re-layouts  64 us (10%)
  Pallas kernels  60.4 us (9%)
  between operations  16.2 us (2%)
    ppermute x27, waiting for transfers between devices, swap(): return lax.ppermute(array, axis_name, [(i, i ^ mask) for i in range(size)])  106 us
    all_to_all x4, waiting for transfers between devices, over_chips(): lax.all_to_all(total, 'blk', split_axis=0, concat_axis=0, axis_index_grou...  61.7 us
    dot_general x10, matrix products, product_nt(): lax.dot_general(a, b, (((1,), (1,)), ((), ())), preferred_element_type=jn...  42.9 us
    dot_general x10, matrix products, product(): return jnp.dot(a, b, preferred_element_type=jnp.float32)  30.2 us
    all_to_all x1, waiting for transfers between devices, route_pixels(): lax.all_to_all(pieces, 'blk', split_axis=0, concat_axis=0, tiled=True)  29.3 us
    dot_general x12, matrix products, product_tn(): lax.dot_general(a, b, (((0,), (0,)), ((), ())), preferred_element_type=jn...  28.1 us
    all_to_all x4, starting transfers between devices, over_chips(): lax.all_to_all(total, 'blk', split_axis=0, concat_axis=0, axis_index_grou...  25.7 us
    ppermute x27, starting transfers between devices, swap(): return lax.ppermute(array, axis_name, [(i, i ^ mask) for i in range(size)])  22.9 us
  transfers between devices with their start and end apart: 40, of which 14 were waited for; matrix products, arithmetic and copies ran while one was open for 36% of the time, Pallas kernels for 8%

profile of v4, /device:TPU:0, one launch (start us, length us, event | category | flops | bytes accessed | tf_op | source)
XLA Modules:
  0.0 650.8 jit_solution(8904703540195889312)
XLA Ops:
  12.4 5.1 prepare_pixels.1
  17.5 7.5 %all-to-all-start = ((bf16[16,2,272,128]{3,2,1,0:T(8,128)(2,1)}), bf16[16,2,272,128]{3,2,1,0:T(8,128)(2,1)S(1)}, u32[]{:S(2)}, u32[]{:S(2)}) async-start(bf16[16,2,272,128]{3,2,1,0:T(8,128)(2,1)} %prepare_pixels.1), calls=%async_computation | async-start | bytes 4456448 | tf_op jit(solution)/shard_map/all_to_all | solution.py:527
  43.8 25.6 %collective-permute-done = bf16[256,1024]{1,0:T(8,128)(2,1)} collective-permute-done((bf16[256,1024]{1,0:T(8,128)(2,1)}, bf16[256,1024]{1,0:T(8,128)(2,1)}, u32[]{:S(2)}, u32[]{:S(2)}) %collective-permute-start) | collective-permute-done | bytes 524320 | tf_op jit(solution)/shard_map/ppermute | solution.py:332
  89.3 9.4 %all-to-all-start.1 = ((bf16[16,2,272,128]{3,2,1,0:T(8,128)(2,1)}), bf16[16,2,272,128]{3,2,1,0:T(8,128)(2,1)S(1)}, u32[]{:S(2)}, u32[]{:S(2)}) async-start(bf16[16,2,272,128]{3,2,1,0:T(8,128)(2,1)} %bitcast.215), calls=%async_computation.1 | async-start | bytes 4456448 | tf_op jit(solution)/shard_map/all_to_all | solution.py:559
  125.1 29.3 %all-to-all-done.1.first_ref = bf16[16,2,272,128]{3,2,1,0:T(8,128)(2,1)S(1)} async-done(((bf16[16,2,272,128]{3,2,1,0:T(8,128)(2,1)}), bf16[16,2,272,128]{3,2,1,0:T(8,128)(2,1)S(1)}, u32[]{:S(2)}, u32[]{:S(2)}) %all-to-all-start.1) | async-done | bytes 2228256 | tf_op jit(solution)/shard_map/all_to_all | solution.py:559
  158.7 8.4 %cross_attention.2 = f32[768,272]{1,0:T(8,128)} custom-call(s32[2]{0:T(128)} %get-tuple-element.210.big_ref, bf16[768,272]{1,0:T(8,128)(2,1)} %pad.23.query_ref, bf16[16,2,272,128]{3,2,1,0:T(8,128)(2,1)} %copy-done.1, bf16[16,2,272,128]{3,2,1,0:T(8,128)(2,1)} %bitcast.213, f32[2,8,4096]{2,1,0:T(8,128)} %broadcast_in_dim.82.mask_ref), custom_call_target="tpu_custom_call" | custom-call | tf_op jit(solution)/shard_map/cross_attention/pallas_call | solution.py:174
  170.4 5.5 collective-permute-start.15
  200.8 5.3 convolution_convert_fusion.q_ref.k_ref.v_ref
  212.6 10.8 %self_forward.1 = bf16[768,1024]{1,0:T(8,128)(2,1)} custom-call(bf16[768,3072]{1,0:T(8,128)(2,1)} %copy-done, bf16[768,3072]{1,0:T(8,128)(2,1)} %copy-done, bf16[768,3072]{1,0:T(8,128)(2,1)} %copy-done, bf16[256,2048]{1,0:T(8,128)(2,1)} %collective-permute-done.10.more_k_ref.more_v_ref, bf16[256,2048]{1,0:T(8,128)(2,1)} %collective-permute-done.10.more_k_ref.more_v_ref), custom_call_target="tpu_custom_call" | custom-call | tf_op jit(solution)/shard_map/self_forward/pallas_call | solution.py:266
  245.7 5.9 multiply_reduce_fusion
  265.5 19.8 %self_backward.1 = (bf16[768,3072]{1,0:T(8,128)(2,1)}, bf16[256,2048]{1,0:T(8,128)(2,1)}) custom-call(bf16[768,3072]{1,0:T(8,128)(2,1)} %copy-done, bf16[768,3072]{1,0:T(8,128)(2,1)} %copy-done, bf16[768,3072]{1,0:T(8,128)(2,1)} %copy-done, bf16[256,2048]{1,0:T(8,128)(2,1)} %collective-permute-done.10.more_k_ref.more_v_ref, ...), custom_call_target="tpu_custom_call" | custom-call | tf_op jit(solution)/shard_map/self_backward/pallas_call | solution.py:281
  293.3 9.7 %all-to-all-start.2 = ((bf16[8,64,1024]{2,1,0:T(8,128)(2,1)}), bf16[8,64,1024]{2,1,0:T(8,128)(2,1)}, u32[]{:S(2)}, u32[]{:S(2)}) async-start(bf16[8,64,1024]{2,1,0:T(8,128)(2,1)} %fusion.44), calls=%async_computation.2 | async-start | bytes 2097152 | tf_op jit(solution)/shard_map/all_to_all | solution.py:493
  318.9 8.2 %multiply_reduce_fusion.1 = (bf16[1024]{0:T(1024)(128)(2,1)S(1)}, f32[768]{0:T(1024)S(1)}, f32[768]{0:T(1024)S(1)}, bf16[1024]{0:T(1024)(128)(2,1)S(1)}, f32[768,1024]{1,0:T(8,128)S(1)}) fusion(f32[768,1024]{1,0:T(8,128)S(1)} %get-tuple-element.322, f32[768]{0:T(1024)S(1)} %add_rsqrt_fusion.1, f32[768]{0:T(1024)S(1)} %broadcast_multiply_fusion.10, ...), kind=kOutput, calls=%fused_computation.51 | convolution fusion | flops 4851494912 | bytes 17321984 | tf_op jit(solution)/shard_map/dot_general | solution.py:28
  339.7 4.6 fusion.27
  344.3 13.3 %collective-permute-done.20 = bf16[1,8,64,1024]{3,2,1,0:T(8,128)(2,1)S(1)} collective-permute-done((bf16[1,8,64,1024]{3,2,1,0:T(8,128)(2,1)S(1)}, bf16[1,8,64,1024]{3,2,1,0:T(8,128)(2,1)S(1)}, u32[]{:S(2)}, u32[]{:S(2)}) %collective-permute-start.20) | collective-permute-done | bytes 1048608 | tf_op jit(solution)/shard_map/ppermute | solution.py:332
  359.5 19.8 %collective-permute-done.22 = bf16[1,8,64,1024]{3,2,1,0:T(8,128)(2,1)S(1)} collective-permute-done((bf16[1,8,64,1024]{3,2,1,0:T(8,128)(2,1)S(1)}, bf16[1,8,64,1024]{3,2,1,0:T(8,128)(2,1)S(1)}, u32[]{:S(2)}, u32[]{:S(2)}) %collective-permute-start.22) | collective-permute-done | bytes 1048608 | tf_op jit(solution)/shard_map/ppermute | solution.py:332
  382.8 6.2 all-to-all-start.3
  406.7 29.9 %all-to-all-done.3 = bf16[8,128,1024]{2,1,0:T(8,128)(2,1)} async-done(((bf16[8,128,1024]{2,1,0:T(8,128)(2,1)}), bf16[8,128,1024]{2,1,0:T(8,128)(2,1)}, u32[]{:S(2)}, u32[]{:S(2)}) %all-to-all-start.3) | async-done | bytes 2097184 | tf_op jit(solution)/shard_map/all_to_all | solution.py:493
  447.0 10.0 %cross_attention.3 = f32[768,272]{1,0:T(8,128)} custom-call(s32[2]{0:T(128)} %get-tuple-element.210.big_ref, bf16[768,272]{1,0:T(8,128)(2,1)} %pad.23.query_ref, bf16[768,272]{1,0:T(8,128)(2,1)} %fusion.62.grad_ref, bf16[16,2,272,128]{3,2,1,0:T(8,128)(2,1)} %copy-done.1, bf16[16,2,272,128]{3,2,1,0:T(8,128)(2,1)} %bitcast.214, ...), custom_call_target="tpu_custom_call" | custom-call | tf_op jit(solution)/shard_map/cross_attention/pallas_call | solution.py:174
  465.0 4.1 reshape.776
  474.4 5.3 fusion.10
  479.9 6.3 maximum_maximum_fusion
  497.4 4.2 fusion.30
  501.6 5.6 all-to-all-start.4
  509.3 22.2 %collective-permute-done.26 = bf16[1,8,56,1024]{3,2,1,0:T(8,128)(2,1)S(1)} collective-permute-done((bf16[1,8,56,1024]{3,2,1,0:T(8,128)(2,1)S(1)}, bf16[1,8,56,1024]{3,2,1,0:T(8,128)(2,1)S(1)}, u32[]{:S(2)}, u32[]{:S(2)}) %collective-permute-start.26) | collective-permute-done | bytes 917536 | tf_op jit(solution)/shard_map/ppermute | solution.py:332
  534.1 10.7 %all-to-all-done.4 = bf16[8,96,1024]{2,1,0:T(8,128)(2,1)S(1)} async-done(((bf16[8,96,1024]{2,1,0:T(8,128)(2,1)}), bf16[8,96,1024]{2,1,0:T(8,128)(2,1)S(1)}, u32[]{:S(2)}, u32[]{:S(2)}) %all-to-all-start.4) | async-done | bytes 1572896 | tf_op jit(solution)/shard_map/all_to_all | solution.py:493
  546.0 4.2 all-to-all-start.5
  552.1 21.0 %all-to-all-done.5 = bf16[8,56,1024]{2,1,0:T(8,128)(2,1)} async-done(((bf16[8,56,1024]{2,1,0:T(8,128)(2,1)}), bf16[8,56,1024]{2,1,0:T(8,128)(2,1)}, u32[]{:S(2)}, u32[]{:S(2)}) %all-to-all-start.5) | async-done | bytes 917536 | tf_op jit(solution)/shard_map/all_to_all | solution.py:493
  582.2 9.1 %collective-permute-done.27 = bf16[256,1024]{1,0:T(8,128)(2,1)S(1)} collective-permute-done((bf16[256,1024]{1,0:T(8,128)(2,1)S(1)}, bf16[256,1024]{1,0:T(8,128)(2,1)S(1)}, u32[]{:S(2)}, u32[]{:S(2)}) %collective-permute-start.27) | collective-permute-done | bytes 524320 | tf_op jit(solution)/shard_map/ppermute | solution.py:332
  592.1 8.2 %collective-permute-done.29 = bf16[256,1024]{1,0:T(8,128)(2,1)S(1)} collective-permute-done((bf16[256,1024]{1,0:T(8,128)(2,1)S(1)}, bf16[256,1024]{1,0:T(8,128)(2,1)S(1)}, u32[]{:S(2)}, u32[]{:S(2)}) %collective-permute-start.29) | collective-permute-done | bytes 524320 | tf_op jit(solution)/shard_map/ppermute | solution.py:332
  604.4 6.3 widen.1
  616.0 12.1 %all-gather.9.cloned.1.call-done = bf16[2432,1024]{1,0:T(8,128)(2,1)} async-done(((bf16[152,1024]{1,0:T(8,128)(2,1)}), bf16[2432,1024]{1,0:T(8,128)(2,1)}) %all-gather.9.cloned.1.call-update) | async-done | bytes 4980752 | tf_op jit(solution)/shard_map/all_gather | solution.py:500
  (547 shorter events, 280.9 us)
Async XLA Ops:
  17.5 53.1 %all-to-all-start = ((bf16[16,2,272,128]{3,2,1,0:T(8,128)(2,1)}), bf16[16,2,272,128]{3,2,1,0:T(8,128)(2,1)S(1)}, u32[]{:S(2)}, u32[]{:S(2)}) async-start(bf16[16,2,272,128]{3,2,1,0:T(8,128)(2,1)} %prepare_pixels.1), calls=%async_computation | async-start | bytes 4456448 | tf_op jit(solution)/shard_map/all_to_all | solution.py:527
  25.1 132.9 %all-gather.7.cloned.1.call-start = ((), (), s32[]{:S(2)}) async-start(), calls=%async_computation.6 | async-start | bytes 2367488 | tf_op jit(solution)/shard_map/all_gather | solution.py:563
  26.0 17.8 %collective-permute-start.3 = (bf16[256,1024]{1,0:T(8,128)(2,1)}, bf16[256,1024]{1,0:T(8,128)(2,1)}, u32[]{:S(2)}, u32[]{:S(2)}) collective-permute-start(bf16[256,1024]{1,0:T(8,128)(2,1)} %constant_dynamic-slice_fusion.9), channel_id=1, source_target_pairs={{0,1},{1,0},{2,3},{3,2},{4,5},{5,4},{6,7},{7,6},{8,9},{9,8},{10,11... | collective-permute-start | bytes 1572872 | tf_op jit(solution)/shard_map/ppermute | solution.py:332
  29.4 39.9 %collective-permute-start.2 = (bf16[265,1024]{1,0:T(8,128)(2,1)}, bf16[265,1024]{1,0:T(8,128)(2,1)}, u32[]{:S(2)}, u32[]{:S(2)}) collective-permute-start(bf16[265,1024]{1,0:T(8,128)(2,1)} %pad_maximum_fusion.41), channel_id=1, source_target_pairs={{0,1},{1,0},{2,3},{3,2},{4,5},{5,4},{6,7},{7,6},{8,9},{9,8},{10,11... | collective-permute-start | bytes 1628168 | tf_op jit(solution)/shard_map/ppermute | solution.py:332
  32.4 11.4 %collective-permute-start.1 = (bf16[256,1024]{1,0:T(8,128)(2,1)}, bf16[256,1024]{1,0:T(8,128)(2,1)S(1)}, u32[]{:S(2)}, u32[]{:S(2)}) collective-permute-start(bf16[256,1024]{1,0:T(8,128)(2,1)} %get-tuple-element.288), channel_id=1, source_target_pairs={{0,0},{2,1},{4,4},{6,5},{8,8},{10,9},{12,12},{14,13},{16,16},{18,1... | collective-permute-start | bytes 1572872 | tf_op jit(solution)/shard_map/ppermute | solution.py:375
  34.2 35.1 %collective-permute-start = (bf16[256,1024]{1,0:T(8,128)(2,1)}, bf16[256,1024]{1,0:T(8,128)(2,1)}, u32[]{:S(2)}, u32[]{:S(2)}) collective-permute-start(bf16[256,1024]{1,0:T(8,128)(2,1)} %get-tuple-element.289), channel_id=1, source_target_pairs={{0,1},{1,0},{2,3},{3,2},{4,5},{5,4},{6,7},{7,6},{8,9},{9,8},{10,11... | collective-permute-start | bytes 1572872 | tf_op jit(solution)/shard_map/ppermute | solution.py:332
  70.6 42.2 %collective-permute-start.5 = (bf16[256,3072]{1,0:T(8,128)(2,1)}, bf16[256,3072]{1,0:T(8,128)(2,1)}, u32[]{:S(2)}, u32[]{:S(2)}) collective-permute-start(bf16[256,3072]{1,0:T(8,128)(2,1)} %pad_maximum_fusion.19), channel_id=1, source_target_pairs={{0,1},{1,0},{2,3},{3,2},{4,5},{5,4},{6,7},{7,6},{8,9},{9,8},{10,11... | collective-permute-start | bytes 4718600 | tf_op jit(solution)/shard_map/ppermute | solution.py:332
  83.2 19.4 %collective-permute-start.4 = (bf16[256,1024]{1,0:T(8,128)(2,1)}, bf16[256,1024]{1,0:T(8,128)(2,1)}, u32[]{:S(2)}, u32[]{:S(2)}) collective-permute-start(bf16[256,1024]{1,0:T(8,128)(2,1)} %collective-permute-done.3), channel_id=1, source_target_pairs={{0,2},{2,0},{4,6},{6,4},{8,10},{10,8},{12,14},{14,12},{16,18},{18,... | collective-permute-start | bytes 1572872 | tf_op jit(solution)/shard_map/ppermute | solution.py:332
  89.3 65.1 %all-to-all-start.1 = ((bf16[16,2,272,128]{3,2,1,0:T(8,128)(2,1)}), bf16[16,2,272,128]{3,2,1,0:T(8,128)(2,1)S(1)}, u32[]{:S(2)}, u32[]{:S(2)}) async-start(bf16[16,2,272,128]{3,2,1,0:T(8,128)(2,1)} %bitcast.215), calls=%async_computation.1 | async-start | bytes 4456448 | tf_op jit(solution)/shard_map/all_to_all | solution.py:559
  101.0 24.1 %collective-permute-start.7 = (bf16[128,3072]{1,0:T(8,128)(2,1)S(1)}, bf16[128,3072]{1,0:T(8,128)(2,1)}, u32[]{:S(2)}, u32[]{:S(2)}) collective-permute-start(bf16[128,3072]{1,0:T(8,128)(2,1)S(1)} %constant_dynamic-slice_fusion.5), channel_id=1, source_target_pairs={{0,1},{1,0},{2,3},{3,2},{4,5},{5,4},{6,7},{7,6},{8,9},{9,8},{10,11... | collective-permute-start | bytes 2359304 | tf_op jit(solution)/shard_map/ppermute | solution.py:332
  114.0 54.5 %collective-permute-start.11 = (bf16[128,3072]{1,0:T(8,128)(2,1)}, bf16[128,3072]{1,0:T(8,128)(2,1)}, u32[]{:S(2)}, u32[]{:S(2)}) collective-permute-start(bf16[128,3072]{1,0:T(8,128)(2,1)} %pad_maximum_fusion.40), channel_id=1, source_target_pairs={{0,1},{1,0},{2,3},{3,2},{4,5},{5,4},{6,7},{7,6},{8,9},{9,8},{10,11... | collective-permute-start | bytes 2359304 | tf_op jit(solution)/shard_map/ppermute | solution.py:332
  154.4 38.0 %collective-permute-start.8 = (bf16[128,3072]{1,0:T(8,128)(2,1)}, bf16[128,3072]{1,0:T(8,128)(2,1)}, u32[]{:S(2)}, u32[]{:S(2)}) collective-permute-start(bf16[128,3072]{1,0:T(8,128)(2,1)} %collective-permute-done.7), channel_id=1, source_target_pairs={{0,4},{2,6},{4,0},{6,2},{8,12},{10,14},{12,8},{14,10},{16,20},{18,... | collective-permute-start | bytes 2359304 | tf_op jit(solution)/shard_map/ppermute | solution.py:332
  168.5 26.7 %collective-permute-start.12 = (bf16[128,3072]{1,0:T(8,128)(2,1)}, bf16[128,3072]{1,0:T(8,128)(2,1)S(1)}, u32[]{:S(2)}, u32[]{:S(2)}) collective-permute-start(bf16[128,3072]{1,0:T(8,128)(2,1)} %collective-permute-done.11), channel_id=1, source_target_pairs={{0,4},{2,6},{4,0},{6,2},{8,12},{10,14},{12,8},{14,10},{16,20},{18,... | collective-permute-start | bytes 2359304 | tf_op jit(solution)/shard_map/ppermute | solution.py:332
  170.4 56.4 %collective-permute-start.15 = (bf16[256,1024]{1,0:T(8,128)(2,1)}, bf16[256,1024]{1,0:T(8,128)(2,1)}, u32[]{:S(2)}, u32[]{:S(2)}) collective-permute-start(bf16[256,1024]{1,0:T(8,128)(2,1)} %get-tuple-element.281), channel_id=1, source_target_pairs={{0,0},{2,1},{4,4},{6,5},{8,8},{10,9},{12,12},{14,13},{16,16},{18,1... | collective-permute-start | bytes 1572872 | tf_op jit(solution)/shard_map/ppermute | solution.py:375
  175.9 50.8 %collective-permute-start.14 = (bf16[256,1024]{1,0:T(8,128)(2,1)}, bf16[256,1024]{1,0:T(8,128)(2,1)}, u32[]{:S(2)}, u32[]{:S(2)}) collective-permute-start(bf16[256,1024]{1,0:T(8,128)(2,1)} %get-tuple-element.282), channel_id=1, source_target_pairs={{0,1},{1,0},{2,3},{3,2},{4,5},{5,4},{6,7},{7,6},{8,9},{9,8},{10,11... | collective-permute-start | bytes 1572872 | tf_op jit(solution)/shard_map/ppermute | solution.py:332
  254.4 30.8 %collective-permute-start.17 = (bf16[1,8,64,1024]{3,2,1,0:T(8,128)(2,1)}, bf16[1,8,64,1024]{3,2,1,0:T(8,128)(2,1)}, u32[]{:S(2)}, u32[]{:S(2)}) collective-permute-start(bf16[1,8,64,1024]{3,2,1,0:T(8,128)(2,1)} %add_convert_fusion.16), channel_id=1, source_target_pairs={{0,1},{1,0},{2,3},{3,2},{4,5},{5,4},{6,7},{7,6},{8,9},{9,8},{10,11... | collective-permute-start | bytes 3145736 | tf_op jit(solution)/shard_map/ppermute | solution.py:332
  285.3 17.8 %collective-permute-start.18 = (bf16[256,2048]{1,0:T(8,128)(2,1)}, bf16[256,2048]{1,0:T(8,128)(2,1)}, u32[]{:S(2)}, u32[]{:S(2)}) collective-permute-start(bf16[256,2048]{1,0:T(8,128)(2,1)} %get-tuple-element.68), channel_id=1, source_target_pairs={{0,2},{2,0},{4,6},{6,4},{8,10},{10,8},{12,14},{14,12},{16,18},{18,... | collective-permute-start | bytes 3145736 | tf_op jit(solution)/shard_map/ppermute | solution.py:332
  293.3 89.4 %all-to-all-start.2 = ((bf16[8,64,1024]{2,1,0:T(8,128)(2,1)}), bf16[8,64,1024]{2,1,0:T(8,128)(2,1)}, u32[]{:S(2)}, u32[]{:S(2)}) async-start(bf16[8,64,1024]{2,1,0:T(8,128)(2,1)} %fusion.44), calls=%async_computation.2 | async-start | bytes 2097152 | tf_op jit(solution)/shard_map/all_to_all | solution.py:493
  315.6 14.1 %collective-permute-start.19 = (bf16[2,8,64,1024]{3,2,1,0:T(8,128)(2,1)}, bf16[2,8,64,1024]{3,2,1,0:T(8,128)(2,1)}, u32[]{:S(2)}, u32[]{:S(2)}) collective-permute-start(bf16[2,8,64,1024]{3,2,1,0:T(8,128)(2,1)} %pad_maximum_fusion.14), channel_id=1, source_target_pairs={{0,2},{2,0},{4,6},{6,4},{8,10},{10,8},{12,14},{14,12},{16,18},{18,... | collective-permute-start | bytes 6291464 | tf_op jit(solution)/shard_map/ppermute | solution.py:332
  317.1 16.6 %collective-permute-start.21 = (bf16[2,8,64,1024]{3,2,1,0:T(8,128)(2,1)}, bf16[2,8,64,1024]{3,2,1,0:T(8,128)(2,1)}, u32[]{:S(2)}, u32[]{:S(2)}) collective-permute-start(bf16[2,8,64,1024]{3,2,1,0:T(8,128)(2,1)} %pad_maximum_fusion.15), channel_id=1, source_target_pairs={{0,2},{2,0},{4,6},{6,4},{8,10},{10,8},{12,14},{14,12},{16,18},{18,... | collective-permute-start | bytes 6291464 | tf_op jit(solution)/shard_map/ppermute | solution.py:332
  331.5 26.1 %collective-permute-start.20 = (bf16[1,8,64,1024]{3,2,1,0:T(8,128)(2,1)S(1)}, bf16[1,8,64,1024]{3,2,1,0:T(8,128)(2,1)S(1)}, u32[]{:S(2)}, u32[]{:S(2)}) collective-permute-start(bf16[1,8,64,1024]{3,2,1,0:T(8,128)(2,1)S(1)} %add_convert_fusion.14), channel_id=1, source_target_pairs={{0,1},{1,0},{2,3},{3,2},{4,5},{5,4},{6,7},{7,6},{8,9},{9,8},{10,11... | collective-permute-start | bytes 3145736 | tf_op jit(solution)/shard_map/ppermute | solution.py:332
  335.6 43.7 %collective-permute-start.22 = (bf16[1,8,64,1024]{3,2,1,0:T(8,128)(2,1)S(1)}, bf16[1,8,64,1024]{3,2,1,0:T(8,128)(2,1)S(1)}, u32[]{:S(2)}, u32[]{:S(2)}) collective-permute-start(bf16[1,8,64,1024]{3,2,1,0:T(8,128)(2,1)S(1)} %add_convert_fusion.13), channel_id=1, source_target_pairs={{0,1},{1,0},{2,3},{3,2},{4,5},{5,4},{6,7},{7,6},{8,9},{9,8},{10,11... | collective-permute-start | bytes 3145736 | tf_op jit(solution)/shard_map/ppermute | solution.py:332
  382.8 53.9 %all-to-all-start.3 = ((bf16[8,128,1024]{2,1,0:T(8,128)(2,1)}), bf16[8,128,1024]{2,1,0:T(8,128)(2,1)}, u32[]{:S(2)}, u32[]{:S(2)}) async-start(bf16[8,128,1024]{2,1,0:T(8,128)(2,1)} %pad_maximum_fusion.16), calls=%async_computation.3 | async-start | bytes 4194304 | tf_op jit(solution)/shard_map/all_to_all | solution.py:493
  388.9 215.5 %all-gather.11.cloned.1.call-start = ((), (), s32[]{:S(2)}) async-start(), calls=%async_computation.8 | async-start | bytes 6684672 | tf_op jit(solution)/shard_map/all_gather | solution.py:500
  405.2 53.9 %collective-permute-start.23 = (bf16[2,8,96,1024]{3,2,1,0:T(8,128)(2,1)}, bf16[2,8,96,1024]{3,2,1,0:T(8,128)(2,1)}, u32[]{:S(2)}, u32[]{:S(2)}) collective-permute-start(bf16[2,8,96,1024]{3,2,1,0:T(8,128)(2,1)} %pad_maximum_fusion.4), channel_id=1, source_target_pairs={{0,2},{2,0},{4,6},{6,4},{8,10},{10,8},{12,14},{14,12},{16,18},{18,... | collective-permute-start | bytes 9437192 | tf_op jit(solution)/shard_map/ppermute | solution.py:332
  462.4 34.9 %collective-permute-start.24 = (bf16[1,8,96,1024]{3,2,1,0:T(8,128)(2,1)}, bf16[1,8,96,1024]{3,2,1,0:T(8,128)(2,1)}, u32[]{:S(2)}, u32[]{:S(2)}) collective-permute-start(bf16[1,8,96,1024]{3,2,1,0:T(8,128)(2,1)} %add_convert_fusion.2), channel_id=1, source_target_pairs={{0,1},{1,0},{2,3},{3,2},{4,5},{5,4},{6,7},{7,6},{8,9},{9,8},{10,11... | collective-permute-start | bytes 4718600 | tf_op jit(solution)/shard_map/ppermute | solution.py:332
  501.6 43.3 %all-to-all-start.4 = ((bf16[8,96,1024]{2,1,0:T(8,128)(2,1)}), bf16[8,96,1024]{2,1,0:T(8,128)(2,1)S(1)}, u32[]{:S(2)}, u32[]{:S(2)}) async-start(bf16[8,96,1024]{2,1,0:T(8,128)(2,1)} %fusion.30), calls=%async_computation.4 | async-start | bytes 3145728 | tf_op jit(solution)/shard_map/all_to_all | solution.py:493
  508.9 22.5 %collective-permute-start.26 = (bf16[1,8,56,1024]{3,2,1,0:T(8,128)(2,1)S(1)}, bf16[1,8,56,1024]{3,2,1,0:T(8,128)(2,1)S(1)}, u32[]{:S(2)}, u32[]{:S(2)}) collective-permute-start(bf16[1,8,56,1024]{3,2,1,0:T(8,128)(2,1)S(1)} %add_convert_fusion.19), channel_id=1, source_target_pairs={{0,1},{1,0},{2,3},{3,2},{4,5},{5,4},{6,7},{7,6},{8,9},{9,8},{10,11... | collective-permute-start | bytes 2752520 | tf_op jit(solution)/shard_map/ppermute | solution.py:332
  546.0 27.2 %all-to-all-start.5 = ((bf16[8,56,1024]{2,1,0:T(8,128)(2,1)}), bf16[8,56,1024]{2,1,0:T(8,128)(2,1)}, u32[]{:S(2)}, u32[]{:S(2)}) async-start(bf16[8,56,1024]{2,1,0:T(8,128)(2,1)} %fusion.57), calls=%async_computation.5 | async-start | bytes 1835008 | tf_op jit(solution)/shard_map/all_to_all | solution.py:493
  550.2 77.9 %all-gather.9.cloned.1.call-start = ((), (), s32[]{:S(2)}) async-start(), calls=%async_computation.7 | async-start | bytes 5292032 | tf_op jit(solution)/shard_map/all_gather | solution.py:500
  576.4 14.9 %collective-permute-start.27 = (bf16[256,1024]{1,0:T(8,128)(2,1)S(1)}, bf16[256,1024]{1,0:T(8,128)(2,1)S(1)}, u32[]{:S(2)}, u32[]{:S(2)}) collective-permute-start(bf16[256,1024]{1,0:T(8,128)(2,1)S(1)} %slice.215), channel_id=1, source_target_pairs={{0,1},{1,0},{2,3},{3,2},{4,5},{5,4},{6,7},{7,6},{8,9},{9,8},{10,11... | collective-permute-start | bytes 1572872 | tf_op jit(solution)/shard_map/ppermute | solution.py:332
  580.4 20.0 %collective-permute-start.29 = (bf16[256,1024]{1,0:T(8,128)(2,1)S(1)}, bf16[256,1024]{1,0:T(8,128)(2,1)S(1)}, u32[]{:S(2)}, u32[]{:S(2)}) collective-permute-start(bf16[256,1024]{1,0:T(8,128)(2,1)S(1)} %slice.218), channel_id=1, source_target_pairs={{0,1},{1,0},{2,3},{3,2},{4,5},{5,4},{6,7},{7,6},{8,9},{9,8},{10,11... | collective-permute-start | bytes 1572872 | tf_op jit(solution)/shard_map/ppermute | solution.py:332
  (140 other events, 1213.2 us)
Sparse Core Ops, SparseCore 0:
  83.3 67.2 all-gather.6
  439.5 62.1 all-gather.10
  575.4 52.6 all-gather.8

commit v5 on v4

--- a/solution.py
+++ b/solution.py
@@ -454,6 +454,8 @@
 
 
 def after(value, *others):
+    if not others:
+        return value
     return lax.optimization_barrier((value,) + others)[0]
 
 
@@ -468,8 +470,8 @@
         )
         self.kept = jnp.concatenate([lax.dynamic_index_in_dim(piece, core, 2, False) for piece in pieces], axis=2)
 
-    def over_core(self):
-        received = swap(self.send, "blk", 1)
+    def over_core(self, *earlier):
+        received = after(swap(self.send, "blk", 1), *earlier)
         mask = self.plan.shards // 2
         while mask:
             bit = jnp.where((self.plan.x & mask) > 0, 1, 0)
@@ -480,19 +482,20 @@
             mask //= 2
         return self.send
 
-    def over_fsdp(self):
-        received = swap(self.send, "fsdp", 1)
+    def over_fsdp(self, *earlier):
+        received = after(swap(self.send, "fsdp", 1), *earlier)
         self.total = added(self.kept, received)[0]
         return received
 
 
-def over_chips(groups):
+def over_chips(groups, *earlier):
     plan = groups[0].plan
     total = jnp.concatenate([group.total for group in groups], axis=1)
     same_core = [list(range(core, plan.blocks, 2)) for core in range(2)]
     arrived = lax.all_to_all(
         total, "blk", split_axis=0, concat_axis=0, axis_index_groups=same_core, tiled=True
     )
+    arrived = after(arrived, *earlier)
     return jnp.sum(arrived.astype(jnp.float32), axis=0).astype(low_type), arrived
 
 
@@ -706,9 +709,11 @@
     upstream, grad_up, unused, gain_one, bias_one = feed_backward(
         upstream, low, first_sum, stored_one, gains[1], w_up, w_down
     )
-    low = after(upstream.astype(low_type), two.over_fsdp(), three.over_core(), arrived_one)
+    grad_up, grad_down = unit(grad_up), unit(grad_down)
+    low = upstream.astype(low_type)
+    low = after(low, grad_up, grad_down, two.over_fsdp(low), three.over_core(low), arrived_one)
     grad_out = product_tn(attended, low)
-    four = Group(plan, [unit(grad_up), unit(grad_down), unit(grad_out)])
+    four = Group(plan, [grad_up, grad_down, unit(grad_out)])
     grad_attended = product_nt(low, w_out).astype(low_type)
     grad_value = product_tn(attended_features, grad_attended)
     grad_features = product_nt(grad_attended, w_value)
@@ -723,8 +728,7 @@
         plan.block_rows,
         plan.per_item,
     )
-    score_sums = after(score_sums, three.over_fsdp(), four.over_core())
-    sums_two, arrived_two = over_chips([two, three])
+    score_sums = after(score_sums, three.over_fsdp(score_sums), four.over_core(score_sums))
     key_sums = (narrowed(score_sums) * scaling).astype(low_type)
     grad_queries = product(key_sums, w_key).astype(low_type)
     grad_key = product_tn(key_sums, queries)
@@ -742,23 +746,29 @@
 
     shards = plan.shards
     width = 2 * model // shards
-    rows_of_pair = jnp.pad(jnp.concatenate([grad_key, grad_value], axis=1), ((0, 264 - features), (0, 0)))
+    if shards == 2:
+        rows_of_pair = jnp.stack([grad_key, grad_value]).astype(low_type)
+    else:
+        rows_of_pair = jnp.concatenate([grad_key, grad_value], axis=1).astype(low_type)
+        rows_of_pair = rows_of_pair.reshape(features, shards, width).transpose(1, 0, 2)
     norm_terms = jnp.stack(
         [gain_zero, gain_one, gain_two, gain_three, bias_zero, bias_one, bias_two, bias_three]
     )
     pixel_terms = jnp.pad(jnp.stack([pixel_gain_term, pixel_bias_term]), ((0, 0), (0, 512 - features)))
     pixel_rows = pixel_terms.reshape(1, -1, width)
-    tall = jnp.concatenate(
+    small = jnp.concatenate(
         [
-            rows_of_pair.reshape(264, shards, width).transpose(1, 0, 2),
             norm_terms.reshape(8, shards, model // shards).transpose(1, 0, 2).reshape(shards, 4, width),
             jnp.broadcast_to(pixel_rows, (shards,) + pixel_rows.shape[1:]),
-            jnp.zeros((shards, 384 - 268 - pixel_rows.shape[1], width), jnp.float32),
         ],
         axis=1,
     )
-    five = Group(plan, [unit(grad_query), tall.astype(low_type).reshape(shards, -1, model)])
-    five.send = after(five.send, four.over_fsdp(), arrived_two)
+    tall = jnp.pad(rows_of_pair, ((0, 0), (0, 384 - features), (0, 0)))
+    tall = lax.dynamic_update_slice(tall, small.astype(low_type), (0, 264, 0))
+    grad_query = unit(grad_query)
+    sums_two, arrived_two = over_chips([two, three], grad_query)
+    five = Group(plan, [grad_query, tall.reshape(shards, -1, model)])
+    five.send = after(five.send, four.over_fsdp(grad_query), arrived_two)
     early_sums = from_all([sums_one, sums_two])
     sums_four, unused = over_chips([four])
     five.over_core()

time: 659 us -> 660 us (level)
  matrix products: 101 us -> 109 us
    ppermute x27, waiting for transfers between devices: 106 us -> 95 us  [swap(): return lax.ppermute(array, axis_name, [(i, i ^ mask) for i in range(size)])]
    concatenate x2 -> x1, other arithmetic: 7.39 us -> 0.02 us  [on_device(): jnp.concatenate([norm_terms.reshape(8, shards, model // shards).transpose...]
    unnamed x273 -> x285, local copies, waits for them, and re-layouts: 13.9 us -> 14.6 us
  transfers between devices with their start and end apart: 40 -> 40, of which waited for: 14 -> 13; matrix products, arithmetic and copies ran while one was open for 36% -> 37% of each run, Pallas kernels for 8% -> 9%
where the time goes in v5:
time: 660 us; the launch traced here: 653 us
  waiting for transfers between devices  204 us (31%)
  other arithmetic  121 us (18%)
  matrix products  109 us (17%)
  starting transfers between devices  73.7 us (11%)
  local copies, waits for them, and re-layouts  66 us (10%)
  Pallas kernels  63.1 us (10%)
  between operations  16.1 us (2%)
    ppermute x27, waiting for transfers between devices, swap(): return lax.ppermute(array, axis_name, [(i, i ^ mask) for i in range(size)])  95 us
    all_to_all x4, waiting for transfers between devices, over_chips(): lax.all_to_all(total, 'blk', split_axis=0, concat_axis=0, axis_index_grou...  67.7 us
    dot_general x10, matrix products, product_nt(): lax.dot_general(a, b, (((1,), (1,)), ((), ())), preferred_element_type=jn...  46.1 us
    dot_general x12, matrix products, product_tn(): lax.dot_general(a, b, (((0,), (0,)), ((), ())), preferred_element_type=jn...  32.7 us
    dot_general x10, matrix products, product(): return jnp.dot(a, b, preferred_element_type=jnp.float32)  30.3 us
    all_to_all x1, waiting for transfers between devices, route_pixels(): lax.all_to_all(pieces, 'blk', split_axis=0, concat_axis=0, tiled=True)  28.8 us
    ppermute x27, starting transfers between devices, swap(): return lax.ppermute(array, axis_name, [(i, i ^ mask) for i in range(size)])  24.3 us
    all_to_all x4, starting transfers between devices, over_chips(): lax.all_to_all(total, 'blk', split_axis=0, concat_axis=0, axis_index_grou...  23.4 us
  transfers between devices with their start and end apart: 40, of which 13 were waited for; matrix products, arithmetic and copies ran while one was open for 37% of the time, Pallas kernels for 9%

profile of v5, /device:TPU:0, one launch (start us, length us, event | category | flops | bytes accessed | tf_op | source)
XLA Modules:
  0.0 652.7 jit_solution(17264206965746662619)
XLA Ops:
  12.4 5.1 prepare_pixels.1
  17.5 7.5 %all-to-all-start = ((bf16[16,2,272,128]{3,2,1,0:T(8,128)(2,1)}), bf16[16,2,272,128]{3,2,1,0:T(8,128)(2,1)S(1)}, u32[]{:S(2)}, u32[]{:S(2)}) async-start(bf16[16,2,272,128]{3,2,1,0:T(8,128)(2,1)} %prepare_pixels.1), calls=%async_computation | async-start | bytes 4456448 | tf_op jit(solution)/shard_map/all_to_all | solution.py:530
  43.8 25.5 %collective-permute-done = bf16[256,1024]{1,0:T(8,128)(2,1)} collective-permute-done((bf16[256,1024]{1,0:T(8,128)(2,1)}, bf16[256,1024]{1,0:T(8,128)(2,1)}, u32[]{:S(2)}, u32[]{:S(2)}) %collective-permute-start) | collective-permute-done | bytes 524320 | tf_op jit(solution)/shard_map/ppermute | solution.py:332
  89.3 9.1 %all-to-all-start.1 = ((bf16[16,2,272,128]{3,2,1,0:T(8,128)(2,1)}), bf16[16,2,272,128]{3,2,1,0:T(8,128)(2,1)S(1)}, u32[]{:S(2)}, u32[]{:S(2)}) async-start(bf16[16,2,272,128]{3,2,1,0:T(8,128)(2,1)} %bitcast.215), calls=%async_computation.1 | async-start | bytes 4456448 | tf_op jit(solution)/shard_map/all_to_all | solution.py:562
  125.1 28.8 %all-to-all-done.1.first_ref = bf16[16,2,272,128]{3,2,1,0:T(8,128)(2,1)S(1)} async-done(((bf16[16,2,272,128]{3,2,1,0:T(8,128)(2,1)}), bf16[16,2,272,128]{3,2,1,0:T(8,128)(2,1)S(1)}, u32[]{:S(2)}, u32[]{:S(2)}) %all-to-all-start.1) | async-done | bytes 2228256 | tf_op jit(solution)/shard_map/all_to_all | solution.py:562
  158.2 9.7 %cross_attention.2 = f32[768,272]{1,0:T(8,128)} custom-call(s32[2]{0:T(128)} %get-tuple-element.222.big_ref, bf16[768,272]{1,0:T(8,128)(2,1)} %pad.22.query_ref, bf16[16,2,272,128]{3,2,1,0:T(8,128)(2,1)} %copy-done.1, bf16[16,2,272,128]{3,2,1,0:T(8,128)(2,1)} %bitcast.213, f32[2,8,4096]{2,1,0:T(8,128)} %broadcast_in_dim.80.mask_ref), custom_call_target="tpu_custom_call" | custom-call | tf_op jit(solution)/shard_map/cross_attention/pallas_call | solution.py:174
  170.6 5.8 collective-permute-start.15
  199.4 5.3 convolution_convert_fusion.q_ref.k_ref.v_ref
  211.2 10.8 %self_forward.1 = bf16[768,1024]{1,0:T(8,128)(2,1)} custom-call(bf16[768,3072]{1,0:T(8,128)(2,1)} %copy-done, bf16[768,3072]{1,0:T(8,128)(2,1)} %copy-done, bf16[768,3072]{1,0:T(8,128)(2,1)} %copy-done, bf16[256,2048]{1,0:T(8,128)(2,1)} %collective-permute-done.10.more_k_ref.more_v_ref, bf16[256,2048]{1,0:T(8,128)(2,1)} %collective-permute-done.10.more_k_ref.more_v_ref), custom_call_target="tpu_custom_call" | custom-call | tf_op jit(solution)/shard_map/self_forward/pallas_call | solution.py:266
  233.7 3.8 fusion.21
  244.2 6.3 multiply_reduce_fusion
  264.5 19.8 %self_backward.1 = (bf16[768,3072]{1,0:T(8,128)(2,1)}, bf16[256,2048]{1,0:T(8,128)(2,1)}) custom-call(bf16[768,3072]{1,0:T(8,128)(2,1)} %copy-done, bf16[768,3072]{1,0:T(8,128)(2,1)} %copy-done, bf16[768,3072]{1,0:T(8,128)(2,1)} %copy-done, bf16[256,2048]{1,0:T(8,128)(2,1)} %collective-permute-done.10.more_k_ref.more_v_ref, ...), custom_call_target="tpu_custom_call" | custom-call | tf_op jit(solution)/shard_map/self_backward/pallas_call | solution.py:281
  292.5 10.2 %all-to-all-start.2 = ((bf16[8,64,1024]{2,1,0:T(8,128)(2,1)}), bf16[8,64,1024]{2,1,0:T(8,128)(2,1)}, u32[]{:S(2)}, u32[]{:S(2)}) async-start(bf16[8,64,1024]{2,1,0:T(8,128)(2,1)} %fusion.46), calls=%async_computation.2 | async-start | bytes 2097152 | tf_op jit(solution)/shard_map/all_to_all | solution.py:495
  319.1 10.2 %multiply_reduce_fusion.1 = (bf16[1024]{0:T(1024)(128)(2,1)}, f32[768]{0:T(1024)S(1)}, f32[768]{0:T(1024)S(1)}, bf16[1024]{0:T(1024)(128)(2,1)}, f32[768,1024]{1,0:T(8,128)}) fusion(f32[768,1024]{1,0:T(8,128)S(1)} %get-tuple-element.334, f32[768]{0:T(1024)S(1)} %add_rsqrt_fusion.1, f32[768]{0:T(1024)S(1)} %broadcast_multiply_fusion.10, ...), kind=kOutput, calls=%fused_computation.54 | convolution fusion | flops 4851494912 | bytes 17321984 | tf_op jit(solution)/shard_map/dot_general | solution.py:28
  355.1 8.3 %collective-permute-done.20 = bf16[1,8,64,1024]{3,2,1,0:T(8,128)(2,1)} collective-permute-done((bf16[1,8,64,1024]{3,2,1,0:T(8,128)(2,1)S(1)}, bf16[1,8,64,1024]{3,2,1,0:T(8,128)(2,1)}, u32[]{:S(2)}, u32[]{:S(2)}) %collective-permute-start.20) | collective-permute-done | bytes 1048608 | tf_op jit(solution)/shard_map/ppermute | solution.py:332
  363.4 3.9 convolution_convert_fusion.12
  377.1 12.0 %cross_attention.3 = f32[768,272]{1,0:T(8,128)} custom-call(s32[2]{0:T(128)} %get-tuple-element.222.big_ref, bf16[768,272]{1,0:T(8,128)(2,1)} %pad.22.query_ref, bf16[768,272]{1,0:T(8,128)(2,1)} %fusion.64.grad_ref, bf16[16,2,272,128]{3,2,1,0:T(8,128)(2,1)} %copy-done.1, bf16[16,2,272,128]{3,2,1,0:T(8,128)(2,1)} %bitcast.214, ...), custom_call_target="tpu_custom_call" | custom-call | tf_op jit(solution)/shard_map/cross_attention/pallas_call | solution.py:174
  395.1 4.3 all-to-all-start.3
  410.6 4.5 convolution_convert_fusion.1
  415.1 31.8 %all-to-all-done.3 = bf16[8,128,1024]{2,1,0:T(8,128)(2,1)} async-done(((bf16[8,128,1024]{2,1,0:T(8,128)(2,1)}), bf16[8,128,1024]{2,1,0:T(8,128)(2,1)}, u32[]{:S(2)}, u32[]{:S(2)}) %all-to-all-start.3) | async-done | bytes 2097184 | tf_op jit(solution)/shard_map/all_to_all | solution.py:495
  461.9 5.0 fusion.10
  477.6 16.5 %collective-permute-done.24 = bf16[1,8,96,1024]{3,2,1,0:T(8,128)(2,1)} collective-permute-done((bf16[1,8,96,1024]{3,2,1,0:T(8,128)(2,1)}, bf16[1,8,96,1024]{3,2,1,0:T(8,128)(2,1)}, u32[]{:S(2)}, u32[]{:S(2)}) %collective-permute-start.24) | collective-permute-done | bytes 1572896 | tf_op jit(solution)/shard_map/ppermute | solution.py:332
  495.1 4.1 fusion.30
  499.2 4.6 all-to-all-start.4
  507.1 21.0 %collective-permute-done.26 = bf16[1,8,56,1024]{3,2,1,0:T(8,128)(2,1)S(1)} collective-permute-done((bf16[1,8,56,1024]{3,2,1,0:T(8,128)(2,1)S(1)}, bf16[1,8,56,1024]{3,2,1,0:T(8,128)(2,1)S(1)}, u32[]{:S(2)}, u32[]{:S(2)}) %collective-permute-start.26) | collective-permute-done | bytes 917536 | tf_op jit(solution)/shard_map/ppermute | solution.py:332
  530.8 14.5 %all-to-all-done.4 = bf16[8,96,1024]{2,1,0:T(8,128)(2,1)S(1)} async-done(((bf16[8,96,1024]{2,1,0:T(8,128)(2,1)}), bf16[8,96,1024]{2,1,0:T(8,128)(2,1)S(1)}, u32[]{:S(2)}, u32[]{:S(2)}) %all-to-all-start.4) | async-done | bytes 1572896 | tf_op jit(solution)/shard_map/all_to_all | solution.py:495
  546.4 4.2 all-to-all-start.5
  552.8 21.3 %all-to-all-done.5 = bf16[8,56,1024]{2,1,0:T(8,128)(2,1)} async-done(((bf16[8,56,1024]{2,1,0:T(8,128)(2,1)}), bf16[8,56,1024]{2,1,0:T(8,128)(2,1)}, u32[]{:S(2)}, u32[]{:S(2)}) %all-to-all-start.5) | async-done | bytes 917536 | tf_op jit(solution)/shard_map/all_to_all | solution.py:495
  583.1 9.1 %collective-permute-done.27 = bf16[256,1024]{1,0:T(8,128)(2,1)S(1)} collective-permute-done((bf16[256,1024]{1,0:T(8,128)(2,1)S(1)}, bf16[256,1024]{1,0:T(8,128)(2,1)S(1)}, u32[]{:S(2)}, u32[]{:S(2)}) %collective-permute-start.27) | collective-permute-done | bytes 524320 | tf_op jit(solution)/shard_map/ppermute | solution.py:332
  593.0 9.4 %collective-permute-done.29 = bf16[256,1024]{1,0:T(8,128)(2,1)S(1)} collective-permute-done((bf16[256,1024]{1,0:T(8,128)(2,1)S(1)}, bf16[256,1024]{1,0:T(8,128)(2,1)S(1)}, u32[]{:S(2)}, u32[]{:S(2)}) %collective-permute-start.29) | collective-permute-done | bytes 524320 | tf_op jit(solution)/shard_map/ppermute | solution.py:332
  606.5 5.8 widen.1
  617.5 12.6 %all-gather.9.cloned.1.call-done = bf16[2432,1024]{1,0:T(8,128)(2,1)} async-done(((bf16[152,1024]{1,0:T(8,128)(2,1)}), bf16[2432,1024]{1,0:T(8,128)(2,1)}) %all-gather.9.cloned.1.call-update) | async-done | bytes 4980752 | tf_op jit(solution)/shard_map/all_gather | solution.py:503
  (557 shorter events, 285.6 us)
Async XLA Ops:
  17.5 53.1 %all-to-all-start = ((bf16[16,2,272,128]{3,2,1,0:T(8,128)(2,1)}), bf16[16,2,272,128]{3,2,1,0:T(8,128)(2,1)S(1)}, u32[]{:S(2)}, u32[]{:S(2)}) async-start(bf16[16,2,272,128]{3,2,1,0:T(8,128)(2,1)} %prepare_pixels.1), calls=%async_computation | async-start | bytes 4456448 | tf_op jit(solution)/shard_map/all_to_all | solution.py:530
  25.1 132.4 %all-gather.7.cloned.1.call-start = ((), (), s32[]{:S(2)}) async-start(), calls=%async_computation.6 | async-start | bytes 2367488 | tf_op jit(solution)/shard_map/all_gather | solution.py:566
  26.0 17.8 %collective-permute-start.3 = (bf16[256,1024]{1,0:T(8,128)(2,1)}, bf16[256,1024]{1,0:T(8,128)(2,1)}, u32[]{:S(2)}, u32[]{:S(2)}) collective-permute-start(bf16[256,1024]{1,0:T(8,128)(2,1)} %constant_dynamic-slice_fusion.7), channel_id=1, source_target_pairs={{0,1},{1,0},{2,3},{3,2},{4,5},{5,4},{6,7},{7,6},{8,9},{9,8},{10,11... | collective-permute-start | bytes 1572872 | tf_op jit(solution)/shard_map/ppermute | solution.py:332
  29.4 39.9 %collective-permute-start.2 = (bf16[265,1024]{1,0:T(8,128)(2,1)}, bf16[265,1024]{1,0:T(8,128)(2,1)}, u32[]{:S(2)}, u32[]{:S(2)}) collective-permute-start(bf16[265,1024]{1,0:T(8,128)(2,1)} %pad_maximum_fusion.41), channel_id=1, source_target_pairs={{0,1},{1,0},{2,3},{3,2},{4,5},{5,4},{6,7},{7,6},{8,9},{9,8},{10,11... | collective-permute-start | bytes 1628168 | tf_op jit(solution)/shard_map/ppermute | solution.py:332
  32.4 11.4 %collective-permute-start.1 = (bf16[256,1024]{1,0:T(8,128)(2,1)}, bf16[256,1024]{1,0:T(8,128)(2,1)S(1)}, u32[]{:S(2)}, u32[]{:S(2)}) collective-permute-start(bf16[256,1024]{1,0:T(8,128)(2,1)} %get-tuple-element.300), channel_id=1, source_target_pairs={{0,0},{2,1},{4,4},{6,5},{8,8},{10,9},{12,12},{14,13},{16,16},{18,1... | collective-permute-start | bytes 1572872 | tf_op jit(solution)/shard_map/ppermute | solution.py:375
  34.2 35.1 %collective-permute-start = (bf16[256,1024]{1,0:T(8,128)(2,1)}, bf16[256,1024]{1,0:T(8,128)(2,1)}, u32[]{:S(2)}, u32[]{:S(2)}) collective-permute-start(bf16[256,1024]{1,0:T(8,128)(2,1)} %get-tuple-element.301), channel_id=1, source_target_pairs={{0,1},{1,0},{2,3},{3,2},{4,5},{5,4},{6,7},{7,6},{8,9},{9,8},{10,11... | collective-permute-start | bytes 1572872 | tf_op jit(solution)/shard_map/ppermute | solution.py:332
  70.6 41.9 %collective-permute-start.5 = (bf16[256,3072]{1,0:T(8,128)(2,1)}, bf16[256,3072]{1,0:T(8,128)(2,1)}, u32[]{:S(2)}, u32[]{:S(2)}) collective-permute-start(bf16[256,3072]{1,0:T(8,128)(2,1)} %pad_maximum_fusion.19), channel_id=1, source_target_pairs={{0,1},{1,0},{2,3},{3,2},{4,5},{5,4},{6,7},{7,6},{8,9},{9,8},{10,11... | collective-permute-start | bytes 4718600 | tf_op jit(solution)/shard_map/ppermute | solution.py:332
  83.2 19.1 %collective-permute-start.4 = (bf16[256,1024]{1,0:T(8,128)(2,1)}, bf16[256,1024]{1,0:T(8,128)(2,1)}, u32[]{:S(2)}, u32[]{:S(2)}) collective-permute-start(bf16[256,1024]{1,0:T(8,128)(2,1)} %collective-permute-done.3), channel_id=1, source_target_pairs={{0,2},{2,0},{4,6},{6,4},{8,10},{10,8},{12,14},{14,12},{16,18},{18,... | collective-permute-start | bytes 1572872 | tf_op jit(solution)/shard_map/ppermute | solution.py:332
  89.3 64.6 %all-to-all-start.1 = ((bf16[16,2,272,128]{3,2,1,0:T(8,128)(2,1)}), bf16[16,2,272,128]{3,2,1,0:T(8,128)(2,1)S(1)}, u32[]{:S(2)}, u32[]{:S(2)}) async-start(bf16[16,2,272,128]{3,2,1,0:T(8,128)(2,1)} %bitcast.215), calls=%async_computation.1 | async-start | bytes 4456448 | tf_op jit(solution)/shard_map/all_to_all | solution.py:562
  100.7 24.4 %collective-permute-start.7 = (bf16[128,3072]{1,0:T(8,128)(2,1)S(1)}, bf16[128,3072]{1,0:T(8,128)(2,1)}, u32[]{:S(2)}, u32[]{:S(2)}) collective-permute-start(bf16[128,3072]{1,0:T(8,128)(2,1)S(1)} %constant_dynamic-slice_fusion.3), channel_id=1, source_target_pairs={{0,1},{1,0},{2,3},{3,2},{4,5},{5,4},{6,7},{7,6},{8,9},{9,8},{10,11... | collective-permute-start | bytes 2359304 | tf_op jit(solution)/shard_map/ppermute | solution.py:332
  113.7 55.6 %collective-permute-start.11 = (bf16[128,3072]{1,0:T(8,128)(2,1)}, bf16[128,3072]{1,0:T(8,128)(2,1)}, u32[]{:S(2)}, u32[]{:S(2)}) collective-permute-start(bf16[128,3072]{1,0:T(8,128)(2,1)} %pad_maximum_fusion.40), channel_id=1, source_target_pairs={{0,1},{1,0},{2,3},{3,2},{4,5},{5,4},{6,7},{7,6},{8,9},{9,8},{10,11... | collective-permute-start | bytes 2359304 | tf_op jit(solution)/shard_map/ppermute | solution.py:332
  153.9 37.1 %collective-permute-start.8 = (bf16[128,3072]{1,0:T(8,128)(2,1)}, bf16[128,3072]{1,0:T(8,128)(2,1)}, u32[]{:S(2)}, u32[]{:S(2)}) collective-permute-start(bf16[128,3072]{1,0:T(8,128)(2,1)} %collective-permute-done.7), channel_id=1, source_target_pairs={{0,4},{2,6},{4,0},{6,2},{8,12},{10,14},{12,8},{14,10},{16,20},{18,... | collective-permute-start | bytes 2359304 | tf_op jit(solution)/shard_map/ppermute | solution.py:332
  169.4 24.5 %collective-permute-start.12 = (bf16[128,3072]{1,0:T(8,128)(2,1)}, bf16[128,3072]{1,0:T(8,128)(2,1)S(1)}, u32[]{:S(2)}, u32[]{:S(2)}) collective-permute-start(bf16[128,3072]{1,0:T(8,128)(2,1)} %collective-permute-done.11), channel_id=1, source_target_pairs={{0,4},{2,6},{4,0},{6,2},{8,12},{10,14},{12,8},{14,10},{16,20},{18,... | collective-permute-start | bytes 2359304 | tf_op jit(solution)/shard_map/ppermute | solution.py:332
  170.6 54.7 %collective-permute-start.15 = (bf16[256,1024]{1,0:T(8,128)(2,1)}, bf16[256,1024]{1,0:T(8,128)(2,1)}, u32[]{:S(2)}, u32[]{:S(2)}) collective-permute-start(bf16[256,1024]{1,0:T(8,128)(2,1)} %get-tuple-element.293), channel_id=1, source_target_pairs={{0,0},{2,1},{4,4},{6,5},{8,8},{10,9},{12,12},{14,13},{16,16},{18,1... | collective-permute-start | bytes 1572872 | tf_op jit(solution)/shard_map/ppermute | solution.py:375
  176.5 48.8 %collective-permute-start.14 = (bf16[256,1024]{1,0:T(8,128)(2,1)}, bf16[256,1024]{1,0:T(8,128)(2,1)}, u32[]{:S(2)}, u32[]{:S(2)}) collective-permute-start(bf16[256,1024]{1,0:T(8,128)(2,1)} %get-tuple-element.294), channel_id=1, source_target_pairs={{0,1},{1,0},{2,3},{3,2},{4,5},{5,4},{6,7},{7,6},{8,9},{9,8},{10,11... | collective-permute-start | bytes 1572872 | tf_op jit(solution)/shard_map/ppermute | solution.py:332
  253.4 30.9 %collective-permute-start.17 = (bf16[1,8,64,1024]{3,2,1,0:T(8,128)(2,1)}, bf16[1,8,64,1024]{3,2,1,0:T(8,128)(2,1)}, u32[]{:S(2)}, u32[]{:S(2)}) collective-permute-start(bf16[1,8,64,1024]{3,2,1,0:T(8,128)(2,1)} %add_convert_fusion.16), channel_id=1, source_target_pairs={{0,1},{1,0},{2,3},{3,2},{4,5},{5,4},{6,7},{7,6},{8,9},{9,8},{10,11... | collective-permute-start | bytes 3145736 | tf_op jit(solution)/shard_map/ppermute | solution.py:332
  284.3 18.5 %collective-permute-start.18 = (bf16[256,2048]{1,0:T(8,128)(2,1)}, bf16[256,2048]{1,0:T(8,128)(2,1)}, u32[]{:S(2)}, u32[]{:S(2)}) collective-permute-start(bf16[256,2048]{1,0:T(8,128)(2,1)} %get-tuple-element.74), channel_id=1, source_target_pairs={{0,2},{2,0},{4,6},{6,4},{8,10},{10,8},{12,14},{14,12},{16,18},{18,... | collective-permute-start | bytes 3145736 | tf_op jit(solution)/shard_map/ppermute | solution.py:332
  292.5 70.9 %all-to-all-start.2 = ((bf16[8,64,1024]{2,1,0:T(8,128)(2,1)}), bf16[8,64,1024]{2,1,0:T(8,128)(2,1)}, u32[]{:S(2)}, u32[]{:S(2)}) async-start(bf16[8,64,1024]{2,1,0:T(8,128)(2,1)} %fusion.46), calls=%async_computation.2 | async-start | bytes 2097152 | tf_op jit(solution)/shard_map/all_to_all | solution.py:495
  315.3 20.0 %collective-permute-start.19 = (bf16[2,8,64,1024]{3,2,1,0:T(8,128)(2,1)}, bf16[2,8,64,1024]{3,2,1,0:T(8,128)(2,1)}, u32[]{:S(2)}, u32[]{:S(2)}) collective-permute-start(bf16[2,8,64,1024]{3,2,1,0:T(8,128)(2,1)} %pad_maximum_fusion.14), channel_id=1, source_target_pairs={{0,2},{2,0},{4,6},{6,4},{8,10},{10,8},{12,14},{14,12},{16,18},{18,... | collective-permute-start | bytes 6291464 | tf_op jit(solution)/shard_map/ppermute | solution.py:332
  317.3 31.4 %collective-permute-start.21 = (bf16[2,8,64,1024]{3,2,1,0:T(8,128)(2,1)}, bf16[2,8,64,1024]{3,2,1,0:T(8,128)(2,1)}, u32[]{:S(2)}, u32[]{:S(2)}) collective-permute-start(bf16[2,8,64,1024]{3,2,1,0:T(8,128)(2,1)} %pad_maximum_fusion.15), channel_id=1, source_target_pairs={{0,2},{2,0},{4,6},{6,4},{8,10},{10,8},{12,14},{14,12},{16,18},{18,... | collective-permute-start | bytes 6291464 | tf_op jit(solution)/shard_map/ppermute | solution.py:332
  337.2 26.2 %collective-permute-start.20 = (bf16[1,8,64,1024]{3,2,1,0:T(8,128)(2,1)S(1)}, bf16[1,8,64,1024]{3,2,1,0:T(8,128)(2,1)}, u32[]{:S(2)}, u32[]{:S(2)}) collective-permute-start(bf16[1,8,64,1024]{3,2,1,0:T(8,128)(2,1)S(1)} %add_convert_fusion.14), channel_id=1, source_target_pairs={{0,1},{1,0},{2,3},{3,2},{4,5},{5,4},{6,7},{7,6},{8,9},{9,8},{10,11... | collective-permute-start | bytes 3145736 | tf_op jit(solution)/shard_map/ppermute | solution.py:332
  351.3 37.7 %collective-permute-start.22 = (bf16[1,8,64,1024]{3,2,1,0:T(8,128)(2,1)}, bf16[1,8,64,1024]{3,2,1,0:T(8,128)(2,1)}, u32[]{:S(2)}, u32[]{:S(2)}) collective-permute-start(bf16[1,8,64,1024]{3,2,1,0:T(8,128)(2,1)} %add_convert_fusion.13), channel_id=1, source_target_pairs={{0,1},{1,0},{2,3},{3,2},{4,5},{5,4},{6,7},{7,6},{8,9},{9,8},{10,11... | collective-permute-start | bytes 3145736 | tf_op jit(solution)/shard_map/ppermute | solution.py:332
  376.1 27.4 %collective-permute-start.23 = (bf16[2,8,96,1024]{3,2,1,0:T(8,128)(2,1)}, bf16[2,8,96,1024]{3,2,1,0:T(8,128)(2,1)}, u32[]{:S(2)}, u32[]{:S(2)}) collective-permute-start(bf16[2,8,96,1024]{3,2,1,0:T(8,128)(2,1)} %pad_maximum_fusion.4), channel_id=1, source_target_pairs={{0,2},{2,0},{4,6},{6,4},{8,10},{10,8},{12,14},{14,12},{16,18},{18,... | collective-permute-start | bytes 9437192 | tf_op jit(solution)/shard_map/ppermute | solution.py:332
  395.1 51.8 %all-to-all-start.3 = ((bf16[8,128,1024]{2,1,0:T(8,128)(2,1)}), bf16[8,128,1024]{2,1,0:T(8,128)(2,1)}, u32[]{:S(2)}, u32[]{:S(2)}) async-start(bf16[8,128,1024]{2,1,0:T(8,128)(2,1)} %pad_maximum_fusion.16), calls=%async_computation.3 | async-start | bytes 4194304 | tf_op jit(solution)/shard_map/all_to_all | solution.py:495
  399.5 207.0 %all-gather.11.cloned.1.call-start = ((), (), s32[]{:S(2)}) async-start(), calls=%async_computation.8 | async-start | bytes 6684672 | tf_op jit(solution)/shard_map/all_gather | solution.py:503
  457.3 36.8 %collective-permute-start.24 = (bf16[1,8,96,1024]{3,2,1,0:T(8,128)(2,1)}, bf16[1,8,96,1024]{3,2,1,0:T(8,128)(2,1)}, u32[]{:S(2)}, u32[]{:S(2)}) collective-permute-start(bf16[1,8,96,1024]{3,2,1,0:T(8,128)(2,1)} %add_convert_fusion.2), channel_id=1, source_target_pairs={{0,1},{1,0},{2,3},{3,2},{4,5},{5,4},{6,7},{7,6},{8,9},{9,8},{10,11... | collective-permute-start | bytes 4718600 | tf_op jit(solution)/shard_map/ppermute | solution.py:332
  499.2 46.1 %all-to-all-start.4 = ((bf16[8,96,1024]{2,1,0:T(8,128)(2,1)}), bf16[8,96,1024]{2,1,0:T(8,128)(2,1)S(1)}, u32[]{:S(2)}, u32[]{:S(2)}) async-start(bf16[8,96,1024]{2,1,0:T(8,128)(2,1)} %fusion.30), calls=%async_computation.4 | async-start | bytes 3145728 | tf_op jit(solution)/shard_map/all_to_all | solution.py:495
  505.4 22.8 %collective-permute-start.26 = (bf16[1,8,56,1024]{3,2,1,0:T(8,128)(2,1)S(1)}, bf16[1,8,56,1024]{3,2,1,0:T(8,128)(2,1)S(1)}, u32[]{:S(2)}, u32[]{:S(2)}) collective-permute-start(bf16[1,8,56,1024]{3,2,1,0:T(8,128)(2,1)S(1)} %add_convert_fusion.19), channel_id=1, source_target_pairs={{0,1},{1,0},{2,3},{3,2},{4,5},{5,4},{6,7},{7,6},{8,9},{9,8},{10,11... | collective-permute-start | bytes 2752520 | tf_op jit(solution)/shard_map/ppermute | solution.py:332
  546.4 27.7 %all-to-all-start.5 = ((bf16[8,56,1024]{2,1,0:T(8,128)(2,1)}), bf16[8,56,1024]{2,1,0:T(8,128)(2,1)}, u32[]{:S(2)}, u32[]{:S(2)}) async-start(bf16[8,56,1024]{2,1,0:T(8,128)(2,1)} %fusion.59), calls=%async_computation.5 | async-start | bytes 1835008 | tf_op jit(solution)/shard_map/all_to_all | solution.py:495
  550.7 79.4 %all-gather.9.cloned.1.call-start = ((), (), s32[]{:S(2)}) async-start(), calls=%async_computation.7 | async-start | bytes 5292032 | tf_op jit(solution)/shard_map/all_gather | solution.py:503
  577.3 14.9 %collective-permute-start.27 = (bf16[256,1024]{1,0:T(8,128)(2,1)S(1)}, bf16[256,1024]{1,0:T(8,128)(2,1)S(1)}, u32[]{:S(2)}, u32[]{:S(2)}) collective-permute-start(bf16[256,1024]{1,0:T(8,128)(2,1)S(1)} %slice.215), channel_id=1, source_target_pairs={{0,1},{1,0},{2,3},{3,2},{4,5},{5,4},{6,7},{7,6},{8,9},{9,8},{10,11... | collective-permute-start | bytes 1572872 | tf_op jit(solution)/shard_map/ppermute | solution.py:332
  582.5 20.0 %collective-permute-start.29 = (bf16[256,1024]{1,0:T(8,128)(2,1)S(1)}, bf16[256,1024]{1,0:T(8,128)(2,1)S(1)}, u32[]{:S(2)}, u32[]{:S(2)}) collective-permute-start(bf16[256,1024]{1,0:T(8,128)(2,1)S(1)} %slice.218), channel_id=1, source_target_pairs={{0,1},{1,0},{2,3},{3,2},{4,5},{5,4},{6,7},{7,6},{8,9},{9,8},{10,11... | collective-permute-start | bytes 1572872 | tf_op jit(solution)/shard_map/ppermute | solution.py:332
  (146 other events, 1293.4 us)
Sparse Core Ops, SparseCore 0:
  83.3 70.3 all-gather.6
  449.9 65.3 all-gather.10
  576.3 53.7 all-gather.8

commit v6 on v5

--- a/solution.py
+++ b/solution.py
@@ -78,7 +78,7 @@
     return pltpu.CompilerParams(dimension_semantics=semantics, vmem_limit_bytes=VMEM_LIMIT)
 
 
-def pixel_kernel(micro_ref, pixel_ref, count_ref, out_ref):
+def pixel_kernel(micro_ref, pixel_ref, out_ref):
     features = pixel_ref.shape[1]
     width = out_ref.shape[3]
     pixels = pixel_ref[0].astype(jnp.float32)
@@ -88,15 +88,12 @@
     pad = jnp.zeros((FEATURE_ROWS - features, normed.shape[1]), jnp.float32)
     tall = jnp.concatenate([normed, pad], axis=0)
     row = lax.broadcasted_iota(jnp.int32, (FEATURE_ROWS, width), 0)
-    high, rest = count_ref[0][:1, :width], count_ref[0][1:2, :width]
     for part in range(out_ref.shape[0]):
         piece = tall[:, part * width : (part + 1) * width]
-        piece = jnp.where(row == features, 1.0, piece)
-        piece = jnp.where(row == features + 1, high, jnp.where(row == features + 2, rest, piece))
-        out_ref[part, 0] = piece.astype(low_type)
-
-
-def prepare_pixels(pixels, micro, counts, width):
+        out_ref[part, 0] = jnp.where(row == features, 1.0, piece).astype(low_type)
+
+
+def prepare_pixels(pixels, micro, width):
     routed = micro.shape[0]
     features, slots = pixels.shape[1:]
     step = min(slots, 1024)
@@ -106,15 +103,12 @@
         grid_spec=pltpu.PrefetchScalarGridSpec(
             num_scalar_prefetch=1,
             grid=(routed, slots // step),
-            in_specs=[
-                pl.BlockSpec((1, features, step), lambda i, s, m: (m[i], 0, s)),
-                pl.BlockSpec((1, 8, 128), lambda i, s, m: (i, 0, 0)),
-            ],
+            in_specs=[pl.BlockSpec((1, features, step), lambda i, s, m: (m[i], 0, s))],
             out_specs=pl.BlockSpec((step // width, 1, FEATURE_ROWS, width), lambda i, s, m: (s, i, 0, 0)),
         ),
         compiler_params=params("arbitrary", "arbitrary"),
         name="prepare_pixels",
-    )(micro, pixels, counts)
+    )(micro, pixels)
 
 
 def side_by_side(ref):
@@ -523,13 +517,10 @@
         return jnp.stack([lax.dynamic_index_in_dim(array, plan.micro[i], 0, False) for i in range(routed)])
 
     picked = of_items(segment_ids)
-    counts = jnp.sum((picked[:, None, :] == label_ids[None, :, None]).astype(jnp.int32), axis=2)
-    counts = jnp.stack([counts >> 4, counts & 15], axis=1).astype(jnp.float32)
-    counts = jnp.pad(counts, ((0, 0), (0, 6), (0, 128 - labels)))
-    chunks = prepare_pixels(jnp.swapaxes(pixels, 1, 2), plan.micro, counts, width)
+    counts = jnp.sum((picked[:, None, :] == label_ids[None, :, None]).astype(jnp.float32), axis=2)
+    chunks = prepare_pixels(jnp.swapaxes(pixels, 1, 2), plan.micro, width)
     spread = lax.all_to_all(chunks, "blk", split_axis=0, concat_axis=0, tiled=True)
-    arrived = spread[:, :, features + 1 : features + 3, :labels].astype(jnp.int32)
-    totals = jnp.sum(16 * arrived[:, :, 0] + arrived[:, :, 1], axis=0)
+    totals = jnp.sum(lax.all_gather(counts, "blk", axis=0), axis=0).astype(jnp.int32)
     owners = of_items(block_map)
     images = label_ids[None, :] != of_items(pad_ids)[:, None]
     totals = jnp.where(images, totals, 0)
@@ -766,9 +757,9 @@
     tall = jnp.pad(rows_of_pair, ((0, 0), (0, 384 - features), (0, 0)))
     tall = lax.dynamic_update_slice(tall, small.astype(low_type), (0, 264, 0))
     grad_query = unit(grad_query)
-    sums_two, arrived_two = over_chips([two, three], grad_query)
     five = Group(plan, [grad_query, tall.reshape(shards, -1, model)])
-    five.send = after(five.send, four.over_fsdp(grad_query), arrived_two)
+    five.send = after(five.send, four.over_fsdp(grad_query))
+    sums_two, arrived_two = over_chips([two, three], five.send)
     early_sums = from_all([sums_one, sums_two])
     sums_four, unused = over_chips([four])
     five.over_core()

time: 660 us -> 656 us (level)
  blocking collectives: 0 us -> 41.2 us
  waiting for transfers between devices: 204 us -> 177 us
  local copies, waits for them, and re-layouts: 66 us -> 56.4 us
    all_gather x0 -> x1, blocking collectives: none -> 41.2 us  [route_pixels(): lax.all_gather(counts, 'blk', axis=0)]
    ppermute x27, waiting for transfers between devices: 95 us -> 81.1 us  [swap(): return lax.ppermute(array, axis_name, [(i, i ^ mask) for i in range(size)])]
    all_to_all x1, waiting for transfers between devices: 28.8 us -> 19.3 us  [route_pixels(): lax.all_to_all(pieces, 'blk', split_axis=0, concat_axis=0, tiled=True)]
    unnamed x285 -> x275, local copies, waits for them, and re-layouts: 14.6 us -> 13.3 us
  transfers between devices with their start and end apart: 40 -> 40, of which waited for: 13 -> 13; matrix products, arithmetic and copies ran while one was open for 37% -> 34% of each run, Pallas kernels for 9% -> 8%
where the time goes in v6:
time: 656 us; the launch traced here: 649 us
  waiting for transfers between devices  177 us (27%)
  other arithmetic  117 us (18%)
  matrix products  107 us (16%)
  starting transfers between devices  74.5 us (11%)
  Pallas kernels  59.7 us (9%)
  local copies, waits for them, and re-layouts  56.4 us (9%)
  blocking collectives  41.2 us (6%)
  between operations  16.1 us (2%)
    ppermute x27, waiting for transfers between devices, swap(): return lax.ppermute(array, axis_name, [(i, i ^ mask) for i in range(size)])  81.1 us
    all_to_all x4, waiting for transfers between devices, over_chips(): lax.all_to_all(total, 'blk', split_axis=0, concat_axis=0, axis_index_grou...  63.7 us
    dot_general x10, matrix products, product_nt(): lax.dot_general(a, b, (((1,), (1,)), ((), ())), preferred_element_type=jn...  45.2 us
    all_gather x1, blocking collectives, route_pixels(): lax.all_gather(counts, 'blk', axis=0)  41.2 us
    dot_general x12, matrix products, product_tn(): lax.dot_general(a, b, (((0,), (0,)), ((), ())), preferred_element_type=jn...  31.3 us
    dot_general x10, matrix products, product(): return jnp.dot(a, b, preferred_element_type=jnp.float32)  30.3 us
    all_to_all x4, starting transfers between devices, over_chips(): lax.all_to_all(total, 'blk', split_axis=0, concat_axis=0, axis_index_grou...  25.5 us
    pallas_call x1, Pallas kernels, self_backward(): pl.pallas_call(functools.partial(self_backward_kernel, groups, head ** (-...  19.8 us
  transfers between devices with their start and end apart: 40, of which 13 were waited for; matrix products, arithmetic and copies ran while one was open for 34% of the time, Pallas kernels for 8%

profile of v6, /device:TPU:0, one launch (start us, length us, event | category | flops | bytes accessed | tf_op | source)
XLA Modules:
  0.0 648.5 jit_solution(7732601549004734039)
XLA Ops:
  10.4 5.1 prepare_pixels.1
  15.5 7.5 %all-to-all-start = ((bf16[16,2,272,128]{3,2,1,0:T(8,128)(2,1)}), bf16[16,2,272,128]{3,2,1,0:T(8,128)(2,1)S(1)}, u32[]{:S(2)}, u32[]{:S(2)}) async-start(bf16[16,2,272,128]{3,2,1,0:T(8,128)(2,1)} %prepare_pixels.1), calls=%async_computation | async-start | bytes 4456448 | tf_op jit(solution)/shard_map/all_to_all | solution.py:522
  34.3 41.2 %all-gather.4 = f32[16,2,17]{2,1,0:T(2,128)S(1)} all-gather(f32[1,2,17]{2,1,0:T(2,128)S(1)} %bitcast.252), channel_id=2, replica_groups=mesh['blk'=16,'fsdp'=2] {'blk'}, dimensions={0}, use_global_device_ids=true | all-gather | bytes 2312 | tf_op jit(solution)/shard_map/all_gather | solution.py:523
  97.5 12.5 %all-to-all-start.1 = ((bf16[16,2,272,128]{3,2,1,0:T(8,128)(2,1)}), bf16[16,2,272,128]{3,2,1,0:T(8,128)(2,1)S(1)}, u32[]{:S(2)}, u32[]{:S(2)}) async-start(bf16[16,2,272,128]{3,2,1,0:T(8,128)(2,1)} %bitcast.209), calls=%async_computation.1 | async-start | bytes 4456448 | tf_op jit(solution)/shard_map/all_to_all | solution.py:553
  134.7 10.7 %collective-permute-done.7 = bf16[128,3072]{1,0:T(8,128)(2,1)} collective-permute-done((bf16[128,3072]{1,0:T(8,128)(2,1)S(1)}, bf16[128,3072]{1,0:T(8,128)(2,1)}, u32[]{:S(2)}, u32[]{:S(2)}) %collective-permute-start.7) | collective-permute-done | bytes 786464 | tf_op jit(solution)/shard_map/ppermute | solution.py:326
  145.3 19.3 %all-to-all-done.1.first_ref = bf16[16,2,272,128]{3,2,1,0:T(8,128)(2,1)S(1)} async-done(((bf16[16,2,272,128]{3,2,1,0:T(8,128)(2,1)}), bf16[16,2,272,128]{3,2,1,0:T(8,128)(2,1)S(1)}, u32[]{:S(2)}, u32[]{:S(2)}) %all-to-all-start.1) | async-done | bytes 2228256 | tf_op jit(solution)/shard_map/all_to_all | solution.py:553
  169.2 8.3 %cross_attention.2 = f32[768,272]{1,0:T(8,128)} custom-call(s32[2]{0:T(128)} %get-tuple-element.220.big_ref, bf16[768,272]{1,0:T(8,128)(2,1)} %pad.17.query_ref, bf16[16,2,272,128]{3,2,1,0:T(8,128)(2,1)} %copy-done.1, bf16[16,2,272,128]{3,2,1,0:T(8,128)(2,1)} %bitcast.207, f32[2,8,4096]{2,1,0:T(8,128)} %broadcast_in_dim.80.mask_ref), custom_call_target="tpu_custom_call" | custom-call | tf_op jit(solution)/shard_map/cross_attention/pallas_call | solution.py:168
  180.9 5.9 collective-permute-start.15
  209.6 5.3 convolution_convert_fusion.q_ref.k_ref.v_ref
  221.4 10.8 %self_forward.1 = bf16[768,1024]{1,0:T(8,128)(2,1)} custom-call(bf16[768,3072]{1,0:T(8,128)(2,1)} %copy-done, bf16[768,3072]{1,0:T(8,128)(2,1)} %copy-done, bf16[768,3072]{1,0:T(8,128)(2,1)} %copy-done, bf16[256,2048]{1,0:T(8,128)(2,1)} %collective-permute-done.10.more_k_ref.more_v_ref, bf16[256,2048]{1,0:T(8,128)(2,1)} %collective-permute-done.10.more_k_ref.more_v_ref), custom_call_target="tpu_custom_call" | custom-call | tf_op jit(solution)/shard_map/self_forward/pallas_call | solution.py:260
  244.0 3.8 fusion.21
  254.4 5.7 multiply_reduce_fusion
  274.2 19.8 %self_backward.1 = (bf16[768,3072]{1,0:T(8,128)(2,1)}, bf16[256,2048]{1,0:T(8,128)(2,1)}) custom-call(bf16[768,3072]{1,0:T(8,128)(2,1)} %copy-done, bf16[768,3072]{1,0:T(8,128)(2,1)} %copy-done, bf16[768,3072]{1,0:T(8,128)(2,1)} %copy-done, bf16[256,2048]{1,0:T(8,128)(2,1)} %collective-permute-done.10.more_k_ref.more_v_ref, ...), custom_call_target="tpu_custom_call" | custom-call | tf_op jit(solution)/shard_map/self_backward/pallas_call | solution.py:275
  302.2 11.8 %all-to-all-start.2 = ((bf16[8,64,1024]{2,1,0:T(8,128)(2,1)}), bf16[8,64,1024]{2,1,0:T(8,128)(2,1)}, u32[]{:S(2)}, u32[]{:S(2)}) async-start(bf16[8,64,1024]{2,1,0:T(8,128)(2,1)} %fusion.46), calls=%async_computation.2 | async-start | bytes 2097152 | tf_op jit(solution)/shard_map/all_to_all | solution.py:489
  330.4 9.7 %multiply_reduce_fusion.1 = (bf16[1024]{0:T(1024)(128)(2,1)S(1)}, f32[768]{0:T(1024)S(1)}, f32[768]{0:T(1024)S(1)}, bf16[1024]{0:T(1024)(128)(2,1)S(1)}, f32[768,1024]{1,0:T(8,128)}) fusion(f32[768,1024]{1,0:T(8,128)S(1)} %get-tuple-element.330, f32[768]{0:T(1024)S(1)} %add_rsqrt_fusion.1, f32[768]{0:T(1024)S(1)} %broadcast_multiply_fusion.10, ...), kind=kOutput, calls=%fused_computation.54 | convolution fusion | flops 4851494912 | bytes 17321984 | tf_op jit(solution)/shard_map/dot_general | solution.py:28
  363.4 9.7 %collective-permute-done.20 = bf16[1,8,64,1024]{3,2,1,0:T(8,128)(2,1)} collective-permute-done((bf16[1,8,64,1024]{3,2,1,0:T(8,128)(2,1)S(1)}, bf16[1,8,64,1024]{3,2,1,0:T(8,128)(2,1)}, u32[]{:S(2)}, u32[]{:S(2)}) %collective-permute-start.20) | collective-permute-done | bytes 1048608 | tf_op jit(solution)/shard_map/ppermute | solution.py:326
  382.0 3.9 convolution_convert_fusion.12
  390.6 9.9 %cross_attention.3 = f32[768,272]{1,0:T(8,128)} custom-call(s32[2]{0:T(128)} %get-tuple-element.220.big_ref, bf16[768,272]{1,0:T(8,128)(2,1)} %pad.17.query_ref, bf16[768,272]{1,0:T(8,128)(2,1)} %fusion.64.grad_ref, bf16[16,2,272,128]{3,2,1,0:T(8,128)(2,1)} %copy-done.1, bf16[16,2,272,128]{3,2,1,0:T(8,128)(2,1)} %bitcast.208, ...), custom_call_target="tpu_custom_call" | custom-call | tf_op jit(solution)/shard_map/cross_attention/pallas_call | solution.py:168
  400.5 5.5 collective-permute-done.22
  411.6 5.8 all-to-all-start.5
  429.1 5.9 fusion.10
  449.1 12.0 %collective-permute-done.24 = bf16[1,8,96,1024]{3,2,1,0:T(8,128)(2,1)} collective-permute-done((bf16[1,8,96,1024]{3,2,1,0:T(8,128)(2,1)}, bf16[1,8,96,1024]{3,2,1,0:T(8,128)(2,1)}, u32[]{:S(2)}, u32[]{:S(2)}) %collective-permute-start.24) | collective-permute-done | bytes 1572896 | tf_op jit(solution)/shard_map/ppermute | solution.py:326
  461.1 4.4 all-to-all-done.5
  468.4 4.1 fusion.30
  478.2 22.3 %collective-permute-done.26 = bf16[1,8,56,1024]{3,2,1,0:T(8,128)(2,1)S(1)} collective-permute-done((bf16[1,8,56,1024]{3,2,1,0:T(8,128)(2,1)S(1)}, bf16[1,8,56,1024]{3,2,1,0:T(8,128)(2,1)S(1)}, u32[]{:S(2)}, u32[]{:S(2)}) %collective-permute-start.26) | collective-permute-done | bytes 917536 | tf_op jit(solution)/shard_map/ppermute | solution.py:326
  503.2 35.6 %all-to-all-done.3 = bf16[8,96,1024]{2,1,0:T(8,128)(2,1)S(1)} async-done(((bf16[8,96,1024]{2,1,0:T(8,128)(2,1)}), bf16[8,96,1024]{2,1,0:T(8,128)(2,1)S(1)}, u32[]{:S(2)}, u32[]{:S(2)}) %all-to-all-start.3) | async-done | bytes 1572896 | tf_op jit(solution)/shard_map/all_to_all | solution.py:489
  539.9 4.2 all-to-all-start.4
  546.3 23.7 %all-to-all-done.4 = bf16[8,56,1024]{2,1,0:T(8,128)(2,1)} async-done(((bf16[8,56,1024]{2,1,0:T(8,128)(2,1)}), bf16[8,56,1024]{2,1,0:T(8,128)(2,1)}, u32[]{:S(2)}, u32[]{:S(2)}) %all-to-all-start.4) | async-done | bytes 917536 | tf_op jit(solution)/shard_map/all_to_all | solution.py:489
  579.0 9.1 %collective-permute-done.27 = bf16[256,1024]{1,0:T(8,128)(2,1)S(1)} collective-permute-done((bf16[256,1024]{1,0:T(8,128)(2,1)S(1)}, bf16[256,1024]{1,0:T(8,128)(2,1)S(1)}, u32[]{:S(2)}, u32[]{:S(2)}) %collective-permute-start.27) | collective-permute-done | bytes 524320 | tf_op jit(solution)/shard_map/ppermute | solution.py:326
  588.9 9.5 %collective-permute-done.29 = bf16[256,1024]{1,0:T(8,128)(2,1)S(1)} collective-permute-done((bf16[256,1024]{1,0:T(8,128)(2,1)S(1)}, bf16[256,1024]{1,0:T(8,128)(2,1)S(1)}, u32[]{:S(2)}, u32[]{:S(2)}) %collective-permute-start.29) | collective-permute-done | bytes 524320 | tf_op jit(solution)/shard_map/ppermute | solution.py:326
  602.4 5.8 widen.1
  613.5 12.5 %all-gather.11.cloned.1.call-done = bf16[2432,1024]{1,0:T(8,128)(2,1)} async-done(((bf16[152,1024]{1,0:T(8,128)(2,1)}), bf16[2432,1024]{1,0:T(8,128)(2,1)}) %all-gather.11.cloned.1.call-update) | async-done | bytes 4980752 | tf_op jit(solution)/shard_map/all_gather | solution.py:497
  (545 shorter events, 271.3 us)
Async XLA Ops:
  15.5 71.9 %all-to-all-start = ((bf16[16,2,272,128]{3,2,1,0:T(8,128)(2,1)}), bf16[16,2,272,128]{3,2,1,0:T(8,128)(2,1)S(1)}, u32[]{:S(2)}, u32[]{:S(2)}) async-start(bf16[16,2,272,128]{3,2,1,0:T(8,128)(2,1)} %prepare_pixels.1), calls=%async_computation | async-start | bytes 4456448 | tf_op jit(solution)/shard_map/all_to_all | solution.py:522
  23.1 145.4 %all-gather.9.cloned.1.call-start = ((), (), s32[]{:S(2)}) async-start(), calls=%async_computation.6 | async-start | bytes 2367488 | tf_op jit(solution)/shard_map/all_gather | solution.py:557
  24.0 60.7 %collective-permute-start.3 = (bf16[256,1024]{1,0:T(8,128)(2,1)}, bf16[256,1024]{1,0:T(8,128)(2,1)}, u32[]{:S(2)}, u32[]{:S(2)}) collective-permute-start(bf16[256,1024]{1,0:T(8,128)(2,1)} %constant_dynamic-slice_fusion.7), channel_id=1, source_target_pairs={{0,1},{1,0},{2,3},{3,2},{4,5},{5,4},{6,7},{7,6},{8,9},{9,8},{10,11... | collective-permute-start | bytes 1572872 | tf_op jit(solution)/shard_map/ppermute | solution.py:326
  27.4 57.2 %collective-permute-start.2 = (bf16[265,1024]{1,0:T(8,128)(2,1)}, bf16[265,1024]{1,0:T(8,128)(2,1)}, u32[]{:S(2)}, u32[]{:S(2)}) collective-permute-start(bf16[265,1024]{1,0:T(8,128)(2,1)} %pad_maximum_fusion.41), channel_id=1, source_target_pairs={{0,1},{1,0},{2,3},{3,2},{4,5},{5,4},{6,7},{7,6},{8,9},{9,8},{10,11... | collective-permute-start | bytes 1628168 | tf_op jit(solution)/shard_map/ppermute | solution.py:326
  30.4 54.2 %collective-permute-start.1 = (bf16[256,1024]{1,0:T(8,128)(2,1)}, bf16[256,1024]{1,0:T(8,128)(2,1)S(1)}, u32[]{:S(2)}, u32[]{:S(2)}) collective-permute-start(bf16[256,1024]{1,0:T(8,128)(2,1)} %get-tuple-element.298), channel_id=1, source_target_pairs={{0,0},{2,1},{4,4},{6,5},{8,8},{10,9},{12,12},{14,13},{16,16},{18,1... | collective-permute-start | bytes 1572872 | tf_op jit(solution)/shard_map/ppermute | solution.py:369
  32.1 52.5 %collective-permute-start = (bf16[256,1024]{1,0:T(8,128)(2,1)}, bf16[256,1024]{1,0:T(8,128)(2,1)}, u32[]{:S(2)}, u32[]{:S(2)}) collective-permute-start(bf16[256,1024]{1,0:T(8,128)(2,1)} %get-tuple-element.299), channel_id=1, source_target_pairs={{0,1},{1,0},{2,3},{3,2},{4,5},{5,4},{6,7},{7,6},{8,9},{9,8},{10,11... | collective-permute-start | bytes 1572872 | tf_op jit(solution)/shard_map/ppermute | solution.py:326
  86.0 36.9 %collective-permute-start.5 = (bf16[256,3072]{1,0:T(8,128)(2,1)}, bf16[256,3072]{1,0:T(8,128)(2,1)}, u32[]{:S(2)}, u32[]{:S(2)}) collective-permute-start(bf16[256,3072]{1,0:T(8,128)(2,1)} %pad_maximum_fusion.19), channel_id=1, source_target_pairs={{0,1},{1,0},{2,3},{3,2},{4,5},{5,4},{6,7},{7,6},{8,9},{9,8},{10,11... | collective-permute-start | bytes 4718600 | tf_op jit(solution)/shard_map/ppermute | solution.py:326
  91.1 18.9 %collective-permute-start.4 = (bf16[256,1024]{1,0:T(8,128)(2,1)}, bf16[256,1024]{1,0:T(8,128)(2,1)}, u32[]{:S(2)}, u32[]{:S(2)}) collective-permute-start(bf16[256,1024]{1,0:T(8,128)(2,1)} %collective-permute-done.3), channel_id=1, source_target_pairs={{0,2},{2,0},{4,6},{6,4},{8,10},{10,8},{12,14},{14,12},{16,18},{18,... | collective-permute-start | bytes 1572872 | tf_op jit(solution)/shard_map/ppermute | solution.py:326
  97.5 67.1 %all-to-all-start.1 = ((bf16[16,2,272,128]{3,2,1,0:T(8,128)(2,1)}), bf16[16,2,272,128]{3,2,1,0:T(8,128)(2,1)S(1)}, u32[]{:S(2)}, u32[]{:S(2)}) async-start(bf16[16,2,272,128]{3,2,1,0:T(8,128)(2,1)} %bitcast.209), calls=%async_computation.1 | async-start | bytes 4456448 | tf_op jit(solution)/shard_map/all_to_all | solution.py:553
  124.8 20.5 %collective-permute-start.7 = (bf16[128,3072]{1,0:T(8,128)(2,1)S(1)}, bf16[128,3072]{1,0:T(8,128)(2,1)}, u32[]{:S(2)}, u32[]{:S(2)}) collective-permute-start(bf16[128,3072]{1,0:T(8,128)(2,1)S(1)} %constant_dynamic-slice_fusion.3), channel_id=1, source_target_pairs={{0,1},{1,0},{2,3},{3,2},{4,5},{5,4},{6,7},{7,6},{8,9},{9,8},{10,11... | collective-permute-start | bytes 2359304 | tf_op jit(solution)/shard_map/ppermute | solution.py:326
  128.3 50.7 %collective-permute-start.11 = (bf16[128,3072]{1,0:T(8,128)(2,1)}, bf16[128,3072]{1,0:T(8,128)(2,1)}, u32[]{:S(2)}, u32[]{:S(2)}) collective-permute-start(bf16[128,3072]{1,0:T(8,128)(2,1)} %pad_maximum_fusion.40), channel_id=1, source_target_pairs={{0,1},{1,0},{2,3},{3,2},{4,5},{5,4},{6,7},{7,6},{8,9},{9,8},{10,11... | collective-permute-start | bytes 2359304 | tf_op jit(solution)/shard_map/ppermute | solution.py:326
  164.7 36.6 %collective-permute-start.8 = (bf16[128,3072]{1,0:T(8,128)(2,1)}, bf16[128,3072]{1,0:T(8,128)(2,1)}, u32[]{:S(2)}, u32[]{:S(2)}) collective-permute-start(bf16[128,3072]{1,0:T(8,128)(2,1)} %collective-permute-done.7), channel_id=1, source_target_pairs={{0,4},{2,6},{4,0},{6,2},{8,12},{10,14},{12,8},{14,10},{16,20},{18,... | collective-permute-start | bytes 2359304 | tf_op jit(solution)/shard_map/ppermute | solution.py:326
  179.0 25.1 %collective-permute-start.12 = (bf16[128,3072]{1,0:T(8,128)(2,1)}, bf16[128,3072]{1,0:T(8,128)(2,1)S(1)}, u32[]{:S(2)}, u32[]{:S(2)}) collective-permute-start(bf16[128,3072]{1,0:T(8,128)(2,1)} %collective-permute-done.11), channel_id=1, source_target_pairs={{0,4},{2,6},{4,0},{6,2},{8,12},{10,14},{12,8},{14,10},{16,20},{18,... | collective-permute-start | bytes 2359304 | tf_op jit(solution)/shard_map/ppermute | solution.py:326
  180.9 54.7 %collective-permute-start.15 = (bf16[256,1024]{1,0:T(8,128)(2,1)}, bf16[256,1024]{1,0:T(8,128)(2,1)}, u32[]{:S(2)}, u32[]{:S(2)}) collective-permute-start(bf16[256,1024]{1,0:T(8,128)(2,1)} %get-tuple-element.291), channel_id=1, source_target_pairs={{0,0},{2,1},{4,4},{6,5},{8,8},{10,9},{12,12},{14,13},{16,16},{18,1... | collective-permute-start | bytes 1572872 | tf_op jit(solution)/shard_map/ppermute | solution.py:369
  186.8 48.8 %collective-permute-start.14 = (bf16[256,1024]{1,0:T(8,128)(2,1)}, bf16[256,1024]{1,0:T(8,128)(2,1)}, u32[]{:S(2)}, u32[]{:S(2)}) collective-permute-start(bf16[256,1024]{1,0:T(8,128)(2,1)} %get-tuple-element.292), channel_id=1, source_target_pairs={{0,1},{1,0},{2,3},{3,2},{4,5},{5,4},{6,7},{7,6},{8,9},{9,8},{10,11... | collective-permute-start | bytes 1572872 | tf_op jit(solution)/shard_map/ppermute | solution.py:326
  263.0 30.9 %collective-permute-start.17 = (bf16[1,8,64,1024]{3,2,1,0:T(8,128)(2,1)}, bf16[1,8,64,1024]{3,2,1,0:T(8,128)(2,1)}, u32[]{:S(2)}, u32[]{:S(2)}) collective-permute-start(bf16[1,8,64,1024]{3,2,1,0:T(8,128)(2,1)} %add_convert_fusion.16), channel_id=1, source_target_pairs={{0,1},{1,0},{2,3},{3,2},{4,5},{5,4},{6,7},{7,6},{8,9},{9,8},{10,11... | collective-permute-start | bytes 3145736 | tf_op jit(solution)/shard_map/ppermute | solution.py:326
  293.9 20.1 %collective-permute-start.18 = (bf16[256,2048]{1,0:T(8,128)(2,1)}, bf16[256,2048]{1,0:T(8,128)(2,1)}, u32[]{:S(2)}, u32[]{:S(2)}) collective-permute-start(bf16[256,2048]{1,0:T(8,128)(2,1)} %get-tuple-element.73), channel_id=1, source_target_pairs={{0,2},{2,0},{4,6},{6,4},{8,10},{10,8},{12,14},{14,12},{16,18},{18,... | collective-permute-start | bytes 3145736 | tf_op jit(solution)/shard_map/ppermute | solution.py:326
  302.2 70.9 %all-to-all-start.2 = ((bf16[8,64,1024]{2,1,0:T(8,128)(2,1)}), bf16[8,64,1024]{2,1,0:T(8,128)(2,1)}, u32[]{:S(2)}, u32[]{:S(2)}) async-start(bf16[8,64,1024]{2,1,0:T(8,128)(2,1)} %fusion.46), calls=%async_computation.2 | async-start | bytes 2097152 | tf_op jit(solution)/shard_map/all_to_all | solution.py:489
  326.6 19.4 %collective-permute-start.19 = (bf16[2,8,64,1024]{3,2,1,0:T(8,128)(2,1)}, bf16[2,8,64,1024]{3,2,1,0:T(8,128)(2,1)}, u32[]{:S(2)}, u32[]{:S(2)}) collective-permute-start(bf16[2,8,64,1024]{3,2,1,0:T(8,128)(2,1)} %pad_maximum_fusion.14), channel_id=1, source_target_pairs={{0,2},{2,0},{4,6},{6,4},{8,10},{10,8},{12,14},{14,12},{16,18},{18,... | collective-permute-start | bytes 6291464 | tf_op jit(solution)/shard_map/ppermute | solution.py:326
  328.6 28.9 %collective-permute-start.21 = (bf16[2,8,64,1024]{3,2,1,0:T(8,128)(2,1)}, bf16[2,8,64,1024]{3,2,1,0:T(8,128)(2,1)}, u32[]{:S(2)}, u32[]{:S(2)}) collective-permute-start(bf16[2,8,64,1024]{3,2,1,0:T(8,128)(2,1)} %pad_maximum_fusion.15), channel_id=1, source_target_pairs={{0,2},{2,0},{4,6},{6,4},{8,10},{10,8},{12,14},{14,12},{16,18},{18,... | collective-permute-start | bytes 6291464 | tf_op jit(solution)/shard_map/ppermute | solution.py:326
  347.9 25.2 %collective-permute-start.20 = (bf16[1,8,64,1024]{3,2,1,0:T(8,128)(2,1)S(1)}, bf16[1,8,64,1024]{3,2,1,0:T(8,128)(2,1)}, u32[]{:S(2)}, u32[]{:S(2)}) collective-permute-start(bf16[1,8,64,1024]{3,2,1,0:T(8,128)(2,1)S(1)} %add_convert_fusion.14), channel_id=1, source_target_pairs={{0,1},{1,0},{2,3},{3,2},{4,5},{5,4},{6,7},{7,6},{8,9},{9,8},{10,11... | collective-permute-start | bytes 3145736 | tf_op jit(solution)/shard_map/ppermute | solution.py:326
  380.1 41.6 %collective-permute-start.23 = (bf16[2,8,96,1024]{3,2,1,0:T(8,128)(2,1)}, bf16[2,8,96,1024]{3,2,1,0:T(8,128)(2,1)}, u32[]{:S(2)}, u32[]{:S(2)}) collective-permute-start(bf16[2,8,96,1024]{3,2,1,0:T(8,128)(2,1)} %pad_maximum_fusion.4), channel_id=1, source_target_pairs={{0,2},{2,0},{4,6},{6,4},{8,10},{10,8},{12,14},{14,12},{16,18},{18,... | collective-permute-start | bytes 9437192 | tf_op jit(solution)/shard_map/ppermute | solution.py:326
  380.2 25.8 %collective-permute-start.22 = (bf16[1,8,64,1024]{3,2,1,0:T(8,128)(2,1)}, bf16[1,8,64,1024]{3,2,1,0:T(8,128)(2,1)S(1)}, u32[]{:S(2)}, u32[]{:S(2)}) collective-permute-start(bf16[1,8,64,1024]{3,2,1,0:T(8,128)(2,1)} %add_convert_fusion.13), channel_id=1, source_target_pairs={{0,1},{1,0},{2,3},{3,2},{4,5},{5,4},{6,7},{7,6},{8,9},{9,8},{10,11... | collective-permute-start | bytes 3145736 | tf_op jit(solution)/shard_map/ppermute | solution.py:326
  411.6 54.0 %all-to-all-start.5 = ((bf16[8,128,1024]{2,1,0:T(8,128)(2,1)}), bf16[8,128,1024]{2,1,0:T(8,128)(2,1)}, u32[]{:S(2)}, u32[]{:S(2)}) async-start(bf16[8,128,1024]{2,1,0:T(8,128)(2,1)} %pad_maximum_fusion.16), calls=%async_computation.5 | async-start | bytes 4194304 | tf_op jit(solution)/shard_map/all_to_all | solution.py:489
  417.4 185.0 %all-gather.13.cloned.1.call-start = ((), (), s32[]{:S(2)}) async-start(), calls=%async_computation.8 | async-start | bytes 6684672 | tf_op jit(solution)/shard_map/all_gather | solution.py:497
  425.1 36.0 %collective-permute-start.24 = (bf16[1,8,96,1024]{3,2,1,0:T(8,128)(2,1)}, bf16[1,8,96,1024]{3,2,1,0:T(8,128)(2,1)}, u32[]{:S(2)}, u32[]{:S(2)}) collective-permute-start(bf16[1,8,96,1024]{3,2,1,0:T(8,128)(2,1)} %add_convert_fusion.2), channel_id=1, source_target_pairs={{0,1},{1,0},{2,3},{3,2},{4,5},{5,4},{6,7},{7,6},{8,9},{9,8},{10,11... | collective-permute-start | bytes 4718600 | tf_op jit(solution)/shard_map/ppermute | solution.py:326
  472.5 66.3 %all-to-all-start.3 = ((bf16[8,96,1024]{2,1,0:T(8,128)(2,1)}), bf16[8,96,1024]{2,1,0:T(8,128)(2,1)S(1)}, u32[]{:S(2)}, u32[]{:S(2)}) async-start(bf16[8,96,1024]{2,1,0:T(8,128)(2,1)} %fusion.30), calls=%async_computation.3 | async-start | bytes 3145728 | tf_op jit(solution)/shard_map/all_to_all | solution.py:489
  477.8 22.8 %collective-permute-start.26 = (bf16[1,8,56,1024]{3,2,1,0:T(8,128)(2,1)S(1)}, bf16[1,8,56,1024]{3,2,1,0:T(8,128)(2,1)S(1)}, u32[]{:S(2)}, u32[]{:S(2)}) collective-permute-start(bf16[1,8,56,1024]{3,2,1,0:T(8,128)(2,1)S(1)} %add_convert_fusion.19), channel_id=1, source_target_pairs={{0,1},{1,0},{2,3},{3,2},{4,5},{5,4},{6,7},{7,6},{8,9},{9,8},{10,11... | collective-permute-start | bytes 2752520 | tf_op jit(solution)/shard_map/ppermute | solution.py:326
  539.9 30.1 %all-to-all-start.4 = ((bf16[8,56,1024]{2,1,0:T(8,128)(2,1)}), bf16[8,56,1024]{2,1,0:T(8,128)(2,1)}, u32[]{:S(2)}, u32[]{:S(2)}) async-start(bf16[8,56,1024]{2,1,0:T(8,128)(2,1)} %fusion.59), calls=%async_computation.4 | async-start | bytes 1835008 | tf_op jit(solution)/shard_map/all_to_all | solution.py:489
  544.2 81.8 %all-gather.11.cloned.1.call-start = ((), (), s32[]{:S(2)}) async-start(), calls=%async_computation.7 | async-start | bytes 5292032 | tf_op jit(solution)/shard_map/all_gather | solution.py:497
  573.2 14.9 %collective-permute-start.27 = (bf16[256,1024]{1,0:T(8,128)(2,1)S(1)}, bf16[256,1024]{1,0:T(8,128)(2,1)S(1)}, u32[]{:S(2)}, u32[]{:S(2)}) collective-permute-start(bf16[256,1024]{1,0:T(8,128)(2,1)S(1)} %slice.203), channel_id=1, source_target_pairs={{0,1},{1,0},{2,3},{3,2},{4,5},{5,4},{6,7},{7,6},{8,9},{9,8},{10,11... | collective-permute-start | bytes 1572872 | tf_op jit(solution)/shard_map/ppermute | solution.py:326
  578.4 19.9 %collective-permute-start.29 = (bf16[256,1024]{1,0:T(8,128)(2,1)S(1)}, bf16[256,1024]{1,0:T(8,128)(2,1)S(1)}, u32[]{:S(2)}, u32[]{:S(2)}) collective-permute-start(bf16[256,1024]{1,0:T(8,128)(2,1)S(1)} %slice.206), channel_id=1, source_target_pairs={{0,1},{1,0},{2,3},{3,2},{4,5},{5,4},{6,7},{7,6},{8,9},{9,8},{10,11... | collective-permute-start | bytes 1572872 | tf_op jit(solution)/shard_map/ppermute | solution.py:326
  (141 other events, 1270.3 us)
Sparse Core Ops, SparseCore 0:
  91.3 69.8 all-gather.8
  468.4 88.2 all-gather.12
  572.2 53.6 all-gather.10

commit v7 on v6

--- a/solution.py
+++ b/solution.py
@@ -144,7 +144,7 @@
         scores = product(query_ref[...], features) + mask
         top = jnp.max(scores, axis=-1, keepdims=True)
         weights = jnp.exp(scores - top)
-        shares = weights / jnp.sum(weights, axis=-1, keepdims=True)
+        shares = weights * (1.0 / jnp.sum(weights, axis=-1, keepdims=True))
         grad_shares = product(grad_ref[...], features)
         inner = jnp.sum(shares * grad_shares, axis=-1, keepdims=True)
         grad_scores = (shares * (grad_shares - inner)).astype(low_type)
@@ -225,7 +225,7 @@
         grads = grad_ref[q_rows]
         scores = nt(keys, queries) * scaling
         weights = jnp.exp(scores - jnp.max(scores, axis=0, keepdims=True))
-        shares = weights / jnp.sum(weights, axis=0, keepdims=True)
+        shares = weights * (1.0 / jnp.sum(weights, axis=0, keepdims=True))
         grad_shares = nt(values, grads)
         inner = jnp.sum(shares * grad_shares, axis=0, keepdims=True)
         grad_scores = (shares * (grad_shares - inner)).astype(low_type)
@@ -520,7 +520,11 @@
     counts = jnp.sum((picked[:, None, :] == label_ids[None, :, None]).astype(jnp.float32), axis=2)
     chunks = prepare_pixels(jnp.swapaxes(pixels, 1, 2), plan.micro, width)
     spread = lax.all_to_all(chunks, "blk", split_axis=0, concat_axis=0, tiled=True)
-    totals = jnp.sum(lax.all_gather(counts, "blk", axis=0), axis=0).astype(jnp.int32)
+    mask = 1
+    while mask < blocks:
+        counts = counts + swap(counts, "blk", mask)
+        mask *= 2
+    totals = counts.astype(jnp.int32)
     owners = of_items(block_map)
     images = label_ids[None, :] != of_items(pad_ids)[:, None]
     totals = jnp.where(images, totals, 0)

time: 656 us -> 653 us (level)
  blocking collectives: 41.2 us -> 0 us
  waiting for transfers between devices: 177 us -> 195 us
  other arithmetic: 117 us -> 128 us
  local copies, waits for them, and re-layouts: 56.4 us -> 65.8 us
    all_gather x1 -> x0, blocking collectives: 41.2 us -> none  [route_pixels(): lax.all_gather(counts, 'blk', axis=0)]
    ppermute x27 -> x31, waiting for transfers between devices: 81.1 us -> 107 us  [swap(): return lax.ppermute(array, axis_name, [(i, i ^ mask) for i in range(size)])]
    ppermute x27 -> x31, starting transfers between devices: 19.7 us -> 28.6 us  [swap(): return lax.ppermute(array, axis_name, [(i, i ^ mask) for i in range(size)])]
    all_to_all x1, starting transfers between devices: 12.5 us -> 4.13 us  [route_pixels(): lax.all_to_all(pieces, 'blk', split_axis=0, concat_axis=0, tiled=True)]
    all_to_all x1, waiting for transfers between devices: 19.3 us -> 11.9 us  [route_pixels(): lax.all_to_all(pieces, 'blk', split_axis=0, concat_axis=0, tiled=True)]
    unnamed x275 -> x279, local copies, waits for them, and re-layouts: 13.3 us -> 13.6 us
  transfers between devices with their start and end apart: 40 -> 44, of which waited for: 13 -> 16; matrix products, arithmetic and copies ran while one was open for 34% -> 37% of each run, Pallas kernels for 8% -> 9%
where the time goes in v7:
time: 653 us; the launch traced here: 645 us
  waiting for transfers between devices  195 us (30%)
  other arithmetic  128 us (20%)
  matrix products  107 us (16%)
  starting transfers between devices  73.8 us (11%)
  local copies, waits for them, and re-layouts  65.8 us (10%)
  Pallas kernels  59.7 us (9%)
  between operations  16.1 us (2%)
    ppermute x31, waiting for transfers between devices, swap(): return lax.ppermute(array, axis_name, [(i, i ^ mask) for i in range(size)])  107 us
    all_to_all x4, waiting for transfers between devices, over_chips(): lax.all_to_all(total, 'blk', split_axis=0, concat_axis=0, axis_index_grou...  63.7 us
    dot_general x10, matrix products, product_nt(): lax.dot_general(a, b, (((1,), (1,)), ((), ())), preferred_element_type=jn...  45.2 us
    dot_general x12, matrix products, product_tn(): lax.dot_general(a, b, (((0,), (0,)), ((), ())), preferred_element_type=jn...  31.3 us
    dot_general x10, matrix products, product(): return jnp.dot(a, b, preferred_element_type=jnp.float32)  30.4 us
    ppermute x31, starting transfers between devices, swap(): return lax.ppermute(array, axis_name, [(i, i ^ mask) for i in range(size)])  28.6 us
    all_to_all x4, starting transfers between devices, over_chips(): lax.all_to_all(total, 'blk', split_axis=0, concat_axis=0, axis_index_grou...  24.7 us
    pallas_call x1, Pallas kernels, self_backward(): pl.pallas_call(functools.partial(self_backward_kernel, groups, head ** (-...  19.8 us
  transfers between devices with their start and end apart: 44, of which 16 were waited for; matrix products, arithmetic and copies ran while one was open for 37% of the time, Pallas kernels for 9%

profile of v7, /device:TPU:0, one launch (start us, length us, event | category | flops | bytes accessed | tf_op | source)
XLA Modules:
  0.0 645.0 jit_solution(3510030131324505580)
XLA Ops:
  9.4 5.1 prepare_pixels.1
  14.5 7.2 %all-to-all-start = ((bf16[16,2,272,128]{3,2,1,0:T(8,128)(2,1)}), bf16[16,2,272,128]{3,2,1,0:T(8,128)(2,1)S(1)}, u32[]{:S(2)}, u32[]{:S(2)}) async-start(bf16[16,2,272,128]{3,2,1,0:T(8,128)(2,1)} %prepare_pixels.1), calls=%async_computation | async-start | bytes 4456448 | tf_op jit(solution)/shard_map/all_to_all | solution.py:522
  51.2 7.8 %collective-permute-done.3 = f32[2,17]{0,1:T(8,128)} collective-permute-done((f32[2,17]{0,1:T(8,128)S(1)}, f32[2,17]{0,1:T(8,128)}, u32[]{:S(2)}, u32[]{:S(2)}) %collective-permute-start.3) | collective-permute-done | bytes 168 | tf_op jit(solution)/shard_map/ppermute | solution.py:326
  59.7 4.6 collective-permute-start.4
  64.3 9.9 %collective-permute-done.4 = f32[2,17]{0,1:T(8,128)} collective-permute-done((f32[2,17]{0,1:T(8,128)S(1)}, f32[2,17]{0,1:T(8,128)}, u32[]{:S(2)}, u32[]{:S(2)}) %collective-permute-start.4) | collective-permute-done | bytes 168 | tf_op jit(solution)/shard_map/ppermute | solution.py:326
  103.2 4.1 all-to-all-start.1
  117.9 9.7 %collective-permute-done.9 = bf16[256,3072]{1,0:T(8,128)(2,1)} collective-permute-done((bf16[256,3072]{1,0:T(8,128)(2,1)}, bf16[256,3072]{1,0:T(8,128)(2,1)}, u32[]{:S(2)}, u32[]{:S(2)}) %collective-permute-start.9) | collective-permute-done | bytes 1572896 | tf_op jit(solution)/shard_map/ppermute | solution.py:326
  139.3 10.7 %collective-permute-done.11 = bf16[128,3072]{1,0:T(8,128)(2,1)} collective-permute-done((bf16[128,3072]{1,0:T(8,128)(2,1)S(1)}, bf16[128,3072]{1,0:T(8,128)(2,1)}, u32[]{:S(2)}, u32[]{:S(2)}) %collective-permute-start.11) | collective-permute-done | bytes 786464 | tf_op jit(solution)/shard_map/ppermute | solution.py:326
  150.0 11.9 %all-to-all-done.1.first_ref = bf16[16,2,272,128]{3,2,1,0:T(8,128)(2,1)S(1)} async-done(((bf16[16,2,272,128]{3,2,1,0:T(8,128)(2,1)}), bf16[16,2,272,128]{3,2,1,0:T(8,128)(2,1)S(1)}, u32[]{:S(2)}, u32[]{:S(2)}) %all-to-all-start.1) | async-done | bytes 2228256 | tf_op jit(solution)/shard_map/all_to_all | solution.py:557
  166.4 8.3 %cross_attention.2 = f32[768,272]{1,0:T(8,128)} custom-call(s32[2]{0:T(128)} %get-tuple-element.206.big_ref, bf16[768,272]{1,0:T(8,128)(2,1)} %pad.17.query_ref, bf16[16,2,272,128]{3,2,1,0:T(8,128)(2,1)} %copy-done.1, bf16[16,2,272,128]{3,2,1,0:T(8,128)(2,1)} %bitcast.200, f32[2,8,4096]{2,1,0:T(8,128)} %broadcast_in_dim.77.mask_ref), custom_call_target="tpu_custom_call" | custom-call | tf_op jit(solution)/shard_map/cross_attention/pallas_call | solution.py:168
  178.2 5.8 collective-permute-start.19
  206.9 5.3 convolution_convert_fusion.q_ref.k_ref.v_ref
  218.7 10.8 %self_forward.1 = bf16[768,1024]{1,0:T(8,128)(2,1)} custom-call(bf16[768,3072]{1,0:T(8,128)(2,1)} %copy-done, bf16[768,3072]{1,0:T(8,128)(2,1)} %copy-done, bf16[768,3072]{1,0:T(8,128)(2,1)} %copy-done, bf16[256,2048]{1,0:T(8,128)(2,1)} %collective-permute-done.14.more_k_ref.more_v_ref, bf16[256,2048]{1,0:T(8,128)(2,1)} %collective-permute-done.14.more_k_ref.more_v_ref), custom_call_target="tpu_custom_call" | custom-call | tf_op jit(solution)/shard_map/self_forward/pallas_call | solution.py:260
  251.6 5.7 multiply_reduce_fusion
  271.5 19.8 %self_backward.1 = (bf16[768,3072]{1,0:T(8,128)(2,1)}, bf16[256,2048]{1,0:T(8,128)(2,1)}) custom-call(bf16[768,3072]{1,0:T(8,128)(2,1)} %copy-done, bf16[768,3072]{1,0:T(8,128)(2,1)} %copy-done, bf16[768,3072]{1,0:T(8,128)(2,1)} %copy-done, bf16[256,2048]{1,0:T(8,128)(2,1)} %collective-permute-done.14.more_k_ref.more_v_ref, ...), custom_call_target="tpu_custom_call" | custom-call | tf_op jit(solution)/shard_map/self_backward/pallas_call | solution.py:275
  299.5 10.9 %all-to-all-start.2 = ((bf16[8,64,1024]{2,1,0:T(8,128)(2,1)}), bf16[8,64,1024]{2,1,0:T(8,128)(2,1)}, u32[]{:S(2)}, u32[]{:S(2)}) async-start(bf16[8,64,1024]{2,1,0:T(8,128)(2,1)} %fusion.46), calls=%async_computation.2 | async-start | bytes 2097152 | tf_op jit(solution)/shard_map/all_to_all | solution.py:489
  326.9 9.7 %multiply_reduce_fusion.1 = (bf16[1024]{0:T(1024)(128)(2,1)S(1)}, f32[768]{0:T(1024)S(1)}, f32[768]{0:T(1024)S(1)}, bf16[1024]{0:T(1024)(128)(2,1)S(1)}, f32[768,1024]{1,0:T(8,128)}) fusion(f32[768,1024]{1,0:T(8,128)S(1)} %get-tuple-element.316, f32[768]{0:T(1024)S(1)} %add_rsqrt_fusion.1, f32[768]{0:T(1024)S(1)} %broadcast_multiply_fusion.10, ...), kind=kOutput, calls=%fused_computation.54 | convolution fusion | flops 4851494912 | bytes 17321984 | tf_op jit(solution)/shard_map/dot_general | solution.py:28
  359.9 9.7 %collective-permute-done.24 = bf16[1,8,64,1024]{3,2,1,0:T(8,128)(2,1)} collective-permute-done((bf16[1,8,64,1024]{3,2,1,0:T(8,128)(2,1)S(1)}, bf16[1,8,64,1024]{3,2,1,0:T(8,128)(2,1)}, u32[]{:S(2)}, u32[]{:S(2)}) %collective-permute-start.24) | collective-permute-done | bytes 1048608 | tf_op jit(solution)/shard_map/ppermute | solution.py:326
  387.1 9.9 %cross_attention.3 = f32[768,272]{1,0:T(8,128)} custom-call(s32[2]{0:T(128)} %get-tuple-element.206.big_ref, bf16[768,272]{1,0:T(8,128)(2,1)} %pad.17.query_ref, bf16[768,272]{1,0:T(8,128)(2,1)} %fusion.64.grad_ref, bf16[16,2,272,128]{3,2,1,0:T(8,128)(2,1)} %copy-done.1, bf16[16,2,272,128]{3,2,1,0:T(8,128)(2,1)} %bitcast.201, ...), custom_call_target="tpu_custom_call" | custom-call | tf_op jit(solution)/shard_map/cross_attention/pallas_call | solution.py:168
  397.0 5.5 collective-permute-done.26
  408.1 5.8 all-to-all-start.5
  425.7 5.9 fusion.10
  445.6 12.0 %collective-permute-done.28 = bf16[1,8,96,1024]{3,2,1,0:T(8,128)(2,1)} collective-permute-done((bf16[1,8,96,1024]{3,2,1,0:T(8,128)(2,1)}, bf16[1,8,96,1024]{3,2,1,0:T(8,128)(2,1)}, u32[]{:S(2)}, u32[]{:S(2)}) %collective-permute-start.28) | collective-permute-done | bytes 1572896 | tf_op jit(solution)/shard_map/ppermute | solution.py:326
  457.6 4.4 all-to-all-done.5
  474.7 22.3 %collective-permute-done.30 = bf16[1,8,56,1024]{3,2,1,0:T(8,128)(2,1)S(1)} collective-permute-done((bf16[1,8,56,1024]{3,2,1,0:T(8,128)(2,1)S(1)}, bf16[1,8,56,1024]{3,2,1,0:T(8,128)(2,1)S(1)}, u32[]{:S(2)}, u32[]{:S(2)}) %collective-permute-start.30) | collective-permute-done | bytes 917536 | tf_op jit(solution)/shard_map/ppermute | solution.py:326
  499.7 35.6 %all-to-all-done.3 = bf16[8,96,1024]{2,1,0:T(8,128)(2,1)S(1)} async-done(((bf16[8,96,1024]{2,1,0:T(8,128)(2,1)}), bf16[8,96,1024]{2,1,0:T(8,128)(2,1)S(1)}, u32[]{:S(2)}, u32[]{:S(2)}) %all-to-all-start.3) | async-done | bytes 1572896 | tf_op jit(solution)/shard_map/all_to_all | solution.py:489
  536.4 4.2 all-to-all-start.4
  542.8 23.7 %all-to-all-done.4 = bf16[8,56,1024]{2,1,0:T(8,128)(2,1)} async-done(((bf16[8,56,1024]{2,1,0:T(8,128)(2,1)}), bf16[8,56,1024]{2,1,0:T(8,128)(2,1)}, u32[]{:S(2)}, u32[]{:S(2)}) %all-to-all-start.4) | async-done | bytes 917536 | tf_op jit(solution)/shard_map/all_to_all | solution.py:489
  575.5 9.1 %collective-permute-done.31 = bf16[256,1024]{1,0:T(8,128)(2,1)S(1)} collective-permute-done((bf16[256,1024]{1,0:T(8,128)(2,1)S(1)}, bf16[256,1024]{1,0:T(8,128)(2,1)S(1)}, u32[]{:S(2)}, u32[]{:S(2)}) %collective-permute-start.31) | collective-permute-done | bytes 524320 | tf_op jit(solution)/shard_map/ppermute | solution.py:326
  585.4 9.5 %collective-permute-done.33 = bf16[256,1024]{1,0:T(8,128)(2,1)S(1)} collective-permute-done((bf16[256,1024]{1,0:T(8,128)(2,1)S(1)}, bf16[256,1024]{1,0:T(8,128)(2,1)S(1)}, u32[]{:S(2)}, u32[]{:S(2)}) %collective-permute-start.33) | collective-permute-done | bytes 524320 | tf_op jit(solution)/shard_map/ppermute | solution.py:326
  598.9 5.8 widen.1
  610.0 12.5 %all-gather.9.cloned.1.call-done = bf16[2432,1024]{1,0:T(8,128)(2,1)} async-done(((bf16[152,1024]{1,0:T(8,128)(2,1)}), bf16[2432,1024]{1,0:T(8,128)(2,1)}) %all-gather.9.cloned.1.call-update) | async-done | bytes 4980752 | tf_op jit(solution)/shard_map/all_gather | solution.py:497
  (559 shorter events, 305.8 us)
Async XLA Ops:
  8.3 35.2 %collective-permute-start.1 = (f32[2,17]{0,1:T(8,128)S(1)}, f32[2,17]{0,1:T(8,128)}, u32[]{:S(2)}, u32[]{:S(2)}) collective-permute-start(f32[2,17]{0,1:T(8,128)S(1)} %fusion.65), channel_id=1, source_target_pairs={{0,2},{2,0},{4,6},{6,4},{8,10},{10,8},{12,14},{14,12},{16,18},{18,... | collective-permute-start | bytes 416 | tf_op jit(solution)/shard_map/ppermute | solution.py:326
  14.5 78.6 %all-to-all-start = ((bf16[16,2,272,128]{3,2,1,0:T(8,128)(2,1)}), bf16[16,2,272,128]{3,2,1,0:T(8,128)(2,1)S(1)}, u32[]{:S(2)}, u32[]{:S(2)}) async-start(bf16[16,2,272,128]{3,2,1,0:T(8,128)(2,1)} %prepare_pixels.1), calls=%async_computation | async-start | bytes 4456448 | tf_op jit(solution)/shard_map/all_to_all | solution.py:522
  21.7 144.0 %all-gather.7.cloned.1.call-start = ((), (), s32[]{:S(2)}) async-start(), calls=%async_computation.6 | async-start | bytes 2367488 | tf_op jit(solution)/shard_map/all_gather | solution.py:561
  22.6 65.3 %collective-permute-start.7 = (bf16[256,1024]{1,0:T(8,128)(2,1)}, bf16[256,1024]{1,0:T(8,128)(2,1)}, u32[]{:S(2)}, u32[]{:S(2)}) collective-permute-start(bf16[256,1024]{1,0:T(8,128)(2,1)} %constant_dynamic-slice_fusion.7), channel_id=1, source_target_pairs={{0,1},{1,0},{2,3},{3,2},{4,5},{5,4},{6,7},{7,6},{8,9},{9,8},{10,11... | collective-permute-start | bytes 1572872 | tf_op jit(solution)/shard_map/ppermute | solution.py:326
  26.1 61.8 %collective-permute-start.6 = (bf16[265,1024]{1,0:T(8,128)(2,1)}, bf16[265,1024]{1,0:T(8,128)(2,1)}, u32[]{:S(2)}, u32[]{:S(2)}) collective-permute-start(bf16[265,1024]{1,0:T(8,128)(2,1)} %pad_maximum_fusion.41), channel_id=1, source_target_pairs={{0,1},{1,0},{2,3},{3,2},{4,5},{5,4},{6,7},{7,6},{8,9},{9,8},{10,11... | collective-permute-start | bytes 1628168 | tf_op jit(solution)/shard_map/ppermute | solution.py:326
  29.0 58.9 %collective-permute-start.5 = (bf16[256,1024]{1,0:T(8,128)(2,1)}, bf16[256,1024]{1,0:T(8,128)(2,1)S(1)}, u32[]{:S(2)}, u32[]{:S(2)}) collective-permute-start(bf16[256,1024]{1,0:T(8,128)(2,1)} %get-tuple-element.284), channel_id=1, source_target_pairs={{0,0},{2,1},{4,4},{6,5},{8,8},{10,9},{12,12},{14,13},{16,16},{18,1... | collective-permute-start | bytes 1572872 | tf_op jit(solution)/shard_map/ppermute | solution.py:369
  30.7 57.2 %collective-permute-start = (bf16[256,1024]{1,0:T(8,128)(2,1)}, bf16[256,1024]{1,0:T(8,128)(2,1)}, u32[]{:S(2)}, u32[]{:S(2)}) collective-permute-start(bf16[256,1024]{1,0:T(8,128)(2,1)} %get-tuple-element.285), channel_id=1, source_target_pairs={{0,1},{1,0},{2,3},{3,2},{4,5},{5,4},{6,7},{7,6},{8,9},{9,8},{10,11... | collective-permute-start | bytes 1572872 | tf_op jit(solution)/shard_map/ppermute | solution.py:326
  91.6 36.0 %collective-permute-start.9 = (bf16[256,3072]{1,0:T(8,128)(2,1)}, bf16[256,3072]{1,0:T(8,128)(2,1)}, u32[]{:S(2)}, u32[]{:S(2)}) collective-permute-start(bf16[256,3072]{1,0:T(8,128)(2,1)} %pad_maximum_fusion.19), channel_id=1, source_target_pairs={{0,1},{1,0},{2,3},{3,2},{4,5},{5,4},{6,7},{7,6},{8,9},{9,8},{10,11... | collective-permute-start | bytes 4718600 | tf_op jit(solution)/shard_map/ppermute | solution.py:326
  103.2 58.7 %all-to-all-start.1 = ((bf16[16,2,272,128]{3,2,1,0:T(8,128)(2,1)}), bf16[16,2,272,128]{3,2,1,0:T(8,128)(2,1)S(1)}, u32[]{:S(2)}, u32[]{:S(2)}) async-start(bf16[16,2,272,128]{3,2,1,0:T(8,128)(2,1)} %bitcast.202), calls=%async_computation.1 | async-start | bytes 4456448 | tf_op jit(solution)/shard_map/all_to_all | solution.py:557
  129.5 20.5 %collective-permute-start.11 = (bf16[128,3072]{1,0:T(8,128)(2,1)S(1)}, bf16[128,3072]{1,0:T(8,128)(2,1)}, u32[]{:S(2)}, u32[]{:S(2)}) collective-permute-start(bf16[128,3072]{1,0:T(8,128)(2,1)S(1)} %constant_dynamic-slice_fusion.3), channel_id=1, source_target_pairs={{0,1},{1,0},{2,3},{3,2},{4,5},{5,4},{6,7},{7,6},{8,9},{9,8},{10,11... | collective-permute-start | bytes 2359304 | tf_op jit(solution)/shard_map/ppermute | solution.py:326
  133.0 43.2 %collective-permute-start.15 = (bf16[128,3072]{1,0:T(8,128)(2,1)}, bf16[128,3072]{1,0:T(8,128)(2,1)}, u32[]{:S(2)}, u32[]{:S(2)}) collective-permute-start(bf16[128,3072]{1,0:T(8,128)(2,1)} %pad_maximum_fusion.40), channel_id=1, source_target_pairs={{0,1},{1,0},{2,3},{3,2},{4,5},{5,4},{6,7},{7,6},{8,9},{9,8},{10,11... | collective-permute-start | bytes 2359304 | tf_op jit(solution)/shard_map/ppermute | solution.py:326
  161.9 36.6 %collective-permute-start.12 = (bf16[128,3072]{1,0:T(8,128)(2,1)}, bf16[128,3072]{1,0:T(8,128)(2,1)}, u32[]{:S(2)}, u32[]{:S(2)}) collective-permute-start(bf16[128,3072]{1,0:T(8,128)(2,1)} %collective-permute-done.11), channel_id=1, source_target_pairs={{0,4},{2,6},{4,0},{6,2},{8,12},{10,14},{12,8},{14,10},{16,20},{18,... | collective-permute-start | bytes 2359304 | tf_op jit(solution)/shard_map/ppermute | solution.py:326
  176.2 25.1 %collective-permute-start.16 = (bf16[128,3072]{1,0:T(8,128)(2,1)}, bf16[128,3072]{1,0:T(8,128)(2,1)S(1)}, u32[]{:S(2)}, u32[]{:S(2)}) collective-permute-start(bf16[128,3072]{1,0:T(8,128)(2,1)} %collective-permute-done.15), channel_id=1, source_target_pairs={{0,4},{2,6},{4,0},{6,2},{8,12},{10,14},{12,8},{14,10},{16,20},{18,... | collective-permute-start | bytes 2359304 | tf_op jit(solution)/shard_map/ppermute | solution.py:326
  178.2 54.6 %collective-permute-start.19 = (bf16[256,1024]{1,0:T(8,128)(2,1)}, bf16[256,1024]{1,0:T(8,128)(2,1)}, u32[]{:S(2)}, u32[]{:S(2)}) collective-permute-start(bf16[256,1024]{1,0:T(8,128)(2,1)} %get-tuple-element.277), channel_id=1, source_target_pairs={{0,0},{2,1},{4,4},{6,5},{8,8},{10,9},{12,12},{14,13},{16,16},{18,1... | collective-permute-start | bytes 1572872 | tf_op jit(solution)/shard_map/ppermute | solution.py:369
  184.1 48.8 %collective-permute-start.18 = (bf16[256,1024]{1,0:T(8,128)(2,1)}, bf16[256,1024]{1,0:T(8,128)(2,1)}, u32[]{:S(2)}, u32[]{:S(2)}) collective-permute-start(bf16[256,1024]{1,0:T(8,128)(2,1)} %get-tuple-element.278), channel_id=1, source_target_pairs={{0,1},{1,0},{2,3},{3,2},{4,5},{5,4},{6,7},{7,6},{8,9},{9,8},{10,11... | collective-permute-start | bytes 1572872 | tf_op jit(solution)/shard_map/ppermute | solution.py:326
  260.2 31.0 %collective-permute-start.21 = (bf16[1,8,64,1024]{3,2,1,0:T(8,128)(2,1)}, bf16[1,8,64,1024]{3,2,1,0:T(8,128)(2,1)}, u32[]{:S(2)}, u32[]{:S(2)}) collective-permute-start(bf16[1,8,64,1024]{3,2,1,0:T(8,128)(2,1)} %add_convert_fusion.16), channel_id=1, source_target_pairs={{0,1},{1,0},{2,3},{3,2},{4,5},{5,4},{6,7},{7,6},{8,9},{9,8},{10,11... | collective-permute-start | bytes 3145736 | tf_op jit(solution)/shard_map/ppermute | solution.py:326
  291.2 19.2 %collective-permute-start.22 = (bf16[256,2048]{1,0:T(8,128)(2,1)}, bf16[256,2048]{1,0:T(8,128)(2,1)}, u32[]{:S(2)}, u32[]{:S(2)}) collective-permute-start(bf16[256,2048]{1,0:T(8,128)(2,1)} %get-tuple-element.73), channel_id=1, source_target_pairs={{0,2},{2,0},{4,6},{6,4},{8,10},{10,8},{12,14},{14,12},{16,18},{18,... | collective-permute-start | bytes 3145736 | tf_op jit(solution)/shard_map/ppermute | solution.py:326
  299.5 70.1 %all-to-all-start.2 = ((bf16[8,64,1024]{2,1,0:T(8,128)(2,1)}), bf16[8,64,1024]{2,1,0:T(8,128)(2,1)}, u32[]{:S(2)}, u32[]{:S(2)}) async-start(bf16[8,64,1024]{2,1,0:T(8,128)(2,1)} %fusion.46), calls=%async_computation.2 | async-start | bytes 2097152 | tf_op jit(solution)/shard_map/all_to_all | solution.py:489
  323.1 19.4 %collective-permute-start.23 = (bf16[2,8,64,1024]{3,2,1,0:T(8,128)(2,1)}, bf16[2,8,64,1024]{3,2,1,0:T(8,128)(2,1)}, u32[]{:S(2)}, u32[]{:S(2)}) collective-permute-start(bf16[2,8,64,1024]{3,2,1,0:T(8,128)(2,1)} %pad_maximum_fusion.14), channel_id=1, source_target_pairs={{0,2},{2,0},{4,6},{6,4},{8,10},{10,8},{12,14},{14,12},{16,18},{18,... | collective-permute-start | bytes 6291464 | tf_op jit(solution)/shard_map/ppermute | solution.py:326
  325.1 28.9 %collective-permute-start.25 = (bf16[2,8,64,1024]{3,2,1,0:T(8,128)(2,1)}, bf16[2,8,64,1024]{3,2,1,0:T(8,128)(2,1)}, u32[]{:S(2)}, u32[]{:S(2)}) collective-permute-start(bf16[2,8,64,1024]{3,2,1,0:T(8,128)(2,1)} %pad_maximum_fusion.15), channel_id=1, source_target_pairs={{0,2},{2,0},{4,6},{6,4},{8,10},{10,8},{12,14},{14,12},{16,18},{18,... | collective-permute-start | bytes 6291464 | tf_op jit(solution)/shard_map/ppermute | solution.py:326
  344.4 25.2 %collective-permute-start.24 = (bf16[1,8,64,1024]{3,2,1,0:T(8,128)(2,1)S(1)}, bf16[1,8,64,1024]{3,2,1,0:T(8,128)(2,1)}, u32[]{:S(2)}, u32[]{:S(2)}) collective-permute-start(bf16[1,8,64,1024]{3,2,1,0:T(8,128)(2,1)S(1)} %add_convert_fusion.14), channel_id=1, source_target_pairs={{0,1},{1,0},{2,3},{3,2},{4,5},{5,4},{6,7},{7,6},{8,9},{9,8},{10,11... | collective-permute-start | bytes 3145736 | tf_op jit(solution)/shard_map/ppermute | solution.py:326
  376.6 41.6 %collective-permute-start.27 = (bf16[2,8,96,1024]{3,2,1,0:T(8,128)(2,1)}, bf16[2,8,96,1024]{3,2,1,0:T(8,128)(2,1)}, u32[]{:S(2)}, u32[]{:S(2)}) collective-permute-start(bf16[2,8,96,1024]{3,2,1,0:T(8,128)(2,1)} %pad_maximum_fusion.4), channel_id=1, source_target_pairs={{0,2},{2,0},{4,6},{6,4},{8,10},{10,8},{12,14},{14,12},{16,18},{18,... | collective-permute-start | bytes 9437192 | tf_op jit(solution)/shard_map/ppermute | solution.py:326
  376.7 25.8 %collective-permute-start.26 = (bf16[1,8,64,1024]{3,2,1,0:T(8,128)(2,1)}, bf16[1,8,64,1024]{3,2,1,0:T(8,128)(2,1)S(1)}, u32[]{:S(2)}, u32[]{:S(2)}) collective-permute-start(bf16[1,8,64,1024]{3,2,1,0:T(8,128)(2,1)} %add_convert_fusion.13), channel_id=1, source_target_pairs={{0,1},{1,0},{2,3},{3,2},{4,5},{5,4},{6,7},{7,6},{8,9},{9,8},{10,11... | collective-permute-start | bytes 3145736 | tf_op jit(solution)/shard_map/ppermute | solution.py:326
  408.1 54.0 %all-to-all-start.5 = ((bf16[8,128,1024]{2,1,0:T(8,128)(2,1)}), bf16[8,128,1024]{2,1,0:T(8,128)(2,1)}, u32[]{:S(2)}, u32[]{:S(2)}) async-start(bf16[8,128,1024]{2,1,0:T(8,128)(2,1)} %pad_maximum_fusion.16), calls=%async_computation.5 | async-start | bytes 4194304 | tf_op jit(solution)/shard_map/all_to_all | solution.py:489
  413.9 185.0 %all-gather.11.cloned.1.call-start = ((), (), s32[]{:S(2)}) async-start(), calls=%async_computation.8 | async-start | bytes 6684672 | tf_op jit(solution)/shard_map/all_gather | solution.py:497
  421.6 36.0 %collective-permute-start.28 = (bf16[1,8,96,1024]{3,2,1,0:T(8,128)(2,1)}, bf16[1,8,96,1024]{3,2,1,0:T(8,128)(2,1)}, u32[]{:S(2)}, u32[]{:S(2)}) collective-permute-start(bf16[1,8,96,1024]{3,2,1,0:T(8,128)(2,1)} %add_convert_fusion.2), channel_id=1, source_target_pairs={{0,1},{1,0},{2,3},{3,2},{4,5},{5,4},{6,7},{7,6},{8,9},{9,8},{10,11... | collective-permute-start | bytes 4718600 | tf_op jit(solution)/shard_map/ppermute | solution.py:326
  469.0 66.3 %all-to-all-start.3 = ((bf16[8,96,1024]{2,1,0:T(8,128)(2,1)}), bf16[8,96,1024]{2,1,0:T(8,128)(2,1)S(1)}, u32[]{:S(2)}, u32[]{:S(2)}) async-start(bf16[8,96,1024]{2,1,0:T(8,128)(2,1)} %fusion.30), calls=%async_computation.3 | async-start | bytes 3145728 | tf_op jit(solution)/shard_map/all_to_all | solution.py:489
  474.3 22.8 %collective-permute-start.30 = (bf16[1,8,56,1024]{3,2,1,0:T(8,128)(2,1)S(1)}, bf16[1,8,56,1024]{3,2,1,0:T(8,128)(2,1)S(1)}, u32[]{:S(2)}, u32[]{:S(2)}) collective-permute-start(bf16[1,8,56,1024]{3,2,1,0:T(8,128)(2,1)S(1)} %add_convert_fusion.19), channel_id=1, source_target_pairs={{0,1},{1,0},{2,3},{3,2},{4,5},{5,4},{6,7},{7,6},{8,9},{9,8},{10,11... | collective-permute-start | bytes 2752520 | tf_op jit(solution)/shard_map/ppermute | solution.py:326
  536.4 30.1 %all-to-all-start.4 = ((bf16[8,56,1024]{2,1,0:T(8,128)(2,1)}), bf16[8,56,1024]{2,1,0:T(8,128)(2,1)}, u32[]{:S(2)}, u32[]{:S(2)}) async-start(bf16[8,56,1024]{2,1,0:T(8,128)(2,1)} %fusion.59), calls=%async_computation.4 | async-start | bytes 1835008 | tf_op jit(solution)/shard_map/all_to_all | solution.py:489
  540.7 81.8 %all-gather.9.cloned.1.call-start = ((), (), s32[]{:S(2)}) async-start(), calls=%async_computation.7 | async-start | bytes 5292032 | tf_op jit(solution)/shard_map/all_gather | solution.py:497
  569.7 14.9 %collective-permute-start.31 = (bf16[256,1024]{1,0:T(8,128)(2,1)S(1)}, bf16[256,1024]{1,0:T(8,128)(2,1)S(1)}, u32[]{:S(2)}, u32[]{:S(2)}) collective-permute-start(bf16[256,1024]{1,0:T(8,128)(2,1)S(1)} %slice.203), channel_id=1, source_target_pairs={{0,1},{1,0},{2,3},{3,2},{4,5},{5,4},{6,7},{7,6},{8,9},{9,8},{10,11... | collective-permute-start | bytes 1572872 | tf_op jit(solution)/shard_map/ppermute | solution.py:326
  574.9 19.9 %collective-permute-start.33 = (bf16[256,1024]{1,0:T(8,128)(2,1)S(1)}, bf16[256,1024]{1,0:T(8,128)(2,1)S(1)}, u32[]{:S(2)}, u32[]{:S(2)}) collective-permute-start(bf16[256,1024]{1,0:T(8,128)(2,1)S(1)} %slice.206), channel_id=1, source_target_pairs={{0,1},{1,0},{2,3},{3,2},{4,5},{5,4},{6,7},{7,6},{8,9},{9,8},{10,11... | collective-permute-start | bytes 1572872 | tf_op jit(solution)/shard_map/ppermute | solution.py:326
  (147 other events, 1202.0 us)
Sparse Core Ops, SparseCore 0:
  96.9 61.4 all-gather.6
  464.9 88.2 all-gather.10
  568.7 53.6 all-gather.8

commit v8 on v5

--- a/solution.py
+++ b/solution.py
@@ -150,7 +150,7 @@
         scores = product(query_ref[...], features) + mask
         top = jnp.max(scores, axis=-1, keepdims=True)
         weights = jnp.exp(scores - top)
-        shares = weights / jnp.sum(weights, axis=-1, keepdims=True)
+        shares = weights * (1.0 / jnp.sum(weights, axis=-1, keepdims=True))
         grad_shares = product(grad_ref[...], features)
         inner = jnp.sum(shares * grad_shares, axis=-1, keepdims=True)
         grad_scores = (shares * (grad_shares - inner)).astype(low_type)
@@ -231,7 +231,7 @@
         grads = grad_ref[q_rows]
         scores = nt(keys, queries) * scaling
         weights = jnp.exp(scores - jnp.max(scores, axis=0, keepdims=True))
-        shares = weights / jnp.sum(weights, axis=0, keepdims=True)
+        shares = weights * (1.0 / jnp.sum(weights, axis=0, keepdims=True))
         grad_shares = nt(values, grads)
         inner = jnp.sum(shares * grad_shares, axis=0, keepdims=True)
         grad_scores = (shares * (grad_shares - inner)).astype(low_type)
@@ -313,6 +313,30 @@
         out_specs=pl.BlockSpec((rows, width), lambda i: (0, i)),
         compiler_params=params("arbitrary"),
         name="widen",
+    )(array)
+
+
+def widen_each_kernel(in_ref, *out_refs):
+    size = out_refs[0].shape[0] // in_ref.shape[0]
+    for i, out_ref in enumerate(out_refs):
+        part = in_ref[:, i * size : (i + 1) * size].astype(jnp.float32)
+        out_ref[...] = part.reshape(out_ref.shape)
+
+
+def rows_of_each(array, size, count):
+    blocks, unused, width = array.shape
+    if size % 16:
+        parts = [array[:, i * size : (i + 1) * size].astype(jnp.float32) for i in range(count)]
+        return [part.reshape(blocks * size, width) for part in parts]
+    half = width // 2
+    return pl.pallas_call(
+        widen_each_kernel,
+        out_shape=[jax.ShapeDtypeStruct((blocks * size, width), jnp.float32)] * count,
+        grid=(2,),
+        in_specs=[pl.BlockSpec((blocks, array.shape[1], half), lambda i: (0, 0, i))],
+        out_specs=[pl.BlockSpec((blocks * size, half), lambda i: (0, i))] * count,
+        compiler_params=params("arbitrary"),
+        name="widen_each",
     )(array)
 
 
@@ -766,9 +790,9 @@
     tall = jnp.pad(rows_of_pair, ((0, 0), (0, 384 - features), (0, 0)))
     tall = lax.dynamic_update_slice(tall, small.astype(low_type), (0, 264, 0))
     grad_query = unit(grad_query)
-    sums_two, arrived_two = over_chips([two, three], grad_query)
     five = Group(plan, [grad_query, tall.reshape(shards, -1, model)])
-    five.send = after(five.send, four.over_fsdp(grad_query), arrived_two)
+    five.send = after(five.send, four.over_fsdp(grad_query))
+    sums_two, arrived_two = over_chips([two, three], five.send)
     early_sums = from_all([sums_one, sums_two])
     sums_four, unused = over_chips([four])
     five.over_core()
@@ -782,7 +806,8 @@
     grad_triple = side_by_side_rows(early_sums, 2, size, 3)
     (grad_self_out,) = gathered(early_sums[:, 5 * size :], [size])
     latents_grad = plan.placed(latents_grad).astype(jnp.float32)
-    grad_up, grad_down, grad_out, grad_query, tall = gathered(late_sums, four.sizes + five.sizes)
+    grad_up, grad_down, grad_out, grad_query = rows_of_each(late_sums, size, 4)
+    (tall,) = gathered(late_sums[:, 4 * size :], five.sizes[1:])
     tall = tall.reshape(384, width)
     norm_part = tall[264:268].reshape(8, model // shards)
     pixel_part = tall[268 : 268 + pixel_rows.shape[1]].reshape(2, 512)

time: 660 us -> 638 us (0.967)
  local copies, waits for them, and re-layouts: 66 us -> 55.6 us
  other arithmetic: 121 us -> 113 us
    reshape x8 -> x4, other arithmetic: 12.8 us -> 5.11 us  [gathered(): results.append(part.reshape(-1, part.shape[2]))]
    unnamed x285 -> x273, local copies, waits for them, and re-layouts: 14.6 us -> 12.2 us
  transfers between devices with their start and end apart: 40 -> 40, of which waited for: 13 -> 14; matrix products, arithmetic and copies ran while one was open for 37% -> 36% of each run, Pallas kernels for 9% -> 9%
where the time goes in v8:
time: 638 us; the launch traced here: 630 us
  waiting for transfers between devices  203 us (32%)
  other arithmetic  113 us (18%)
  matrix products  107 us (17%)
  starting transfers between devices  70.8 us (11%)
  Pallas kernels  64.8 us (10%)
  local copies, waits for them, and re-layouts  55.6 us (9%)
  between operations  16.1 us (3%)
    ppermute x27, waiting for transfers between devices, swap(): return lax.ppermute(array, axis_name, [(i, i ^ mask) for i in range(size)])  97.4 us
    all_to_all x4, waiting for transfers between devices, over_chips(): lax.all_to_all(total, 'blk', split_axis=0, concat_axis=0, axis_index_grou...  63.8 us
    dot_general x10, matrix products, product_nt(): lax.dot_general(a, b, (((1,), (1,)), ((), ())), preferred_element_type=jn...  45.2 us
    dot_general x12, matrix products, product_tn(): lax.dot_general(a, b, (((0,), (0,)), ((), ())), preferred_element_type=jn...  31.3 us
    dot_general x10, matrix products, product(): return jnp.dot(a, b, preferred_element_type=jnp.float32)  30.3 us
    all_to_all x1, waiting for transfers between devices, route_pixels(): lax.all_to_all(pieces, 'blk', split_axis=0, concat_axis=0, tiled=True)  28.8 us
    all_to_all x4, starting transfers between devices, over_chips(): lax.all_to_all(total, 'blk', split_axis=0, concat_axis=0, axis_index_grou...  23.7 us
    ppermute x27, starting transfers between devices, swap(): return lax.ppermute(array, axis_name, [(i, i ^ mask) for i in range(size)])  21 us
  transfers between devices with their start and end apart: 40, of which 14 were waited for; matrix products, arithmetic and copies ran while one was open for 36% of the time, Pallas kernels for 9%

profile of v8, /device:TPU:0, one launch (start us, length us, event | category | flops | bytes accessed | tf_op | source)
XLA Modules:
  0.0 629.8 jit_solution(12651569777253988389)
XLA Ops:
  12.4 5.1 prepare_pixels.1
  17.5 7.5 %all-to-all-start = ((bf16[16,2,272,128]{3,2,1,0:T(8,128)(2,1)}), bf16[16,2,272,128]{3,2,1,0:T(8,128)(2,1)S(1)}, u32[]{:S(2)}, u32[]{:S(2)}) async-start(bf16[16,2,272,128]{3,2,1,0:T(8,128)(2,1)} %prepare_pixels.1), calls=%async_computation | async-start | bytes 4456448 | tf_op jit(solution)/shard_map/all_to_all | solution.py:554
  43.8 25.6 %collective-permute-done = bf16[256,1024]{1,0:T(8,128)(2,1)} collective-permute-done((bf16[256,1024]{1,0:T(8,128)(2,1)}, bf16[256,1024]{1,0:T(8,128)(2,1)}, u32[]{:S(2)}, u32[]{:S(2)}) %collective-permute-start) | collective-permute-done | bytes 524320 | tf_op jit(solution)/shard_map/ppermute | solution.py:356
  89.4 9.1 %all-to-all-start.1 = ((bf16[16,2,272,128]{3,2,1,0:T(8,128)(2,1)}), bf16[16,2,272,128]{3,2,1,0:T(8,128)(2,1)S(1)}, u32[]{:S(2)}, u32[]{:S(2)}) async-start(bf16[16,2,272,128]{3,2,1,0:T(8,128)(2,1)} %bitcast.202), calls=%async_computation.1 | async-start | bytes 4456448 | tf_op jit(solution)/shard_map/all_to_all | solution.py:586
  125.1 28.8 %all-to-all-done.1.first_ref = bf16[16,2,272,128]{3,2,1,0:T(8,128)(2,1)S(1)} async-done(((bf16[16,2,272,128]{3,2,1,0:T(8,128)(2,1)}), bf16[16,2,272,128]{3,2,1,0:T(8,128)(2,1)S(1)}, u32[]{:S(2)}, u32[]{:S(2)}) %all-to-all-start.1) | async-done | bytes 2228256 | tf_op jit(solution)/shard_map/all_to_all | solution.py:586
  158.2 8.3 %cross_attention.2 = f32[768,272]{1,0:T(8,128)} custom-call(s32[2]{0:T(128)} %get-tuple-element.228.big_ref, bf16[768,272]{1,0:T(8,128)(2,1)} %pad.22.query_ref, bf16[16,2,272,128]{3,2,1,0:T(8,128)(2,1)} %copy-done.1, bf16[16,2,272,128]{3,2,1,0:T(8,128)(2,1)} %bitcast.200, f32[2,8,4096]{2,1,0:T(8,128)} %broadcast_in_dim.80.mask_ref), custom_call_target="tpu_custom_call" | custom-call | tf_op jit(solution)/shard_map/cross_attention/pallas_call | solution.py:174
  170.0 5.9 collective-permute-start.15
  199.4 5.3 convolution_convert_fusion.q_ref.k_ref.v_ref
  211.3 10.8 %self_forward.1 = bf16[768,1024]{1,0:T(8,128)(2,1)} custom-call(bf16[768,3072]{1,0:T(8,128)(2,1)} %copy-done, bf16[768,3072]{1,0:T(8,128)(2,1)} %copy-done, bf16[768,3072]{1,0:T(8,128)(2,1)} %copy-done, bf16[256,2048]{1,0:T(8,128)(2,1)} %collective-permute-done.10.more_k_ref.more_v_ref, bf16[256,2048]{1,0:T(8,128)(2,1)} %collective-permute-done.10.more_k_ref.more_v_ref), custom_call_target="tpu_custom_call" | custom-call | tf_op jit(solution)/shard_map/self_forward/pallas_call | solution.py:266
  233.8 3.8 fusion.21
  244.3 5.7 multiply_reduce_fusion
  263.3 19.8 %self_backward.1 = (bf16[768,3072]{1,0:T(8,128)(2,1)}, bf16[256,2048]{1,0:T(8,128)(2,1)}) custom-call(bf16[768,3072]{1,0:T(8,128)(2,1)} %copy-done, bf16[768,3072]{1,0:T(8,128)(2,1)} %copy-done, bf16[768,3072]{1,0:T(8,128)(2,1)} %copy-done, bf16[256,2048]{1,0:T(8,128)(2,1)} %collective-permute-done.10.more_k_ref.more_v_ref, ...), custom_call_target="tpu_custom_call" | custom-call | tf_op jit(solution)/shard_map/self_backward/pallas_call | solution.py:281
  291.3 10.0 %all-to-all-start.2 = ((bf16[8,64,1024]{2,1,0:T(8,128)(2,1)}), bf16[8,64,1024]{2,1,0:T(8,128)(2,1)}, u32[]{:S(2)}, u32[]{:S(2)}) async-start(bf16[8,64,1024]{2,1,0:T(8,128)(2,1)} %fusion.46), calls=%async_computation.2 | async-start | bytes 2097152 | tf_op jit(solution)/shard_map/all_to_all | solution.py:519
  317.7 9.6 %multiply_reduce_fusion.1 = (bf16[1024]{0:T(1024)(128)(2,1)S(1)}, f32[768]{0:T(1024)S(1)}, f32[768]{0:T(1024)S(1)}, bf16[1024]{0:T(1024)(128)(2,1)S(1)}, f32[768,1024]{1,0:T(8,128)}) fusion(f32[768,1024]{1,0:T(8,128)S(1)} %get-tuple-element.336, f32[768]{0:T(1024)S(1)} %add_rsqrt_fusion.1, f32[768]{0:T(1024)S(1)} %broadcast_multiply_fusion.10, ...), kind=kOutput, calls=%fused_computation.54 | convolution fusion | flops 4851494912 | bytes 17321984 | tf_op jit(solution)/shard_map/dot_general | solution.py:28
  351.1 9.6 %collective-permute-done.20 = bf16[1,8,64,1024]{3,2,1,0:T(8,128)(2,1)} collective-permute-done((bf16[1,8,64,1024]{3,2,1,0:T(8,128)(2,1)S(1)}, bf16[1,8,64,1024]{3,2,1,0:T(8,128)(2,1)}, u32[]{:S(2)}, u32[]{:S(2)}) %collective-permute-start.20) | collective-permute-done | bytes 1048608 | tf_op jit(solution)/shard_map/ppermute | solution.py:356
  370.0 3.9 convolution_convert_fusion.12
  378.5 9.9 %cross_attention.3 = f32[768,272]{1,0:T(8,128)} custom-call(s32[2]{0:T(128)} %get-tuple-element.228.big_ref, bf16[768,272]{1,0:T(8,128)(2,1)} %pad.22.query_ref, bf16[768,272]{1,0:T(8,128)(2,1)} %fusion.64.grad_ref, bf16[16,2,272,128]{3,2,1,0:T(8,128)(2,1)} %copy-done.1, bf16[16,2,272,128]{3,2,1,0:T(8,128)(2,1)} %bitcast.201, ...), custom_call_target="tpu_custom_call" | custom-call | tf_op jit(solution)/shard_map/cross_attention/pallas_call | solution.py:174
  388.4 5.1 collective-permute-done.22
  399.1 5.7 all-to-all-start.5
  417.0 5.9 fusion.10
  437.0 11.6 %collective-permute-done.24 = bf16[1,8,96,1024]{3,2,1,0:T(8,128)(2,1)} collective-permute-done((bf16[1,8,96,1024]{3,2,1,0:T(8,128)(2,1)}, bf16[1,8,96,1024]{3,2,1,0:T(8,128)(2,1)}, u32[]{:S(2)}, u32[]{:S(2)}) %collective-permute-start.24) | collective-permute-done | bytes 1572896 | tf_op jit(solution)/shard_map/ppermute | solution.py:356
  448.6 4.4 all-to-all-done.5
  455.9 4.1 fusion.30
  466.0 22.0 %collective-permute-done.26 = bf16[1,8,56,1024]{3,2,1,0:T(8,128)(2,1)S(1)} collective-permute-done((bf16[1,8,56,1024]{3,2,1,0:T(8,128)(2,1)S(1)}, bf16[1,8,56,1024]{3,2,1,0:T(8,128)(2,1)S(1)}, u32[]{:S(2)}, u32[]{:S(2)}) %collective-permute-start.26) | collective-permute-done | bytes 917536 | tf_op jit(solution)/shard_map/ppermute | solution.py:356
  490.7 35.7 %all-to-all-done.3 = bf16[8,96,1024]{2,1,0:T(8,128)(2,1)S(1)} async-done(((bf16[8,96,1024]{2,1,0:T(8,128)(2,1)}), bf16[8,96,1024]{2,1,0:T(8,128)(2,1)S(1)}, u32[]{:S(2)}, u32[]{:S(2)}) %all-to-all-start.3) | async-done | bytes 1572896 | tf_op jit(solution)/shard_map/all_to_all | solution.py:519
  527.5 4.2 all-to-all-start.4
  533.9 23.7 %all-to-all-done.4 = bf16[8,56,1024]{2,1,0:T(8,128)(2,1)} async-done(((bf16[8,56,1024]{2,1,0:T(8,128)(2,1)}), bf16[8,56,1024]{2,1,0:T(8,128)(2,1)}, u32[]{:S(2)}, u32[]{:S(2)}) %all-to-all-start.4) | async-done | bytes 917536 | tf_op jit(solution)/shard_map/all_to_all | solution.py:519
  566.6 9.1 %collective-permute-done.27 = bf16[256,1024]{1,0:T(8,128)(2,1)S(1)} collective-permute-done((bf16[256,1024]{1,0:T(8,128)(2,1)S(1)}, bf16[256,1024]{1,0:T(8,128)(2,1)S(1)}, u32[]{:S(2)}, u32[]{:S(2)}) %collective-permute-start.27) | collective-permute-done | bytes 524320 | tf_op jit(solution)/shard_map/ppermute | solution.py:356
  576.5 9.5 %collective-permute-done.29 = bf16[256,1024]{1,0:T(8,128)(2,1)S(1)} collective-permute-done((bf16[256,1024]{1,0:T(8,128)(2,1)S(1)}, bf16[256,1024]{1,0:T(8,128)(2,1)S(1)}, u32[]{:S(2)}, u32[]{:S(2)}) %collective-permute-start.29) | collective-permute-done | bytes 524320 | tf_op jit(solution)/shard_map/ppermute | solution.py:356
  590.0 5.8 widen.1
  601.0 12.5 %all-gather.9.cloned.1.call-done = bf16[2432,1024]{1,0:T(8,128)(2,1)} async-done(((bf16[152,1024]{1,0:T(8,128)(2,1)}), bf16[2432,1024]{1,0:T(8,128)(2,1)}) %all-gather.9.cloned.1.call-update) | async-done | bytes 4980752 | tf_op jit(solution)/shard_map/all_gather | solution.py:527
  616.1 5.2 widen_each.1
  (541 shorter events, 270.6 us)
Async XLA Ops:
  17.5 53.1 %all-to-all-start = ((bf16[16,2,272,128]{3,2,1,0:T(8,128)(2,1)}), bf16[16,2,272,128]{3,2,1,0:T(8,128)(2,1)S(1)}, u32[]{:S(2)}, u32[]{:S(2)}) async-start(bf16[16,2,272,128]{3,2,1,0:T(8,128)(2,1)} %prepare_pixels.1), calls=%async_computation | async-start | bytes 4456448 | tf_op jit(solution)/shard_map/all_to_all | solution.py:554
  25.1 132.4 %all-gather.7.cloned.1.call-start = ((), (), s32[]{:S(2)}) async-start(), calls=%async_computation.6 | async-start | bytes 2367488 | tf_op jit(solution)/shard_map/all_gather | solution.py:590
  26.0 17.8 %collective-permute-start.3 = (bf16[256,1024]{1,0:T(8,128)(2,1)}, bf16[256,1024]{1,0:T(8,128)(2,1)}, u32[]{:S(2)}, u32[]{:S(2)}) collective-permute-start(bf16[256,1024]{1,0:T(8,128)(2,1)} %constant_dynamic-slice_fusion.7), channel_id=1, source_target_pairs={{0,1},{1,0},{2,3},{3,2},{4,5},{5,4},{6,7},{7,6},{8,9},{9,8},{10,11... | collective-permute-start | bytes 1572872 | tf_op jit(solution)/shard_map/ppermute | solution.py:356
  29.4 39.9 %collective-permute-start.2 = (bf16[265,1024]{1,0:T(8,128)(2,1)}, bf16[265,1024]{1,0:T(8,128)(2,1)}, u32[]{:S(2)}, u32[]{:S(2)}) collective-permute-start(bf16[265,1024]{1,0:T(8,128)(2,1)} %pad_maximum_fusion.41), channel_id=1, source_target_pairs={{0,1},{1,0},{2,3},{3,2},{4,5},{5,4},{6,7},{7,6},{8,9},{9,8},{10,11... | collective-permute-start | bytes 1628168 | tf_op jit(solution)/shard_map/ppermute | solution.py:356
  32.4 11.4 %collective-permute-start.1 = (bf16[256,1024]{1,0:T(8,128)(2,1)}, bf16[256,1024]{1,0:T(8,128)(2,1)S(1)}, u32[]{:S(2)}, u32[]{:S(2)}) collective-permute-start(bf16[256,1024]{1,0:T(8,128)(2,1)} %get-tuple-element.302), channel_id=1, source_target_pairs={{0,0},{2,1},{4,4},{6,5},{8,8},{10,9},{12,12},{14,13},{16,16},{18,1... | collective-permute-start | bytes 1572872 | tf_op jit(solution)/shard_map/ppermute | solution.py:399
  34.2 35.1 %collective-permute-start = (bf16[256,1024]{1,0:T(8,128)(2,1)}, bf16[256,1024]{1,0:T(8,128)(2,1)}, u32[]{:S(2)}, u32[]{:S(2)}) collective-permute-start(bf16[256,1024]{1,0:T(8,128)(2,1)} %get-tuple-element.303), channel_id=1, source_target_pairs={{0,1},{1,0},{2,3},{3,2},{4,5},{5,4},{6,7},{7,6},{8,9},{9,8},{10,11... | collective-permute-start | bytes 1572872 | tf_op jit(solution)/shard_map/ppermute | solution.py:356
  70.6 42.0 %collective-permute-start.5 = (bf16[256,3072]{1,0:T(8,128)(2,1)}, bf16[256,3072]{1,0:T(8,128)(2,1)}, u32[]{:S(2)}, u32[]{:S(2)}) collective-permute-start(bf16[256,3072]{1,0:T(8,128)(2,1)} %pad_maximum_fusion.19), channel_id=1, source_target_pairs={{0,1},{1,0},{2,3},{3,2},{4,5},{5,4},{6,7},{7,6},{8,9},{9,8},{10,11... | collective-permute-start | bytes 4718600 | tf_op jit(solution)/shard_map/ppermute | solution.py:356
  83.3 19.1 %collective-permute-start.4 = (bf16[256,1024]{1,0:T(8,128)(2,1)}, bf16[256,1024]{1,0:T(8,128)(2,1)}, u32[]{:S(2)}, u32[]{:S(2)}) collective-permute-start(bf16[256,1024]{1,0:T(8,128)(2,1)} %collective-permute-done.3), channel_id=1, source_target_pairs={{0,2},{2,0},{4,6},{6,4},{8,10},{10,8},{12,14},{14,12},{16,18},{18,... | collective-permute-start | bytes 1572872 | tf_op jit(solution)/shard_map/ppermute | solution.py:356
  89.4 64.6 %all-to-all-start.1 = ((bf16[16,2,272,128]{3,2,1,0:T(8,128)(2,1)}), bf16[16,2,272,128]{3,2,1,0:T(8,128)(2,1)S(1)}, u32[]{:S(2)}, u32[]{:S(2)}) async-start(bf16[16,2,272,128]{3,2,1,0:T(8,128)(2,1)} %bitcast.202), calls=%async_computation.1 | async-start | bytes 4456448 | tf_op jit(solution)/shard_map/all_to_all | solution.py:586
  100.8 24.3 %collective-permute-start.7 = (bf16[128,3072]{1,0:T(8,128)(2,1)S(1)}, bf16[128,3072]{1,0:T(8,128)(2,1)}, u32[]{:S(2)}, u32[]{:S(2)}) collective-permute-start(bf16[128,3072]{1,0:T(8,128)(2,1)S(1)} %constant_dynamic-slice_fusion.3), channel_id=1, source_target_pairs={{0,1},{1,0},{2,3},{3,2},{4,5},{5,4},{6,7},{7,6},{8,9},{9,8},{10,11... | collective-permute-start | bytes 2359304 | tf_op jit(solution)/shard_map/ppermute | solution.py:356
  113.8 54.3 %collective-permute-start.11 = (bf16[128,3072]{1,0:T(8,128)(2,1)}, bf16[128,3072]{1,0:T(8,128)(2,1)}, u32[]{:S(2)}, u32[]{:S(2)}) collective-permute-start(bf16[128,3072]{1,0:T(8,128)(2,1)} %pad_maximum_fusion.40), channel_id=1, source_target_pairs={{0,1},{1,0},{2,3},{3,2},{4,5},{5,4},{6,7},{7,6},{8,9},{9,8},{10,11... | collective-permute-start | bytes 2359304 | tf_op jit(solution)/shard_map/ppermute | solution.py:356
  154.0 36.4 %collective-permute-start.8 = (bf16[128,3072]{1,0:T(8,128)(2,1)}, bf16[128,3072]{1,0:T(8,128)(2,1)}, u32[]{:S(2)}, u32[]{:S(2)}) collective-permute-start(bf16[128,3072]{1,0:T(8,128)(2,1)} %collective-permute-done.7), channel_id=1, source_target_pairs={{0,4},{2,6},{4,0},{6,2},{8,12},{10,14},{12,8},{14,10},{16,20},{18,... | collective-permute-start | bytes 2359304 | tf_op jit(solution)/shard_map/ppermute | solution.py:356
  168.1 25.8 %collective-permute-start.12 = (bf16[128,3072]{1,0:T(8,128)(2,1)}, bf16[128,3072]{1,0:T(8,128)(2,1)S(1)}, u32[]{:S(2)}, u32[]{:S(2)}) collective-permute-start(bf16[128,3072]{1,0:T(8,128)(2,1)} %collective-permute-done.11), channel_id=1, source_target_pairs={{0,4},{2,6},{4,0},{6,2},{8,12},{10,14},{12,8},{14,10},{16,20},{18,... | collective-permute-start | bytes 2359304 | tf_op jit(solution)/shard_map/ppermute | solution.py:356
  170.0 55.4 %collective-permute-start.15 = (bf16[256,1024]{1,0:T(8,128)(2,1)}, bf16[256,1024]{1,0:T(8,128)(2,1)}, u32[]{:S(2)}, u32[]{:S(2)}) collective-permute-start(bf16[256,1024]{1,0:T(8,128)(2,1)} %get-tuple-element.295), channel_id=1, source_target_pairs={{0,0},{2,1},{4,4},{6,5},{8,8},{10,9},{12,12},{14,13},{16,16},{18,1... | collective-permute-start | bytes 1572872 | tf_op jit(solution)/shard_map/ppermute | solution.py:399
  175.9 49.5 %collective-permute-start.14 = (bf16[256,1024]{1,0:T(8,128)(2,1)}, bf16[256,1024]{1,0:T(8,128)(2,1)}, u32[]{:S(2)}, u32[]{:S(2)}) collective-permute-start(bf16[256,1024]{1,0:T(8,128)(2,1)} %get-tuple-element.296), channel_id=1, source_target_pairs={{0,1},{1,0},{2,3},{3,2},{4,5},{5,4},{6,7},{7,6},{8,9},{9,8},{10,11... | collective-permute-start | bytes 1572872 | tf_op jit(solution)/shard_map/ppermute | solution.py:356
  252.9 30.2 %collective-permute-start.17 = (bf16[1,8,64,1024]{3,2,1,0:T(8,128)(2,1)}, bf16[1,8,64,1024]{3,2,1,0:T(8,128)(2,1)}, u32[]{:S(2)}, u32[]{:S(2)}) collective-permute-start(bf16[1,8,64,1024]{3,2,1,0:T(8,128)(2,1)} %add_convert_fusion.16), channel_id=1, source_target_pairs={{0,1},{1,0},{2,3},{3,2},{4,5},{5,4},{6,7},{7,6},{8,9},{9,8},{10,11... | collective-permute-start | bytes 3145736 | tf_op jit(solution)/shard_map/ppermute | solution.py:356
  283.0 18.3 %collective-permute-start.18 = (bf16[256,2048]{1,0:T(8,128)(2,1)}, bf16[256,2048]{1,0:T(8,128)(2,1)}, u32[]{:S(2)}, u32[]{:S(2)}) collective-permute-start(bf16[256,2048]{1,0:T(8,128)(2,1)} %get-tuple-element.77), channel_id=1, source_target_pairs={{0,2},{2,0},{4,6},{6,4},{8,10},{10,8},{12,14},{14,12},{16,18},{18,... | collective-permute-start | bytes 3145736 | tf_op jit(solution)/shard_map/ppermute | solution.py:356
  291.3 69.4 %all-to-all-start.2 = ((bf16[8,64,1024]{2,1,0:T(8,128)(2,1)}), bf16[8,64,1024]{2,1,0:T(8,128)(2,1)}, u32[]{:S(2)}, u32[]{:S(2)}) async-start(bf16[8,64,1024]{2,1,0:T(8,128)(2,1)} %fusion.46), calls=%async_computation.2 | async-start | bytes 2097152 | tf_op jit(solution)/shard_map/all_to_all | solution.py:519
  314.0 19.4 %collective-permute-start.19 = (bf16[2,8,64,1024]{3,2,1,0:T(8,128)(2,1)}, bf16[2,8,64,1024]{3,2,1,0:T(8,128)(2,1)}, u32[]{:S(2)}, u32[]{:S(2)}) collective-permute-start(bf16[2,8,64,1024]{3,2,1,0:T(8,128)(2,1)} %pad_maximum_fusion.14), channel_id=1, source_target_pairs={{0,2},{2,0},{4,6},{6,4},{8,10},{10,8},{12,14},{14,12},{16,18},{18,... | collective-permute-start | bytes 6291464 | tf_op jit(solution)/shard_map/ppermute | solution.py:356
  316.0 29.2 %collective-permute-start.21 = (bf16[2,8,64,1024]{3,2,1,0:T(8,128)(2,1)}, bf16[2,8,64,1024]{3,2,1,0:T(8,128)(2,1)}, u32[]{:S(2)}, u32[]{:S(2)}) collective-permute-start(bf16[2,8,64,1024]{3,2,1,0:T(8,128)(2,1)} %pad_maximum_fusion.15), channel_id=1, source_target_pairs={{0,2},{2,0},{4,6},{6,4},{8,10},{10,8},{12,14},{14,12},{16,18},{18,... | collective-permute-start | bytes 6291464 | tf_op jit(solution)/shard_map/ppermute | solution.py:356
  335.2 25.4 %collective-permute-start.20 = (bf16[1,8,64,1024]{3,2,1,0:T(8,128)(2,1)S(1)}, bf16[1,8,64,1024]{3,2,1,0:T(8,128)(2,1)}, u32[]{:S(2)}, u32[]{:S(2)}) collective-permute-start(bf16[1,8,64,1024]{3,2,1,0:T(8,128)(2,1)S(1)} %add_convert_fusion.14), channel_id=1, source_target_pairs={{0,1},{1,0},{2,3},{3,2},{4,5},{5,4},{6,7},{7,6},{8,9},{9,8},{10,11... | collective-permute-start | bytes 3145736 | tf_op jit(solution)/shard_map/ppermute | solution.py:356
  367.6 41.6 %collective-permute-start.23 = (bf16[2,8,96,1024]{3,2,1,0:T(8,128)(2,1)}, bf16[2,8,96,1024]{3,2,1,0:T(8,128)(2,1)}, u32[]{:S(2)}, u32[]{:S(2)}) collective-permute-start(bf16[2,8,96,1024]{3,2,1,0:T(8,128)(2,1)} %pad_maximum_fusion.4), channel_id=1, source_target_pairs={{0,2},{2,0},{4,6},{6,4},{8,10},{10,8},{12,14},{14,12},{16,18},{18,... | collective-permute-start | bytes 9437192 | tf_op jit(solution)/shard_map/ppermute | solution.py:356
  367.7 25.8 %collective-permute-start.22 = (bf16[1,8,64,1024]{3,2,1,0:T(8,128)(2,1)}, bf16[1,8,64,1024]{3,2,1,0:T(8,128)(2,1)S(1)}, u32[]{:S(2)}, u32[]{:S(2)}) collective-permute-start(bf16[1,8,64,1024]{3,2,1,0:T(8,128)(2,1)} %add_convert_fusion.13), channel_id=1, source_target_pairs={{0,1},{1,0},{2,3},{3,2},{4,5},{5,4},{6,7},{7,6},{8,9},{9,8},{10,11... | collective-permute-start | bytes 3145736 | tf_op jit(solution)/shard_map/ppermute | solution.py:356
  399.1 53.9 %all-to-all-start.5 = ((bf16[8,128,1024]{2,1,0:T(8,128)(2,1)}), bf16[8,128,1024]{2,1,0:T(8,128)(2,1)}, u32[]{:S(2)}, u32[]{:S(2)}) async-start(bf16[8,128,1024]{2,1,0:T(8,128)(2,1)} %pad_maximum_fusion.16), calls=%async_computation.5 | async-start | bytes 4194304 | tf_op jit(solution)/shard_map/all_to_all | solution.py:519
  404.8 185.1 %all-gather.11.cloned.1.call-start = ((), (), s32[]{:S(2)}) async-start(), calls=%async_computation.8 | async-start | bytes 6684672 | tf_op jit(solution)/shard_map/all_gather | solution.py:527
  412.6 36.0 %collective-permute-start.24 = (bf16[1,8,96,1024]{3,2,1,0:T(8,128)(2,1)}, bf16[1,8,96,1024]{3,2,1,0:T(8,128)(2,1)}, u32[]{:S(2)}, u32[]{:S(2)}) collective-permute-start(bf16[1,8,96,1024]{3,2,1,0:T(8,128)(2,1)} %add_convert_fusion.2), channel_id=1, source_target_pairs={{0,1},{1,0},{2,3},{3,2},{4,5},{5,4},{6,7},{7,6},{8,9},{9,8},{10,11... | collective-permute-start | bytes 4718600 | tf_op jit(solution)/shard_map/ppermute | solution.py:356
  459.9 66.4 %all-to-all-start.3 = ((bf16[8,96,1024]{2,1,0:T(8,128)(2,1)}), bf16[8,96,1024]{2,1,0:T(8,128)(2,1)S(1)}, u32[]{:S(2)}, u32[]{:S(2)}) async-start(bf16[8,96,1024]{2,1,0:T(8,128)(2,1)} %fusion.30), calls=%async_computation.3 | async-start | bytes 3145728 | tf_op jit(solution)/shard_map/all_to_all | solution.py:519
  465.3 22.8 %collective-permute-start.26 = (bf16[1,8,56,1024]{3,2,1,0:T(8,128)(2,1)S(1)}, bf16[1,8,56,1024]{3,2,1,0:T(8,128)(2,1)S(1)}, u32[]{:S(2)}, u32[]{:S(2)}) collective-permute-start(bf16[1,8,56,1024]{3,2,1,0:T(8,128)(2,1)S(1)} %add_convert_fusion.19), channel_id=1, source_target_pairs={{0,1},{1,0},{2,3},{3,2},{4,5},{5,4},{6,7},{7,6},{8,9},{9,8},{10,11... | collective-permute-start | bytes 2752520 | tf_op jit(solution)/shard_map/ppermute | solution.py:356
  527.5 30.1 %all-to-all-start.4 = ((bf16[8,56,1024]{2,1,0:T(8,128)(2,1)}), bf16[8,56,1024]{2,1,0:T(8,128)(2,1)}, u32[]{:S(2)}, u32[]{:S(2)}) async-start(bf16[8,56,1024]{2,1,0:T(8,128)(2,1)} %fusion.59), calls=%async_computation.4 | async-start | bytes 1835008 | tf_op jit(solution)/shard_map/all_to_all | solution.py:519
  531.8 81.8 %all-gather.9.cloned.1.call-start = ((), (), s32[]{:S(2)}) async-start(), calls=%async_computation.7 | async-start | bytes 5292032 | tf_op jit(solution)/shard_map/all_gather | solution.py:527
  560.8 14.9 %collective-permute-start.27 = (bf16[256,1024]{1,0:T(8,128)(2,1)S(1)}, bf16[256,1024]{1,0:T(8,128)(2,1)S(1)}, u32[]{:S(2)}, u32[]{:S(2)}) collective-permute-start(bf16[256,1024]{1,0:T(8,128)(2,1)S(1)} %slice.203), channel_id=1, source_target_pairs={{0,1},{1,0},{2,3},{3,2},{4,5},{5,4},{6,7},{7,6},{8,9},{9,8},{10,11... | collective-permute-start | bytes 1572872 | tf_op jit(solution)/shard_map/ppermute | solution.py:356
  566.0 19.9 %collective-permute-start.29 = (bf16[256,1024]{1,0:T(8,128)(2,1)S(1)}, bf16[256,1024]{1,0:T(8,128)(2,1)S(1)}, u32[]{:S(2)}, u32[]{:S(2)}) collective-permute-start(bf16[256,1024]{1,0:T(8,128)(2,1)S(1)} %slice.206), channel_id=1, source_target_pairs={{0,1},{1,0},{2,3},{3,2},{4,5},{5,4},{6,7},{7,6},{8,9},{9,8},{10,11... | collective-permute-start | bytes 1572872 | tf_op jit(solution)/shard_map/ppermute | solution.py:356
  (140 other events, 1238.4 us)
Sparse Core Ops, SparseCore 0:
  83.4 70.3 all-gather.6
  455.9 88.3 all-gather.10
  559.8 53.6 all-gather.8

commit v9 on v8

--- a/solution.py
+++ b/solution.py
@@ -794,13 +794,12 @@
     five.send = after(five.send, four.over_fsdp(grad_query))
     sums_two, arrived_two = over_chips([two, three], five.send)
     early_sums = from_all([sums_one, sums_two])
-    sums_four, unused = over_chips([four])
     five.over_core()
     arrived = five.over_fsdp()
     mixed = plan.send_back(after(mixed, arrived))
     latents_grad = plan.send_back(after(latents_grad, arrived))
-    sums_five, unused = over_chips([five])
-    late_sums = from_all([sums_four, sums_five])
+    sums_late, unused = over_chips([four, five])
+    late_sums = from_all([sums_late])
     size = one.sizes[0]
     grad_self_up, grad_self_down = gathered(early_sums, one.sizes)
     grad_triple = side_by_side_rows(early_sums, 2, size, 3)

time: 638 us -> 646 us (1.013)
  blocking collectives: 0 us -> 81 us
  waiting for transfers between devices: 203 us -> 139 us
  starting transfers between devices: 70.8 us -> 56.2 us
  Pallas kernels: 64.8 us -> 74.3 us
    all_to_all x0 -> x1, blocking collectives: none -> 81 us  [over_chips(): lax.all_to_all(total, 'blk', split_axis=0, concat_axis=0, axis_index_grou...]
    all_to_all x4 -> x2, waiting for transfers between devices: 63.8 us -> 4.4 us  [over_chips(): lax.all_to_all(total, 'blk', split_axis=0, concat_axis=0, axis_index_grou...]
    all_to_all x4 -> x2, starting transfers between devices: 23.7 us -> 11.5 us  [over_chips(): lax.all_to_all(total, 'blk', split_axis=0, concat_axis=0, axis_index_grou...]
    pallas_call x2, Pallas kernels: 18.2 us -> 27.7 us  [cross_call(): pl.pallas_call(functools.partial(kernel, per_item), out_shape=jax.ShapeDt...]
  transfers between devices with their start and end apart: 40 -> 38, of which waited for: 14 -> 13; matrix products, arithmetic and copies ran while one was open for 36% -> 35% of each run, Pallas kernels for 9% -> 10%
where the time goes in v9:
time: 646 us; the launch traced here: 639 us
  waiting for transfers between devices  139 us (22%)
  other arithmetic  109 us (17%)
  matrix products  107 us (17%)
  blocking collectives  81 us (13%)
  Pallas kernels  74.3 us (12%)
  starting transfers between devices  56.2 us (9%)
  local copies, waits for them, and re-layouts  56.1 us (9%)
  between operations  16.1 us (2%)
    ppermute x27, waiting for transfers between devices, swap(): return lax.ppermute(array, axis_name, [(i, i ^ mask) for i in range(size)])  92.9 us
    all_to_all x1, blocking collectives, over_chips(): lax.all_to_all(total, 'blk', split_axis=0, concat_axis=0, axis_index_grou...  81 us
    dot_general x10, matrix products, product_nt(): lax.dot_general(a, b, (((1,), (1,)), ((), ())), preferred_element_type=jn...  45.2 us
    dot_general x12, matrix products, product_tn(): lax.dot_general(a, b, (((0,), (0,)), ((), ())), preferred_element_type=jn...  31.3 us
    dot_general x10, matrix products, product(): return jnp.dot(a, b, preferred_element_type=jnp.float32)  30.3 us
    all_to_all x1, waiting for transfers between devices, route_pixels(): lax.all_to_all(pieces, 'blk', split_axis=0, concat_axis=0, tiled=True)  28.8 us
    pallas_call x2, Pallas kernels, cross_call(): pl.pallas_call(functools.partial(kernel, per_item), out_shape=jax.ShapeDt...  27.7 us
    pallas_call x1, Pallas kernels, self_backward(): pl.pallas_call(functools.partial(self_backward_kernel, groups, head ** (-...  19.8 us
  transfers between devices with their start and end apart: 38, of which 13 were waited for; matrix products, arithmetic and copies ran while one was open for 35% of the time, Pallas kernels for 10%

profile of v9, /device:TPU:0, one launch (start us, length us, event | category | flops | bytes accessed | tf_op | source)
XLA Modules:
  0.0 638.6 jit_solution(7682505067640489762)
XLA Ops:
  12.4 5.1 prepare_pixels.1
  17.5 7.5 %all-to-all-start = ((bf16[16,2,272,128]{3,2,1,0:T(8,128)(2,1)}), bf16[16,2,272,128]{3,2,1,0:T(8,128)(2,1)S(1)}, u32[]{:S(2)}, u32[]{:S(2)}) async-start(bf16[16,2,272,128]{3,2,1,0:T(8,128)(2,1)} %prepare_pixels.1), calls=%async_computation | async-start | bytes 4456448 | tf_op jit(solution)/shard_map/all_to_all | solution.py:554
  43.7 25.6 %collective-permute-done = bf16[256,1024]{1,0:T(8,128)(2,1)} collective-permute-done((bf16[256,1024]{1,0:T(8,128)(2,1)}, bf16[256,1024]{1,0:T(8,128)(2,1)}, u32[]{:S(2)}, u32[]{:S(2)}) %collective-permute-start) | collective-permute-done | bytes 524320 | tf_op jit(solution)/shard_map/ppermute | solution.py:356
  89.4 9.1 %all-to-all-start.1 = ((bf16[16,2,272,128]{3,2,1,0:T(8,128)(2,1)}), bf16[16,2,272,128]{3,2,1,0:T(8,128)(2,1)S(1)}, u32[]{:S(2)}, u32[]{:S(2)}) async-start(bf16[16,2,272,128]{3,2,1,0:T(8,128)(2,1)} %bitcast.202), calls=%async_computation.1 | async-start | bytes 4456448 | tf_op jit(solution)/shard_map/all_to_all | solution.py:586
  118.1 3.7 broadcast_select_fusion.15
  125.1 28.8 %all-to-all-done.1.first_ref = bf16[16,2,272,128]{3,2,1,0:T(8,128)(2,1)S(1)} async-done(((bf16[16,2,272,128]{3,2,1,0:T(8,128)(2,1)}), bf16[16,2,272,128]{3,2,1,0:T(8,128)(2,1)S(1)}, u32[]{:S(2)}, u32[]{:S(2)}) %all-to-all-start.1) | async-done | bytes 2228256 | tf_op jit(solution)/shard_map/all_to_all | solution.py:586
  158.2 12.4 %cross_attention.2 = f32[768,272]{1,0:T(8,128)} custom-call(s32[2]{0:T(128)} %get-tuple-element.228.big_ref, bf16[768,272]{1,0:T(8,128)(2,1)} %pad.22.query_ref, bf16[16,2,272,128]{3,2,1,0:T(8,128)(2,1)} %copy-done.1, bf16[16,2,272,128]{3,2,1,0:T(8,128)(2,1)} %bitcast.200, f32[2,8,4096]{2,1,0:T(8,128)} %broadcast_in_dim.80.mask_ref), custom_call_target="tpu_custom_call" | custom-call | tf_op jit(solution)/shard_map/cross_attention/pallas_call | solution.py:174
  173.4 5.8 collective-permute-start.15
  202.0 5.3 convolution_convert_fusion.q_ref.k_ref.v_ref
  213.9 10.8 %self_forward.1 = bf16[768,1024]{1,0:T(8,128)(2,1)} custom-call(bf16[768,3072]{1,0:T(8,128)(2,1)} %copy-done, bf16[768,3072]{1,0:T(8,128)(2,1)} %copy-done, bf16[768,3072]{1,0:T(8,128)(2,1)} %copy-done, bf16[256,2048]{1,0:T(8,128)(2,1)} %collective-permute-done.10.more_k_ref.more_v_ref, bf16[256,2048]{1,0:T(8,128)(2,1)} %collective-permute-done.10.more_k_ref.more_v_ref), custom_call_target="tpu_custom_call" | custom-call | tf_op jit(solution)/shard_map/self_forward/pallas_call | solution.py:266
  236.5 3.8 fusion.21
  246.4 5.7 multiply_reduce_fusion
  266.7 19.8 %self_backward.1 = (bf16[768,3072]{1,0:T(8,128)(2,1)}, bf16[256,2048]{1,0:T(8,128)(2,1)}) custom-call(bf16[768,3072]{1,0:T(8,128)(2,1)} %copy-done, bf16[768,3072]{1,0:T(8,128)(2,1)} %copy-done, bf16[768,3072]{1,0:T(8,128)(2,1)} %copy-done, bf16[256,2048]{1,0:T(8,128)(2,1)} %collective-permute-done.10.more_k_ref.more_v_ref, ...), custom_call_target="tpu_custom_call" | custom-call | tf_op jit(solution)/shard_map/self_backward/pallas_call | solution.py:281
  294.8 6.3 all-to-all-start.2
  317.5 9.6 %multiply_reduce_fusion.1 = (bf16[1024]{0:T(1024)(128)(2,1)S(1)}, f32[768]{0:T(1024)S(1)}, f32[768]{0:T(1024)S(1)}, bf16[1024]{0:T(1024)(128)(2,1)S(1)}, f32[768,1024]{1,0:T(8,128)}) fusion(f32[768,1024]{1,0:T(8,128)S(1)} %get-tuple-element.336, f32[768]{0:T(1024)S(1)} %add_rsqrt_fusion.1, f32[768]{0:T(1024)S(1)} %broadcast_multiply_fusion.10, ...), kind=kOutput, calls=%fused_computation.54 | convolution fusion | flops 4851494912 | bytes 17321984 | tf_op jit(solution)/shard_map/dot_general | solution.py:28
  335.8 3.8 fusion.27
  350.9 9.4 %collective-permute-done.20 = bf16[1,8,64,1024]{3,2,1,0:T(8,128)(2,1)} collective-permute-done((bf16[1,8,64,1024]{3,2,1,0:T(8,128)(2,1)S(1)}, bf16[1,8,64,1024]{3,2,1,0:T(8,128)(2,1)}, u32[]{:S(2)}, u32[]{:S(2)}) %collective-permute-start.20) | collective-permute-done | bytes 1048608 | tf_op jit(solution)/shard_map/ppermute | solution.py:356
  360.3 3.7 convolution_convert_fusion.2
  369.7 3.9 convolution_convert_fusion.12
  378.3 15.3 %cross_attention.3 = f32[768,272]{1,0:T(8,128)} custom-call(s32[2]{0:T(128)} %get-tuple-element.228.big_ref, bf16[768,272]{1,0:T(8,128)(2,1)} %pad.22.query_ref, bf16[768,272]{1,0:T(8,128)(2,1)} %fusion.64.grad_ref, bf16[16,2,272,128]{3,2,1,0:T(8,128)(2,1)} %copy-done.1, bf16[16,2,272,128]{3,2,1,0:T(8,128)(2,1)} %bitcast.201, ...), custom_call_target="tpu_custom_call" | custom-call | tf_op jit(solution)/shard_map/cross_attention/pallas_call | solution.py:174
  399.4 5.1 all-to-all-start.4
  416.8 5.9 fusion.10
  436.8 11.5 %collective-permute-done.24 = bf16[1,8,96,1024]{3,2,1,0:T(8,128)(2,1)} collective-permute-done((bf16[1,8,96,1024]{3,2,1,0:T(8,128)(2,1)}, bf16[1,8,96,1024]{3,2,1,0:T(8,128)(2,1)}, u32[]{:S(2)}, u32[]{:S(2)}) %collective-permute-start.24) | collective-permute-done | bytes 1572896 | tf_op jit(solution)/shard_map/ppermute | solution.py:356
  448.3 4.4 all-to-all-done.4
  455.6 4.0 collective-permute-done.25
  465.0 18.5 %collective-permute-done.26 = bf16[1,8,56,1024]{3,2,1,0:T(8,128)(2,1)S(1)} collective-permute-done((bf16[1,8,56,1024]{3,2,1,0:T(8,128)(2,1)S(1)}, bf16[1,8,56,1024]{3,2,1,0:T(8,128)(2,1)S(1)}, u32[]{:S(2)}, u32[]{:S(2)}) %collective-permute-start.26) | collective-permute-done | bytes 917536 | tf_op jit(solution)/shard_map/ppermute | solution.py:356
  484.4 81.0 %all_to_all.25 = bf16[8,152,1024]{2,1,0:T(8,128)(2,1)} all-to-all(bf16[8,152,1024]{2,1,0:T(8,128)(2,1)S(1)} %pad_maximum_fusion.6), channel_id=1, replica_groups={{0,4,8,12,16,20,24,28},{2,6,10,14,18,22,26,30},{1,5,9,13,17,21,25,29},{..., dimensions={0} | all-to-all | bytes 4980736 | tf_op jit(solution)/shard_map/all_to_all | solution.py:519
  575.4 9.1 %collective-permute-done.27 = bf16[256,1024]{1,0:T(8,128)(2,1)S(1)} collective-permute-done((bf16[256,1024]{1,0:T(8,128)(2,1)S(1)}, bf16[256,1024]{1,0:T(8,128)(2,1)S(1)}, u32[]{:S(2)}, u32[]{:S(2)}) %collective-permute-start.27) | collective-permute-done | bytes 524320 | tf_op jit(solution)/shard_map/ppermute | solution.py:356
  585.4 9.4 %collective-permute-done.29 = bf16[256,1024]{1,0:T(8,128)(2,1)S(1)} collective-permute-done((bf16[256,1024]{1,0:T(8,128)(2,1)S(1)}, bf16[256,1024]{1,0:T(8,128)(2,1)S(1)}, u32[]{:S(2)}, u32[]{:S(2)}) %collective-permute-start.29) | collective-permute-done | bytes 524320 | tf_op jit(solution)/shard_map/ppermute | solution.py:356
  598.8 5.8 widen.1
  609.9 12.4 %all-gather.9.cloned.1.call-done = bf16[2432,1024]{1,0:T(8,128)(2,1)} async-done(((bf16[152,1024]{1,0:T(8,128)(2,1)}), bf16[2432,1024]{1,0:T(8,128)(2,1)}) %all-gather.9.cloned.1.call-update) | async-done | bytes 4980752 | tf_op jit(solution)/shard_map/all_gather | solution.py:527
  624.8 5.2 widen_each.1
  (535 shorter events, 254.6 us)
Async XLA Ops:
  17.5 53.1 %all-to-all-start = ((bf16[16,2,272,128]{3,2,1,0:T(8,128)(2,1)}), bf16[16,2,272,128]{3,2,1,0:T(8,128)(2,1)S(1)}, u32[]{:S(2)}, u32[]{:S(2)}) async-start(bf16[16,2,272,128]{3,2,1,0:T(8,128)(2,1)} %prepare_pixels.1), calls=%async_computation | async-start | bytes 4456448 | tf_op jit(solution)/shard_map/all_to_all | solution.py:554
  25.1 132.4 %all-gather.7.cloned.1.call-start = ((), (), s32[]{:S(2)}) async-start(), calls=%async_computation.5 | async-start | bytes 2367488 | tf_op jit(solution)/shard_map/all_gather | solution.py:590
  26.0 17.8 %collective-permute-start.3 = (bf16[256,1024]{1,0:T(8,128)(2,1)}, bf16[256,1024]{1,0:T(8,128)(2,1)}, u32[]{:S(2)}, u32[]{:S(2)}) collective-permute-start(bf16[256,1024]{1,0:T(8,128)(2,1)} %constant_dynamic-slice_fusion.7), channel_id=1, source_target_pairs={{0,1},{1,0},{2,3},{3,2},{4,5},{5,4},{6,7},{7,6},{8,9},{9,8},{10,11... | collective-permute-start | bytes 1572872 | tf_op jit(solution)/shard_map/ppermute | solution.py:356
  29.4 39.9 %collective-permute-start.2 = (bf16[265,1024]{1,0:T(8,128)(2,1)}, bf16[265,1024]{1,0:T(8,128)(2,1)}, u32[]{:S(2)}, u32[]{:S(2)}) collective-permute-start(bf16[265,1024]{1,0:T(8,128)(2,1)} %pad_maximum_fusion.42), channel_id=1, source_target_pairs={{0,1},{1,0},{2,3},{3,2},{4,5},{5,4},{6,7},{7,6},{8,9},{9,8},{10,11... | collective-permute-start | bytes 1628168 | tf_op jit(solution)/shard_map/ppermute | solution.py:356
  32.4 11.3 %collective-permute-start.1 = (bf16[256,1024]{1,0:T(8,128)(2,1)}, bf16[256,1024]{1,0:T(8,128)(2,1)S(1)}, u32[]{:S(2)}, u32[]{:S(2)}) collective-permute-start(bf16[256,1024]{1,0:T(8,128)(2,1)} %get-tuple-element.302), channel_id=1, source_target_pairs={{0,0},{2,1},{4,4},{6,5},{8,8},{10,9},{12,12},{14,13},{16,16},{18,1... | collective-permute-start | bytes 1572872 | tf_op jit(solution)/shard_map/ppermute | solution.py:399
  34.2 35.1 %collective-permute-start = (bf16[256,1024]{1,0:T(8,128)(2,1)}, bf16[256,1024]{1,0:T(8,128)(2,1)}, u32[]{:S(2)}, u32[]{:S(2)}) collective-permute-start(bf16[256,1024]{1,0:T(8,128)(2,1)} %get-tuple-element.303), channel_id=1, source_target_pairs={{0,1},{1,0},{2,3},{3,2},{4,5},{5,4},{6,7},{7,6},{8,9},{9,8},{10,11... | collective-permute-start | bytes 1572872 | tf_op jit(solution)/shard_map/ppermute | solution.py:356
  70.6 42.0 %collective-permute-start.5 = (bf16[256,3072]{1,0:T(8,128)(2,1)}, bf16[256,3072]{1,0:T(8,128)(2,1)}, u32[]{:S(2)}, u32[]{:S(2)}) collective-permute-start(bf16[256,3072]{1,0:T(8,128)(2,1)} %pad_maximum_fusion.20), channel_id=1, source_target_pairs={{0,1},{1,0},{2,3},{3,2},{4,5},{5,4},{6,7},{7,6},{8,9},{9,8},{10,11... | collective-permute-start | bytes 4718600 | tf_op jit(solution)/shard_map/ppermute | solution.py:356
  83.3 19.1 %collective-permute-start.4 = (bf16[256,1024]{1,0:T(8,128)(2,1)}, bf16[256,1024]{1,0:T(8,128)(2,1)}, u32[]{:S(2)}, u32[]{:S(2)}) collective-permute-start(bf16[256,1024]{1,0:T(8,128)(2,1)} %collective-permute-done.3), channel_id=1, source_target_pairs={{0,2},{2,0},{4,6},{6,4},{8,10},{10,8},{12,14},{14,12},{16,18},{18,... | collective-permute-start | bytes 1572872 | tf_op jit(solution)/shard_map/ppermute | solution.py:356
  89.4 64.6 %all-to-all-start.1 = ((bf16[16,2,272,128]{3,2,1,0:T(8,128)(2,1)}), bf16[16,2,272,128]{3,2,1,0:T(8,128)(2,1)S(1)}, u32[]{:S(2)}, u32[]{:S(2)}) async-start(bf16[16,2,272,128]{3,2,1,0:T(8,128)(2,1)} %bitcast.202), calls=%async_computation.1 | async-start | bytes 4456448 | tf_op jit(solution)/shard_map/all_to_all | solution.py:586
  100.8 24.3 %collective-permute-start.7 = (bf16[128,3072]{1,0:T(8,128)(2,1)S(1)}, bf16[128,3072]{1,0:T(8,128)(2,1)}, u32[]{:S(2)}, u32[]{:S(2)}) collective-permute-start(bf16[128,3072]{1,0:T(8,128)(2,1)S(1)} %constant_dynamic-slice_fusion.3), channel_id=1, source_target_pairs={{0,1},{1,0},{2,3},{3,2},{4,5},{5,4},{6,7},{7,6},{8,9},{9,8},{10,11... | collective-permute-start | bytes 2359304 | tf_op jit(solution)/shard_map/ppermute | solution.py:356
  113.8 58.3 %collective-permute-start.11 = (bf16[128,3072]{1,0:T(8,128)(2,1)}, bf16[128,3072]{1,0:T(8,128)(2,1)}, u32[]{:S(2)}, u32[]{:S(2)}) collective-permute-start(bf16[128,3072]{1,0:T(8,128)(2,1)} %pad_maximum_fusion.41), channel_id=1, source_target_pairs={{0,1},{1,0},{2,3},{3,2},{4,5},{5,4},{6,7},{7,6},{8,9},{9,8},{10,11... | collective-permute-start | bytes 2359304 | tf_op jit(solution)/shard_map/ppermute | solution.py:356
  154.0 39.8 %collective-permute-start.8 = (bf16[128,3072]{1,0:T(8,128)(2,1)}, bf16[128,3072]{1,0:T(8,128)(2,1)}, u32[]{:S(2)}, u32[]{:S(2)}) collective-permute-start(bf16[128,3072]{1,0:T(8,128)(2,1)} %collective-permute-done.7), channel_id=1, source_target_pairs={{0,4},{2,6},{4,0},{6,2},{8,12},{10,14},{12,8},{14,10},{16,20},{18,... | collective-permute-start | bytes 2359304 | tf_op jit(solution)/shard_map/ppermute | solution.py:356
  172.1 24.4 %collective-permute-start.12 = (bf16[128,3072]{1,0:T(8,128)(2,1)}, bf16[128,3072]{1,0:T(8,128)(2,1)S(1)}, u32[]{:S(2)}, u32[]{:S(2)}) collective-permute-start(bf16[128,3072]{1,0:T(8,128)(2,1)} %collective-permute-done.11), channel_id=1, source_target_pairs={{0,4},{2,6},{4,0},{6,2},{8,12},{10,14},{12,8},{14,10},{16,20},{18,... | collective-permute-start | bytes 2359304 | tf_op jit(solution)/shard_map/ppermute | solution.py:356
  173.4 54.6 %collective-permute-start.15 = (bf16[256,1024]{1,0:T(8,128)(2,1)}, bf16[256,1024]{1,0:T(8,128)(2,1)}, u32[]{:S(2)}, u32[]{:S(2)}) collective-permute-start(bf16[256,1024]{1,0:T(8,128)(2,1)} %get-tuple-element.295), channel_id=1, source_target_pairs={{0,0},{2,1},{4,4},{6,5},{8,8},{10,9},{12,12},{14,13},{16,16},{18,1... | collective-permute-start | bytes 1572872 | tf_op jit(solution)/shard_map/ppermute | solution.py:399
  179.2 48.8 %collective-permute-start.14 = (bf16[256,1024]{1,0:T(8,128)(2,1)}, bf16[256,1024]{1,0:T(8,128)(2,1)}, u32[]{:S(2)}, u32[]{:S(2)}) collective-permute-start(bf16[256,1024]{1,0:T(8,128)(2,1)} %get-tuple-element.296), channel_id=1, source_target_pairs={{0,1},{1,0},{2,3},{3,2},{4,5},{5,4},{6,7},{7,6},{8,9},{9,8},{10,11... | collective-permute-start | bytes 1572872 | tf_op jit(solution)/shard_map/ppermute | solution.py:356
  198.5 9.1 %collective-permute-start.13 = (bf16[256,3072]{1,0:T(8,128)(2,1)S(1)}, bf16[256,3072]{1,0:T(8,128)(2,1)S(1)}, u32[]{:S(2)}, u32[]{:S(2)}) collective-permute-start(bf16[256,3072]{1,0:T(8,128)(2,1)S(1)} %pad_maximum_fusion.22), channel_id=1, source_target_pairs={{0,2},{2,0},{4,6},{6,4},{8,10},{10,8},{12,14},{14,12},{16,18},{18,... | collective-permute-start | bytes 4718600 | tf_op jit(solution)/shard_map/ppermute | solution.py:356
  255.0 31.4 %collective-permute-start.17 = (bf16[1,8,64,1024]{3,2,1,0:T(8,128)(2,1)}, bf16[1,8,64,1024]{3,2,1,0:T(8,128)(2,1)}, u32[]{:S(2)}, u32[]{:S(2)}) collective-permute-start(bf16[1,8,64,1024]{3,2,1,0:T(8,128)(2,1)} %add_convert_fusion.16), channel_id=1, source_target_pairs={{0,1},{1,0},{2,3},{3,2},{4,5},{5,4},{6,7},{7,6},{8,9},{9,8},{10,11... | collective-permute-start | bytes 3145736 | tf_op jit(solution)/shard_map/ppermute | solution.py:356
  286.4 14.7 %collective-permute-start.18 = (bf16[256,2048]{1,0:T(8,128)(2,1)}, bf16[256,2048]{1,0:T(8,128)(2,1)}, u32[]{:S(2)}, u32[]{:S(2)}) collective-permute-start(bf16[256,2048]{1,0:T(8,128)(2,1)} %get-tuple-element.77), channel_id=1, source_target_pairs={{0,2},{2,0},{4,6},{6,4},{8,10},{10,8},{12,14},{14,12},{16,18},{18,... | collective-permute-start | bytes 3145736 | tf_op jit(solution)/shard_map/ppermute | solution.py:356
  294.8 65.5 %all-to-all-start.2 = ((bf16[8,64,1024]{2,1,0:T(8,128)(2,1)}), bf16[8,64,1024]{2,1,0:T(8,128)(2,1)}, u32[]{:S(2)}, u32[]{:S(2)}) async-start(bf16[8,64,1024]{2,1,0:T(8,128)(2,1)} %fusion.46), calls=%async_computation.2 | async-start | bytes 2097152 | tf_op jit(solution)/shard_map/all_to_all | solution.py:519
  313.8 19.4 %collective-permute-start.19 = (bf16[2,8,64,1024]{3,2,1,0:T(8,128)(2,1)}, bf16[2,8,64,1024]{3,2,1,0:T(8,128)(2,1)}, u32[]{:S(2)}, u32[]{:S(2)}) collective-permute-start(bf16[2,8,64,1024]{3,2,1,0:T(8,128)(2,1)} %pad_maximum_fusion.15), channel_id=1, source_target_pairs={{0,2},{2,0},{4,6},{6,4},{8,10},{10,8},{12,14},{14,12},{16,18},{18,... | collective-permute-start | bytes 6291464 | tf_op jit(solution)/shard_map/ppermute | solution.py:356
  315.7 29.2 %collective-permute-start.21 = (bf16[2,8,64,1024]{3,2,1,0:T(8,128)(2,1)}, bf16[2,8,64,1024]{3,2,1,0:T(8,128)(2,1)}, u32[]{:S(2)}, u32[]{:S(2)}) collective-permute-start(bf16[2,8,64,1024]{3,2,1,0:T(8,128)(2,1)} %pad_maximum_fusion.16), channel_id=1, source_target_pairs={{0,2},{2,0},{4,6},{6,4},{8,10},{10,8},{12,14},{14,12},{16,18},{18,... | collective-permute-start | bytes 6291464 | tf_op jit(solution)/shard_map/ppermute | solution.py:356
  335.0 25.2 %collective-permute-start.20 = (bf16[1,8,64,1024]{3,2,1,0:T(8,128)(2,1)S(1)}, bf16[1,8,64,1024]{3,2,1,0:T(8,128)(2,1)}, u32[]{:S(2)}, u32[]{:S(2)}) collective-permute-start(bf16[1,8,64,1024]{3,2,1,0:T(8,128)(2,1)S(1)} %add_convert_fusion.14), channel_id=1, source_target_pairs={{0,1},{1,0},{2,3},{3,2},{4,5},{5,4},{6,7},{7,6},{8,9},{9,8},{10,11... | collective-permute-start | bytes 3145736 | tf_op jit(solution)/shard_map/ppermute | solution.py:356
  367.2 41.6 %collective-permute-start.23 = (bf16[2,8,96,1024]{3,2,1,0:T(8,128)(2,1)}, bf16[2,8,96,1024]{3,2,1,0:T(8,128)(2,1)}, u32[]{:S(2)}, u32[]{:S(2)}) collective-permute-start(bf16[2,8,96,1024]{3,2,1,0:T(8,128)(2,1)} %pad_maximum_fusion.4), channel_id=1, source_target_pairs={{0,2},{2,0},{4,6},{6,4},{8,10},{10,8},{12,14},{14,12},{16,18},{18,... | collective-permute-start | bytes 9437192 | tf_op jit(solution)/shard_map/ppermute | solution.py:356
  367.3 26.3 %collective-permute-start.22 = (bf16[1,8,64,1024]{3,2,1,0:T(8,128)(2,1)}, bf16[1,8,64,1024]{3,2,1,0:T(8,128)(2,1)S(1)}, u32[]{:S(2)}, u32[]{:S(2)}) collective-permute-start(bf16[1,8,64,1024]{3,2,1,0:T(8,128)(2,1)} %add_convert_fusion.13), channel_id=1, source_target_pairs={{0,1},{1,0},{2,3},{3,2},{4,5},{5,4},{6,7},{7,6},{8,9},{9,8},{10,11... | collective-permute-start | bytes 3145736 | tf_op jit(solution)/shard_map/ppermute | solution.py:356
  399.4 53.3 %all-to-all-start.4 = ((bf16[8,128,1024]{2,1,0:T(8,128)(2,1)}), bf16[8,128,1024]{2,1,0:T(8,128)(2,1)}, u32[]{:S(2)}, u32[]{:S(2)}) async-start(bf16[8,128,1024]{2,1,0:T(8,128)(2,1)} %pad_maximum_fusion.17), calls=%async_computation.4 | async-start | bytes 4194304 | tf_op jit(solution)/shard_map/all_to_all | solution.py:519
  404.5 194.3 %all-gather.11.cloned.1.call-start = ((), (), s32[]{:S(2)}) async-start(), calls=%async_computation.7 | async-start | bytes 6684672 | tf_op jit(solution)/shard_map/all_gather | solution.py:527
  412.3 36.0 %collective-permute-start.24 = (bf16[1,8,96,1024]{3,2,1,0:T(8,128)(2,1)}, bf16[1,8,96,1024]{3,2,1,0:T(8,128)(2,1)}, u32[]{:S(2)}, u32[]{:S(2)}) collective-permute-start(bf16[1,8,96,1024]{3,2,1,0:T(8,128)(2,1)} %add_convert_fusion.2), channel_id=1, source_target_pairs={{0,1},{1,0},{2,3},{3,2},{4,5},{5,4},{6,7},{7,6},{8,9},{9,8},{10,11... | collective-permute-start | bytes 4718600 | tf_op jit(solution)/shard_map/ppermute | solution.py:356
  455.4 166.8 %all-gather.9.cloned.1.call-start = ((), (), s32[]{:S(2)}) async-start(), calls=%async_computation.6 | async-start | bytes 5292032 | tf_op jit(solution)/shard_map/all_gather | solution.py:527
  461.1 22.5 %collective-permute-start.26 = (bf16[1,8,56,1024]{3,2,1,0:T(8,128)(2,1)S(1)}, bf16[1,8,56,1024]{3,2,1,0:T(8,128)(2,1)S(1)}, u32[]{:S(2)}, u32[]{:S(2)}) collective-permute-start(bf16[1,8,56,1024]{3,2,1,0:T(8,128)(2,1)S(1)} %add_convert_fusion.19), channel_id=1, source_target_pairs={{0,1},{1,0},{2,3},{3,2},{4,5},{5,4},{6,7},{7,6},{8,9},{9,8},{10,11... | collective-permute-start | bytes 2752520 | tf_op jit(solution)/shard_map/ppermute | solution.py:356
  569.6 14.9 %collective-permute-start.27 = (bf16[256,1024]{1,0:T(8,128)(2,1)S(1)}, bf16[256,1024]{1,0:T(8,128)(2,1)S(1)}, u32[]{:S(2)}, u32[]{:S(2)}) collective-permute-start(bf16[256,1024]{1,0:T(8,128)(2,1)S(1)} %slice.203), channel_id=1, source_target_pairs={{0,1},{1,0},{2,3},{3,2},{4,5},{5,4},{6,7},{7,6},{8,9},{9,8},{10,11... | collective-permute-start | bytes 1572872 | tf_op jit(solution)/shard_map/ppermute | solution.py:356
  574.8 20.0 %collective-permute-start.29 = (bf16[256,1024]{1,0:T(8,128)(2,1)S(1)}, bf16[256,1024]{1,0:T(8,128)(2,1)S(1)}, u32[]{:S(2)}, u32[]{:S(2)}) collective-permute-start(bf16[256,1024]{1,0:T(8,128)(2,1)S(1)} %slice.206), channel_id=1, source_target_pairs={{0,1},{1,0},{2,3},{3,2},{4,5},{5,4},{6,7},{7,6},{8,9},{9,8},{10,11... | collective-permute-start | bytes 1572872 | tf_op jit(solution)/shard_map/ppermute | solution.py:356
  584.7 10.9 %collective-permute-start.28 = (bf16[256,1024]{1,0:T(8,128)(2,1)S(1)}, bf16[256,1024]{1,0:T(8,128)(2,1)S(1)}, u32[]{:S(2)}, u32[]{:S(2)}) collective-permute-start(bf16[256,1024]{1,0:T(8,128)(2,1)S(1)} %get-tuple-element.291), channel_id=1, source_target_pairs={{0,0},{2,1},{4,4},{6,5},{8,8},{10,9},{12,12},{14,13},{16,16},{18,1... | collective-permute-start | bytes 1572872 | tf_op jit(solution)/shard_map/ppermute | solution.py:399
  (137 other events, 1278.8 us)
Sparse Core Ops, SparseCore 0:
  83.4 70.3 all-gather.6
  455.6 85.3 all-gather.10
  568.6 53.5 all-gather.8
